TPU v7x, 32 devices: a whole 2x2x4 slice. The times are simulated.
32 devices in a mesh: mp: 2 (over y), dp: 16 (over z, x, core).
Axes of the slice: x: 2, y: 2, z: 4, core: 2. Of those that a mesh axis runs over, the one named last changes fastest.
Arguments:
- stream: bfloat16 [32768, 1024], P(('dp', 'mp')), may hold values from -6 to 6
- cotangent: bfloat16 [32768, 1024], P(('dp', 'mp')), may hold values from -6 to 6
- segments: int32 [16, 2048], P('dp'), may hold values from 0 to 7, never falling along the last dimension, each value on 1 to 1500 neighbouring positions
- owners: int32 [2, 736], P('mp'), may hold values from 0 to 735, as said below
- master: float32 [2, 736, 128, 128], P('mp', 'dp'), may hold values from -1 to 1
- average: float32 [2, 736, 128, 128], P('mp', 'dp'), may hold values from -1 to 1
- left_stats: float32 [2, 736, 128, 128], P('mp', 'dp'), may hold values from -27596 to 55189, as said below
- right_stats: float32 [2, 736, 128, 128], P('mp', 'dp'), may hold values from -27596 to 55189, as said below
- left_root: float32 [2, 736, 128, 128], P('mp', 'dp'), may hold values from -4 to 10, as said below
- right_root: float32 [2, 736, 128, 128], P('mp', 'dp'), may hold values from -4 to 10, as said below
- gains: float32 [5, 1024], replicated, may hold values from 0.5 to 1.5
- kernel: float32 [5, 1024], replicated, may hold values from -2.5 to 2.5
Outputs:
- output: bfloat16 [32768, 1024], P(('dp', 'mp'))
- stream_grad: float32 [32768, 1024], P(('dp', 'mp'))
- block_grads: float32 [2, 736, 128, 128], P('mp', 'dp')
- left_new: float32 [2, 736, 128, 128], P('mp', 'dp')
- right_new: float32 [2, 736, 128, 128], P('mp', 'dp')
- master_new: float32 [2, 736, 128, 128], P('mp', 'dp')
- average_new: float32 [2, 736, 128, 128], P('mp', 'dp')
- gain_grads: float32 [5, 1024], replicated
- gains_new: float32 [5, 1024], replicated
- kernel_grads: float32 [5, 1024], replicated
- kernel_new: float32 [5, 1024], replicated
Inputs may be any that keep to these rules, and one draw needn't show every extreme that they name: `owners`: each row names 736 different slots. `segments`: along each row the numbers never fall, every number up to 7 is used, and no number holds more than 1500 rows. `left_stats`: each block is symmetric. `right_stats`: each block is symmetric. `left_root`: each block is symmetric. `right_root`: each block is symmetric.
All inputs are finite; a program needn't handle non-finite values.
Results may differ from a plain program's by a relative error of at most 0.025.
Values may be sent and summed in bfloat16 or wider, within the bound.
No kernel may reach another device: no remote copies, remote signals or barrier semaphores. Data moves between devices by JAX's collectives and lax.ppermute only.
A program may use at most 320 MiB of HBM per device.

v0:
```python
import math

import jax
import jax.numpy as jnp
from jax import lax
from jax.sharding import PartitionSpec as P

D = 1024
FF = 4096
HEADS = 8
HEAD_DIM = 128
KERNEL = 5
STEP = 4
BLOCK = 128
ATT_ROWS = 512


EPSILON = 1e-05
DECAY_STAT = 0.95
RATE_BLOCK = 0.02
RATE_VECTOR = 0.2
DECAY_AVERAGE = 0.9999
MASKED = -1e30
HIGH = lax.Precision.HIGHEST


def silu(values):
    return values * jax.nn.sigmoid(values)


def silu_slope(values):
    sigma = jax.nn.sigmoid(values)
    return sigma * (1.0 + values * (1.0 - sigma))


def layer_norm(values, norm_gain):
    center = values - jnp.mean(values, axis=-1, keepdims=True)
    spread = jnp.mean(center * center, axis=-1, keepdims=True)
    return center * lax.rsqrt(spread + EPSILON) * norm_gain


def norm_back(values, norm_gain, grad_out):
    unused, pullback = jax.vjp(layer_norm, values, norm_gain)
    return pullback(grad_out)


def dense(left_op, right_op):
    return jnp.dot(left_op, right_op, preferred_element_type=jnp.float32)


def dense_left(left_op, right_op):
    return lax.dot_general(
        left_op, right_op, (((0,), (0,)), ((), ())), preferred_element_type=jnp.float32
    )


def dense_right(left_op, right_op):
    return lax.dot_general(
        left_op, right_op, (((1,), (1,)), ((), ())), preferred_element_type=jnp.float32
    )


def shard_shapes(ranks):
    fshard = FF // ranks
    cshard = D // ranks
    return [
        (D, fshard),
        (fshard, D),
        (D, cshard),
        (D, cshard),
        (D, cshard),
        (cshard, D),
        (D, cshard),
        (D, cshard),
        (cshard, D),
        (D, fshard),
        (fshard, D),
    ]


def unblock(blocks, height, breadth):
    shaped = blocks.reshape(height // BLOCK, breadth // BLOCK, BLOCK, BLOCK)
    return shaped.transpose(0, 2, 1, 3).reshape(height, breadth)


def regroup_blocks(square_matrix):
    height, breadth = square_matrix.shape
    shaped = square_matrix.reshape(height // BLOCK, BLOCK, breadth // BLOCK, BLOCK)
    return shaped.transpose(0, 2, 1, 3).reshape(-1, BLOCK, BLOCK)


def split_blocks(blocks, ranks):
    pieces = []
    offset = 0
    for height, breadth in shard_shapes(ranks):
        block_count = height * breadth // (BLOCK * BLOCK)
        pieces.append(unblock(blocks[offset : offset + block_count], height, breadth))
        offset = offset + block_count
    return pieces


def neighbour_masks(segment_ids):
    half = KERNEL // 2
    length = segment_ids.shape[0]
    padded = jnp.pad(segment_ids, (half, half), constant_values=-1)
    return [
        (padded[tap_index : tap_index + length] == segment_ids).astype(jnp.float32)[:, None]
        for tap_index in range(KERNEL)
    ]


def depthwise(glu_rows, taps, seg_masks):
    half = KERNEL // 2
    length = glu_rows.shape[0]
    padded = jnp.pad(glu_rows, ((half, half), (0, 0)))
    summed = jnp.zeros_like(glu_rows)
    for tap_index in range(KERNEL):
        summed = (
            summed + taps[tap_index] * padded[tap_index : tap_index + length] * seg_masks[tap_index]
        )
    return summed


def depthwise_back(glu_rows, taps, seg_masks, grad_out):
    half = KERNEL // 2
    length = glu_rows.shape[0]
    padded_glu = jnp.pad(glu_rows, ((half, half), (0, 0)))
    glu_grad = jnp.zeros_like(glu_rows)
    tap_grads = []
    for tap_index in range(KERNEL):
        masked_grad = grad_out * seg_masks[tap_index]
        padded_grad = jnp.pad(masked_grad, ((half, half), (0, 0)))
        start_row = 2 * half - tap_index
        glu_grad = glu_grad + taps[tap_index] * padded_grad[start_row : start_row + length]
        tap_grads.append(jnp.sum(masked_grad * padded_glu[tap_index : tap_index + length], axis=0))
    return (glu_grad, jnp.stack(tap_grads))


def split_rows(array):
    return array.reshape((array.shape[0] // ATT_ROWS, ATT_ROWS) + array.shape[1:])


def score_rows(query_block, query_seg, query_pos, key_rows, segment_ids, slopes):
    length = key_rows.shape[0]
    raw_scores = jnp.einsum(
        "qhd,khd->hqk", query_block, key_rows, preferred_element_type=jnp.float32
    )
    key_pos = jnp.arange(length)
    distance = jnp.abs(query_pos[:, None] - key_pos[None, :]).astype(jnp.float32)
    scores = (
        raw_scores * (1.0 / math.sqrt(query_block.shape[-1]))
        - slopes[:, None, None] * distance[None]
    )
    same_seg = (query_seg[:, None] == segment_ids[None, :])[None]
    return (scores, same_seg)


def attend_forward(queries, key_rows, value_rows, segment_ids, slopes):
    length, heads_local, head_width = queries.shape
    positions = jnp.arange(length)

    def per_query(query_items):
        query_block, query_seg, query_pos = query_items
        scores, same_seg = score_rows(
            query_block, query_seg, query_pos, key_rows, segment_ids, slopes
        )
        masked = jnp.where(same_seg, scores, MASKED)
        row_peak = jnp.max(masked, axis=-1)
        shifted = jnp.where(same_seg, jnp.exp(masked - row_peak[..., None]), 0.0)
        log_total = row_peak + jnp.log(jnp.sum(shifted, axis=-1))
        weights = jnp.where(same_seg, jnp.exp(scores - log_total[..., None]), 0.0).astype(
            jnp.bfloat16
        )
        mixed = jnp.einsum("hqk,khd->qhd", weights, value_rows, preferred_element_type=jnp.float32)
        return (log_total, mixed)

    log_totals, mixed_sum = lax.map(
        per_query, (split_rows(queries), split_rows(segment_ids), split_rows(positions))
    )
    return (log_totals, mixed_sum.reshape(length, heads_local, head_width))


def attend_back(queries, key_rows, value_rows, segment_ids, slopes, log_totals, out_grad, deltas):
    length, heads_local, head_width = queries.shape
    score_scale = 1.0 / math.sqrt(head_width)
    positions = jnp.arange(length)
    zero_keys = jnp.zeros((length, heads_local, head_width), jnp.float32)

    def per_query(sums, query_items):
        key_sum, value_sum = sums
        query_block, query_seg, query_pos, log_total, grad_block, delta_block = query_items
        scores, same_seg = score_rows(
            query_block, query_seg, query_pos, key_rows, segment_ids, slopes
        )
        probs = jnp.where(same_seg, jnp.exp(scores - log_total[..., None]), 0.0)
        prob_grad = jnp.einsum(
            "qhd,khd->hqk", grad_block, value_rows, preferred_element_type=jnp.float32
        )
        score_grad = (probs * (prob_grad - delta_block[..., None])).astype(jnp.bfloat16)
        query_grad = (
            jnp.einsum("hqk,khd->qhd", score_grad, key_rows, preferred_element_type=jnp.float32)
            * score_scale
        )
        key_part = (
            jnp.einsum("hqk,qhd->khd", score_grad, query_block, preferred_element_type=jnp.float32)
            * score_scale
        )
        value_part = jnp.einsum(
            "hqk,qhd->khd",
            probs.astype(jnp.bfloat16),
            grad_block,
            preferred_element_type=jnp.float32,
        )
        return ((key_sum + key_part, value_sum + value_part), query_grad)

    (key_sum, value_sum), query_grads = lax.scan(
        per_query,
        (zero_keys, zero_keys),
        (
            split_rows(queries),
            split_rows(segment_ids),
            split_rows(positions),
            log_totals,
            split_rows(out_grad),
            deltas,
        ),
    )
    width_all = heads_local * head_width
    return (
        query_grads.reshape(length, width_all),
        key_sum.reshape(length, width_all),
        value_sum.reshape(length, width_all),
    )


def vector_step(params, grads):
    mean_sq = jnp.mean(grads * grads, axis=-1, keepdims=True)
    return params - RATE_VECTOR * grads * lax.rsqrt(mean_sq + 1e-06)


def shampoo(grads, left_stats, right_stats, left_root, right_root, master, average):
    left_new = DECAY_STAT * left_stats + (1.0 - DECAY_STAT) * jnp.einsum(
        "...ij,...kj->...ik", grads, grads, precision=HIGH
    )
    right_new = DECAY_STAT * right_stats + (1.0 - DECAY_STAT) * jnp.einsum(
        "...ji,...jk->...ik", grads, grads, precision=HIGH
    )
    inner_side = jnp.einsum("...ij,...jk->...ik", grads, right_root, precision=HIGH)
    direction = jnp.einsum("...ij,...jk->...ik", left_root, inner_side, precision=HIGH)
    mean_sq = jnp.mean(direction * direction, axis=(-2, -1), keepdims=True)
    master_new = master - RATE_BLOCK * direction * lax.rsqrt(mean_sq + 1e-06)
    old_bias = 1.0 - DECAY_AVERAGE ** (STEP - 1)
    new_bias = 1.0 - DECAY_AVERAGE**STEP
    average_new = (
        DECAY_AVERAGE * (average * old_bias) + (1.0 - DECAY_AVERAGE) * master_new
    ) / new_bias
    return (left_new, right_new, master_new, average_new)


def gather_rows(values):
    return lax.all_gather(values, "mp", axis=0, tiled=True)


def row_totals(partial_value):
    return lax.psum_scatter(
        partial_value.astype(jnp.bfloat16), "mp", scatter_dimension=0, tiled=True
    ).astype(jnp.float32)


def gather_grads(values):
    return lax.all_gather(values, "mp", axis=0, tiled=True)


def sum_grads(partial_value):
    return lax.psum_scatter(
        partial_value.astype(jnp.bfloat16), "mp", scatter_dimension=0, tiled=True
    ).astype(jnp.float32)


def inputs_for(normed):
    return lax.all_gather(normed, "mp", axis=0, tiled=True)


def reduce_blocks(gradient_listing):
    stacked_pieces = jnp.concatenate(
        [regroup_blocks(gradient_matrix) for gradient_matrix in gradient_listing], axis=0
    )
    return stacked_pieces


def local(
    stream,
    cotangent,
    segments,
    owners,
    master,
    average,
    left_stats,
    right_stats,
    left_root,
    right_root,
    gains,
    kernel,
):
    ranks = lax.axis_size("mp")
    model_parallel_rank = lax.axis_index("mp")
    slot_dev = master.shape[1]
    slot_total = slot_dev * lax.axis_size("dp")
    owned = owners[0]
    fetched = lax.all_gather(master.astype(jnp.bfloat16), "dp", axis=1, tiled=True)[0]
    (
        up_first,
        down_first,
        query_weight,
        key_weight,
        value_weight,
        out_weight,
        conv_value,
        conv_gate,
        conv_out,
        up_second,
        down_second,
    ) = split_blocks(jnp.take(fetched, owned, axis=0), ranks)
    cshard = D // ranks
    heads_local = cshard // HEAD_DIM
    segment_ids = segments[0]
    length = segment_ids.shape[0]
    all_slopes = 2.0 ** (-8.0 * (jnp.arange(HEADS).astype(jnp.float32) + 1.0) / HEADS)
    slopes = lax.dynamic_slice_in_dim(all_slopes, model_parallel_rank * heads_local, heads_local)
    taps = lax.dynamic_slice_in_dim(kernel, model_parallel_rank * cshard, cshard, 1)
    seg_masks = neighbour_masks(segment_ids)

    def ffn_forward(current, norm_gain, upper, lower):
        normed = layer_norm(current, norm_gain).astype(jnp.bfloat16)
        gathered = gather_rows(normed)
        pre_act = dense(gathered, upper)
        activated = silu(pre_act).astype(jnp.bfloat16)
        return (
            current + 0.5 * row_totals(dense(activated, lower)),
            (normed, gathered, pre_act, activated),
        )

    def ffn_back(grad_stream, current, saved, norm_gain, upper, lower):
        normed, gathered, pre_act, activated = saved
        incoming = gather_grads((0.5 * grad_stream).astype(jnp.bfloat16))
        pre_grad = (dense_right(incoming, lower) * silu_slope(pre_act)).astype(jnp.bfloat16)
        upper_grad = dense_left(inputs_for(normed), pre_grad)
        lower_grad = dense_left(activated, incoming)
        input_back, gain_grad = norm_back(
            current, norm_gain, sum_grads(dense_right(pre_grad, upper))
        )
        return (grad_stream + input_back, gain_grad, reduce_blocks([upper_grad, lower_grad]))

    stream_in = stream.astype(jnp.float32)
    after_first, saved_first = ffn_forward(stream_in, gains[0], up_first, down_first)
    normed_attn = layer_norm(after_first, gains[1]).astype(jnp.bfloat16)
    gathered_attn = gather_rows(normed_attn)
    queries = (
        dense(gathered_attn, query_weight)
        .astype(jnp.bfloat16)
        .reshape(length, heads_local, HEAD_DIM)
    )
    key_rows = (
        dense(gathered_attn, key_weight).astype(jnp.bfloat16).reshape(length, heads_local, HEAD_DIM)
    )
    value_rows = (
        dense(gathered_attn, value_weight)
        .astype(jnp.bfloat16)
        .reshape(length, heads_local, HEAD_DIM)
    )
    log_totals, mixed_sum = attend_forward(queries, key_rows, value_rows, segment_ids, slopes)
    attended = mixed_sum.astype(jnp.bfloat16).reshape(length, cshard)
    after_attn = after_first + row_totals(dense(attended, out_weight))
    normed_conv = layer_norm(after_attn, gains[2]).astype(jnp.bfloat16)
    gathered_conv = gather_rows(normed_conv)
    linear = dense(gathered_conv, conv_value)
    gate_pre = dense(gathered_conv, conv_gate)
    gate_sigma = jax.nn.sigmoid(gate_pre)
    glu_rows = linear * gate_sigma
    conved = depthwise(glu_rows, taps, seg_masks)
    conv_act = silu(conved).astype(jnp.bfloat16)
    after_conv = after_attn + row_totals(dense(conv_act, conv_out))
    after_second, saved_second = ffn_forward(after_conv, gains[3], up_second, down_second)
    output = layer_norm(after_second, gains[4]).astype(jnp.bfloat16)
    grad_last, gain_last = norm_back(after_second, gains[4], cotangent.astype(jnp.float32))
    grad_conv, gain_ffn_two, blocks_ffn_two = ffn_back(
        grad_last, after_conv, saved_second, gains[3], up_second, down_second
    )
    incoming_conv = gather_grads(grad_conv.astype(jnp.bfloat16))
    conved_grad = dense_right(incoming_conv, conv_out) * silu_slope(conved)
    glu_grad, tap_grads = depthwise_back(glu_rows, taps, seg_masks, conved_grad)
    linear_grad = (glu_grad * gate_sigma).astype(jnp.bfloat16)
    gate_grad = (glu_grad * linear * gate_sigma * (1.0 - gate_sigma)).astype(jnp.bfloat16)
    conv_inputs = inputs_for(normed_conv)
    conv_blocks = reduce_blocks(
        [
            dense_left(conv_inputs, linear_grad),
            dense_left(conv_inputs, gate_grad),
            dense_left(conv_act, incoming_conv),
        ]
    )
    conv_partial = dense_right(linear_grad, conv_value) + dense_right(gate_grad, conv_gate)
    input_back_conv, gain_conv = norm_back(after_attn, gains[2], sum_grads(conv_partial))
    grad_attn = grad_conv + input_back_conv
    incoming_attn = gather_grads(grad_attn.astype(jnp.bfloat16))
    out_grad = (
        dense_right(incoming_attn, out_weight)
        .astype(jnp.bfloat16)
        .reshape(length, heads_local, HEAD_DIM)
    )
    out_weight_grad = dense_left(attended, incoming_attn)
    row_deltas = jnp.sum(out_grad.astype(jnp.float32) * mixed_sum, axis=-1)
    deltas = split_rows(row_deltas).transpose(0, 2, 1)
    query_grad, key_grad, value_grad = attend_back(
        queries, key_rows, value_rows, segment_ids, slopes, log_totals, out_grad, deltas
    )
    query_grad = query_grad.astype(jnp.bfloat16)
    key_grad = key_grad.astype(jnp.bfloat16)
    value_grad = value_grad.astype(jnp.bfloat16)
    attn_inputs = inputs_for(normed_attn)
    attn_blocks = reduce_blocks(
        [
            dense_left(attn_inputs, query_grad),
            dense_left(attn_inputs, key_grad),
            dense_left(attn_inputs, value_grad),
            out_weight_grad,
        ]
    )
    attn_partial = (
        dense_right(query_grad, query_weight)
        + dense_right(key_grad, key_weight)
        + dense_right(value_grad, value_weight)
    )
    input_gradient_attention, gain_attn = norm_back(after_first, gains[1], sum_grads(attn_partial))
    grad_first = grad_attn + input_gradient_attention
    grad_stream, gain_ffn_one, blocks_ffn_one = ffn_back(
        grad_first, stream_in, saved_first, gains[0], up_first, down_first
    )
    all_grads = jnp.concatenate([blocks_ffn_one, attn_blocks, conv_blocks, blocks_ffn_two], axis=0)
    slot_match = owned[None, :] == jnp.arange(slot_total)[:, None]
    slot_source = jnp.sum(jnp.where(slot_match, jnp.arange(owned.shape[0])[None, :], 0), axis=1)
    slot_filled = jnp.any(slot_match, axis=1).astype(jnp.float32)[:, None, None]
    own_grads = lax.psum_scatter(
        (jnp.take(all_grads, slot_source, axis=0) * slot_filled).astype(jnp.bfloat16),
        "dp",
        scatter_dimension=0,
        tiled=True,
    ).astype(jnp.float32)
    gain_partial = jnp.stack([gain_ffn_one, gain_attn, gain_conv, gain_ffn_two, gain_last])
    kernel_partial = lax.dynamic_update_slice_in_dim(
        jnp.zeros_like(kernel), tap_grads, model_parallel_rank * cshard, 1
    )
    gain_grads, kernel_grads = lax.psum((gain_partial, kernel_partial), ("mp", "dp"))
    left_new, right_new, master_new, average_new = shampoo(
        own_grads, left_stats[0], right_stats[0], left_root[0], right_root[0], master[0], average[0]
    )
    return (
        output,
        grad_stream,
        own_grads[None],
        left_new[None],
        right_new[None],
        master_new[None],
        average_new[None],
        gain_grads,
        vector_step(gains, gain_grads),
        kernel_grads,
        vector_step(kernel, kernel_grads),
    )


def solution(mesh):
    return jax.shard_map(
        local,
        mesh=mesh,
        in_specs=(
            P(("dp", "mp"), None),
            P(("dp", "mp"), None),
            P("dp", None),
            P("mp", None),
            P("mp", "dp", None, None),
            P("mp", "dp", None, None),
            P("mp", "dp", None, None),
            P("mp", "dp", None, None),
            P("mp", "dp", None, None),
            P("mp", "dp", None, None),
            P(),
            P(),
        ),
        out_specs=(
            P(("dp", "mp"), None),
            P(("dp", "mp"), None),
            P("mp", "dp", None, None),
            P("mp", "dp", None, None),
            P("mp", "dp", None, None),
            P("mp", "dp", None, None),
            P("mp", "dp", None, None),
            P(),
            P(),
            P(),
            P(),
        ),
        check_vma=False,
    )
```

profile of v0, /device:TPU:0, one launch (start us, length us, event | category | flops | bytes accessed | tf_op | source)
XLA Modules:
  0.0 2061.5 jit_solution(10546730255026212768)
XLA Ops:
  19.6 117.6 %all-gather.12.cloned.1.call-done = bf16[1,736,128,128]{3,2,0,1:T(8,128)(2,1)} async-done(((bf16[1,46,128,128]{3,2,0,1:T(8,128)(2,1)}), bf16[1,736,128,128]{3,2,0,1:T(8,128)(2,1)}) %all-gather.12.cloned.1.call-update) | async-done | bytes 24117264 | tf_op jit(solution)/shard_map/all_gather | solution.py:310
  137.2 26.8 %gather_fusion = bf16[736,128,128]{2,1,0:T(8,128)(2,1)} fusion(bf16[736,128,128]{2,1,0:T(8,128)(2,1)} %bitcast.489, s32[1024]{0:T(1024)S(1)} %pad_clamp_fusion.1), kind=kCustom, calls=%fused_computation | custom fusion | bytes 48237440 | tf_op jit(solution)/shard_map/jit(_take)/gather | solution.py:323
  164.0 21.1 %broadcast_select_fusion = bf16[736,128,128]{2,1,0:T(8,128)(2,1)} fusion(bf16[736,128,128]{2,1,0:T(8,128)(2,1)} %gather_fusion, pred[736]{0:T(1024)(128)(4,1)S(1)} %compare_and_fusion.1), kind=kLoop, calls=%fused_computation.53 | loop fusion | flops 12058624 | bytes 48235232 | tf_op jit(solution)/shard_map/jit(_take)/select_n | solution.py:323
  185.0 11.1 fusion.178
  206.6 17.4 multiply_convert_fusion.5
  227.2 10.9 fusion.83
  238.2 54.4 %reduce-scatter.10.cloned.1.call-done = bf16[1024,1024]{1,0:T(8,128)(2,1)} async-done(((bf16[2048,1024]{1,0:T(8,128)(2,1)}), bf16[1024,1024]{1,0:T(8,128)(2,1)}) %reduce-scatter.10.cloned.1.call-update) | async-done | bytes 2097168 | tf_op jit(solution)/shard_map/reduce_scatter | solution.py:265
  301.9 7.3 fusion.179
  318.1 38.9 %all-gather.14.cloned.1.call-done = bf16[2048,1024]{1,0:T(8,128)(2,1)} async-done(((bf16[1024,1024]{1,0:T(8,128)(2,1)}), bf16[2048,1024]{1,0:T(8,128)(2,1)}) %all-gather.14.cloned.1.call-update) | async-done | bytes 4194320 | tf_op jit(solution)/shard_map/all_gather | solution.py:261
  390.7 105.4 %while.29 = (s32[]{:T(128)}, f32[4,4,512]{2,1,0:T(4,128)S(1)}, f32[4,512,4,128]{3,1,2,0:T(8,128)}, s32[4,512]{1,0:T(4,128)S(1)}, s32[1,2048]{1,0:T(1,128)S(1)}, ...) while((s32[]{:T(128)}, f32[4,4,512]{2,1,0:T(4,128)S(1)}, ...), condition=%wide.region_8.9_spmd.clone, body=%wide.region_5.8_spmd.sunk.clone | while | flops 2227173376 | bytes 77156520 | solution.py:177
  394.3 7.0 select_reduce_fusion.7
  401.3 7.5 select_reduce_fusion.8
  408.8 8.4 fusion.269
  420.6 7.0 select_reduce_fusion.7
  427.6 7.5 select_reduce_fusion.8
  435.1 8.4 fusion.269
  446.9 7.0 select_reduce_fusion.7
  453.9 7.5 select_reduce_fusion.8
  461.4 8.4 fusion.269
  473.2 7.0 select_reduce_fusion.7
  480.2 7.5 select_reduce_fusion.8
  487.8 8.4 fusion.269
  506.2 54.4 %reduce-scatter.12.cloned.1.call-done = bf16[1024,1024]{1,0:T(8,128)(2,1)} async-done(((bf16[2048,1024]{1,0:T(8,128)(2,1)}), bf16[1024,1024]{1,0:T(8,128)(2,1)}) %reduce-scatter.12.cloned.1.call-update) | async-done | bytes 2097168 | tf_op jit(solution)/shard_map/reduce_scatter | solution.py:265
  577.8 47.8 %all-gather.16.cloned.1.call-done = bf16[2048,1024]{1,0:T(8,128)(2,1)} async-done(((bf16[1024,1024]{1,0:T(8,128)(2,1)}), bf16[2048,1024]{1,0:T(8,128)(2,1)}) %all-gather.16.cloned.1.call-update) | async-done | bytes 4194320 | tf_op jit(solution)/shard_map/all_gather | solution.py:261
  645.9 54.4 %reduce-scatter.14.cloned.1.call-done = bf16[1024,1024]{1,0:T(8,128)(2,1)} async-done(((bf16[2048,1024]{1,0:T(8,128)(2,1)}), bf16[1024,1024]{1,0:T(8,128)(2,1)}) %reduce-scatter.14.cloned.1.call-update) | async-done | bytes 2097168 | tf_op jit(solution)/shard_map/reduce_scatter | solution.py:265
  708.0 8.0 copy.143
  720.8 43.6 %all-gather.18.cloned.1.call-done = bf16[2048,1024]{1,0:T(8,128)(2,1)} async-done(((bf16[1024,1024]{1,0:T(8,128)(2,1)}), bf16[2048,1024]{1,0:T(8,128)(2,1)}) %all-gather.18.cloned.1.call-update) | async-done | bytes 4194320 | tf_op jit(solution)/shard_map/all_gather | solution.py:261
  764.4 17.4 multiply_convert_fusion.4
  785.1 10.9 fusion.89
  796.1 54.4 %reduce-scatter.16.cloned.1.call-done = bf16[1024,1024]{1,0:T(8,128)(2,1)} async-done(((bf16[2048,1024]{1,0:T(8,128)(2,1)}), bf16[1024,1024]{1,0:T(8,128)(2,1)}) %reduce-scatter.16.cloned.1.call-update) | async-done | bytes 2097168 | tf_op jit(solution)/shard_map/reduce_scatter | solution.py:265
  865.1 56.9 %all-gather.20.cloned.1.call-done = bf16[2048,1024]{1,0:T(8,128)(2,1)} async-done(((bf16[1024,1024]{1,0:T(8,128)(2,1)}), bf16[2048,1024]{1,0:T(8,128)(2,1)}) %all-gather.20.cloned.1.call-update) | async-done | bytes 4194320 | tf_op jit(solution)/shard_map/all_gather | solution.py:271
  921.9 20.8 %multiply_convert_fusion.3 = bf16[2048,2048]{1,0:T(8,128)(2,1)} fusion(f32[2048,2048]{1,0:T(8,128)} %get-tuple-element.456, bf16[2048,1024]{1,0:T(8,128)(2,1)} %all-gather.20.cloned.1.call-done, bf16[256,8,8,128]{3,2,1,0:T(8,128)(2,1)} %bitcast.521), kind=kOutput, calls=%fused_computation.55 | convolution fusion | flops 8627683328 | bytes 33554432 | tf_op jit(solution)/shard_map/dot_general | solution.py:58
  942.7 12.6 fusion.86
  955.3 54.4 %reduce-scatter.18.cloned.1.call-done = bf16[1024,1024]{1,0:T(8,128)(2,1)} async-done(((bf16[2048,1024]{1,0:T(8,128)(2,1)}), bf16[1024,1024]{1,0:T(8,128)(2,1)}) %reduce-scatter.18.cloned.1.call-update) | async-done | bytes 2097168 | tf_op jit(solution)/shard_map/reduce_scatter | solution.py:275
  1021.4 56.8 %all-gather.22.cloned.1.call-done = bf16[2048,1024]{1,0:T(8,128)(2,1)} async-done(((bf16[1024,1024]{1,0:T(8,128)(2,1)}), bf16[2048,1024]{1,0:T(8,128)(2,1)}) %all-gather.22.cloned.1.call-update) | async-done | bytes 4194320 | tf_op jit(solution)/shard_map/all_gather | solution.py:271
  1078.2 20.3 multiply_reduce_fusion
  1098.5 11.1 multiply_convert_fusion.7
  1118.5 54.4 %reduce-scatter.20.cloned.1.call-done = bf16[1024,1024]{1,0:T(8,128)(2,1)} async-done(((bf16[2048,1024]{1,0:T(8,128)(2,1)}), bf16[1024,1024]{1,0:T(8,128)(2,1)}) %reduce-scatter.20.cloned.1.call-update) | async-done | bytes 2097168 | tf_op jit(solution)/shard_map/reduce_scatter | solution.py:275
  1185.2 55.1 %all-gather.24.cloned.1.call-done = bf16[2048,1024]{1,0:T(8,128)(2,1)} async-done(((bf16[1024,1024]{1,0:T(8,128)(2,1)}), bf16[2048,1024]{1,0:T(8,128)(2,1)}) %all-gather.24.cloned.1.call-update) | async-done | bytes 4194320 | tf_op jit(solution)/shard_map/all_gather | solution.py:271
  1257.0 200.5 %while.30 = (s32[]{:T(128)}, f32[2048,4,128]{0,2,1:T(8,128)}, f32[2048,4,128]{0,2,1:T(8,128)}, bf16[4,512,4,128]{3,1,2,0:T(8,128)(2,1)}, bf16[4,512,4,128]{3,1,2...) while((s32[]{:T(128)}, f32[2048,4,128]{0,2,1:T(8,128)}, ...), condition=%wide.region_28.29_spmd.clone.clone, body=%wide.region_27.28_spmd.clone.sunk.clone | while | flops 5437128704 | bytes 213987696 | solution.py:216
  1260.5 9.6 fusion.280
  1270.1 10.3 bitcast_add_fusion.10
  1280.4 13.7 multiply_convert_fusion.19
  1309.8 9.6 fusion.280
  1319.4 11.2 bitcast_add_fusion.10
  1330.6 13.7 multiply_convert_fusion.19
  1360.0 9.6 fusion.280
  1369.6 11.2 bitcast_add_fusion.10
  1380.8 13.7 multiply_convert_fusion.19
  1410.2 9.6 fusion.280
  1419.8 11.2 bitcast_add_fusion.10
  1431.0 13.7 multiply_convert_fusion.19
  1491.8 6.7 copy.171
  1498.5 13.0 convolution_bitcast_fusion.2
  1518.3 13.4 convolution_bitcast_fusion
  1616.8 20.9 %multiply_convert_fusion.2 = bf16[2048,2048]{1,0:T(8,128)(2,1)} fusion(f32[2048,2048]{1,0:T(8,128)} %get-tuple-element.452, bf16[2048,1024]{1,0:T(8,128)(2,1)} %all-gather.26.cloned.1.call-done, bf16[256,8,8,128]{3,2,1,0:T(8,128)(2,1)} %bitcast.517), kind=kOutput, calls=%fused_computation.54 | convolution fusion | flops 8627683328 | bytes 33554432 | tf_op jit(solution)/shard_map/dot_general | solution.py:58
  1637.7 12.6 fusion.80
  1650.4 13.2 convolution_bitcast_fusion.3
  1667.2 15.0 convolution_bitcast_fusion.1
  1693.5 7.9 constant_dynamic-update-slice_fusion.10
  1726.5 34.8 %gather_fusion.1 = f32[736,128,128]{2,1,0:T(8,128)} fusion(f32[736,128,128]{2,1,0:T(8,128)} %constant_dynamic-update-slice_fusion, s32[1024]{0:T(1024)S(1)} %copy-done.132), kind=kCustom, calls=%fused_computation.1 | custom fusion | bytes 96471936 | tf_op jit(solution)/shard_map/jit(_take)/gather | solution.py:444
  1761.3 26.8 %multiply_convert_fusion.1 = bf16[736,128,128]{2,1,0:T(8,128)(2,1)} fusion(f32[736,128,128]{2,1,0:T(8,128)} %gather_fusion.1, f32[736]{0:T(1024)S(1)} %copy-done.131, pred[736]{0:T(1024)(128)(4,1)S(1)} %copy-done.140), kind=kLoop, calls=%fused_computation.52 | loop fusion | flops 36175872 | bytes 72355424 | tf_op jit(solution)/shard_map/convert_element_type | solution.py:444
  1803.7 41.2 %all-reduce.6 = (f32[5,1024]{1,0:T(8,128)S(1)}, f32[5,1024]{1,0:T(8,128)S(1)}) all-reduce(f32[5,1024]{1,0:T(8,128)S(1)} %stack.26, f32[5,1024]{1,0:T(8,128)S(1)} %constant_dynamic-update-slice_fusion.11), channel_id=1, replica_groups=mesh['mp'=2,'dp'=16] {'mp','dp'}, use_global_device_ids=true, to_apply=%region_44.45 | all-reduce | flops 10240 | bytes 81920 | tf_op jit(solution)/shard_map/psum | solution.py:453
  1851.6 172.1 %reduce-scatter.26.cloned.1.call-done = bf16[46,128,128]{2,1,0:T(8,128)(2,1)} async-done(((bf16[736,128,128]{2,1,0:T(8,128)(2,1)}), bf16[46,128,128]{2,1,0:T(8,128)(2,1)}) %reduce-scatter.26.cloned.1.call-update) | async-done | bytes 1507344 | tf_op jit(solution)/shard_map/reduce_scatter | solution.py:443
  (590 shorter events, 499.6 us)
Async XLA Ops:
  7.2 2021.4 %copy-start = (f32[1,46,128,128]{3,2,1,0:T(8,128)S(1)}, f32[1,46,128,128]{3,2,1,0:T(8,128)}, u32[]{:S(2)}) copy-start(f32[1,46,128,128]{3,2,1,0:T(8,128)} %param.24) | copy-start | bytes 9043972
  7.2 8.5 copy-start.90
  7.2 130.0 %all-gather.12.cloned.1.call-start = ((), (), s32[]{:S(2)}) async-start(), calls=%async_computation.10 | async-start | bytes 25624576 | tf_op jit(solution)/shard_map/all_gather | solution.py:310
  10.6 196.0 %all-gather.10.cloned.1.call-start = ((), (), s32[]{:S(2)}) async-start(), calls=%async_computation.9 | async-start | bytes 6291456 | tf_op jit(solution)/shard_map/all_gather | solution.py:261
  16.3 281.3 %copy-start.86 = (f32[1,1024]{1,0:T(1,128)}, f32[1,1024]{1,0:T(1,128)S(1)}, u32[]{:S(2)}) copy-start(f32[1,1024]{1,0:T(1,128)S(1)} %get-tuple-element.440) | copy-start | bytes 12292
  19.0 273.6 %reduce-scatter.10.cloned.1.call-start = ((), (), s32[]{:S(2)}) async-start(), calls=%async_computation.11 | async-start | bytes 6291456 | tf_op jit(solution)/shard_map/reduce_scatter | solution.py:265
  19.5 144.5 %copy-start.92 = (s32[736]{0:T(1024)}, s32[736]{0:T(1024)S(1)}, u32[]{:S(2)}) copy-start(s32[736]{0:T(1024)S(1)} %reduce.2) | copy-start | bytes 8836
  206.6 20.6 %copy-start.50 = (bf16[16,8,128,128]{3,1,2,0:T(8,128)(2,1)S(1)}, bf16[16,8,128,128]{3,1,2,0:T(8,128)(2,1)}, u32[]{:S(2)}) copy-start(bf16[16,8,128,128]{3,1,2,0:T(8,128)(2,1)} %copy.130) | copy-start | bytes 12582916
  238.1 118.9 %all-gather.14.cloned.1.call-start = ((), (), s32[]{:S(2)}) async-start(), calls=%async_computation.12 | async-start | bytes 6291456 | tf_op jit(solution)/shard_map/all_gather | solution.py:261
  300.1 260.5 %reduce-scatter.12.cloned.1.call-start = ((), (), s32[]{:S(2)}) async-start(), calls=%async_computation.13 | async-start | bytes 6291456 | tf_op jit(solution)/shard_map/reduce_scatter | solution.py:265
  506.1 119.4 %all-gather.16.cloned.1.call-start = ((), (), s32[]{:S(2)}) async-start(), calls=%async_computation.14 | async-start | bytes 6291456 | tf_op jit(solution)/shard_map/all_gather | solution.py:261
  568.6 131.7 %reduce-scatter.14.cloned.1.call-start = ((), (), s32[]{:S(2)}) async-start(), calls=%async_computation.15 | async-start | bytes 6291456 | tf_op jit(solution)/shard_map/reduce_scatter | solution.py:265
  569.7 66.0 %copy-start.121 = (f32[1,512]{1,0:T(1,128)}, f32[1,512]{1,0:T(1,128)S(1)}, u32[]{:S(2)}) copy-start(f32[1,512]{1,0:T(1,128)S(1)} %get-tuple-element.442) | copy-start | bytes 6148
  569.7 66.0 %copy-start.123 = (f32[1,512]{1,0:T(1,128)}, f32[1,512]{1,0:T(1,128)S(1)}, u32[]{:S(2)}) copy-start(f32[1,512]{1,0:T(1,128)S(1)} %get-tuple-element.443) | copy-start | bytes 6148
  569.7 66.0 %copy-start.125 = (f32[1,512]{1,0:T(1,128)}, f32[1,512]{1,0:T(1,128)S(1)}, u32[]{:S(2)}) copy-start(f32[1,512]{1,0:T(1,128)S(1)} %get-tuple-element.444) | copy-start | bytes 6148
  569.7 66.0 %copy-start.127 = (f32[1,512]{1,0:T(1,128)}, f32[1,512]{1,0:T(1,128)S(1)}, u32[]{:S(2)}) copy-start(f32[1,512]{1,0:T(1,128)S(1)} %get-tuple-element.445) | copy-start | bytes 6148
  569.7 66.0 %copy-start.129 = (f32[1,512]{1,0:T(1,128)}, f32[1,512]{1,0:T(1,128)S(1)}, u32[]{:S(2)}) copy-start(f32[1,512]{1,0:T(1,128)S(1)} %get-tuple-element.446) | copy-start | bytes 6148
  569.8 65.9 %copy-start.113 = (f32[2048]{0:T(1024)}, f32[2048]{0:T(1024)S(1)}, u32[]{:S(2)}) copy-start(f32[2048]{0:T(1024)S(1)} %get-tuple-element.447) | copy-start | bytes 24580
  569.8 65.9 %copy-start.115 = (f32[2048]{0:T(1024)}, f32[2048]{0:T(1024)S(1)}, u32[]{:S(2)}) copy-start(f32[2048]{0:T(1024)S(1)} %get-tuple-element.448) | copy-start | bytes 24580
  569.8 65.9 %copy-start.117 = (f32[2048]{0:T(1024)}, f32[2048]{0:T(1024)S(1)}, u32[]{:S(2)}) copy-start(f32[2048]{0:T(1024)S(1)} %get-tuple-element.449) | copy-start | bytes 24580
  569.8 65.9 %copy-start.119 = (f32[2048]{0:T(1024)}, f32[2048]{0:T(1024)S(1)}, u32[]{:S(2)}) copy-start(f32[2048]{0:T(1024)S(1)} %get-tuple-element.450) | copy-start | bytes 24580
  645.8 118.6 %all-gather.18.cloned.1.call-start = ((), (), s32[]{:S(2)}) async-start(), calls=%async_computation.16 | async-start | bytes 6291456 | tf_op jit(solution)/shard_map/all_gather | solution.py:261
  707.5 143.0 %reduce-scatter.16.cloned.1.call-start = ((), (), s32[]{:S(2)}) async-start(), calls=%async_computation.17 | async-start | bytes 6291456 | tf_op jit(solution)/shard_map/reduce_scatter | solution.py:265
  764.4 20.7 %copy-start.53 = (bf16[16,8,128,128]{3,1,2,0:T(8,128)(2,1)S(1)}, bf16[16,8,128,128]{3,1,2,0:T(8,128)(2,1)}, u32[]{:S(2)}) copy-start(bf16[16,8,128,128]{3,1,2,0:T(8,128)(2,1)} %copy.143) | copy-start | bytes 12582916
  796.1 125.8 %all-gather.20.cloned.1.call-start = ((), (), s32[]{:S(2)}) async-start(), calls=%async_computation.18 | async-start | bytes 6291456 | tf_op jit(solution)/shard_map/all_gather | solution.py:271
  865.0 144.7 %reduce-scatter.18.cloned.1.call-start = ((), (), s32[]{:S(2)}) async-start(), calls=%async_computation.19 | async-start | bytes 6291456 | tf_op jit(solution)/shard_map/reduce_scatter | solution.py:275
  921.9 20.8 %copy-start.54 = (bf16[8,16,128,128]{3,1,2,0:T(8,128)(2,1)S(1)}, bf16[8,16,128,128]{3,1,2,0:T(8,128)(2,1)}, u32[]{:S(2)}) copy-start(bf16[8,16,128,128]{3,1,2,0:T(8,128)(2,1)} %copy.142) | copy-start | bytes 12582916
  955.3 122.9 %all-gather.22.cloned.1.call-start = ((), (), s32[]{:S(2)}) async-start(), calls=%async_computation.20 | async-start | bytes 6291456 | tf_op jit(solution)/shard_map/all_gather | solution.py:271
  1017.7 60.5 %copy-start.114 = (f32[2048]{0:T(1024)S(1)}, f32[2048]{0:T(1024)}, u32[]{:S(2)}) copy-start(f32[2048]{0:T(1024)} %copy-done.113) | copy-start | bytes 24580
  1017.7 60.5 %copy-start.116 = (f32[2048]{0:T(1024)S(1)}, f32[2048]{0:T(1024)}, u32[]{:S(2)}) copy-start(f32[2048]{0:T(1024)} %copy-done.115) | copy-start | bytes 24580
  1017.7 60.5 %copy-start.118 = (f32[2048]{0:T(1024)S(1)}, f32[2048]{0:T(1024)}, u32[]{:S(2)}) copy-start(f32[2048]{0:T(1024)} %copy-done.117) | copy-start | bytes 24580
  1017.7 60.5 %copy-start.120 = (f32[2048]{0:T(1024)S(1)}, f32[2048]{0:T(1024)}, u32[]{:S(2)}) copy-start(f32[2048]{0:T(1024)} %copy-done.119) | copy-start | bytes 24580
  1021.3 77.2 %copy-start.122 = (f32[1,512]{1,0:T(1,128)S(1)}, f32[1,512]{1,0:T(1,128)}, u32[]{:S(2)}) copy-start(f32[1,512]{1,0:T(1,128)} %copy-done.121) | copy-start | bytes 6148
  1021.3 77.2 %copy-start.124 = (f32[1,512]{1,0:T(1,128)S(1)}, f32[1,512]{1,0:T(1,128)}, u32[]{:S(2)}) copy-start(f32[1,512]{1,0:T(1,128)} %copy-done.123) | copy-start | bytes 6148
  1021.3 77.2 %copy-start.126 = (f32[1,512]{1,0:T(1,128)S(1)}, f32[1,512]{1,0:T(1,128)}, u32[]{:S(2)}) copy-start(f32[1,512]{1,0:T(1,128)} %copy-done.125) | copy-start | bytes 6148
  1021.3 77.2 %copy-start.128 = (f32[1,512]{1,0:T(1,128)S(1)}, f32[1,512]{1,0:T(1,128)}, u32[]{:S(2)}) copy-start(f32[1,512]{1,0:T(1,128)} %copy-done.127) | copy-start | bytes 6148
  1021.3 77.2 %copy-start.130 = (f32[1,512]{1,0:T(1,128)S(1)}, f32[1,512]{1,0:T(1,128)}, u32[]{:S(2)}) copy-start(f32[1,512]{1,0:T(1,128)} %copy-done.129) | copy-start | bytes 6148
  1021.3 151.6 %reduce-scatter.20.cloned.1.call-start = ((), (), s32[]{:S(2)}) async-start(), calls=%async_computation.21 | async-start | bytes 6291456 | tf_op jit(solution)/shard_map/reduce_scatter | solution.py:275
  1098.5 11.1 copy-start.18
  1118.4 54.5 %copy-start.85 = (f32[1024]{0:T(1024)S(1)}, f32[1024]{0:T(1024)}, u32[]{:S(2)}) copy-start(f32[1024]{0:T(1024)} %copy-done.84) | copy-start | bytes 12292
  1118.4 54.5 %copy-start.97 = (f32[1,1024]{1,0:T(1,128)S(1)}, f32[1,1024]{1,0:T(1,128)}, u32[]{:S(2)}) copy-start(f32[1,1024]{1,0:T(1,128)} %get-tuple-element.439) | copy-start | bytes 12292
  1118.4 54.5 %copy-start.99 = (f32[1024]{0:T(1024)S(1)}, f32[1024]{0:T(1024)}, u32[]{:S(2)}) copy-start(f32[1024]{0:T(1024)} %copy-done.98) | copy-start | bytes 12292
  1118.5 59.4 %copy-start.110 = (f32[1024]{0:T(1024)S(1)}, f32[1024]{0:T(1024)}, u32[]{:S(2)}) copy-start(f32[1024]{0:T(1024)} %copy-done.109) | copy-start | bytes 12292
  1118.5 121.9 %all-gather.24.cloned.1.call-start = ((), (), s32[]{:S(2)}) async-start(), calls=%async_computation.22 | async-start | bytes 6291456 | tf_op jit(solution)/shard_map/all_gather | solution.py:271
  1183.5 356.1 %reduce-scatter.22.cloned.1.call-start = ((), (), s32[]{:S(2)}) async-start(), calls=%async_computation.23 | async-start | bytes 6291456 | tf_op jit(solution)/shard_map/reduce_scatter | solution.py:275
  1259.7 10.4 copy-start.30
  1260.5 9.6 copy-start.13
  1309.0 10.4 copy-start.30
  1309.8 9.6 copy-start.13
  1359.2 10.4 copy-start.30
  1360.0 9.6 copy-start.13
  1409.4 10.4 copy-start.30
  1410.2 9.6 copy-start.13
  1475.9 140.9 %all-gather.26.cloned.1.call-start = ((), (), s32[]{:S(2)}) async-start(), calls=%async_computation.24 | async-start | bytes 6291456 | tf_op jit(solution)/shard_map/all_gather | solution.py:271
  1539.6 9.8 copy-start.28
  1554.8 240.5 %reduce-scatter.24.cloned.1.call-start = ((), (), s32[]{:S(2)}) async-start(), calls=%async_computation.25 | async-start | bytes 6291456 | tf_op jit(solution)/shard_map/reduce_scatter | solution.py:275
  1616.8 20.9 %copy-start.49 = (bf16[8,16,128,128]{3,1,2,0:T(8,128)(2,1)S(1)}, bf16[8,16,128,128]{3,1,2,0:T(8,128)(2,1)}, u32[]{:S(2)}) copy-start(bf16[8,16,128,128]{3,1,2,0:T(8,128)(2,1)} %copy.129) | copy-start | bytes 12582916
  1650.4 373.3 %reduce-scatter.26.cloned.1.call-start = ((), (), s32[]{:S(2)}) async-start(), calls=%async_computation.26 | async-start | bytes 25624576 | tf_op jit(solution)/shard_map/reduce_scatter | solution.py:443
  1707.6 9.0 slice-start.2
  1713.6 8.8 slice-start
  1726.5 34.8 %copy-start.131 = (f32[736]{0:T(1024)S(1)}, f32[736]{0:T(1024)}, u32[]{:S(2)}) copy-start(f32[736]{0:T(1024)} %convert_element_type.263) | copy-start | bytes 8836
  1726.5 34.8 %copy-start.140 = (pred[736]{0:T(1024)(128)(4,1)S(1)}, pred[736]{0:T(1024)(128)(4,1)}, u32[]{:S(2)}) copy-start(pred[736]{0:T(1024)(128)(4,1)} %compare_and_fusion) | copy-start | bytes 2212
  1795.4 49.8 %copy-start.91 = (f32[5,1024]{1,0:T(8,128)S(1)}, f32[5,1024]{1,0:T(8,128)}, u32[]{:S(2)}) copy-start(f32[5,1024]{1,0:T(8,128)} %param.26) | copy-start | bytes 61444
  1795.4 49.8 %copy-start.102 = (f32[5,1024]{1,0:T(8,128)S(1)}, f32[5,1024]{1,0:T(8,128)}, u32[]{:S(2)}) copy-start(f32[5,1024]{1,0:T(8,128)} %param.27) | copy-start | bytes 61444
  (124 other events, 510.0 us)
Sparse Core Ops, SparseCore 0:
  10.8 126.3 all-gather.11
  139.3 56.7 all-gather.9
  238.2 54.2 reduce-scatter.9
  300.2 56.7 all-gather.13
  506.3 54.2 reduce-scatter.11
  568.7 56.7 all-gather.15
  646.0 54.2 reduce-scatter.13
  707.7 56.7 all-gather.17
  796.2 54.3 reduce-scatter.15
  865.1 56.7 all-gather.19
  955.4 54.2 reduce-scatter.17
  1021.4 56.7 all-gather.21
  1118.6 54.2 reduce-scatter.19
  1183.6 56.7 all-gather.23
  1476.1 54.2 reduce-scatter.21
  1554.9 56.8 all-gather.25
  1650.5 54.3 reduce-scatter.23
  1788.3 235.3 reduce-scatter.25
where the time goes:
time: 2070 us; the launch traced here: 2060 us
  waiting for transfers between devices  916 us (44%)
  matrix products  549 us (27%)
  local copies, waits for them, and re-layouts  313 us (15%)
  other arithmetic  224 us (11%)
  blocking collectives  41.2 us (2%)
    reduce_scatter x4, waiting for transfers between devices, row_totals(): lax.psum_scatter(partial_value.astype(jnp.bfloat16), 'mp', scatter_dimens...  218 us
    reduce_scatter x1, waiting for transfers between devices, local(): lax.psum_scatter((jnp.take(all_grads, slot_source, axis=0) * slot_filled)...  172 us
    all_gather x4, waiting for transfers between devices, gather_grads(): return lax.all_gather(values, 'mp', axis=0, tiled=True)  169 us
    all_gather x4, waiting for transfers between devices, gather_rows(): return lax.all_gather(values, 'mp', axis=0, tiled=True)  130 us
    all_gather x1, waiting for transfers between devices, local(): lax.all_gather(master.astype(jnp.bfloat16), 'dp', axis=1, tiled=True)[0]  118 us
    dot_general x11, matrix products, dense_right(): lax.dot_general(left_op, right_op, (((1,), (1,)), ((), ())), preferred_el...  111 us
    reduce_scatter x4, waiting for transfers between devices, sum_grads(): lax.psum_scatter(partial_value.astype(jnp.bfloat16), 'mp', scatter_dimens...  109 us
    dot_general x11, matrix products, dense(): return jnp.dot(left_op, right_op, preferred_element_type=jnp.float32)  94 us
  transfers between devices with their start and end apart: 18, of which 14 were waited for; matrix products, arithmetic and copies ran while one was open for 19% of the time, Pallas kernels for 0%

commit v1 on v0

v1 whole, which is shorter than its diff:
```python
import math

import jax
import jax.numpy as jnp
import numpy as np
from jax import lax
from jax.experimental import pallas as pl
from jax.experimental.pallas import tpu as pltpu
from jax.sharding import Mesh
from jax.sharding import PartitionSpec as P

D = 1024
FF = 4096
HEADS = 8
HEAD_DIM = 128
KERNEL = 5
STEP = 4
BLOCK = 128
HALO = 16
WIDE = 8

EPSILON = 1e-05
DECAY_STAT = 0.95
RATE_BLOCK = 0.02
RATE_VECTOR = 0.2
DECAY_AVERAGE = 0.9999
MASKED = -1e30
LOG2E = math.log2(math.e)
SCORE_SCALE = 1.0 / math.sqrt(HEAD_DIM)

f32 = jnp.float32
bf16 = jnp.bfloat16
ANY = pl.BlockSpec(memory_space=pl.ANY)
SMEM = pl.BlockSpec(memory_space=pltpu.SMEM)

MATRICES = [
    (0, D, FF, True),
    (4, FF, D, False),
    (8, D, D, True),
    (9, D, D, True),
    (10, D, D, True),
    (11, D, D, False),
    (12, D, D, True),
    (13, D, D, True),
    (14, D, D, False),
    (15, D, FF, True),
    (19, FF, D, False),
]
UP1, DOWN1, QUERY, KEY, VALUE, OUT, CONV_VALUE, CONV_GATE, CONV_OUT, UP2, DOWN2 = range(11)
CHUNKS = 23
WEIGHT_BLOCKS = CHUNKS * 8 * WIDE


def at(matrix):
    return MATRICES[matrix][0]


GATHER_PIECES = [
    (0, 3, "x"),
    (3, 3, "y"),
    (6, 7, "x"),
    (13, 7, "y"),
    (20, 7, "x"),
    (27, 7, "y"),
    (34, 6, "x"),
    (40, 6, "y"),
]
SCATTER_PIECES = [
    (0, 6, "x"),
    (6, 6, "y"),
    (12, 7, "x"),
    (19, 7, "y"),
    (26, 7, "x"),
    (33, 7, "y"),
    (40, 3, "x"),
    (43, 3, "y"),
]


def params(**kw):
    return pltpu.CompilerParams(vmem_limit_bytes=58 * 2**20, **kw)


def const_spec(shape):
    return pl.BlockSpec(shape, lambda *ids: (0,) * len(shape), pipeline_mode=pl.Buffered(1))


def row_tile(rows):
    return 256 if rows % 256 == 0 else 128


def cost(flops, moved):
    return pl.CostEstimate(flops=int(flops), bytes_accessed=int(moved), transcendentals=0)


def offsets(ranks):
    out = []
    offset = 0
    for unused, height, breadth, by_columns in MATRICES:
        out.append(offset)
        offset = offset + height * breadth // (BLOCK * BLOCK * ranks)
    return out, offset


def block_number(matrix, row_block, column_block, ranks):
    starts, total = offsets(ranks)
    unused, height, breadth, by_columns = MATRICES[matrix]
    if by_columns:
        part = breadth // BLOCK // ranks
        return (
            (column_block // part) * total + starts[matrix] + row_block * part + column_block % part
        )
    part = height // BLOCK // ranks
    breadth_blocks = breadth // BLOCK
    return (
        (row_block // part) * total
        + starts[matrix]
        + (row_block % part) * breadth_blocks
        + column_block
    )


def weight_places(ranks):
    unused, total = offsets(ranks)
    places = np.zeros((ranks * total,), np.int32)
    for matrix, (chunk, height, breadth, by_columns) in enumerate(MATRICES):
        for row in range(height // BLOCK):
            for column in range(breadth // BLOCK):
                place = ((chunk + column // WIDE) * 8 + row) * WIDE + column % WIDE
                places[block_number(matrix, row, column, ranks)] = place
    return places.reshape(ranks, total)


def place_weights(weights, arrays, bases, slot_places, lanes, depth, width, rows_all):
    count = arrays[0].shape[0]
    total = count * len(arrays)

    def body(table, base_ref, *rest):
        sources = rest[: len(arrays)]
        out, sem = rest[-2], rest[-1]

        def one(t, unused):
            step = (t // width) * depth + t % width
            for number, source in enumerate(sources):
                place = table[base_ref[number] + step]
                row = pl.multiple_of((place // WIDE) * BLOCK, BLOCK)
                column = pl.multiple_of((place % WIDE) * BLOCK, BLOCK)
                pltpu.make_async_copy(
                    source.at[t], out.at[pl.ds(row, BLOCK), pl.ds(column, BLOCK)], sem
                ).start()
            return unused

        lax.fori_loop(0, count, one, 0)
        whole = sources[0] if len(sources) == 1 else out.at[pl.ds(0, total * BLOCK // WIDE), :]
        pltpu.make_async_copy(whole, whole, sem).wait()

    operands = [slot_places, bases, *arrays]
    aliases = {}
    specs = [SMEM, SMEM] + [ANY] * len(arrays)
    if weights is not None:
        aliases = {len(operands): 0}
        operands.append(weights)
        specs.append(ANY)
    return pl.pallas_call(
        body,
        out_shape=jax.ShapeDtypeStruct((rows_all, D), bf16),
        in_specs=specs,
        out_specs=ANY,
        scratch_shapes=[pltpu.SemaphoreType.DMA],
        input_output_aliases=aliases,
        compiler_params=params(has_side_effects=True),
        cost_estimate=cost(0, 2 * total * BLOCK * BLOCK * 2),
        name="place_weights",
    )(*operands)


def swap(value, axis):
    return lax.ppermute(value, axis, [(0, 1), (1, 0)])


def gather_weights(own, slot_places, coords, fast, rows_all):
    slot_dev = own.shape[0]
    if not fast:
        everything = lax.all_gather(own, ("mp", "z", "x", "core"), axis=0, tiled=True)
        return place_weights(
            None, [everything], jnp.zeros((1,), jnp.int32), slot_places, None, 0,
            everything.shape[0], rows_all,
        )
    rank, x_at, core_at = coords
    zs = lax.axis_size("z")
    weights = None
    for first, count, kind in GATHER_PIECES:
        column = lax.all_gather(own[first : first + count], "z", axis=0, tiled=True)
        if kind == "x":
            beside = swap(column, "x")
            parts = [
                (column, 0, 0),
                (beside, 0, 1),
                (swap(column, "mp"), 1, 0),
                (swap(beside, "mp"), 1, 1),
            ]
        else:
            beside = swap(column, "mp")
            parts = [
                (column, 0, 0),
                (beside, 1, 0),
                (swap(column, "x"), 0, 1),
                (swap(beside, "x"), 1, 1),
            ]
        arrays, bases = [], []
        for flip in (0, 1):
            for value, dy, dx in parts:
                arrays.append(swap(value, "core") if flip else value)
                bases.append(
                    (
                        ((rank ^ dy) * zs * 2 + (x_at ^ dx)) * 2 + (core_at ^ flip)
                    )
                    * slot_dev
                    + first
                )
        weights = place_weights(
            weights, arrays, jnp.stack(bases).astype(jnp.int32), slot_places, None,
            4 * slot_dev, count, rows_all,
        )
    return weights


def sigmoid(values):
    return 0.5 * jnp.tanh(0.5 * values) + 0.5


def norm_parts(values):
    center = values - jnp.mean(values, axis=-1, keepdims=True)
    spread = jnp.mean(center * center, axis=-1, keepdims=True)
    scale = lax.rsqrt(spread + EPSILON)
    return center * scale, scale


def norm(values, gain):
    return norm_parts(values)[0] * gain


def norm_back(values, gain, grad):
    hat, scale = norm_parts(values)
    inner = grad * gain
    mean_inner = jnp.mean(inner, axis=-1, keepdims=True)
    mean_hat = jnp.mean(inner * hat, axis=-1, keepdims=True)
    return (
        scale * (inner - mean_inner - hat * mean_hat),
        jnp.sum(grad * hat, axis=0, keepdims=True),
    )


def dot(a, b):
    return jnp.dot(a, b, preferred_element_type=f32)


def dot_right(a, b):
    return lax.dot_general(a, b, (((1,), (1,)), ((), ())), preferred_element_type=f32)


def dot_left(a, b):
    return lax.dot_general(a, b, (((0,), (0,)), ((), ())), preferred_element_type=f32)


def start_blocks(table, sums, source, sem, matrix, row_block, column_block, ranks):
    height, breadth = source.shape
    for i in range(height // BLOCK):
        for j in range(breadth // BLOCK):
            place = table[block_number(matrix, row_block + i, column_block + j, ranks)]
            pltpu.make_async_copy(
                source.at[pl.ds(i * BLOCK, BLOCK), pl.ds(j * BLOCK, BLOCK)], sums.at[place], sem
            ).start()


def wait_blocks(source, sem):
    pltpu.make_async_copy(source, source, sem).wait()


def ffn_forward(stream, gain, next_gain, weights, upper, lower):
    rows = stream.shape[0]
    tile = row_tile(rows)
    wide = 512
    steps = FF // wide

    def body(x_ref, gain_ref, next_gain_ref, up_ref, down_ref, out_ref, pre_ref, next_ref, normed):
        step = pl.program_id(0)

        @pl.when(step == 0)
        def _():
            for t in range(0, rows, tile):
                x = x_ref[t : t + tile].astype(f32)
                normed[t : t + tile] = norm(x, gain_ref[...]).astype(bf16)
                out_ref[t : t + tile] = jnp.zeros((tile, D), f32)

        for t in range(0, rows, tile):
            pre = dot(normed[t : t + tile], up_ref[...])
            pre_ref[t : t + tile] = pre.astype(bf16)
            act = (pre * sigmoid(pre)).astype(bf16)
            out_ref[t : t + tile] += dot(act, down_ref[...])

        @pl.when(step == steps - 1)
        def _():
            for t in range(0, rows, tile):
                y = x_ref[t : t + tile].astype(f32) + 0.5 * out_ref[t : t + tile]
                out_ref[t : t + tile] = y
                next_ref[t : t + tile] = norm(y, next_gain_ref[...]).astype(bf16)

    return pl.pallas_call(
        body,
        grid=(steps,),
        out_shape=(
            jax.ShapeDtypeStruct((rows, D), f32),
            jax.ShapeDtypeStruct((rows, FF), bf16),
            jax.ShapeDtypeStruct((rows, D), bf16),
        ),
        in_specs=[
            const_spec((rows, D)),
            const_spec((1, D)),
            const_spec((1, D)),
            pl.BlockSpec((D, wide), lambda f: (at(upper) + f // 2, f % 2)),
            pl.BlockSpec((wide, D), lambda f: (at(lower) * 2 + f, 0)),
        ],
        out_specs=(
            const_spec((rows, D)),
            pl.BlockSpec((rows, wide), lambda f: (0, f)),
            const_spec((rows, D)),
        ),
        scratch_shapes=[pltpu.VMEM((rows, D), bf16)],
        compiler_params=params(),
        cost_estimate=cost(4 * rows * D * FF, 4 * D * FF + 2 * rows * FF),
        name="ffn_forward",
    )(stream, gain, next_gain, weights, weights)


def ffn_backward(
    after, after_gain, after_grads, base, stream, gain, pre, weights, upper, lower, sums, table,
    ranks,
):
    rows = stream.shape[0]
    tile = row_tile(rows)
    wide = 512
    steps = FF // wide
    parts = len(after_grads)
    with_base = base is not None

    def body(table_ref, *refs):
        refs = list(refs)
        after_ref, after_gain_ref = refs[0], refs[1]
        grad_refs = refs[2 : 2 + parts]
        at_ref = 2 + parts
        base_ref = None
        if with_base:
            base_ref = refs[at_ref]
            at_ref += 1
        x_ref, gain_ref, pre_ref, up_ref, down_ref, sums_in = refs[at_ref : at_ref + 6]
        out_ref, gains_ref, sums_ref = refs[at_ref + 6 : at_ref + 9]
        (half, normed_t, grad_sum, pre_grad, act_t, up_part, down_part, up_sem, down_sem) = refs[
            at_ref + 9 :
        ]
        step = pl.program_id(0)
        slot = lax.rem(step, 2)

        @pl.when(step == 0)
        def _():
            gain_sum = jnp.zeros((1, D), f32)
            for t in range(0, rows, tile):
                here = slice(t, t + tile)
                grad = grad_refs[0][here].astype(f32)
                for other in grad_refs[1:]:
                    grad = grad + other[here].astype(f32)
                back, part = norm_back(after_ref[here], after_gain_ref[...], grad)
                gain_sum = gain_sum + part
                if with_base:
                    back = back + base_ref[here]
                out_ref[here] = back
                half[here] = (0.5 * back).astype(bf16)
                normed = norm(x_ref[here].astype(f32), gain_ref[...]).astype(bf16)
                normed_t[:, here] = normed.T
                grad_sum[here] = jnp.zeros((tile, D), f32)
            gains_ref[0:1] = gain_sum

        for t in range(0, rows, tile):
            here = slice(t, t + tile)
            act_grad = dot_right(half[here], down_ref[...])
            pre_act = pre_ref[here].astype(f32)
            sigma = sigmoid(pre_act)
            act = pre_act * sigma
            act_t[:, here] = act.astype(bf16).T
            slope = sigma + act * (1.0 - sigma)
            moved = (act_grad * slope).astype(bf16)
            pre_grad[here] = moved
            grad_sum[here] += dot_right(moved, up_ref[...])

        @pl.when(step >= 2)
        def _():
            wait_blocks(up_part.at[slot], up_sem.at[slot])
            wait_blocks(down_part.at[slot], down_sem.at[slot])

        for t in range(0, D, 256):
            up_part[slot, t : t + 256] = dot(normed_t[t : t + 256], pre_grad[...]).astype(bf16)
        for t in range(0, wide, 256):
            down_part[slot, t : t + 256] = dot(act_t[t : t + 256], half[...]).astype(bf16)
        start_blocks(
            table_ref, sums_ref, up_part.at[slot], up_sem.at[slot], upper, 0, step * 4, ranks
        )
        start_blocks(
            table_ref, sums_ref, down_part.at[slot], down_sem.at[slot], lower, step * 4, 0, ranks
        )

        @pl.when(step == steps - 1)
        def _():
            gain_sum = jnp.zeros((1, D), f32)
            for t in range(0, rows, tile):
                here = slice(t, t + tile)
                back, part = norm_back(x_ref[here].astype(f32), gain_ref[...], grad_sum[here])
                gain_sum = gain_sum + part
                out_ref[here] += back
            gains_ref[1:2] = gain_sum
            for s in range(2):
                wait_blocks(up_part.at[s], up_sem.at[s])
                wait_blocks(down_part.at[s], down_sem.at[s])

    operands = [table, after, after_gain, *after_grads]
    specs = [SMEM, const_spec((rows, D)), const_spec((1, D))] + [const_spec((rows, D))] * parts
    if with_base:
        operands.append(base)
        specs.append(const_spec((rows, D)))
    operands += [stream, gain, pre, weights, weights, sums]
    specs += [
        const_spec((rows, D)),
        const_spec((1, D)),
        pl.BlockSpec((rows, wide), lambda f: (0, f)),
        pl.BlockSpec((D, wide), lambda f: (at(upper) + f // 2, f % 2)),
        pl.BlockSpec((wide, D), lambda f: (at(lower) * 2 + f, 0)),
        ANY,
    ]
    return pl.pallas_call(
        body,
        grid=(steps,),
        out_shape=(
            jax.ShapeDtypeStruct((rows, D), f32),
            jax.ShapeDtypeStruct((2, D), f32),
            jax.ShapeDtypeStruct(sums.shape, bf16),
        ),
        in_specs=specs,
        out_specs=(const_spec((rows, D)), const_spec((2, D)), ANY),
        scratch_shapes=[
            pltpu.VMEM((rows, D), bf16),
            pltpu.VMEM((D, rows), bf16),
            pltpu.VMEM((rows, D), f32),
            pltpu.VMEM((rows, wide), bf16),
            pltpu.VMEM((wide, rows), bf16),
            pltpu.VMEM((2, D, wide), bf16),
            pltpu.VMEM((2, wide, D), bf16),
            pltpu.SemaphoreType.DMA((2,)),
            pltpu.SemaphoreType.DMA((2,)),
        ],
        input_output_aliases={len(operands) - 1: 2},
        compiler_params=params(has_side_effects=True),
        cost_estimate=cost(8 * rows * D * FF, 8 * D * FF + 2 * rows * FF),
        name="ffn_backward",
    )(*operands)


def project(values, weights, first, count):
    rows = values.shape[0]
    tile = row_tile(rows)
    wide = 512

    def body(x_ref, w_ref, out_ref):
        for t in range(0, rows, tile):
            out_ref[t : t + tile] = dot(x_ref[t : t + tile], w_ref[...]).astype(bf16)

    return pl.pallas_call(
        body,
        grid=(2 * count,),
        out_shape=jax.ShapeDtypeStruct((rows, count * D), bf16),
        in_specs=[
            const_spec((rows, D)),
            pl.BlockSpec((D, wide), lambda f: (at(first) + f // 2, f % 2)),
        ],
        out_specs=pl.BlockSpec((rows, wide), lambda f: (0, f)),
        compiler_params=params(),
        cost_estimate=cost(2 * rows * D * D * count, 2 * count * D * (D + rows)),
        name="project",
    )(values, weights)


def project_out(values, weights, matrix, stream):
    rows = values.shape[0]
    tile = row_tile(rows)

    def body(x_ref, w_ref, s_ref, out_ref):
        out_ref[...] = s_ref[...] + dot(x_ref[...], w_ref[...])

    return pl.pallas_call(
        body,
        grid=(rows // tile,),
        out_shape=jax.ShapeDtypeStruct((rows, D), f32),
        in_specs=[
            pl.BlockSpec((tile, D), lambda t: (t, 0)),
            pl.BlockSpec((D, D), lambda t: (at(matrix), 0)),
            pl.BlockSpec((tile, D), lambda t: (t, 0)),
        ],
        out_specs=pl.BlockSpec((tile, D), lambda t: (t, 0)),
        compiler_params=params(),
        cost_estimate=cost(2 * rows * D * D, 2 * D * D + 10 * rows * D),
        name="project_out",
    )(values, weights, stream)


def project_out_back(grad, weights, matrix, attended, sums, table, ranks):
    rows = grad.shape[0]
    tile = row_tile(rows)
    wide = 512

    def body(table_ref, g_ref, w_ref, a_ref, sums_in, out_ref, sums_ref, low, part, sem):
        step = pl.program_id(0)

        @pl.when(step == 0)
        def _():
            for t in range(0, rows, tile):
                low[t : t + tile] = g_ref[t : t + tile].astype(bf16)

        for t in range(0, rows, tile):
            out_ref[t : t + tile] = dot_right(low[t : t + tile], w_ref[...]).astype(bf16)
        for t in range(0, wide, 256):
            part[step, t : t + 256] = dot_left(a_ref[:, t : t + 256], low[...]).astype(bf16)
        start_blocks(table_ref, sums_ref, part.at[step], sem.at[step], matrix, step * 4, 0, ranks)

        @pl.when(step == 1)
        def _():
            for s in range(2):
                wait_blocks(part.at[s], sem.at[s])

    return pl.pallas_call(
        body,
        grid=(2,),
        out_shape=(
            jax.ShapeDtypeStruct((rows, D), bf16),
            jax.ShapeDtypeStruct(sums.shape, bf16),
        ),
        in_specs=[
            SMEM,
            const_spec((rows, D)),
            pl.BlockSpec((wide, D), lambda f: (at(matrix) * 2 + f, 0)),
            pl.BlockSpec((rows, wide), lambda f: (0, f)),
            ANY,
        ],
        out_specs=(pl.BlockSpec((rows, wide), lambda f: (0, f)), ANY),
        scratch_shapes=[
            pltpu.VMEM((rows, D), bf16),
            pltpu.VMEM((2, wide, D), bf16),
            pltpu.SemaphoreType.DMA((2,)),
        ],
        input_output_aliases={4: 1},
        compiler_params=params(has_side_effects=True),
        cost_estimate=cost(4 * rows * D * D, 4 * D * D + 8 * rows * D),
        name="project_out_back",
    )(table, grad, weights, attended, sums)


def input_gradient(key_grad, value_grad, weights):
    rows = key_grad.shape[0]
    tile = row_tile(rows)

    def body(k_ref, v_ref, wk_ref, wv_ref, out_ref):
        out_ref[...] = (
            dot_right(k_ref[...], wk_ref[...]) + dot_right(v_ref[...], wv_ref[...])
        ).astype(bf16)

    return pl.pallas_call(
        body,
        grid=(rows // tile,),
        out_shape=jax.ShapeDtypeStruct((rows, D), bf16),
        in_specs=[
            pl.BlockSpec((tile, D), lambda t: (t, 0)),
            pl.BlockSpec((tile, D), lambda t: (t, 0)),
            pl.BlockSpec((D, D), lambda t: (at(KEY), 0)),
            pl.BlockSpec((D, D), lambda t: (at(VALUE), 0)),
        ],
        out_specs=pl.BlockSpec((tile, D), lambda t: (t, 0)),
        compiler_params=params(),
        cost_estimate=cost(4 * rows * D * D, 4 * D * D + 6 * rows * D),
        name="input_gradient",
    )(key_grad, value_grad, weights, weights)


def projections_back(normed, query_grad, sources, own_keys, weights, sums, table, ranks):
    rows = normed.shape[0]
    tile = row_tile(rows)
    wide = 512
    count = len(sources)
    lengths = [source[0].shape[0] for source in sources]

    def body(table_ref, n_ref, q_ref, *refs):
        normed_refs = refs[:count]
        key_refs = refs[count : 2 * count]
        value_refs = refs[2 * count : 3 * count]
        w_ref, sums_in, out_ref, sums_ref = refs[3 * count : 3 * count + 4]
        scratch = refs[3 * count + 4 :]
        own_t = scratch[0]
        source_t = scratch[1 : 1 + count]
        part, sem = scratch[1 + count :]
        step = pl.program_id(0)
        slot = lax.rem(step, 2)

        @pl.when(step == 0)
        def _():
            for t in range(0, rows, tile):
                own_t[:, t : t + tile] = n_ref[t : t + tile].T
            for n_from, n_to, length in zip(normed_refs, source_t, lengths):
                small = row_tile(length)
                for t in range(0, length, small):
                    n_to[:, t : t + small] = n_from[t : t + small].T

        @pl.when(step >= 2)
        def _():
            wait_blocks(part.at[slot], sem.at[slot])

        @pl.when(step < 2)
        def _():
            for t in range(0, rows, tile):
                new = dot_right(q_ref[t : t + tile], w_ref[...])

                @pl.when(step == 0)
                def _():
                    out_ref[t : t + tile] = new

                @pl.when(step == 1)
                def _():
                    out_ref[t : t + tile] += new

            for t in range(0, D, 256):
                part[slot, t : t + 256] = dot(own_t[t : t + 256], q_ref[...]).astype(bf16)
            start_blocks(
                table_ref, sums_ref, part.at[slot], sem.at[slot], QUERY, 0, lax.rem(step, 2) * 4,
                ranks,
            )

        def other(grad_refs, matrix):
            if own_keys:
                for t in range(0, rows, tile):
                    out_ref[t : t + tile] += dot_right(grad_refs[0][t : t + tile], w_ref[...])
            for t in range(0, D, 256):
                total = dot(source_t[0][t : t + 256], grad_refs[0][...])
                for n_t, grad_ref in zip(source_t[1:], grad_refs[1:]):
                    total = total + dot(n_t[t : t + 256], grad_ref[...])
                part[slot, t : t + 256] = total.astype(bf16)
            start_blocks(
                table_ref, sums_ref, part.at[slot], sem.at[slot], matrix, 0, lax.rem(step, 2) * 4,
                ranks,
            )

        @pl.when((step >= 2) & (step < 4))
        def _():
            other(key_refs, KEY)

        @pl.when(step >= 4)
        def _():
            other(value_refs, VALUE)

        @pl.when(step == 5)
        def _():
            for s in range(2):
                wait_blocks(part.at[s], sem.at[s])

    operands = [table, normed, query_grad]
    specs = [
        SMEM,
        const_spec((rows, D)),
        pl.BlockSpec((rows, wide), lambda f: (0, jnp.minimum(f, 1))),
    ]
    operands += [source[0] for source in sources]
    specs += [const_spec((length, D)) for length in lengths]
    operands += [source[1] for source in sources]
    specs += [
        pl.BlockSpec((length, wide), lambda f: (0, jnp.clip(f - 2, 0, 1))) for length in lengths
    ]
    operands += [source[2] for source in sources]
    specs += [
        pl.BlockSpec((length, wide), lambda f: (0, jnp.clip(f - 4, 0, 1))) for length in lengths
    ]
    operands += [weights, sums]
    specs += [pl.BlockSpec((D, wide), lambda f: (at(QUERY) + f // 2, f % 2)), ANY]
    return pl.pallas_call(
        body,
        grid=(6,),
        out_shape=(
            jax.ShapeDtypeStruct((rows, D), f32),
            jax.ShapeDtypeStruct(sums.shape, bf16),
        ),
        in_specs=specs,
        out_specs=(const_spec((rows, D)), ANY),
        scratch_shapes=[pltpu.VMEM((D, rows), bf16)]
        + [pltpu.VMEM((D, length), bf16) for length in lengths]
        + [pltpu.VMEM((2, D, wide), bf16), pltpu.SemaphoreType.DMA((2,))],
        input_output_aliases={len(operands) - 1: 1},
        compiler_params=params(has_side_effects=True),
        cost_estimate=cost(
            (4 * rows + sum(4 * length for length in lengths) + 4 * rows) * D * D, 30 * D * D
        ),
        name="projections_back",
    )(*operands)


def attention_forward(queries, sources, segments, rank, spans, slopes):
    rows = queries.shape[0]
    tall = row_tile(rows)
    broad = 512
    count = len(sources)
    lengths = [source[0].shape[0] for source in sources]
    bases = jnp.stack([jnp.asarray(source[2], jnp.int32) for source in sources] + [rank * rows])
    columns = [
        lax.dynamic_slice_in_dim(segments, source[2], length).reshape(1, length)
        for source, length in zip(sources, lengths)
    ]
    own = lax.dynamic_slice_in_dim(segments, rank * rows, rows).reshape(rows, 1)

    def body(base_ref, span_ref, slope_ref, seg_ref, *refs):
        q_ref, own_ref = refs[0], refs[1]
        key_refs = refs[2 : 2 + count]
        value_refs = refs[2 + count : 2 + 2 * count]
        column_refs = refs[2 + 2 * count : 2 + 3 * count]
        out_ref, total_ref = refs[2 + 3 * count : 4 + 3 * count]
        peak, total, mixed = refs[4 + 3 * count :]
        head, block = pl.program_id(0), pl.program_id(1)
        slope = slope_ref[head] * LOG2E
        first = base_ref[count] + block * tall
        peak[...] = jnp.full(peak.shape, MASKED, f32)
        total[...] = jnp.zeros(total.shape, f32)
        mixed[...] = jnp.zeros(mixed.shape, f32)
        query = q_ref[...]
        apart = (
            lax.broadcasted_iota(jnp.int32, (tall, broad), 0)
            - lax.broadcasted_iota(jnp.int32, (tall, broad), 1)
        ).astype(f32)
        same_rows = seg_ref[first] == seg_ref[first + tall - 1]

        for number in range(count):
            base = base_ref[number]

            def step(k, unused, number=number, base=base):
                here = pl.ds(pl.multiple_of(k * broad, broad), broad)
                key = key_refs[number][here, :]
                value = value_refs[number][here, :]
                start = base + k * broad
                scores = dot_right(query, key) * (SCORE_SCALE * LOG2E)
                scores = scores - slope * jnp.abs(apart + (first - start).astype(f32))

                def finish(scores):
                    old = peak[:, 0:1]
                    new = jnp.maximum(old, jnp.max(scores, axis=-1, keepdims=True))
                    shifted = jnp.exp2(scores - new)
                    fade = jnp.exp2(old - new)
                    peak[...] = jnp.broadcast_to(new, peak.shape)
                    total[...] = total[...] * fade + jnp.sum(shifted, axis=-1, keepdims=True)
                    mixed[...] = mixed[...] * fade + dot(shifted.astype(bf16), value)

                inside = (
                    same_rows
                    & (seg_ref[start] == seg_ref[start + broad - 1])
                    & (seg_ref[start] == seg_ref[first])
                )

                @pl.when(inside)
                def _():
                    finish(scores)

                @pl.when(jnp.logical_not(inside))
                def _():
                    related = own_ref[...] == column_refs[number][:, here]
                    finish(jnp.where(related, scores, MASKED))

                return unused

            span = (block * count + number) * 2
            lax.fori_loop(span_ref[span], span_ref[span + 1], step, 0)
        out_ref[...] = (mixed[...] / total[...]).astype(bf16)
        logs = peak[...] + jnp.log2(total[...])
        total_ref[...] = logs.T[0:1, :].reshape(1, 1, tall)

    specs = [SMEM, SMEM, SMEM, SMEM]
    specs += [
        pl.BlockSpec((tall, HEAD_DIM), lambda h, q: (q, h)),
        pl.BlockSpec((tall, 1), lambda h, q: (q, 0)),
    ]
    operands = [bases, spans, slopes, segments, queries, own]
    for shift in (0, HEADS):
        for (array, column, unused), length in zip(sources, lengths):
            operands.append(array)
            specs.append(
                pl.BlockSpec(
                    (length, HEAD_DIM), lambda h, q, c=column + shift: (0, c + h)
                )
            )
    for segment_row, length in zip(columns, lengths):
        operands.append(segment_row)
        specs.append(const_spec((1, length)))
    return pl.pallas_call(
        body,
        grid=(HEADS, rows // tall),
        out_shape=(
            jax.ShapeDtypeStruct((rows, D), bf16),
            jax.ShapeDtypeStruct((HEADS, 1, rows), f32),
        ),
        in_specs=specs,
        out_specs=(
            pl.BlockSpec((tall, HEAD_DIM), lambda h, q: (q, h)),
            pl.BlockSpec((1, 1, tall), lambda h, q: (h, 0, q)),
        ),
        scratch_shapes=[pltpu.VMEM((tall, HEAD_DIM), f32)] * 3,
        compiler_params=params(),
        cost_estimate=cost(2 * rows * sum(lengths) * D, 8 * rows * D),
        name="attention_forward",
    )(*operands)


def attention_backward(queries, sources, segments, rank, spans, slopes, logs, grads, attended):
    rows = queries.shape[0]
    tall = row_tile(rows)
    broad = 512
    count = len(sources)
    lengths = [source[0].shape[0] for source in sources]
    bases = jnp.stack([jnp.asarray(source[2], jnp.int32) for source in sources] + [rank * rows])
    columns = [
        lax.dynamic_slice_in_dim(segments, source[2], length).reshape(length, 1)
        for source, length in zip(sources, lengths)
    ]
    own = lax.dynamic_slice_in_dim(segments, rank * rows, rows).reshape(1, rows)

    def body(base_ref, span_ref, slope_ref, seg_ref, *refs):
        q_ref, own_ref, log_ref, grad_ref, att_ref = refs[:5]
        key_refs = refs[5 : 5 + count]
        value_refs = refs[5 + count : 5 + 2 * count]
        column_refs = refs[5 + 2 * count : 5 + 3 * count]
        out_ref = refs[5 + 3 * count]
        key_out = refs[6 + 3 * count : 6 + 4 * count]
        value_out = refs[6 + 4 * count : 6 + 5 * count]
        scratch = refs[6 + 5 * count :]
        query_sum = scratch[0]
        key_sum = scratch[1 : 1 + count]
        value_sum = scratch[1 + count : 1 + 2 * count]
        head, block = pl.program_id(0), pl.program_id(1)
        slope = slope_ref[head] * LOG2E
        first = base_ref[count] + block * tall

        @pl.when(block == 0)
        def _():
            for ref in (*key_sum, *value_sum):
                ref[...] = jnp.zeros(ref.shape, f32)

        query_sum[...] = jnp.zeros(query_sum.shape, f32)
        query = q_ref[...]
        grad = grad_ref[...]
        products = grad.astype(f32) * att_ref[...].astype(f32)
        delta = lax.dot_general(
            jnp.ones((8, HEAD_DIM), f32),
            products,
            (((1,), (1,)), ((), ())),
            precision=lax.Precision.HIGHEST,
            preferred_element_type=f32,
        )[0:1, :]
        log_row = log_ref[0]
        apart = (
            lax.broadcasted_iota(jnp.int32, (broad, tall), 1)
            - lax.broadcasted_iota(jnp.int32, (broad, tall), 0)
        ).astype(f32)
        same_rows = seg_ref[first] == seg_ref[first + tall - 1]

        for number in range(count):
            base = base_ref[number]

            def step(k, unused, number=number, base=base):
                here = pl.ds(pl.multiple_of(k * broad, broad), broad)
                key = key_refs[number][here, :]
                value = value_refs[number][here, :]
                start = base + k * broad
                scores = dot_right(key, query) * (SCORE_SCALE * LOG2E)
                scores = scores - slope * jnp.abs(apart + (first - start).astype(f32))

                def finish(scores):
                    probs = jnp.exp2(scores - log_row)
                    value_sum[number][here, :] += dot(probs.astype(bf16), grad)
                    prob_grad = dot_right(value, grad)
                    score_grad = (probs * (prob_grad - delta)).astype(bf16)
                    key_sum[number][here, :] += dot(score_grad, query)
                    query_sum[...] += dot_left(score_grad, key)

                inside = (
                    same_rows
                    & (seg_ref[start] == seg_ref[start + broad - 1])
                    & (seg_ref[start] == seg_ref[first])
                )

                @pl.when(inside)
                def _():
                    finish(scores)

                @pl.when(jnp.logical_not(inside))
                def _():
                    related = own_ref[...] == column_refs[number][here, :]
                    finish(jnp.where(related, scores, MASKED))

                return unused

            span = (block * count + number) * 2
            lax.fori_loop(span_ref[span], span_ref[span + 1], step, 0)
        out_ref[...] = (query_sum[...] * SCORE_SCALE).astype(bf16)

        @pl.when(block == pl.num_programs(1) - 1)
        def _():
            for number in range(count):
                key_out[number][...] = (key_sum[number][...] * SCORE_SCALE).astype(bf16)
                value_out[number][...] = value_sum[number][...].astype(bf16)

    row_spec = pl.BlockSpec((tall, HEAD_DIM), lambda h, q: (q, h))
    specs = [SMEM, SMEM, SMEM, SMEM]
    specs += [
        row_spec,
        pl.BlockSpec((1, tall), lambda h, q: (0, q)),
        pl.BlockSpec((1, 1, tall), lambda h, q: (h, 0, q)),
        row_spec,
        row_spec,
    ]
    operands = [bases, spans, slopes, segments, queries, own, logs, grads, attended]
    for shift in (0, HEADS):
        for (array, column, unused), length in zip(sources, lengths):
            operands.append(array)
            specs.append(
                pl.BlockSpec(
                    (length, HEAD_DIM), lambda h, q, c=column + shift: (0, c + h)
                )
            )
    for segment_column, length in zip(columns, lengths):
        operands.append(segment_column)
        specs.append(const_spec((length, 1)))
    source_specs = [pl.BlockSpec((length, HEAD_DIM), lambda h, q: (0, h)) for length in lengths]
    source_shapes = [jax.ShapeDtypeStruct((length, D), bf16) for length in lengths]
    sums = [pltpu.VMEM((length, HEAD_DIM), f32) for length in lengths]
    out = pl.pallas_call(
        body,
        grid=(HEADS, rows // tall),
        out_shape=(jax.ShapeDtypeStruct((rows, D), bf16), *source_shapes, *source_shapes),
        in_specs=specs,
        out_specs=(row_spec, *source_specs, *source_specs),
        scratch_shapes=[pltpu.VMEM((tall, HEAD_DIM), f32), *sums, *sums],
        compiler_params=params(),
        cost_estimate=cost(5 * rows * sum(lengths) * D, 12 * rows * D),
        name="attention_backward",
    )(*operands)
    return out[0], out[1 : 1 + count], out[1 + count :]


def key_spans(segments, rank, rows, sources):
    tall = row_tile(rows)
    broad = 512
    blocks = rows // tall
    own = lax.dynamic_slice_in_dim(segments, rank * rows, rows).reshape(blocks, tall)
    low = jnp.sum(segments[None, :] < own[:, :1], axis=1)
    high = jnp.sum(segments[None, :] <= own[:, -1:], axis=1)
    spans = []
    for length, base in sources:
        start = jnp.clip(low - base, 0, length)
        end = jnp.clip(high - base, 0, length)
        first = start // broad
        last = jnp.where(end > start, (end + broad - 1) // broad, first)
        spans.append(jnp.stack([first, last], axis=-1))
    return jnp.stack(spans, axis=1).reshape(-1).astype(jnp.int32)


def conv_forward(stream, before, behind, gain, weights, taps, masks):
    rows = stream.shape[0]
    tall = rows + 2 * HALO
    tile = row_tile(rows)
    wide = 256
    steps = D // wide

    def body(
        x_ref, before_ref, behind_ref, gain_ref, taps_ref, mask_ref, value_ref, gate_ref, out_w_ref,
        out_ref, linear_ref, gate_out_ref, normed, glu,
    ):
        step = pl.program_id(0)

        @pl.when(step == 0)
        def _():
            gain_row = gain_ref[...]
            normed[0:HALO] = norm(before_ref[...], gain_row).astype(bf16)
            normed[rows + HALO :] = norm(behind_ref[...], gain_row).astype(bf16)
            for t in range(0, rows, tile):
                x = x_ref[t : t + tile]
                normed[HALO + t : HALO + t + tile] = norm(x, gain_row).astype(bf16)
                out_ref[t : t + tile] = x

        pieces = [(0, HALO)]
        pieces += [(HALO + t, tile) for t in range(0, rows, tile)]
        pieces += [(rows + HALO, HALO)]
        for t, size in pieces:
            here = slice(t, t + size)
            linear = dot(normed[here], value_ref[...])
            gate = dot(normed[here], gate_ref[...])
            linear_ref[here] = linear.astype(bf16)
            gate_out_ref[here] = gate.astype(bf16)
            glu[here] = linear * sigmoid(gate)
        for t in range(0, rows, tile):
            sums = []
            for half in range(0, wide, 128):
                total = jnp.zeros((tile, 128), f32)
                for k in range(KERNEL):
                    moved = glu[HALO + t + k - 2 : HALO + t + k - 2 + tile, half : half + 128]
                    mask = mask_ref[k, HALO + t : HALO + t + tile]
                    total = total + taps_ref[k : k + 1, half : half + 128] * moved * mask
                sums.append(total)
            conved = jnp.concatenate(sums, axis=1)
            act = (conved * sigmoid(conved)).astype(bf16)
            out_ref[t : t + tile] += dot(act, out_w_ref[...])

    return pl.pallas_call(
        body,
        grid=(steps,),
        out_shape=(
            jax.ShapeDtypeStruct((rows, D), f32),
            jax.ShapeDtypeStruct((tall, D), bf16),
            jax.ShapeDtypeStruct((tall, D), bf16),
        ),
        in_specs=[
            const_spec((rows, D)),
            const_spec((HALO, D)),
            const_spec((HALO, D)),
            const_spec((1, D)),
            pl.BlockSpec((KERNEL, wide), lambda c: (0, c)),
            const_spec((KERNEL, tall, 128)),
            pl.BlockSpec((D, wide), lambda c: (at(CONV_VALUE), c)),
            pl.BlockSpec((D, wide), lambda c: (at(CONV_GATE), c)),
            pl.BlockSpec((wide, D), lambda c: (at(CONV_OUT) * 4 + c, 0)),
        ],
        out_specs=(
            const_spec((rows, D)),
            pl.BlockSpec((tall, wide), lambda c: (0, c)),
            pl.BlockSpec((tall, wide), lambda c: (0, c)),
        ),
        scratch_shapes=[pltpu.VMEM((tall, D), bf16), pltpu.VMEM((tall, wide), f32)],
        compiler_params=params(),
        cost_estimate=cost(6 * rows * D * D, 6 * D * D + 12 * rows * D),
        name="conv_forward",
    )(stream, before, behind, gain, taps, masks, weights, weights, weights)


def conv_backward(
    grad, before, behind, stream, gain, linear, gate, weights, taps, masks, sums, table, ranks
):
    rows = stream.shape[0]
    tall = rows + 2 * HALO
    tile = row_tile(rows)
    wide = 256
    steps = D // wide

    def body(
        table_ref, g_ref, before_ref, behind_ref, x_ref, gain_ref, linear_ref, gate_ref, taps_ref,
        mask_ref, value_ref, gate_w_ref, out_w_ref, sums_in, out_ref, gain_out_ref, taps_out_ref,
        sums_ref, low, normed_t, grad_sum, glu, conv_grad, act_t, value_grad, gate_grad,
        value_part, gate_part, out_part, value_sem, gate_sem, out_sem,
    ):
        step = pl.program_id(0)
        slot = lax.rem(step, 2)

        @pl.when(step == 0)
        def _():
            low[0:HALO] = before_ref[...]
            low[rows + HALO :] = behind_ref[...]
            for t in range(0, rows, tile):
                here = slice(t, t + tile)
                low[HALO + t : HALO + t + tile] = g_ref[here].astype(bf16)
                normed_t[:, here] = norm(x_ref[here], gain_ref[...]).astype(bf16).T
                grad_sum[here] = jnp.zeros((tile, D), f32)

        pieces = [(0, HALO)]
        pieces += [(HALO + t, tile) for t in range(0, rows, tile)]
        pieces += [(rows + HALO, HALO)]
        for t, size in pieces:
            here = slice(t, t + size)
            glu[here] = linear_ref[here].astype(f32) * sigmoid(gate_ref[here].astype(f32))

        edge = 8
        pieces = [(HALO - edge, edge)]
        pieces += [(HALO + t, tile) for t in range(0, rows, tile)]
        pieces += [(rows + HALO, edge)]
        for t, size in pieces:
            totals = []
            for half in range(0, wide, 128):
                total = jnp.zeros((size, 128), f32)
                for k in range(KERNEL):
                    moved = glu[t + k - 2 : t + k - 2 + size, half : half + 128]
                    mask = mask_ref[k, t : t + size]
                    total = total + taps_ref[k : k + 1, half : half + 128] * moved * mask
                totals.append(total)
            conved = jnp.concatenate(totals, axis=1)
            sigma = sigmoid(conved)
            act = conved * sigma
            if size == tile:
                act_t[:, t - HALO : t - HALO + size] = act.astype(bf16).T
                rows_grad = dot_right(low[t : t + size], out_w_ref[...])
            elif t < HALO:
                rows_grad = dot_right(low[0:HALO], out_w_ref[...])[edge:]
            else:
                rows_grad = dot_right(low[rows + HALO :], out_w_ref[...])[:edge]
            conv_grad[t : t + size] = rows_grad * (sigma + act * (1.0 - sigma))

        tap_sums = [[jnp.zeros((1, 128), f32) for k in range(KERNEL)] for half in range(2)]
        for t in range(0, rows, tile):
            values, gates = [], []
            for number, half in enumerate(range(0, wide, 128)):
                lanes = slice(half, half + 128)
                start = HALO + t
                center = conv_grad[start : start + tile, lanes]
                total = jnp.zeros((tile, 128), f32)
                for k in range(KERNEL):
                    back = KERNEL - 1 - k
                    moved = conv_grad[start + 2 - k : start + 2 - k + tile, lanes]
                    total = total + taps_ref[k : k + 1, lanes] * moved * mask_ref[
                        back, start : start + tile
                    ]
                    shifted = glu[start + k - 2 : start + k - 2 + tile, lanes]
                    tap_sums[number][k] = tap_sums[number][k] + jnp.sum(
                        center * shifted * mask_ref[k, start : start + tile],
                        axis=0,
                        keepdims=True,
                    )
                sigma = sigmoid(gate_ref[start : start + tile, lanes].astype(f32))
                moved_value = total * sigma
                values.append(moved_value.astype(bf16))
                gates.append(
                    (
                        moved_value
                        * linear_ref[start : start + tile, lanes].astype(f32)
                        * (1.0 - sigma)
                    ).astype(bf16)
                )
            value_tile = jnp.concatenate(values, axis=1)
            gate_tile = jnp.concatenate(gates, axis=1)
            here = slice(t, t + tile)
            value_grad[here] = value_tile
            gate_grad[here] = gate_tile
            grad_sum[here] += dot_right(value_tile, value_ref[...]) + dot_right(
                gate_tile, gate_w_ref[...]
            )
        for k in range(KERNEL):
            taps_out_ref[k : k + 1] = jnp.concatenate([tap_sums[0][k], tap_sums[1][k]], axis=1)

        @pl.when(step >= 2)
        def _():
            wait_blocks(value_part.at[slot], value_sem.at[slot])
            wait_blocks(gate_part.at[slot], gate_sem.at[slot])
            wait_blocks(out_part.at[slot], out_sem.at[slot])

        for t in range(0, D, 256):
            value_part[slot, t : t + 256] = dot(normed_t[t : t + 256], value_grad[...]).astype(bf16)
            gate_part[slot, t : t + 256] = dot(normed_t[t : t + 256], gate_grad[...]).astype(bf16)
        out_part[slot] = dot(act_t[...], low[HALO : rows + HALO]).astype(bf16)
        start_blocks(
            table_ref, sums_ref, value_part.at[slot], value_sem.at[slot], CONV_VALUE, 0, step * 2,
            ranks,
        )
        start_blocks(
            table_ref, sums_ref, gate_part.at[slot], gate_sem.at[slot], CONV_GATE, 0, step * 2,
            ranks,
        )
        start_blocks(
            table_ref, sums_ref, out_part.at[slot], out_sem.at[slot], CONV_OUT, step * 2, 0, ranks
        )

        @pl.when(step == steps - 1)
        def _():
            gain_sum = jnp.zeros((1, D), f32)
            for t in range(0, rows, tile):
                here = slice(t, t + tile)
                back, part = norm_back(x_ref[here], gain_ref[...], grad_sum[here])
                gain_sum = gain_sum + part
                out_ref[here] = g_ref[here] + back
            gain_out_ref[...] = gain_sum
            for s in range(2):
                wait_blocks(value_part.at[s], value_sem.at[s])
                wait_blocks(gate_part.at[s], gate_sem.at[s])
                wait_blocks(out_part.at[s], out_sem.at[s])

    operands = [
        table, grad, before, behind, stream, gain, linear, gate, taps, masks, weights, weights,
        weights, sums,
    ]
    return pl.pallas_call(
        body,
        grid=(steps,),
        out_shape=(
            jax.ShapeDtypeStruct((rows, D), f32),
            jax.ShapeDtypeStruct((1, D), f32),
            jax.ShapeDtypeStruct((KERNEL, D), f32),
            jax.ShapeDtypeStruct(sums.shape, bf16),
        ),
        in_specs=[
            SMEM,
            const_spec((rows, D)),
            const_spec((HALO, D)),
            const_spec((HALO, D)),
            const_spec((rows, D)),
            const_spec((1, D)),
            pl.BlockSpec((tall, wide), lambda c: (0, c)),
            pl.BlockSpec((tall, wide), lambda c: (0, c)),
            pl.BlockSpec((KERNEL, wide), lambda c: (0, c)),
            const_spec((KERNEL, tall, 128)),
            pl.BlockSpec((D, wide), lambda c: (at(CONV_VALUE), c)),
            pl.BlockSpec((D, wide), lambda c: (at(CONV_GATE), c)),
            pl.BlockSpec((wide, D), lambda c: (at(CONV_OUT) * 4 + c, 0)),
            ANY,
        ],
        out_specs=(
            const_spec((rows, D)),
            const_spec((1, D)),
            pl.BlockSpec((KERNEL, wide), lambda c: (0, c)),
            ANY,
        ),
        scratch_shapes=[
            pltpu.VMEM((tall, D), bf16),
            pltpu.VMEM((D, rows), bf16),
            pltpu.VMEM((rows, D), f32),
            pltpu.VMEM((tall, wide), f32),
            pltpu.VMEM((tall, wide), f32),
            pltpu.VMEM((wide, rows), bf16),
            pltpu.VMEM((rows, wide), bf16),
            pltpu.VMEM((rows, wide), bf16),
            pltpu.VMEM((2, D, wide), bf16),
            pltpu.VMEM((2, D, wide), bf16),
            pltpu.VMEM((2, wide, D), bf16),
            pltpu.SemaphoreType.DMA((2,)),
            pltpu.SemaphoreType.DMA((2,)),
            pltpu.SemaphoreType.DMA((2,)),
        ],
        input_output_aliases={len(operands) - 1: 3},
        compiler_params=params(has_side_effects=True),
        cost_estimate=cost(12 * rows * D * D, 12 * D * D + 16 * rows * D),
        name="conv_backward",
    )(*operands)


def shampoo(grads, left_stats, right_stats, left_root, right_root, master, average):
    slots = grads.shape[0]
    each = 2 if slots % 2 == 0 else 1
    old_bias = 1.0 - DECAY_AVERAGE ** (STEP - 1)
    new_bias = 1.0 - DECAY_AVERAGE**STEP

    def body(g_ref, ls_ref, rs_ref, lr_ref, rr_ref, m_ref, a_ref, go, lo, ro, mo, ao):
        for n in range(each):
            grad = g_ref[n]
            go[n] = grad.astype(f32)
            lo[n] = DECAY_STAT * ls_ref[n] + (1.0 - DECAY_STAT) * dot_right(grad, grad)
            ro[n] = DECAY_STAT * rs_ref[n] + (1.0 - DECAY_STAT) * dot_left(grad, grad)
            inner = dot(grad, rr_ref[n].astype(bf16))
            turned = dot(lr_ref[n].astype(bf16), inner.astype(bf16))
            mean_sq = jnp.mean(turned * turned, axis=(0, 1), keepdims=True)
            new = m_ref[n] - RATE_BLOCK * turned * lax.rsqrt(mean_sq + 1e-06)
            mo[n] = new
            ao[n] = (DECAY_AVERAGE * old_bias / new_bias) * a_ref[n] + (
                (1.0 - DECAY_AVERAGE) / new_bias
            ) * new

    spec = pl.BlockSpec((each, BLOCK, BLOCK), lambda s: (s, 0, 0))
    shape = jax.ShapeDtypeStruct((slots, BLOCK, BLOCK), f32)
    return pl.pallas_call(
        body,
        grid=(slots // each,),
        out_shape=(shape,) * 5,
        in_specs=[spec] * 7,
        out_specs=(spec,) * 5,
        compiler_params=params(),
        name="shampoo",
    )(grads, left_stats, right_stats, left_root, right_root, master, average)


def vector_step(values, grads):
    mean_sq = jnp.mean(grads * grads, axis=-1, keepdims=True)
    return values - RATE_VECTOR * grads * lax.rsqrt(mean_sq + 1e-06)


def scatter_position(owner, rank, coords, fast, slot_dev):
    if not fast:
        slots = slot_dev * lax.axis_size(("z", "x", "core"))
        return rank * slots + owner
    own_rank, own_x, unused = coords
    device = owner // slot_dev
    slot = owner % slot_dev
    core = device % 2
    x_at = (device // 2) % 2
    z_at = device // 4
    dy = rank ^ own_rank
    dx = x_at ^ own_x
    position = jnp.zeros_like(owner)
    for first, count, kind in SCATTER_PIECES:
        outer, inner = (dx, dy) if kind == "x" else (dy, dx)
        here = (
            32 * first
            + (((core * 2 + outer) * 2 + inner) * 4 + z_at) * count
            + slot
            - first
        )
        position = jnp.where((slot >= first) & (slot < first + count), here, position)
    return position


def scatter_sums(sums, fast):
    if not fast:
        return lax.psum_scatter(sums, ("mp", "z", "x", "core"), scatter_dimension=0, tiled=True)
    results = []
    for first, count, kind in SCATTER_PIECES:
        piece = sums[32 * first : 32 * (first + count)]
        mine = lax.psum_scatter(piece, "core", scatter_dimension=0, tiled=True)
        for axis in ("x", "mp") if kind == "x" else ("mp", "x"):
            half = mine.shape[0] // 2
            arrived = swap(mine[half:], axis)
            mine = (mine[:half].astype(f32) + arrived.astype(f32)).astype(bf16)
        results.append(lax.psum_scatter(mine, "z", scatter_dimension=0, tiled=True))
    return jnp.concatenate(results, axis=0)


def total(values):
    return lax.psum(values, ("mp", "z", "x", "core"))


def edges(first_rows, last_rows, ranks):
    before = lax.ppermute(last_rows, "mp", [(r, r + 1) for r in range(ranks - 1)])
    behind = lax.ppermute(first_rows, "mp", [(r + 1, r) for r in range(ranks - 1)])
    return before, behind


def local(fast):
    def run(
        stream, cotangent, segments, owners, master, average, left_stats, right_stats, left_root,
        right_root, gains, kernel,
    ):
        ranks = lax.axis_size("mp")
        rank = lax.axis_index("mp")
        coords = (rank, lax.axis_index("x"), lax.axis_index("core"))
        rows = stream.shape[0]
        slot_dev = master.shape[1]
        chips = lax.axis_size("z") * lax.axis_size("x") * 2
        slots = slot_dev * chips
        segment_ids = segments[0]
        group = segment_ids.shape[0]
        unused, blocks = offsets(ranks)

        owners_all = lax.all_gather(owners, "mp", axis=0, tiled=True)
        places = jnp.asarray(weight_places(ranks))
        match = owners_all[:, None, :] == jnp.arange(slots)[None, :, None]
        slot_places = jnp.sum(jnp.where(match, places[:, None, :], 0), axis=-1)
        rows_all = CHUNKS * D
        if slots > blocks:
            slot_places = jnp.where(jnp.any(match, axis=-1), slot_places, WEIGHT_BLOCKS)
            rows_all = rows_all + BLOCK
        slot_places = slot_places.reshape(-1).astype(jnp.int32)
        table = scatter_position(
            owners_all, jnp.arange(ranks)[:, None], coords, fast, slot_dev
        ).reshape(-1).astype(jnp.int32)

        slopes = 2.0 ** (-8.0 * (jnp.arange(HEADS).astype(f32) + 1.0) / HEADS)
        padded = jnp.pad(segment_ids, (HALO, HALO), constant_values=-1)
        wide_ids = jnp.pad(padded, (2, 2), constant_values=-2)
        tall = rows + 2 * HALO
        here = lax.dynamic_slice_in_dim(padded, rank * rows, tall)
        masks = jnp.stack(
            [
                (lax.dynamic_slice_in_dim(wide_ids, rank * rows + k, tall) == here).astype(f32)
                for k in range(KERNEL)
            ]
        )
        masks = jnp.broadcast_to(masks[:, :, None], (KERNEL, tall, 128))
        if fast:
            source_rows = [(rows, rank * rows), (rows, (1 - rank) * rows)]
        else:
            source_rows = [(group, 0)]
        spans = key_spans(segment_ids, rank, rows, source_rows)

        weights = gather_weights(
            master[0].astype(bf16), slot_places, coords, fast, rows_all
        )

        def gain(n):
            return gains[n : n + 1]

        after_first, pre_first, normed_attn = ffn_forward(
            stream, gain(0), gain(1), weights, UP1, DOWN1
        )
        if fast:
            other = swap(normed_attn, "mp")
            qkv = project(normed_attn, weights, QUERY, 3)
            other_kv = project(other, weights, KEY, 2)
            queries = qkv
            sources = [(qkv, HEADS, source_rows[0][1]), (other_kv, 0, source_rows[1][1])]
        else:
            other = lax.all_gather(normed_attn, "mp", axis=0, tiled=True)
            queries = project(normed_attn, weights, QUERY, 1)
            sources = [(project(other, weights, KEY, 2), 0, 0)]
        attended, logs = attention_forward(queries, sources, segment_ids, rank, spans, slopes)
        after_attn = project_out(attended, weights, OUT, after_first)
        before, behind = edges(after_attn[:HALO], after_attn[-HALO:], ranks)
        after_conv, linear, gate = conv_forward(
            after_attn, before, behind, gain(2), weights, kernel, masks
        )
        after_second, pre_second, output = ffn_forward(
            after_conv, gain(3), gain(4), weights, UP2, DOWN2
        )

        sums_shape = (ranks * slots, BLOCK, BLOCK)
        sums = jnp.zeros(sums_shape, bf16)
        grad_conv, gains_a, sums = ffn_backward(
            after_second, gain(4), [cotangent], None, after_conv, gain(3), pre_second, weights,
            UP2, DOWN2, sums, table, ranks,
        )
        before, behind = edges(
            grad_conv[:HALO].astype(bf16), grad_conv[-HALO:].astype(bf16), ranks
        )
        grad_attn, gains_b, tap_grads, sums = conv_backward(
            grad_conv, before, behind, after_attn, gain(2), linear, gate, weights, kernel, masks,
            sums, table, ranks,
        )
        mixed_grad, sums = project_out_back(
            grad_attn, weights, OUT, attended, sums, table, ranks
        )
        query_grad, key_grads, value_grads = attention_backward(
            queries, sources, segment_ids, rank, spans, slopes, logs, mixed_grad, attended
        )
        away = input_gradient(key_grads[-1], value_grads[-1], weights)
        if fast:
            arrived = swap(away, "mp")
            normed_sources = [normed_attn, other]
        else:
            arrived = lax.psum_scatter(away, "mp", scatter_dimension=0, tiled=True)
            normed_sources = [other]
        near, sums = projections_back(
            normed_attn, query_grad, list(zip(normed_sources, key_grads, value_grads)), fast,
            weights, sums, table, ranks,
        )
        stream_grad, gains_c, sums = ffn_backward(
            after_first, gain(1), [near, arrived], grad_attn, stream, gain(0), pre_first, weights,
            UP1, DOWN1, sums, table, ranks,
        )

        own_grads = scatter_sums(sums, fast)
        small = jnp.concatenate(
            [gains_c[1:2], gains_c[0:1], gains_b, gains_a[1:2], gains_a[0:1], tap_grads]
        )
        small = total(small)
        gain_grads, kernel_grads = small[:5], small[5:]
        block_grads, left_new, right_new, master_new, average_new = shampoo(
            own_grads, left_stats[0], right_stats[0], left_root[0], right_root[0], master[0],
            average[0],
        )
        return (
            output,
            stream_grad,
            block_grads[None],
            left_new[None],
            right_new[None],
            master_new[None],
            average_new[None],
            gain_grads,
            vector_step(gains, gain_grads),
            kernel_grads,
            vector_step(kernel, kernel_grads),
        )

    return run


def solution(mesh):
    ranks, pieces = mesh.shape["mp"], mesh.shape["dp"]
    fast = ranks == 2 and pieces == 16
    xs = 2 if fast else 1
    grid = Mesh(
        np.asarray(mesh.devices).reshape(ranks, pieces // (2 * xs), xs, 2), ("mp", "z", "x", "core")
    )
    dp = ("z", "x", "core")
    rows = P((*dp, "mp"), None)
    slots = P("mp", dp, None, None)
    return jax.shard_map(
        local(fast),
        mesh=grid,
        in_specs=(
            rows, rows, P(dp, None), P("mp", None), slots, slots, slots, slots, slots, slots, P(),
            P(),
        ),
        out_specs=(rows, rows, slots, slots, slots, slots, slots, P(), P(), P(), P()),
        check_vma=False,
    )
```

time: 2070 us -> 2940 us (1.42)
  Pallas kernels: 0 us -> 2050 us
  matrix products: 549 us -> 0 us
  waiting for transfers between devices: 916 us -> 461 us
  local copies, waits for them, and re-layouts: 313 us -> 109 us
  other arithmetic: 224 us -> 37.7 us
  blocking collectives: 41.2 us -> 201 us
  starting transfers between devices: 2.02 us -> 49.3 us
    pallas_call x0 -> x23, Pallas kernels: none -> 2050 us  [the longest x8 1480 us: place_weights(): pl.pallas_call(body, out_shape=jax.ShapeDtypeStruct((rows_all, D), bf16),...]
    dot_general x65 -> x0, matrix products: 549 us -> none  [the longest x11 111 us: dense_right(): lax.dot_general(left_op, right_op, (((1,), (1,)), ((), ())), preferred_el...]
    reduce_scatter x9 -> x16, waiting for transfers between devices: 498 us -> 21.7 us  [the longest x8 21.5 us: scatter_sums(): results.append(lax.psum_scatter(mine, 'z', scatter_dimension=0, tiled=True))]
    ppermute x0 -> x78, waiting for transfers between devices: none -> 437 us  [the longest x74 429 us: swap(): return lax.ppermute(value, axis, [(0, 1), (1, 0)])]
    all_gather x9 -> x0, waiting for transfers between devices: 417 us -> none  [the longest x4 169 us: gather_grads(): return lax.all_gather(values, 'mp', axis=0, tiled=True)]
    all_gather x0 -> x9, blocking collectives: none -> 153 us  [the longest x8 149 us: gather_weights(): column = lax.all_gather(own[first:first + count], 'z', axis=0, tiled=True)]
    reduce_sum x26 -> x2, other arithmetic: 92.3 us -> 0.85 us  [the longest x1 0.62 us: run(): slot_places = jnp.sum(jnp.where(match, places[:, None, :], 0), axis=-1)]
    unnamed x316 -> x156, local copies, waits for them, and re-layouts: 93.3 us -> 14.7 us
  transfers between devices with their start and end apart: 18 -> 94, of which waited for: 14 -> 26; matrix products, arithmetic and copies ran while one was open for 19% -> 4% of each run, Pallas kernels for 0% -> 45%
where the time goes in v1:
time: 2940 us; the launch traced here: 2930 us
  Pallas kernels  2050 us (70%)
  waiting for transfers between devices  461 us (16%)
  blocking collectives  201 us (7%)
  local copies, waits for them, and re-layouts  109 us (4%)
  starting transfers between devices  49.3 us (2%)
  other arithmetic  37.7 us (1%)
    pallas_call x8, Pallas kernels, place_weights(): pl.pallas_call(body, out_shape=jax.ShapeDtypeStruct((rows_all, D), bf16),...  1480 us
    ppermute x74, waiting for transfers between devices, swap(): return lax.ppermute(value, axis, [(0, 1), (1, 0)])  429 us
    all_gather x8, blocking collectives, gather_weights(): column = lax.all_gather(own[first:first + count], 'z', axis=0, tiled=True)  149 us
    pallas_call x2, Pallas kernels, ffn_backward(): pl.pallas_call(body, grid=(steps,), out_shape=(jax.ShapeDtypeStruct((rows...  122 us
    pallas_call x1, Pallas kernels, attention_backward(): pl.pallas_call(body, grid=(HEADS, rows // tall), out_shape=(jax.ShapeDtyp...  116 us
    pallas_call x1, Pallas kernels, attention_forward(): pl.pallas_call(body, grid=(HEADS, rows // tall), out_shape=(jax.ShapeDtyp...  114 us
    pallas_call x2, Pallas kernels, ffn_forward(): pl.pallas_call(body, grid=(steps,), out_shape=(jax.ShapeDtypeStruct((rows...  62.6 us
  transfers between devices with their start and end apart: 94, of which 26 were waited for; matrix products, arithmetic and copies ran while one was open for 4% of the time, Pallas kernels for 45%

profile of v1, /device:TPU:0, one launch (start us, length us, event | category | flops | bytes accessed | tf_op | source)
XLA Modules:
  0.0 2929.1 jit_solution(1352300420718338647)
XLA Ops:
  9.3 16.2 all_gather.34.rest_0_
  28.6 15.5 all_gather.35.rest_0_
  45.2 18.7 all_gather.28.rest_0_
  64.0 18.7 all_gather.29.rest_0_
  87.7 15.9 collective-permute-done.rest_1_
  105.1 16.7 collective-permute-done.7.rest_1_
  121.8 20.0 all_gather.30.rest_0_
  145.9 19.9 all_gather.31.rest_0_
  165.9 5.9 collective-permute-done.51.rest_3_
  173.8 20.3 all_gather.32.rest_0_
  196.7 19.7 all_gather.33.rest_0_
  219.1 18.8 collective-permute-done.35.rest_1_
  241.0 34.3 %collective-permute-done.2.rest_3_ = bf16[24,128,128]{2,1,0:T(8,128)(2,1)} collective-permute-done((bf16[24,128,128]{2,1,0:T(8,128)(2,1)}, bf16[24,128,128]{2,1,0:T(8,128)(2,1)}, u32[]{:S(2)}, u32[]{:S(2)}) %collective-permute-start.2) | collective-permute-done | bytes 786464 | tf_op jit(solution)/shard_map/ppermute | solution.py:178
  279.3 18.9 collective-permute-done.23.rest_3_
  300.9 20.1 collective-permute-done.37.rest_3_
  327.1 4.3 all-gather
  340.0 97.7 %place_weights.8.rest_8_ = bf16[23552,1024]{1,0:T(8,128)(2,1)} custom-call(s32[1472]{0:T(1024)} %reshape.343.table, s32[8]{0:T(128)} %stack.354.base_ref, bf16[12,128,128]{2,1,0:T(8,128)(2,1)} %copy-done.11, bf16[12,128,128]{2,1,0:T(8,128)(2,1)} %copy-done.50, bf16[12,128,128]{2,1,0:T(8,128)(2,1)} %copy-done.51, ...), custom_call_target="tpu_custom_call" | custom-call | bytes 6291456 | tf_op jit(solution)/shard_map/place_weights/pallas_call | solution.py:164
  437.8 97.2 %place_weights.9.rest_8_ = bf16[23552,1024]{1,0:T(8,128)(2,1)} custom-call(s32[1472]{0:T(1024)} %reshape.343.table, s32[8]{0:T(128)} %stack.345.base_ref, bf16[12,128,128]{2,1,0:T(8,128)(2,1)} %copy-done.10, bf16[12,128,128]{2,1,0:T(8,128)(2,1)} %copy-done.47, bf16[12,128,128]{2,1,0:T(8,128)(2,1)} %copy-done.48, ...), custom_call_target="tpu_custom_call", output_to_operand_aliasing={{}: (10, {})} | custom-call | bytes 6291456 | tf_op jit(solution)/shard_map/place_weights/pallas_call | solution.py:164
  535.0 224.3 %place_weights.10.rest_8_ = bf16[23552,1024]{1,0:T(8,128)(2,1)} custom-call(s32[1472]{0:T(1024)} %reshape.343.table, s32[8]{0:T(128)} %stack.336.base_ref, bf16[28,128,128]{2,1,0:T(8,128)(2,1)} %copy-done.4, bf16[28,128,128]{2,1,0:T(8,128)(2,1)} %copy-done.24, bf16[28,128,128]{2,1,0:T(8,128)(2,1)} %copy-done.25, ...), custom_call_target="tpu_custom_call", output_to_operand_aliasing={{}: (10, {})} | custom-call | bytes 14680064 | tf_op jit(solution)/shard_map/place_weights/pallas_call | solution.py:164
  759.3 224.3 %place_weights.11.rest_8_ = bf16[23552,1024]{1,0:T(8,128)(2,1)} custom-call(s32[1472]{0:T(1024)} %reshape.343.table, s32[8]{0:T(128)} %stack.327.base_ref, bf16[28,128,128]{2,1,0:T(8,128)(2,1)} %copy-done.3, bf16[28,128,128]{2,1,0:T(8,128)(2,1)} %copy-done.20, bf16[28,128,128]{2,1,0:T(8,128)(2,1)} %copy-done.21, ...), custom_call_target="tpu_custom_call", output_to_operand_aliasing={{}: (10, {})} | custom-call | bytes 14680064 | tf_op jit(solution)/shard_map/place_weights/pallas_call | solution.py:164
  983.5 224.3 %place_weights.12.rest_8_ = bf16[23552,1024]{1,0:T(8,128)(2,1)} custom-call(s32[1472]{0:T(1024)} %reshape.343.table, s32[8]{0:T(128)} %stack.318.base_ref, bf16[28,128,128]{2,1,0:T(8,128)(2,1)} %copy-done.2, bf16[28,128,128]{2,1,0:T(8,128)(2,1)} %copy-done.17, bf16[28,128,128]{2,1,0:T(8,128)(2,1)} %copy-done.18, ...), custom_call_target="tpu_custom_call", output_to_operand_aliasing={{}: (10, {})} | custom-call | bytes 14680064 | tf_op jit(solution)/shard_map/place_weights/pallas_call | solution.py:164
  1207.8 224.3 %place_weights.13.rest_8_ = bf16[23552,1024]{1,0:T(8,128)(2,1)} custom-call(s32[1472]{0:T(1024)} %reshape.343.table, s32[8]{0:T(128)} %stack.309.base_ref, bf16[28,128,128]{2,1,0:T(8,128)(2,1)} %copy-done.1, bf16[28,128,128]{2,1,0:T(8,128)(2,1)} %copy-done.14, bf16[28,128,128]{2,1,0:T(8,128)(2,1)} %copy-done.15, ...), custom_call_target="tpu_custom_call", output_to_operand_aliasing={{}: (10, {})} | custom-call | bytes 14680064 | tf_op jit(solution)/shard_map/place_weights/pallas_call | solution.py:164
  1432.1 192.5 %place_weights.14.rest_8_ = bf16[23552,1024]{1,0:T(8,128)(2,1)} custom-call(s32[1472]{0:T(1024)} %reshape.343.table, s32[8]{0:T(128)} %stack.300.base_ref, bf16[24,128,128]{2,1,0:T(8,128)(2,1)} %copy-done.7, bf16[24,128,128]{2,1,0:T(8,128)(2,1)} %copy-done.42, bf16[24,128,128]{2,1,0:T(8,128)(2,1)} %copy-done.43, ...), custom_call_target="tpu_custom_call", output_to_operand_aliasing={{}: (10, {})} | custom-call | bytes 12582912 | tf_op jit(solution)/shard_map/place_weights/pallas_call | solution.py:164
  1624.6 192.5 %place_weights.15.up_ref.down_ref.w_ref.value_ref.gate_ref.out_w_ref.refs_6_.refs_7_.gate_w_ref.wk_ref.wv_ref.refs_8_.refs_9_ = bf16[23552,1024]{1,0:T(8,128)(2,1)} custom-call(s32[1472]{0:T(1024)} %reshape.343.table, s32[8]{0:T(128)} %stack.291.base_ref, bf16[24,128,128]{2,1,0:T(8,128)(2,1)} %all_gather.28.rest_0_, ...), custom_call_target="tpu_custom_call", output_to_operand_aliasing={{}: (10, {})} | custom-call | bytes 12582912 | tf_op jit(solution)/shard_map/place_weights/pallas_call | solution.py:164
  1817.1 31.1 %ffn_forward.2 = (f32[1024,1024]{1,0:T(8,128)}, bf16[1024,4096]{1,0:T(8,128)(2,1)}, bf16[1024,1024]{1,0:T(8,128)(2,1)}) custom-call(bf16[1024,1024]{1,0:T(8,128)(2,1)} %refs_5_.1, f32[1,1024]{1,0:T(1,128)} %get-tuple-element.117.gain_ref.refs_6_, f32[1,1024]{1,0:T(1,128)} %get-tuple-element.116.next_gain_ref.refs_1_, ...), custom_call_target="tpu_custom_call" | custom-call | flops 17179869184 | bytes 25165824 | tf_op jit(solution)/shard_map/ffn_forward/pallas_call | solution.py:309
  1854.0 11.4 project.2.refs_0_.refs_2_.refs_4_.refs_5_.refs_7_
  1865.4 29.6 %collective-permute-done.56.x_ref.refs_1_ = bf16[1024,1024]{1,0:T(8,128)(2,1)S(1)} collective-permute-done((bf16[1024,1024]{1,0:T(8,128)(2,1)}, bf16[1024,1024]{1,0:T(8,128)(2,1)S(1)}, u32[]{:S(2)}, u32[]{:S(2)}) %collective-permute-start.56) | collective-permute-done | bytes 2097184 | tf_op jit(solution)/shard_map/ppermute | solution.py:178
  1896.3 8.4 project.3.refs_3_.refs_5_.refs_6_.refs_8_
  1904.7 114.3 %attention_forward.1 = (bf16[1024,1024]{1,0:T(8,128)(2,1)}, f32[8,1,1024]{2,1,0:T(1,128)}) custom-call(s32[3]{0:T(128)} %pad_add_fusion.1.base_ref, s32[16]{0:T(128)} %reshape.342.span_ref, f32[8]{0:T(128)} %multiply_power_fusion.slope_ref, s32[2048]{0:T(1024)} %bitcast.137, bf16[1024,3072]{1,0:T(8,128)(2,1)} %project.2.refs_0_.refs_2_.refs_4_.refs_5_.refs_7_, ...), custom_call_target="tpu_custom_call" | custom-call | flops 4294967296 | bytes 8388608 | tf_op jit(solution)/shard_map/attention_forward/pallas_call | solution.py:801
  2018.9 7.3 project_out.1.x_ref
  2030.7 3.9 collective-permute-done.58.behind_ref
  2036.7 18.2 conv_forward.1
  2054.9 31.4 %ffn_forward.3 = (f32[1024,1024]{1,0:T(8,128)}, bf16[1024,4096]{1,0:T(8,128)(2,1)}, bf16[1024,1024]{1,0:T(8,128)(2,1)}) custom-call(f32[1024,1024]{1,0:T(8,128)} %get-tuple-element.49.x_ref.refs_3_, f32[1,1024]{1,0:T(1,128)} %get-tuple-element.114.gain_ref.refs_4_, f32[1,1024]{1,0:T(1,128)} %get-tuple-element.113.next_gain_ref.refs_1_, ...), custom_call_target="tpu_custom_call" | custom-call | flops 17179869184 | bytes 25165824 | tf_op jit(solution)/shard_map/ffn_forward/pallas_call | solution.py:309
  2086.3 15.8 broadcast_in_dim.45.refs_8_
  2102.1 59.7 %ffn_backward.2 = (f32[1024,1024]{1,0:T(8,128)}, f32[2,1024]{1,0:T(2,128)}, bf16[1472,128,128]{2,1,0:T(8,128)(2,1)}) custom-call(s32[1472]{0:T(1024)} %reshape.345.table_ref, f32[1024,1024]{1,0:T(8,128)} %get-tuple-element.52.refs_0_, f32[1,1024]{1,0:T(1,128)} %get-tuple-element.113.next_gain_ref.refs_1_, ...), custom_call_target="tpu_custom_call", output_to_operand_aliasing={{2}: (9, {})} | custom-call | flops 34359738368 | bytes 41943040 | tf_op jit(solution)/shard_map/ffn_backward/pallas_call | solution.py:438
  2161.8 2.5 convert.10
  2168.2 3.5 collective-permute-done.60.behind_ref
  2172.3 43.2 %conv_backward.1 = (f32[1024,1024]{1,0:T(8,128)}, f32[1,1024]{1,0:T(1,128)}, f32[5,1024]{1,0:T(8,128)}, bf16[1472,128,128]{2,1,0:T(8,128)(2,1)}) custom-call(s32[1472]{0:T(1024)} %reshape.345.table_ref, f32[1024,1024]{1,0:T(8,128)} %get-tuple-element.54.g_ref, bf16[16,1024]{1,0:T(8,128)(2,1)} %copy-done.67, ...), custom_call_target="tpu_custom_call", output_to_operand_aliasing={{3}: (13, {})} | custom-call | flops 12884901888 | bytes 29360128 | tf_op jit(solution)/shard_map/conv_backward/pallas_call | solution.py:1191
  2215.5 9.9 project_out_back.1
  2225.4 116.3 %attention_backward.1 = (bf16[1024,1024]{1,0:T(8,128)(2,1)}, bf16[1024,1024]{1,0:T(8,128)(2,1)}, bf16[1024,1024]{1,0:T(8,128)(2,1)}, bf16[1024,1024]{1,0:T(8,128)(2,1)}, bf16[1024,1024]{1,0:T(8,128)(2,1)}) custom-call(s32[3]{0:T(128)} %pad_add_fusion.1.base_ref, s32[16]{0:T(128)} %reshape.342.span_ref, f32[8]{0:T(128)} %multiply_power_fusion.slope_ref, ...), custom_call_target="tpu_custom_call" | custom-call | flops 10737418240 | bytes 12582912 | tf_op jit(solution)/shard_map/attention_backward/pallas_call | solution.py:942
  2341.8 8.7 input_gradient.1
  2350.4 31.5 %projections_back.1 = (f32[1024,1024]{1,0:T(8,128)}, bf16[1472,128,128]{2,1,0:T(8,128)(2,1)}) custom-call(s32[1472]{0:T(1024)} %reshape.345.table_ref, bf16[1024,1024]{1,0:T(8,128)(2,1)} %get-tuple-element.46.x_ref.n_ref.refs_0_, bf16[1024,1024]{1,0:T(8,128)(2,1)} %get-tuple-element.61.q_ref, ...), custom_call_target="tpu_custom_call", output_to_operand_aliasing={{1}: (10, {})} | custom-call | flops 17179869184 | bytes 31457280 | tf_op jit(solution)/shard_map/projections_back/pallas_call | solution.py:687
  2382.0 12.0 collective-permute-done.61.refs_3_
  2395.3 62.1 %ffn_backward.3 = (f32[1024,1024]{1,0:T(8,128)}, f32[2,1024]{1,0:T(2,128)}, bf16[1472,128,128]{2,1,0:T(8,128)(2,1)}) custom-call(s32[1472]{0:T(1024)} %reshape.345.table_ref, f32[1024,1024]{1,0:T(8,128)} %get-tuple-element.48.s_ref.refs_0_, f32[1,1024]{1,0:T(1,128)} %get-tuple-element.116.next_gain_ref.refs_1_, ...), custom_call_target="tpu_custom_call", output_to_operand_aliasing={{2}: (11, {})} | custom-call | flops 34359738368 | bytes 41943040 | tf_op jit(solution)/shard_map/ffn_backward/pallas_call | solution.py:438
  2457.4 10.7 fusion.13
  2468.9 21.4 fusion.12
  2492.1 9.2 fusion.11
  2503.7 2.7 slice.286
  2506.7 29.3 collective-permute-done.62
  2542.4 13.7 collective-permute-done.63
  2563.7 2.9 slice.294
  2568.1 29.6 %collective-permute-done.65 = bf16[24,128,128]{2,1,0:T(8,128)(2,1)} collective-permute-done((bf16[24,128,128]{2,1,0:T(8,128)(2,1)}, bf16[24,128,128]{2,1,0:T(8,128)(2,1)}, u32[]{:S(2)}, u32[]{:S(2)}) %collective-permute-start.65) | collective-permute-done | bytes 786464 | tf_op jit(solution)/shard_map/ppermute | solution.py:178
  2600.1 3.4 add_convert_fusion.3
  2603.6 22.7 collective-permute-done.67
  2633.9 54.3 %collective-permute-done.69 = bf16[28,128,128]{2,1,0:T(8,128)(2,1)S(1)} collective-permute-done((bf16[28,128,128]{2,1,0:T(8,128)(2,1)S(1)}, bf16[28,128,128]{2,1,0:T(8,128)(2,1)S(1)}, u32[]{:S(2)}, u32[]{:S(2)}) %collective-permute-start.69) | collective-permute-done | bytes 917536 | tf_op jit(solution)/shard_map/ppermute | solution.py:178
  2689.5 3.1 slice.302
  2697.0 53.6 %collective-permute-done.71 = bf16[28,128,128]{2,1,0:T(8,128)(2,1)S(1)} collective-permute-done((bf16[28,128,128]{2,1,0:T(8,128)(2,1)S(1)}, bf16[28,128,128]{2,1,0:T(8,128)(2,1)S(1)}, u32[]{:S(2)}, u32[]{:S(2)}) %collective-permute-start.71) | collective-permute-done | bytes 917536 | tf_op jit(solution)/shard_map/ppermute | solution.py:178
  2751.9 2.7 add_convert_fusion
  2755.1 17.2 collective-permute-done.73
  2776.4 47.9 %psum.7 = f32[10,1024]{1,0:T(8,128)S(1)} all-reduce(f32[10,1024]{1,0:T(8,128)S(1)} %concatenate.7), channel_id=1, replica_groups=mesh['mp'=2,'z'=4,'x'=2,'core'=2] {'mp','z','x','core'}, use_global_device_ids=true, to_apply=%region_19.20 | all-reduce | flops 10240 | bytes 81920 | tf_op jit(solution)/shard_map/psum | solution.py:1325
  2831.2 23.3 collective-permute-done.75
  2859.3 7.2 collective-permute-done.77
  2875.5 20.2 reduce-scatter.47.cloned.1.call-done
  2897.7 24.6 shampoo.1
  (419 shorter events, 132.5 us)
Async XLA Ops:
  7.2 2494.9 %reduce-scatter.17.cloned.1.call-start = ((), (), s32[]{:S(2)}) async-start(), calls=%async_computation.16 | async-start | bytes 9437184 | tf_op jit(solution)/shard_map/reduce_scatter | solution.py:1315
  25.6 38.3 %collective-permute-start.42 = (bf16[12,128,128]{2,1,0:T(8,128)(2,1)S(1)}, bf16[12,128,128]{2,1,0:T(8,128)(2,1)S(1)}, u32[]{:S(2)}, u32[]{:S(2)}) collective-permute-start(bf16[12,128,128]{2,1,0:T(8,128)(2,1)S(1)} %all_gather.34.rest_0_), channel_id=1, source_target_pairs={{0,16},{16,0},{1,17},{17,1},{2,18},{18,2},{3,19},{19,3},{4,20},{20... | collective-permute-start | bytes 1179656 | tf_op jit(solution)/shard_map/ppermute | solution.py:178
  27.1 55.6 %collective-permute-start.43 = (bf16[12,128,128]{2,1,0:T(8,128)(2,1)S(1)}, bf16[12,128,128]{2,1,0:T(8,128)(2,1)S(1)}, u32[]{:S(2)}, u32[]{:S(2)}) collective-permute-start(bf16[12,128,128]{2,1,0:T(8,128)(2,1)S(1)} %all_gather.34.rest_0_), channel_id=1, source_target_pairs={{0,2},{2,0},{1,3},{3,1},{4,6},{6,4},{5,7},{7,5},{8,10},{10,8},{9,1... | collective-permute-start | bytes 1179656 | tf_op jit(solution)/shard_map/ppermute | solution.py:178
  28.6 55.7 %collective-permute-start.45 = (bf16[12,128,128]{2,1,0:T(8,128)(2,1)S(1)}, bf16[12,128,128]{2,1,0:T(8,128)(2,1)S(1)}, u32[]{:S(2)}, u32[]{:S(2)}) collective-permute-start(bf16[12,128,128]{2,1,0:T(8,128)(2,1)S(1)} %all_gather.34.rest_0_), channel_id=1, source_target_pairs={{0,1},{1,0},{2,3},{3,2},{4,5},{5,4},{6,7},{7,6},{8,9},{9,8},{10,11... | collective-permute-start | bytes 1179656 | tf_op jit(solution)/shard_map/ppermute | solution.py:178
  44.1 41.6 %collective-permute-start.49 = (bf16[12,128,128]{2,1,0:T(8,128)(2,1)S(1)}, bf16[12,128,128]{2,1,0:T(8,128)(2,1)S(1)}, u32[]{:S(2)}, u32[]{:S(2)}) collective-permute-start(bf16[12,128,128]{2,1,0:T(8,128)(2,1)S(1)} %all_gather.35.rest_0_), channel_id=1, source_target_pairs={{0,2},{2,0},{1,3},{3,1},{4,6},{6,4},{5,7},{7,5},{8,10},{10,8},{9,1... | collective-permute-start | bytes 1179656 | tf_op jit(solution)/shard_map/ppermute | solution.py:178
  44.7 41.6 %collective-permute-start.50 = (bf16[12,128,128]{2,1,0:T(8,128)(2,1)S(1)}, bf16[12,128,128]{2,1,0:T(8,128)(2,1)S(1)}, u32[]{:S(2)}, u32[]{:S(2)}) collective-permute-start(bf16[12,128,128]{2,1,0:T(8,128)(2,1)S(1)} %all_gather.35.rest_0_), channel_id=1, source_target_pairs={{0,16},{16,0},{1,17},{17,1},{2,18},{18,2},{3,19},{19,3},{4,20},{20... | collective-permute-start | bytes 1179656 | tf_op jit(solution)/shard_map/ppermute | solution.py:178
  63.9 22.9 collective-permute-start.52
  85.8 36.0 %collective-permute-start.7 = (bf16[24,128,128]{2,1,0:T(8,128)(2,1)S(1)}, bf16[24,128,128]{2,1,0:T(8,128)(2,1)S(1)}, u32[]{:S(2)}, u32[]{:S(2)}) collective-permute-start(bf16[24,128,128]{2,1,0:T(8,128)(2,1)S(1)} %all_gather.29.rest_0_), channel_id=1, source_target_pairs={{0,2},{2,0},{1,3},{3,1},{4,6},{6,4},{5,7},{7,5},{8,10},{10,8},{9,1... | collective-permute-start | bytes 2359304 | tf_op jit(solution)/shard_map/ppermute | solution.py:178
  86.3 55.5 %collective-permute-start.8 = (bf16[24,128,128]{2,1,0:T(8,128)(2,1)S(1)}, bf16[24,128,128]{2,1,0:T(8,128)(2,1)S(1)}, u32[]{:S(2)}, u32[]{:S(2)}) collective-permute-start(bf16[24,128,128]{2,1,0:T(8,128)(2,1)S(1)} %all_gather.29.rest_0_), channel_id=1, source_target_pairs={{0,16},{16,0},{1,17},{17,1},{2,18},{18,2},{3,19},{19,3},{4,20},{20... | collective-permute-start | bytes 2359304 | tf_op jit(solution)/shard_map/ppermute | solution.py:178
  87.6 54.8 %collective-permute-start.10 = (bf16[24,128,128]{2,1,0:T(8,128)(2,1)S(1)}, bf16[24,128,128]{2,1,0:T(8,128)(2,1)S(1)}, u32[]{:S(2)}, u32[]{:S(2)}) collective-permute-start(bf16[24,128,128]{2,1,0:T(8,128)(2,1)S(1)} %all_gather.29.rest_0_), channel_id=1, source_target_pairs={{0,1},{1,0},{2,3},{3,2},{4,5},{5,4},{6,7},{7,6},{8,9},{9,8},{10,11... | collective-permute-start | bytes 2359304 | tf_op jit(solution)/shard_map/ppermute | solution.py:178
  103.5 40.3 %collective-permute-start.44 = (bf16[12,128,128]{2,1,0:T(8,128)(2,1)S(1)}, bf16[12,128,128]{2,1,0:T(8,128)(2,1)}, u32[]{:S(2)}, u32[]{:S(2)}) collective-permute-start(bf16[12,128,128]{2,1,0:T(8,128)(2,1)S(1)} %collective-permute-done.42.rest_1_), channel_id=1, source_target_pairs={{0,2},{2,0},{1,3},{3,1},{4,6},{6,4},{5,7},{7,5},{8,10},{10,8},{9,1... | collective-permute-start | bytes 1179656 | tf_op jit(solution)/shard_map/ppermute | solution.py:178
  105.1 40.3 %collective-permute-start.46 = (bf16[12,128,128]{2,1,0:T(8,128)(2,1)S(1)}, bf16[12,128,128]{2,1,0:T(8,128)(2,1)}, u32[]{:S(2)}, u32[]{:S(2)}) collective-permute-start(bf16[12,128,128]{2,1,0:T(8,128)(2,1)S(1)} %collective-permute-done.42.rest_1_), channel_id=1, source_target_pairs={{0,1},{1,0},{2,3},{3,2},{4,5},{5,4},{6,7},{7,6},{8,9},{9,8},{10,11... | collective-permute-start | bytes 1179656 | tf_op jit(solution)/shard_map/ppermute | solution.py:178
  121.8 23.6 collective-permute-start.47
  141.8 52.3 %collective-permute-start.14 = (bf16[28,128,128]{2,1,0:T(8,128)(2,1)S(1)}, bf16[28,128,128]{2,1,0:T(8,128)(2,1)S(1)}, u32[]{:S(2)}, u32[]{:S(2)}) collective-permute-start(bf16[28,128,128]{2,1,0:T(8,128)(2,1)S(1)} %all_gather.30.rest_0_), channel_id=1, source_target_pairs={{0,16},{16,0},{1,17},{17,1},{2,18},{18,2},{3,19},{19,3},{4,20},{20... | collective-permute-start | bytes 2752520 | tf_op jit(solution)/shard_map/ppermute | solution.py:178
  142.4 51.8 %collective-permute-start.15 = (bf16[28,128,128]{2,1,0:T(8,128)(2,1)S(1)}, bf16[28,128,128]{2,1,0:T(8,128)(2,1)S(1)}, u32[]{:S(2)}, u32[]{:S(2)}) collective-permute-start(bf16[28,128,128]{2,1,0:T(8,128)(2,1)S(1)} %all_gather.30.rest_0_), channel_id=1, source_target_pairs={{0,2},{2,0},{1,3},{3,1},{4,6},{6,4},{5,7},{7,5},{8,10},{10,8},{9,1... | collective-permute-start | bytes 2752520 | tf_op jit(solution)/shard_map/ppermute | solution.py:178
  143.9 27.9 collective-permute-start.51
  145.4 26.4 collective-permute-start.53
  145.4 27.9 collective-permute-start.54
  171.8 24.0 collective-permute-start.17
  171.8 24.6 collective-permute-start.21
  173.3 43.1 %collective-permute-start.22 = (bf16[28,128,128]{2,1,0:T(8,128)(2,1)S(1)}, bf16[28,128,128]{2,1,0:T(8,128)(2,1)S(1)}, u32[]{:S(2)}, u32[]{:S(2)}) collective-permute-start(bf16[28,128,128]{2,1,0:T(8,128)(2,1)S(1)} %all_gather.31.rest_0_), channel_id=1, source_target_pairs={{0,16},{16,0},{1,17},{17,1},{2,18},{18,2},{3,19},{19,3},{4,20},{20... | collective-permute-start | bytes 2752520 | tf_op jit(solution)/shard_map/ppermute | solution.py:178
  194.1 23.8 collective-permute-start.24
  194.2 24.2 collective-permute-start.28
  237.9 38.9 %collective-permute-start.16 = (bf16[28,128,128]{2,1,0:T(8,128)(2,1)S(1)}, bf16[28,128,128]{2,1,0:T(8,128)(2,1)S(1)}, u32[]{:S(2)}, u32[]{:S(2)}) collective-permute-start(bf16[28,128,128]{2,1,0:T(8,128)(2,1)S(1)} %collective-permute-done.14.rest_1_), channel_id=1, source_target_pairs={{0,2},{2,0},{1,3},{3,1},{4,6},{6,4},{5,7},{7,5},{8,10},{10,8},{9,1... | collective-permute-start | bytes 2752520 | tf_op jit(solution)/shard_map/ppermute | solution.py:178
  239.3 36.1 %collective-permute-start.2 = (bf16[24,128,128]{2,1,0:T(8,128)(2,1)}, bf16[24,128,128]{2,1,0:T(8,128)(2,1)}, u32[]{:S(2)}, u32[]{:S(2)}) collective-permute-start(bf16[24,128,128]{2,1,0:T(8,128)(2,1)} %collective-permute-done.rest_1_), channel_id=1, source_target_pairs={{0,2},{2,0},{1,3},{3,1},{4,6},{6,4},{5,7},{7,5},{8,10},{10,8},{9,1... | collective-permute-start | bytes 2359304 | tf_op jit(solution)/shard_map/ppermute | solution.py:178
  239.9 35.4 %collective-permute-start.9 = (bf16[24,128,128]{2,1,0:T(8,128)(2,1)S(1)}, bf16[24,128,128]{2,1,0:T(8,128)(2,1)}, u32[]{:S(2)}, u32[]{:S(2)}) collective-permute-start(bf16[24,128,128]{2,1,0:T(8,128)(2,1)S(1)} %collective-permute-done.7.rest_1_), channel_id=1, source_target_pairs={{0,16},{16,0},{1,17},{17,1},{2,18},{18,2},{3,19},{19,3},{4,20},{20... | collective-permute-start | bytes 2359304 | tf_op jit(solution)/shard_map/ppermute | solution.py:178
  240.4 35.4 %collective-permute-start.11 = (bf16[24,128,128]{2,1,0:T(8,128)(2,1)S(1)}, bf16[24,128,128]{2,1,0:T(8,128)(2,1)S(1)}, u32[]{:S(2)}, u32[]{:S(2)}) collective-permute-start(bf16[24,128,128]{2,1,0:T(8,128)(2,1)S(1)} %collective-permute-done.7.rest_1_), channel_id=1, source_target_pairs={{0,1},{1,0},{2,3},{3,2},{4,5},{5,4},{6,7},{7,6},{8,9},{9,8},{10,11... | collective-permute-start | bytes 2359304 | tf_op jit(solution)/shard_map/ppermute | solution.py:178
  240.5 35.6 %collective-permute-start.12 = (bf16[24,128,128]{2,1,0:T(8,128)(2,1)S(1)}, bf16[24,128,128]{2,1,0:T(8,128)(2,1)S(1)}, u32[]{:S(2)}, u32[]{:S(2)}) collective-permute-start(bf16[24,128,128]{2,1,0:T(8,128)(2,1)S(1)} %collective-permute-done.8.rest_2_), channel_id=1, source_target_pairs={{0,1},{1,0},{2,3},{3,2},{4,5},{5,4},{6,7},{7,6},{8,9},{9,8},{10,11... | collective-permute-start | bytes 2359304 | tf_op jit(solution)/shard_map/ppermute | solution.py:178
  298.2 22.8 collective-permute-start.37
  321.5 1303.0 %collective-permute-start.3 = (bf16[24,128,128]{2,1,0:T(8,128)(2,1)}, bf16[24,128,128]{2,1,0:T(8,128)(2,1)}, u32[]{:S(2)}, u32[]{:S(2)}) collective-permute-start(bf16[24,128,128]{2,1,0:T(8,128)(2,1)} %all_gather.28.rest_0_), channel_id=1, source_target_pairs={{0,1},{1,0},{2,3},{3,2},{4,5},{5,4},{6,7},{7,6},{8,9},{9,8},{10,11... | collective-permute-start | bytes 2359304 | tf_op jit(solution)/shard_map/ppermute | solution.py:178
  321.6 1110.4 %collective-permute-start.13 = (bf16[24,128,128]{2,1,0:T(8,128)(2,1)}, bf16[24,128,128]{2,1,0:T(8,128)(2,1)}, u32[]{:S(2)}, u32[]{:S(2)}) collective-permute-start(bf16[24,128,128]{2,1,0:T(8,128)(2,1)} %collective-permute-done.9.rest_3_), channel_id=1, source_target_pairs={{0,1},{1,0},{2,3},{3,2},{4,5},{5,4},{6,7},{7,6},{8,9},{9,8},{10,11... | collective-permute-start | bytes 2359304 | tf_op jit(solution)/shard_map/ppermute | solution.py:178
  322.1 1302.4 %collective-permute-start.4 = (bf16[24,128,128]{2,1,0:T(8,128)(2,1)}, bf16[24,128,128]{2,1,0:T(8,128)(2,1)}, u32[]{:S(2)}, u32[]{:S(2)}) collective-permute-start(bf16[24,128,128]{2,1,0:T(8,128)(2,1)} %collective-permute-done.rest_1_), channel_id=1, source_target_pairs={{0,1},{1,0},{2,3},{3,2},{4,5},{5,4},{6,7},{7,6},{8,9},{9,8},{10,11... | collective-permute-start | bytes 2359304 | tf_op jit(solution)/shard_map/ppermute | solution.py:178
  323.5 1301.1 %collective-permute-start.5 = (bf16[24,128,128]{2,1,0:T(8,128)(2,1)}, bf16[24,128,128]{2,1,0:T(8,128)(2,1)}, u32[]{:S(2)}, u32[]{:S(2)}) collective-permute-start(bf16[24,128,128]{2,1,0:T(8,128)(2,1)} %collective-permute-done.1.rest_2_), channel_id=1, source_target_pairs={{0,1},{1,0},{2,3},{3,2},{4,5},{5,4},{6,7},{7,6},{8,9},{9,8},{10,11... | collective-permute-start | bytes 2359304 | tf_op jit(solution)/shard_map/ppermute | solution.py:178
  326.1 1298.5 %collective-permute-start.6 = (bf16[24,128,128]{2,1,0:T(8,128)(2,1)}, bf16[24,128,128]{2,1,0:T(8,128)(2,1)}, u32[]{:S(2)}, u32[]{:S(2)}) collective-permute-start(bf16[24,128,128]{2,1,0:T(8,128)(2,1)} %collective-permute-done.2.rest_3_), channel_id=1, source_target_pairs={{0,1},{1,0},{2,3},{3,2},{4,5},{5,4},{6,7},{7,6},{8,9},{9,8},{10,11... | collective-permute-start | bytes 2359304 | tf_op jit(solution)/shard_map/ppermute | solution.py:178
  1848.2 46.7 %collective-permute-start.56 = (bf16[1024,1024]{1,0:T(8,128)(2,1)}, bf16[1024,1024]{1,0:T(8,128)(2,1)S(1)}, u32[]{:S(2)}, u32[]{:S(2)}) collective-permute-start(bf16[1024,1024]{1,0:T(8,128)(2,1)} %get-tuple-element.46.x_ref.n_ref.refs_0_), channel_id=1, source_target_pairs={{0,16},{16,0},{1,17},{17,1},{2,18},{18,2},{3,19},{19,3},{4,20},{20... | collective-permute-start | bytes 6291464 | tf_op jit(solution)/shard_map/ppermute | solution.py:178
  2350.4 43.5 %collective-permute-start.61 = (bf16[1024,1024]{1,0:T(8,128)(2,1)}, bf16[1024,1024]{1,0:T(8,128)(2,1)S(1)}, u32[]{:S(2)}, u32[]{:S(2)}) collective-permute-start(bf16[1024,1024]{1,0:T(8,128)(2,1)} %input_gradient.1), channel_id=1, source_target_pairs={{0,16},{16,0},{1,17},{17,1},{2,18},{18,2},{3,19},{19,3},{4,20},{20... | collective-permute-start | bytes 6291464 | tf_op jit(solution)/shard_map/ppermute | solution.py:178
  2468.1 35.6 %reduce-scatter.21.cloned.1.call-start = ((), (), s32[]{:S(2)}) async-start(), calls=%async_computation.18 | async-start | bytes 9437184 | tf_op jit(solution)/shard_map/reduce_scatter | solution.py:1315
  2468.9 71.6 %reduce-scatter.25.cloned.1.call-start = ((), (), s32[]{:S(2)}) async-start(), calls=%async_computation.20 | async-start | bytes 11010048 | tf_op jit(solution)/shard_map/reduce_scatter | solution.py:1315
  2490.3 73.4 %reduce-scatter.29.cloned.1.call-start = ((), (), s32[]{:S(2)}) async-start(), calls=%async_computation.22 | async-start | bytes 11010048 | tf_op jit(solution)/shard_map/reduce_scatter | solution.py:1315
  2490.9 136.7 %reduce-scatter.33.cloned.1.call-start = ((), (), s32[]{:S(2)}) async-start(), calls=%async_computation.24 | async-start | bytes 11010048 | tf_op jit(solution)/shard_map/reduce_scatter | solution.py:1315
  2491.5 198.0 %reduce-scatter.37.cloned.1.call-start = ((), (), s32[]{:S(2)}) async-start(), calls=%async_computation.26 | async-start | bytes 11010048 | tf_op jit(solution)/shard_map/reduce_scatter | solution.py:1315
  2492.1 281.5 %reduce-scatter.41.cloned.1.call-start = ((), (), s32[]{:S(2)}) async-start(), calls=%async_computation.28 | async-start | bytes 4718592 | tf_op jit(solution)/shard_map/reduce_scatter | solution.py:1315
  2501.3 323.2 %reduce-scatter.45.cloned.1.call-start = ((), (), s32[]{:S(2)}) async-start(), calls=%async_computation.30 | async-start | bytes 4718592 | tf_op jit(solution)/shard_map/reduce_scatter | solution.py:1315
  2502.0 365.4 %reduce-scatter.19.cloned.1.call-start = ((), (), s32[]{:S(2)}) async-start(), calls=%async_computation.17 | async-start | bytes 983040 | tf_op jit(solution)/shard_map/reduce_scatter | solution.py:1320
  2503.6 32.3 %collective-permute-start.62 = (bf16[48,128,128]{2,1,0:T(8,128)(2,1)S(1)}, bf16[48,128,128]{2,1,0:T(8,128)(2,1)S(1)}, u32[]{:S(2)}, u32[]{:S(2)}) collective-permute-start(bf16[48,128,128]{2,1,0:T(8,128)(2,1)S(1)} %slice.282), channel_id=1, source_target_pairs={{0,2},{2,0},{1,3},{3,1},{4,6},{6,4},{5,7},{7,5},{8,10},{10,8},{9,1... | collective-permute-start | bytes 4718600 | tf_op jit(solution)/shard_map/ppermute | solution.py:178
  2506.5 52.1 %collective-permute-start.64 = (bf16[48,128,128]{2,1,0:T(8,128)(2,1)}, bf16[48,128,128]{2,1,0:T(8,128)(2,1)}, u32[]{:S(2)}, u32[]{:S(2)}) collective-permute-start(bf16[48,128,128]{2,1,0:T(8,128)(2,1)} %slice.286), channel_id=1, source_target_pairs={{0,16},{16,0},{1,17},{17,1},{2,18},{18,2},{3,19},{19,3},{4,20},{20... | collective-permute-start | bytes 4718600 | tf_op jit(solution)/shard_map/ppermute | solution.py:178
  2542.1 58.0 %collective-permute-start.66 = (bf16[56,128,128]{2,1,0:T(8,128)(2,1)S(1)}, bf16[56,128,128]{2,1,0:T(8,128)(2,1)}, u32[]{:S(2)}, u32[]{:S(2)}) collective-permute-start(bf16[56,128,128]{2,1,0:T(8,128)(2,1)S(1)} %slice.290), channel_id=1, source_target_pairs={{0,2},{2,0},{1,3},{3,1},{4,6},{6,4},{5,7},{7,5},{8,10},{10,8},{9,1... | collective-permute-start | bytes 5505032 | tf_op jit(solution)/shard_map/ppermute | solution.py:178
  2558.5 309.9 %reduce-scatter.23.cloned.1.call-start = ((), (), s32[]{:S(2)}) async-start(), calls=%async_computation.19 | async-start | bytes 983040 | tf_op jit(solution)/shard_map/reduce_scatter | solution.py:1320
  2561.9 35.8 %collective-permute-start.65 = (bf16[24,128,128]{2,1,0:T(8,128)(2,1)}, bf16[24,128,128]{2,1,0:T(8,128)(2,1)}, u32[]{:S(2)}, u32[]{:S(2)}) collective-permute-start(bf16[24,128,128]{2,1,0:T(8,128)(2,1)} %slice.288), channel_id=1, source_target_pairs={{0,2},{2,0},{1,3},{3,1},{4,6},{6,4},{5,7},{7,5},{8,10},{10,8},{9,1... | collective-permute-start | bytes 2359304 | tf_op jit(solution)/shard_map/ppermute | solution.py:178
  2566.6 63.2 %collective-permute-start.68 = (bf16[56,128,128]{2,1,0:T(8,128)(2,1)}, bf16[56,128,128]{2,1,0:T(8,128)(2,1)}, u32[]{:S(2)}, u32[]{:S(2)}) collective-permute-start(bf16[56,128,128]{2,1,0:T(8,128)(2,1)} %slice.294), channel_id=1, source_target_pairs={{0,16},{16,0},{1,17},{17,1},{2,18},{18,2},{3,19},{19,3},{4,20},{20... | collective-permute-start | bytes 5505032 | tf_op jit(solution)/shard_map/ppermute | solution.py:178
  2600.0 269.4 %reduce-scatter.27.cloned.1.call-start = ((), (), s32[]{:S(2)}) async-start(), calls=%async_computation.21 | async-start | bytes 1146880 | tf_op jit(solution)/shard_map/reduce_scatter | solution.py:1320
  2603.5 22.8 collective-permute-start.67
  2627.6 242.8 %reduce-scatter.31.cloned.1.call-start = ((), (), s32[]{:S(2)}) async-start(), calls=%async_computation.23 | async-start | bytes 1146880 | tf_op jit(solution)/shard_map/reduce_scatter | solution.py:1320
  2629.4 64.6 %collective-permute-start.70 = (bf16[56,128,128]{2,1,0:T(8,128)(2,1)S(1)}, bf16[56,128,128]{2,1,0:T(8,128)(2,1)}, u32[]{:S(2)}, u32[]{:S(2)}) collective-permute-start(bf16[56,128,128]{2,1,0:T(8,128)(2,1)S(1)} %slice.298), channel_id=1, source_target_pairs={{0,2},{2,0},{1,3},{3,1},{4,6},{6,4},{5,7},{7,5},{8,10},{10,8},{9,1... | collective-permute-start | bytes 5505032 | tf_op jit(solution)/shard_map/ppermute | solution.py:178
  2632.5 55.6 %collective-permute-start.69 = (bf16[28,128,128]{2,1,0:T(8,128)(2,1)S(1)}, bf16[28,128,128]{2,1,0:T(8,128)(2,1)S(1)}, u32[]{:S(2)}, u32[]{:S(2)}) collective-permute-start(bf16[28,128,128]{2,1,0:T(8,128)(2,1)S(1)} %slice.296), channel_id=1, source_target_pairs={{0,2},{2,0},{1,3},{3,1},{4,6},{6,4},{5,7},{7,5},{8,10},{10,8},{9,1... | collective-permute-start | bytes 2752520 | tf_op jit(solution)/shard_map/ppermute | solution.py:178
  2689.4 182.0 %reduce-scatter.35.cloned.1.call-start = ((), (), s32[]{:S(2)}) async-start(), calls=%async_computation.25 | async-start | bytes 1146880 | tf_op jit(solution)/shard_map/reduce_scatter | solution.py:1320
  2692.6 59.3 %collective-permute-start.72 = (bf16[56,128,128]{2,1,0:T(8,128)(2,1)}, bf16[56,128,128]{2,1,0:T(8,128)(2,1)}, u32[]{:S(2)}, u32[]{:S(2)}) collective-permute-start(bf16[56,128,128]{2,1,0:T(8,128)(2,1)} %slice.302), channel_id=1, source_target_pairs={{0,16},{16,0},{1,17},{17,1},{2,18},{18,2},{3,19},{19,3},{4,20},{20... | collective-permute-start | bytes 5505032 | tf_op jit(solution)/shard_map/ppermute | solution.py:178
  2696.4 54.1 %collective-permute-start.71 = (bf16[28,128,128]{2,1,0:T(8,128)(2,1)S(1)}, bf16[28,128,128]{2,1,0:T(8,128)(2,1)S(1)}, u32[]{:S(2)}, u32[]{:S(2)}) collective-permute-start(bf16[28,128,128]{2,1,0:T(8,128)(2,1)S(1)} %slice.300), channel_id=1, source_target_pairs={{0,16},{16,0},{1,17},{17,1},{2,18},{18,2},{3,19},{19,3},{4,20},{20... | collective-permute-start | bytes 2752520 | tf_op jit(solution)/shard_map/ppermute | solution.py:178
  2751.8 120.6 %reduce-scatter.39.cloned.1.call-start = ((), (), s32[]{:S(2)}) async-start(), calls=%async_computation.27 | async-start | bytes 1146880 | tf_op jit(solution)/shard_map/reduce_scatter | solution.py:1320
  2773.5 101.1 %reduce-scatter.43.cloned.1.call-start = ((), (), s32[]{:S(2)}) async-start(), calls=%async_computation.29 | async-start | bytes 491520 | tf_op jit(solution)/shard_map/reduce_scatter | solution.py:1320
  2775.8 53.0 %collective-permute-start.74 = (bf16[24,128,128]{2,1,0:T(8,128)(2,1)}, bf16[24,128,128]{2,1,0:T(8,128)(2,1)}, u32[]{:S(2)}, u32[]{:S(2)}) collective-permute-start(bf16[24,128,128]{2,1,0:T(8,128)(2,1)} %slice.306), channel_id=1, source_target_pairs={{0,2},{2,0},{1,3},{3,1},{4,6},{6,4},{5,7},{7,5},{8,10},{10,8},{9,1... | collective-permute-start | bytes 2359304 | tf_op jit(solution)/shard_map/ppermute | solution.py:178
  2826.6 28.8 collective-permute-start.76
  2830.3 24.2 collective-permute-start.75
  2855.3 40.4 %reduce-scatter.47.cloned.1.call-start = ((), (), s32[]{:S(2)}) async-start(), calls=%async_computation.31 | async-start | bytes 491520 | tf_op jit(solution)/shard_map/reduce_scatter | solution.py:1320
  (104 other events, 4428.2 us)
Sparse Core Ops, SparseCore 0:
  2468.2 13.2 reduce-scatter.16
  2484.0 15.6 reduce-scatter.20
  2502.0 17.0 reduce-scatter.24
  2521.3 16.9 reduce-scatter.28
  2540.5 16.9 reduce-scatter.32
  2559.8 17.0 reduce-scatter.36
  2579.1 12.0 reduce-scatter.40
  2593.5 12.0 reduce-scatter.44
  2608.5 24.4 reduce-scatter.18
  2635.1 22.5 reduce-scatter.22
  2660.6 24.3 reduce-scatter.26
  2689.5 24.6 reduce-scatter.30
  2751.9 24.8 reduce-scatter.34
  2779.6 24.1 reduce-scatter.38
  2855.5 19.0 reduce-scatter.42
  2876.8 18.8 reduce-scatter.46

commit v2 on v1

v2 whole, which is shorter than its diff:
```python
import math

import jax
import jax.numpy as jnp
import numpy as np
from jax import lax
from jax.experimental import pallas as pl
from jax.experimental.pallas import tpu as pltpu
from jax.sharding import Mesh
from jax.sharding import PartitionSpec as P

D = 1024
FF = 4096
HEADS = 8
HEAD_DIM = 128
KERNEL = 5
STEP = 4
BLOCK = 128
HALO = 16
WIDE = 8

EPSILON = 1e-05
DECAY_STAT = 0.95
RATE_BLOCK = 0.02
RATE_VECTOR = 0.2
DECAY_AVERAGE = 0.9999
MASKED = -1e30
LOG2E = math.log2(math.e)
SCORE_SCALE = 1.0 / math.sqrt(HEAD_DIM)

f32 = jnp.float32
bf16 = jnp.bfloat16
ANY = pl.BlockSpec(memory_space=pl.ANY)
SMEM = pl.BlockSpec(memory_space=pltpu.SMEM)

MATRICES = [
    (0, 0, D, FF, True),
    (0, 4, FF, D, False),
    (1, 0, D, D, True),
    (1, 1, D, D, True),
    (1, 2, D, D, True),
    (1, 3, D, D, False),
    (2, 0, D, D, True),
    (2, 1, D, D, True),
    (2, 2, D, D, False),
    (3, 0, D, FF, True),
    (3, 4, FF, D, False),
]
UP1, DOWN1, QUERY, KEY, VALUE, OUT, CONV_VALUE, CONV_GATE, CONV_OUT, UP2, DOWN2 = range(11)
GROUPS = [(0, 2), (2, 6), (6, 9), (9, 11)]
GROUP_CHUNKS = [8, 4, 3, 8]


def at(matrix):
    return MATRICES[matrix][1]


ROUNDS = [4, 3, 4, 9, 3]
LARGE = 3
EARLY = [9, 6, 2]


def params(**kw):
    return pltpu.CompilerParams(vmem_limit_bytes=58 * 2**20, **kw)


def const_spec(shape):
    return pl.BlockSpec(shape, lambda *ids: (0,) * len(shape), pipeline_mode=pl.Buffered(1))


def row_tile(rows):
    return 256 if rows % 256 == 0 else 128


def cost(flops, moved):
    return pl.CostEstimate(flops=int(flops), bytes_accessed=int(moved), transcendentals=0)


def offsets(ranks):
    out = []
    offset = 0
    for unused, unused_chunk, height, breadth, by_columns in MATRICES:
        out.append(offset)
        offset = offset + height * breadth // (BLOCK * BLOCK * ranks)
    return out, offset


def block_number(matrix, row_block, column_block, ranks):
    starts, total = offsets(ranks)
    unused, unused_chunk, height, breadth, by_columns = MATRICES[matrix]
    if by_columns:
        part = breadth // BLOCK // ranks
        return (
            (column_block // part) * total + starts[matrix] + row_block * part + column_block % part
        )
    part = height // BLOCK // ranks
    breadth_blocks = breadth // BLOCK
    return (
        (row_block // part) * total
        + starts[matrix]
        + (row_block % part) * breadth_blocks
        + column_block
    )


def weight_places(ranks):
    unused, total = offsets(ranks)
    places = np.zeros((ranks * total,), np.int32)
    for matrix, (unused, chunk, height, breadth, by_columns) in enumerate(MATRICES):
        for row in range(height // BLOCK):
            for column in range(breadth // BLOCK):
                place = ((chunk + column // WIDE) * 8 + row) * WIDE + column % WIDE
                places[block_number(matrix, row, column, ranks)] = place
    return places.reshape(ranks, total)


def copy_in_place(out, source, place, sem):
    row = pl.multiple_of((place // WIDE) * BLOCK, BLOCK)
    column = pl.multiple_of((place % WIDE) * BLOCK, BLOCK)
    pltpu.make_async_copy(
        source, out.at[pl.ds(row, BLOCK), pl.ds(column, BLOCK)], sem
    ).start()


def unsort(slots, sources, places, chunks, listed):
    count = sources.shape[0]
    each = max(n for n in range(1, 65) if count % n == 0)
    steps = count // each

    def body(source_ref, place_ref, slots_ref, *rest):
        out = rest[0]
        list_ref = rest[1] if listed else None
        held, read_sem, write_sem, list_sem = rest[-4:]
        step = pl.program_id(0)
        slot = lax.rem(step, 2)

        def read(number, into):
            def one(n, unused):
                pltpu.make_async_copy(
                    slots_ref.at[source_ref[number * each + n]], held.at[into, n], read_sem.at[into]
                ).start()
                return unused

            lax.fori_loop(0, each, one, 0)

        def written(number, into):
            pltpu.make_async_copy(held.at[into], held.at[into], write_sem.at[into]).wait()
            if listed:
                pltpu.make_async_copy(held.at[into], held.at[into], list_sem.at[into]).wait()

        @pl.when(step == 0)
        def _():
            read(0, 0)

        @pl.when(step >= 1)
        def _():
            written(step - 1, 1 - slot)

        @pl.when(step + 1 < steps)
        def _():
            read(step + 1, 1 - slot)

        pltpu.make_async_copy(held.at[slot], held.at[slot], read_sem.at[slot]).wait()

        def one(n, unused):
            copy_in_place(out, held.at[slot, n], place_ref[step * each + n], write_sem.at[slot])
            return unused

        lax.fori_loop(0, each, one, 0)
        if listed:
            pltpu.make_async_copy(
                held.at[slot], list_ref.at[pl.ds(step * each, each)], list_sem.at[slot]
            ).start()

        @pl.when(step == steps - 1)
        def _():
            written(step, slot)

    shapes = [jax.ShapeDtypeStruct((chunks * D, D), bf16)]
    if listed:
        shapes.append(jax.ShapeDtypeStruct((count, BLOCK, BLOCK), bf16))
    return pl.pallas_call(
        body,
        grid=(steps,),
        out_shape=tuple(shapes),
        in_specs=[SMEM, SMEM, ANY],
        out_specs=(ANY,) * len(shapes),
        scratch_shapes=[
            pltpu.VMEM((2, each, BLOCK, BLOCK), bf16),
            pltpu.SemaphoreType.DMA((2,)),
            pltpu.SemaphoreType.DMA((2,)),
            pltpu.SemaphoreType.DMA((2,)),
        ],
        compiler_params=params(has_side_effects=True),
        cost_estimate=cost(0, 3 * count * BLOCK * BLOCK * 2),
        name="unsort",
    )(sources, places, slots)


def place_weights(weights, arrays, bases, places):
    count = arrays[0].shape[0]
    number = len(arrays)
    each = max(n for n in range(1, 128 // number + 1) if count % n == 0)

    def body(table, base_ref, *rest):
        sources = rest[:number]
        out, sem = rest[-2], rest[-1]
        start = pl.program_id(0) * each

        def one(t, unused):
            for a, source in enumerate(sources):
                copy_in_place(out, source.at[t], table[base_ref[a] + start + t], sem.at[a])
            return unused

        lax.fori_loop(0, each, one, 0)
        for a, source in enumerate(sources):
            pltpu.make_async_copy(source, source, sem.at[a]).wait()

    operands = [places, jnp.stack(bases).astype(jnp.int32), *arrays, weights]
    return pl.pallas_call(
        body,
        grid=(count // each,),
        out_shape=jax.ShapeDtypeStruct(weights.shape, bf16),
        in_specs=[SMEM, SMEM]
        + [pl.BlockSpec((each, BLOCK, BLOCK), lambda n: (n, 0, 0))] * number
        + [ANY],
        out_specs=ANY,
        scratch_shapes=[pltpu.SemaphoreType.DMA((number,))],
        input_output_aliases={len(operands) - 1: 0},
        compiler_params=params(has_side_effects=True),
        cost_estimate=cost(0, 2 * number * count * BLOCK * BLOCK * 2),
        name="place_weights",
    )(*operands)


PAIR = [(0, 1), (1, 0)]
MOVES = {
    "x": ("x", PAIR),
    "mp": ("mp", PAIR),
    "core": ("core", PAIR),
    "near": ("z", [(0, 1), (1, 0), (2, 3), (3, 2)]),
    "far": ("z", [(0, 2), (2, 0), (1, 3), (3, 1)]),
    "both": (("x", "core"), [(n, 3 - n) for n in range(4)]),
    "across": (("mp", "z"), [(n, (n // 4 * 4) ^ 4 | (n % 4) ^ 1) for n in range(8)]),
}
for _step in (-3, -2, -1, 1, 2, 3):
    MOVES[_step] = ("z", [(z, z + _step) for z in range(4) if 0 <= z + _step < 4])


def swap(value, move):
    axis, pairs = MOVES[move]
    return lax.ppermute(value, axis, pairs)


def tied(*values):
    return lax.optimization_barrier(values)


def together(transfers, *held):
    values = tied(*[value for value, unused in transfers])
    arrived = [swap(value, move) for value, (unused, move) in zip(values, transfers)]
    out = tied(*arrived, *held)
    return list(out[: len(arrived)]), out[len(arrived) :]


def sigmoid(values):
    return 0.5 * jnp.tanh(0.5 * values) + 0.5


def norm_parts(values):
    center = values - jnp.mean(values, axis=-1, keepdims=True)
    spread = jnp.mean(center * center, axis=-1, keepdims=True)
    scale = lax.rsqrt(spread + EPSILON)
    return center * scale, scale


def norm(values, gain):
    return norm_parts(values)[0] * gain


def norm_back(values, gain, grad):
    hat, scale = norm_parts(values)
    inner = grad * gain
    mean_inner = jnp.mean(inner, axis=-1, keepdims=True)
    mean_hat = jnp.mean(inner * hat, axis=-1, keepdims=True)
    return (
        scale * (inner - mean_inner - hat * mean_hat),
        jnp.sum(grad * hat, axis=0, keepdims=True),
    )


def dot(a, b):
    return jnp.dot(a, b, preferred_element_type=f32)


def dot_right(a, b):
    return lax.dot_general(a, b, (((1,), (1,)), ((), ())), preferred_element_type=f32)


def dot_left(a, b):
    return lax.dot_general(a, b, (((0,), (0,)), ((), ())), preferred_element_type=f32)


def start_blocks(table, targets, source, sem, matrix, row_block, column_block, ranks):
    height, breadth = source.shape
    for i in range(height // BLOCK):
        for j in range(breadth // BLOCK):
            place = table[block_number(matrix, row_block + i, column_block + j, ranks)]
            block = source.at[pl.ds(i * BLOCK, BLOCK), pl.ds(j * BLOCK, BLOCK)]
            if len(targets) == 1:
                pltpu.make_async_copy(block, targets[0].at[place], sem).start()
                continue
            limit = targets[0].shape[0]

            @pl.when(place < limit)
            def _(place=place, block=block):
                pltpu.make_async_copy(block, targets[0].at[place], sem).start()

            @pl.when(place >= limit)
            def _(place=place, block=block):
                pltpu.make_async_copy(block, targets[1].at[place - limit], sem).start()


def wait_blocks(source, sem):
    pltpu.make_async_copy(source, source, sem).wait()


def ffn_forward(stream, gain, next_gain, weights, upper, lower):
    rows = stream.shape[0]
    tile = row_tile(rows)
    wide = D
    steps = FF // wide

    def body(x_ref, gain_ref, next_gain_ref, up_ref, down_ref, out_ref, pre_ref, next_ref, normed):
        step = pl.program_id(0)

        @pl.when(step == 0)
        def _():
            for t in range(0, rows, tile):
                x = x_ref[t : t + tile].astype(f32)
                normed[t : t + tile] = norm(x, gain_ref[...]).astype(bf16)
                out_ref[t : t + tile] = jnp.zeros((tile, D), f32)

        for t in range(0, rows, tile):
            pre = dot(normed[t : t + tile], up_ref[...])
            pre_ref[t : t + tile] = pre.astype(bf16)
            act = (pre * sigmoid(pre)).astype(bf16)
            out_ref[t : t + tile] += dot(act, down_ref[...])

        @pl.when(step == steps - 1)
        def _():
            for t in range(0, rows, tile):
                y = x_ref[t : t + tile].astype(f32) + 0.5 * out_ref[t : t + tile]
                out_ref[t : t + tile] = y
                next_ref[t : t + tile] = norm(y, next_gain_ref[...]).astype(bf16)

    return pl.pallas_call(
        body,
        grid=(steps,),
        out_shape=(
            jax.ShapeDtypeStruct((rows, D), f32),
            jax.ShapeDtypeStruct((rows, FF), bf16),
            jax.ShapeDtypeStruct((rows, D), bf16),
        ),
        in_specs=[
            const_spec((rows, D)),
            const_spec((1, D)),
            const_spec((1, D)),
            pl.BlockSpec((D, wide), lambda f: (at(upper) + f, 0)),
            pl.BlockSpec((wide, D), lambda f: (at(lower) + f, 0)),
        ],
        out_specs=(
            const_spec((rows, D)),
            pl.BlockSpec((rows, wide), lambda f: (0, f)),
            const_spec((rows, D)),
        ),
        scratch_shapes=[pltpu.VMEM((rows, D), bf16)],
        compiler_params=params(),
        cost_estimate=cost(4 * rows * D * FF, 4 * D * FF + 2 * rows * FF),
        name="ffn_forward",
    )(stream, gain, next_gain, weights, weights)


def norm_rows(values, gain):
    rows = values.shape[0]
    tile = row_tile(rows)

    def body(x_ref, gain_ref, out_ref):
        out_ref[...] = norm(x_ref[...].astype(f32), gain_ref[...]).astype(bf16)

    spec = pl.BlockSpec((tile, D), lambda t: (t, 0))
    return pl.pallas_call(
        body,
        grid=(rows // tile,),
        out_shape=jax.ShapeDtypeStruct((rows, D), bf16),
        in_specs=[spec, const_spec((1, D))],
        out_specs=spec,
        compiler_params=params(),
        name="norm_rows",
    )(values, gain)


def ffn_half(normed, weights, upper, lower, part, keep, pre=None):
    rows = normed.shape[0]
    tile = row_tile(rows)
    steps = FF // D // 2

    def body(part_ref, x_ref, up_ref, down_ref, *rest):
        out_ref = rest[-3] if keep else rest[-2]
        pre_ref = rest[-2]
        total = rest[-1]
        step = pl.program_id(0)
        for t in range(0, rows, tile):
            here = slice(t, t + tile)
            value = dot(x_ref[here], up_ref[...])
            if keep:
                pre_ref[here] = value.astype(bf16)
            act = (value * sigmoid(value)).astype(bf16)
            new = dot(act, down_ref[...])

            @pl.when(step == 0)
            def _(new=new, here=here):
                total[here] = new

            @pl.when(step == steps - 1)
            def _(new=new, here=here):
                out_ref[here] = (total[here] + new).astype(bf16)

    operands = [part.reshape(1), normed, weights, weights]
    specs = [
        pl.BlockSpec((rows, D), lambda f, p: (0, 0), pipeline_mode=pl.Buffered(1)),
        pl.BlockSpec((D, D), lambda f, p: (at(upper) + p[0] * steps + f, 0)),
        pl.BlockSpec((D, D), lambda f, p: (at(lower) + p[0] * steps + f, 0)),
    ]
    shapes = [jax.ShapeDtypeStruct((rows, D), bf16)]
    out_specs = [pl.BlockSpec((rows, D), lambda f, p: (0, 0), pipeline_mode=pl.Buffered(1))]
    aliases = {}
    if keep:
        shapes.append(jax.ShapeDtypeStruct((rows, FF), bf16))
        out_specs.append(pl.BlockSpec((rows, D), lambda f, p: (0, p[0] * steps + f)))
        if pre is not None:
            aliases = {len(operands): 1}
            operands.append(pre)
            specs.append(ANY)
    return pl.pallas_call(
        body,
        grid_spec=pltpu.PrefetchScalarGridSpec(
            num_scalar_prefetch=1,
            grid=(steps,),
            in_specs=specs,
            out_specs=tuple(out_specs),
            scratch_shapes=[pltpu.VMEM((rows, D), f32)],
        ),
        out_shape=tuple(shapes),
        input_output_aliases=aliases,
        compiler_params=params(),
        cost_estimate=cost(2 * rows * D * FF, 2 * D * FF),
        name="ffn_half",
    )(*operands)


def join(base, one, other, next_gain):
    rows = base.shape[0]
    tile = row_tile(rows)

    def body(base_ref, one_ref, other_ref, gain_ref, out_ref, next_ref):
        both = one_ref[...].astype(f32) + other_ref[...].astype(f32)
        y = base_ref[...].astype(f32) + 0.5 * both
        out_ref[...] = y
        next_ref[...] = norm(y, gain_ref[...]).astype(bf16)

    spec = pl.BlockSpec((tile, D), lambda t: (t, 0))
    return pl.pallas_call(
        body,
        grid=(rows // tile,),
        out_shape=(
            jax.ShapeDtypeStruct((rows, D), f32),
            jax.ShapeDtypeStruct((rows, D), bf16),
        ),
        in_specs=[spec, spec, spec, const_spec((1, D))],
        out_specs=(spec, spec),
        compiler_params=params(),
        name="join",
    )(base, one, other, next_gain)


def ffn_backward(
    after, after_gain, after_grads, base, stream, gain, pre, weights, upper, lower, sums, table,
    ranks, kept=None,
):
    rows = stream.shape[0]
    tile = row_tile(rows)
    wide = 512
    steps = FF // wide
    parts = len(after_grads)
    targets = len(sums)
    with_base = base is not None
    again = kept is not None

    def body(table_ref, *refs):
        refs = list(refs)
        after_ref, after_gain_ref = refs[0], refs[1]
        grad_refs = refs[2 : 2 + parts]
        at_ref = 2 + parts
        base_ref = None
        if with_base:
            base_ref = refs[at_ref]
            at_ref += 1
        x_ref, gain_ref, up_ref, down_ref, pre_ref = refs[at_ref : at_ref + 5]
        kept_ref = refs[at_ref + 5]
        out_ref, gains_ref = refs[-13 - targets : -11 - targets]
        sums_ref = refs[-11 - targets : -11]
        (
            half, normed, pre_here, normed_t, grad_sum, pre_grad, act_t, up_part, down_part, up_sem,
            down_sem,
        ) = refs[-11:]
        step = pl.program_id(0)

        @pl.when(step == 0)
        def _():
            gain_sum = jnp.zeros((1, D), f32)
            for t in range(0, rows, tile):
                here = slice(t, t + tile)
                grad = grad_refs[0][here].astype(f32)
                for other in grad_refs[1:]:
                    grad = grad + other[here].astype(f32)
                back, part = norm_back(after_ref[here], after_gain_ref[...], grad)
                gain_sum = gain_sum + part
                if with_base:
                    back = back + base_ref[here]
                out_ref[here] = back
                half[here] = (0.5 * back).astype(bf16)
                low = norm(x_ref[here].astype(f32), gain_ref[...]).astype(bf16)
                if again:
                    normed[here] = low
                normed_t[:, here] = low.T
                grad_sum[here] = jnp.zeros((tile, D), f32)
            gains_ref[0:1] = gain_sum

        if again:

            @pl.when(step // (steps // 2) == kept_ref[0])
            def _():
                pre_here[...] = pre_ref[...]

            @pl.when(step // (steps // 2) != kept_ref[0])
            def _():
                for t in range(0, rows, tile):
                    here = slice(t, t + tile)
                    pre_here[here] = dot(normed[here], up_ref[...]).astype(bf16)

        for t in range(0, rows, tile):
            here = slice(t, t + tile)
            act_grad = dot_right(half[here], down_ref[...])
            pre_act = (pre_here if again else pre_ref)[here].astype(f32)
            sigma = sigmoid(pre_act)
            act = pre_act * sigma
            act_t[:, here] = act.astype(bf16).T
            slope = sigma + act * (1.0 - sigma)
            moved = (act_grad * slope).astype(bf16)
            pre_grad[here] = moved
            grad_sum[here] += dot_right(moved, up_ref[...])

        @pl.when(step >= 1)
        def _():
            wait_blocks(up_part, up_sem)
            wait_blocks(down_part, down_sem)

        for t in range(0, D, 256):
            up_part[t : t + 256] = dot(normed_t[t : t + 256], pre_grad[...]).astype(bf16)
        for t in range(0, wide, 256):
            down_part[t : t + 256] = dot(act_t[t : t + 256], half[...]).astype(bf16)
        start_blocks(
            table_ref, sums_ref, up_part, up_sem, upper, 0, step * 4, ranks
        )
        start_blocks(
            table_ref, sums_ref, down_part, down_sem, lower, step * 4, 0, ranks
        )

        @pl.when(step == steps - 1)
        def _():
            gain_sum = jnp.zeros((1, D), f32)
            for t in range(0, rows, tile):
                here = slice(t, t + tile)
                back, part = norm_back(x_ref[here].astype(f32), gain_ref[...], grad_sum[here])
                gain_sum = gain_sum + part
                out_ref[here] += back
            gains_ref[1:2] = gain_sum
            wait_blocks(up_part, up_sem)
            wait_blocks(down_part, down_sem)

    operands = [table, after, after_gain, *after_grads]
    specs = [SMEM, const_spec((rows, D)), const_spec((1, D))] + [const_spec((rows, D))] * parts
    if with_base:
        operands.append(base)
        specs.append(const_spec((rows, D)))
    operands += [stream, gain, weights, weights]
    specs += [
        const_spec((rows, D)),
        const_spec((1, D)),
        pl.BlockSpec((D, wide), lambda f: (at(upper) + f // 2, f % 2)),
        pl.BlockSpec((wide, D), lambda f: (at(lower) * 2 + f, 0)),
    ]
    operands.append(pre)
    specs.append(pl.BlockSpec((rows, wide), lambda f: (0, f)))
    if again:
        operands.append(kept.reshape(1))
        specs.append(SMEM)
    aliases = {}
    if not isinstance(sums[0], tuple):
        for n, target in enumerate(sums):
            aliases[len(operands)] = 2 + n
            operands.append(target)
            specs.append(ANY)
        sums = [target.shape for target in sums]
    return pl.pallas_call(
        body,
        grid=(steps,),
        out_shape=(
            jax.ShapeDtypeStruct((rows, D), f32),
            jax.ShapeDtypeStruct((2, D), f32),
            *[jax.ShapeDtypeStruct(shape, bf16) for shape in sums],
        ),
        in_specs=specs,
        out_specs=(const_spec((rows, D)), const_spec((2, D))) + (ANY,) * targets,
        scratch_shapes=[
            pltpu.VMEM((rows, D), bf16),
            pltpu.VMEM((rows, D) if again else (16, 128), bf16),
            pltpu.VMEM((rows, wide) if again else (16, 128), bf16),
            pltpu.VMEM((D, rows), bf16),
            pltpu.VMEM((rows, D), f32),
            pltpu.VMEM((rows, wide), bf16),
            pltpu.VMEM((wide, rows), bf16),
            pltpu.VMEM((D, wide), bf16),
            pltpu.VMEM((wide, D), bf16),
            pltpu.SemaphoreType.DMA,
            pltpu.SemaphoreType.DMA,
        ],
        input_output_aliases=aliases,
        compiler_params=params(has_side_effects=True),
        cost_estimate=cost(8 * rows * D * FF, 8 * D * FF + 2 * rows * FF),
        name="ffn_backward",
    )(*operands)


def project(values, weights, first, count, part=None, parts=1, into=None):
    rows = values.shape[0]
    tile = row_tile(rows)
    wide = D

    def body(part_ref, x_ref, w_ref, *rest):
        out_ref = rest[-1]
        for t in range(0, rows, tile):
            out_ref[t : t + tile] = dot(x_ref[t : t + tile], w_ref[...]).astype(bf16)

    operands = [jnp.asarray(0 if part is None else part, jnp.int32).reshape(1), values, weights]
    specs = [
        pl.BlockSpec((rows, D), lambda f, part: (0, 0), pipeline_mode=pl.Buffered(1)),
        pl.BlockSpec((D, wide), lambda f, part: (at(first) + f, 0)),
    ]
    aliases = {}
    if into is not None:
        aliases = {3: 0}
        operands.append(into)
        specs.append(ANY)
    return pl.pallas_call(
        body,
        grid_spec=pltpu.PrefetchScalarGridSpec(
            num_scalar_prefetch=1,
            grid=(count,),
            in_specs=specs,
            out_specs=pl.BlockSpec((rows, wide), lambda f, part: (part[0], f)),
        ),
        out_shape=jax.ShapeDtypeStruct((parts * rows, count * D), bf16),
        input_output_aliases=aliases,
        compiler_params=params(),
        cost_estimate=cost(2 * rows * D * D * count, 2 * count * D * (D + rows)),
        name="project",
    )(*operands)


def project_out(values, weights, matrix, stream):
    rows = values.shape[0]
    tile = row_tile(rows)

    def body(x_ref, w_ref, s_ref, out_ref):
        out_ref[...] = s_ref[...] + dot(x_ref[...], w_ref[...])

    return pl.pallas_call(
        body,
        grid=(rows // tile,),
        out_shape=jax.ShapeDtypeStruct((rows, D), f32),
        in_specs=[
            pl.BlockSpec((tile, D), lambda t: (t, 0)),
            pl.BlockSpec((D, D), lambda t: (at(matrix), 0)),
            pl.BlockSpec((tile, D), lambda t: (t, 0)),
        ],
        out_specs=pl.BlockSpec((tile, D), lambda t: (t, 0)),
        compiler_params=params(),
        cost_estimate=cost(2 * rows * D * D, 2 * D * D + 10 * rows * D),
        name="project_out",
    )(values, weights, stream)


def project_out_back(grad, weights, matrix, attended, sums, table, ranks):
    rows = grad.shape[0]
    tile = row_tile(rows)
    wide = 512

    targets = len(sums)

    def body(table_ref, g_ref, w_ref, a_ref, *refs):
        out_ref = refs[targets]
        sums_ref = refs[targets + 1 : 2 * targets + 1]
        low, part, sem = refs[2 * targets + 1 :]
        step = pl.program_id(0)

        @pl.when(step == 0)
        def _():
            for t in range(0, rows, tile):
                low[t : t + tile] = g_ref[t : t + tile].astype(bf16)

        for t in range(0, rows, tile):
            out_ref[t : t + tile] = dot_right(low[t : t + tile], w_ref[...]).astype(bf16)
        for t in range(0, wide, 256):
            part[step, t : t + 256] = dot_left(a_ref[:, t : t + 256], low[...]).astype(bf16)
        start_blocks(table_ref, sums_ref, part.at[step], sem.at[step], matrix, step * 4, 0, ranks)

        @pl.when(step == 1)
        def _():
            for s in range(2):
                wait_blocks(part.at[s], sem.at[s])

    return pl.pallas_call(
        body,
        grid=(2,),
        out_shape=(
            jax.ShapeDtypeStruct((rows, D), bf16),
            *[jax.ShapeDtypeStruct(target.shape, bf16) for target in sums],
        ),
        in_specs=[
            SMEM,
            const_spec((rows, D)),
            pl.BlockSpec((wide, D), lambda f: (at(matrix) * 2 + f, 0)),
            pl.BlockSpec((rows, wide), lambda f: (0, f)),
        ]
        + [ANY] * targets,
        out_specs=(pl.BlockSpec((rows, wide), lambda f: (0, f)),) + (ANY,) * targets,
        scratch_shapes=[
            pltpu.VMEM((rows, D), bf16),
            pltpu.VMEM((2, wide, D), bf16),
            pltpu.SemaphoreType.DMA((2,)),
        ],
        input_output_aliases={4 + n: 1 + n for n in range(targets)},
        compiler_params=params(has_side_effects=True),
        cost_estimate=cost(4 * rows * D * D, 4 * D * D + 8 * rows * D),
        name="project_out_back",
    )(table, grad, weights, attended, *sums)


def input_gradient(key_grad, value_grad, weights, part, rows):
    tile = row_tile(rows)
    steps = rows // tile

    def body(part_ref, k_ref, v_ref, wk_ref, wv_ref, out_ref):
        out_ref[...] = (
            dot_right(k_ref[...], wk_ref[...]) + dot_right(v_ref[...], wv_ref[...])
        ).astype(bf16)

    return pl.pallas_call(
        body,
        grid_spec=pltpu.PrefetchScalarGridSpec(
            num_scalar_prefetch=1,
            grid=(steps,),
            in_specs=[
                pl.BlockSpec((tile, D), lambda t, part: (part[0] * steps + t, 0)),
                pl.BlockSpec((tile, D), lambda t, part: (part[0] * steps + t, 0)),
                pl.BlockSpec((D, D), lambda t, part: (at(KEY), 0)),
                pl.BlockSpec((D, D), lambda t, part: (at(VALUE), 0)),
            ],
            out_specs=pl.BlockSpec((tile, D), lambda t, part: (t, 0)),
        ),
        out_shape=jax.ShapeDtypeStruct((rows, D), bf16),
        compiler_params=params(),
        cost_estimate=cost(4 * rows * D * D, 4 * D * D + 6 * rows * D),
        name="input_gradient",
    )(part.reshape(1), key_grad, value_grad, weights, weights)


def projections_back(
    normed, query_grad, key_grad, value_grad, sources, own_keys, weights, sums, table, ranks
):
    rows = normed.shape[0]
    tile = row_tile(rows)
    wide = 512
    count = len(sources)
    targets = len(sums)
    lengths = [source[0].shape[0] for source in sources]

    def body(part_ref, table_ref, n_ref, q_ref, *refs):
        normed_refs = refs[:count]
        key_refs = refs[count : 2 * count]
        value_refs = refs[2 * count : 3 * count]
        w_ref = refs[3 * count]
        outs = refs[3 * count + 1 + targets :]
        out_ref, sums_ref, scratch = outs[0], outs[1 : 1 + targets], outs[1 + targets :]
        own_t = scratch[0]
        source_t = scratch[1 : 1 + count]
        part, sem = scratch[1 + count :]
        step = pl.program_id(0)
        slot = lax.rem(step, 2)

        @pl.when(step == 0)
        def _():
            for t in range(0, rows, tile):
                own_t[:, t : t + tile] = n_ref[t : t + tile].T
            for n_from, n_to, length in zip(normed_refs, source_t, lengths):
                small = row_tile(length)
                for t in range(0, length, small):
                    n_to[:, t : t + small] = n_from[t : t + small].T

        @pl.when(step >= 2)
        def _():
            wait_blocks(part.at[slot], sem.at[slot])

        @pl.when(step < 2)
        def _():
            for t in range(0, rows, tile):
                new = dot_right(q_ref[t : t + tile], w_ref[...])

                @pl.when(step == 0)
                def _():
                    out_ref[t : t + tile] = new

                @pl.when(step == 1)
                def _():
                    out_ref[t : t + tile] += new

            for t in range(0, D, 256):
                part[slot, t : t + 256] = dot(own_t[t : t + 256], q_ref[...]).astype(bf16)
            start_blocks(
                table_ref, sums_ref, part.at[slot], sem.at[slot], QUERY, 0, lax.rem(step, 2) * 4,
                ranks,
            )

        def other(grad_refs, matrix):
            if own_keys:
                for t in range(0, rows, tile):
                    out_ref[t : t + tile] += dot_right(grad_refs[0][t : t + tile], w_ref[...])
            for t in range(0, D, 256):
                total = dot(source_t[0][t : t + 256], grad_refs[0][...])
                for n_t, grad_ref in zip(source_t[1:], grad_refs[1:]):
                    total = total + dot(n_t[t : t + 256], grad_ref[...])
                part[slot, t : t + 256] = total.astype(bf16)
            start_blocks(
                table_ref, sums_ref, part.at[slot], sem.at[slot], matrix, 0, lax.rem(step, 2) * 4,
                ranks,
            )

        @pl.when((step >= 2) & (step < 4))
        def _():
            other(key_refs, KEY)

        @pl.when(step >= 4)
        def _():
            other(value_refs, VALUE)

        @pl.when(step == 5)
        def _():
            for s in range(2):
                wait_blocks(part.at[s], sem.at[s])

    parts = jnp.stack([jnp.asarray(source[1], jnp.int32) for source in sources])
    operands = [parts, table, normed, query_grad]

    def whole(shape):
        return pl.BlockSpec(shape, lambda f, part: (0, 0), pipeline_mode=pl.Buffered(1))

    specs = [
        SMEM,
        whole((rows, D)),
        pl.BlockSpec((rows, wide), lambda f, part: (0, jnp.minimum(f, 1))),
    ]
    operands += [source[0] for source in sources]
    specs += [whole((length, D)) for length in lengths]
    for grads, first in ((key_grad, 2), (value_grad, 4)):
        for n, length in enumerate(lengths):
            operands.append(grads)
            specs.append(
                pl.BlockSpec(
                    (length, wide),
                    lambda f, part, n=n, first=first: (part[n], jnp.clip(f - first, 0, 1)),
                )
            )
    operands += [weights, *sums]
    specs += [pl.BlockSpec((D, wide), lambda f, part: (at(QUERY) + f // 2, f % 2))]
    specs += [ANY] * targets
    return pl.pallas_call(
        body,
        grid_spec=pltpu.PrefetchScalarGridSpec(
            num_scalar_prefetch=1,
            grid=(6,),
            in_specs=specs,
            out_specs=(whole((rows, D)),) + (ANY,) * targets,
            scratch_shapes=[pltpu.VMEM((D, rows), bf16)]
            + [pltpu.VMEM((D, length), bf16) for length in lengths]
            + [pltpu.VMEM((2, D, wide), bf16), pltpu.SemaphoreType.DMA((2,))],
        ),
        out_shape=(
            jax.ShapeDtypeStruct((rows, D), f32),
            *[jax.ShapeDtypeStruct(target.shape, bf16) for target in sums],
        ),
        input_output_aliases={len(operands) - targets + n: 1 + n for n in range(targets)},
        compiler_params=params(has_side_effects=True),
        cost_estimate=cost(
            (4 * rows + sum(4 * length for length in lengths) + 4 * rows) * D * D, 30 * D * D
        ),
        name="projections_back",
    )(*operands)


def attention_tiles(rows):
    return (512 if rows % 512 == 0 else row_tile(rows)), 256


def key_windows(segments, rank, rows):
    tall, broad = attention_tiles(rows)
    group = segments.shape[0]
    blocks = rows // tall
    own = lax.dynamic_slice_in_dim(segments, rank * rows, rows).reshape(blocks, tall)
    low = jnp.sum(segments[None, :] < own[:, :1], axis=1)
    high = jnp.sum(segments[None, :] <= own[:, -1:], axis=1)
    start = low // 128 * 128
    steps = (high - start + broad - 1) // broad
    start = jnp.minimum(start, group - steps * broad)
    return jnp.stack([start, steps], axis=-1).reshape(-1).astype(jnp.int32)

def attention_forward(queries, keys, segments, rank, windows, slopes):
    rows = queries.shape[0]
    group = keys.shape[0]
    tall, broad = attention_tiles(rows)
    most = group // broad
    own = lax.dynamic_slice_in_dim(segments, rank * rows, rows).reshape(rows, 1)

    def body(rank_ref, window_ref, slope_ref, q_ref, own_ref, key_ref, value_ref, columns_ref, out_ref, total_ref, scores):
        head, block = pl.program_id(0), pl.program_id(1)
        slope = slope_ref[head] * LOG2E
        start = window_ref[2 * block]
        steps = window_ref[2 * block + 1]
        first = rank_ref[0] * rows + block * tall
        query = q_ref[...]
        apart = (
            lax.broadcasted_iota(jnp.int32, (tall, broad), 0)
            - lax.broadcasted_iota(jnp.int32, (tall, broad), 1)
        ).astype(f32)

        def attend(count):
            peak = jnp.full((tall, 128), MASKED, f32)
            for b in range(count):
                begin = pl.multiple_of(start + b * broad, 128)
                here = pl.ds(begin, broad)
                score = dot_right(query, key_ref[here, :]) * (SCORE_SCALE * LOG2E)
                score = score - slope * jnp.abs(apart + (first - begin).astype(f32))
                score = jnp.where(own_ref[...] == columns_ref[:, here], score, MASKED)
                scores[:, b * broad : (b + 1) * broad] = score
                for lane in range(0, broad, 128):
                    peak = jnp.maximum(peak, score[:, lane : lane + 128])
            top = jnp.max(peak, axis=-1, keepdims=True)
            total = jnp.zeros((tall, 128), f32)
            mixed = jnp.zeros((tall, HEAD_DIM), f32)
            for b in range(count):
                here = pl.ds(pl.multiple_of(start + b * broad, 128), broad)
                shifted = jnp.exp2(scores[:, b * broad : (b + 1) * broad] - top)
                for lane in range(0, broad, 128):
                    total = total + shifted[:, lane : lane + 128]
                mixed = mixed + dot(shifted.astype(bf16), value_ref[here, :])
            total = jnp.sum(total, axis=-1, keepdims=True)
            out_ref[...] = (mixed / total).astype(bf16)
            logs = jnp.broadcast_to(top + jnp.log2(total), (tall, 128))
            total_ref[...] = logs.T[0:1, :].reshape(1, 1, tall)

        for count in range(1, most + 1):
            @pl.when(steps == count)
            def _(count=count):
                attend(count)

    return pl.pallas_call(
        body,
        grid=(HEADS, rows // tall),
        out_shape=(
            jax.ShapeDtypeStruct((rows, D), bf16),
            jax.ShapeDtypeStruct((HEADS, 1, rows), f32),
        ),
        in_specs=[
            SMEM, SMEM, SMEM,
            pl.BlockSpec((tall, HEAD_DIM), lambda h, q: (q, h)),
            pl.BlockSpec((tall, 1), lambda h, q: (q, 0)),
            pl.BlockSpec((group, HEAD_DIM), lambda h, q: (0, h)),
            pl.BlockSpec((group, HEAD_DIM), lambda h, q: (0, HEADS + h)),
            const_spec((1, group)),
        ],
        out_specs=(
            pl.BlockSpec((tall, HEAD_DIM), lambda h, q: (q, h)),
            pl.BlockSpec((1, 1, tall), lambda h, q: (h, 0, q)),
        ),
        scratch_shapes=[pltpu.VMEM((tall, group), f32)],
        compiler_params=params(),
        name="attention_forward",
    )(jnp.asarray(rank,jnp.int32).reshape(1), windows, slopes, queries, own, keys, keys, segments.reshape(1, group))

def attention_backward(queries, keys, segments, rank, windows, slopes, logs, grads, attended):
    rows = queries.shape[0]
    group = keys.shape[0]
    tall, broad = attention_tiles(rows)
    most = group // broad
    own = lax.dynamic_slice_in_dim(segments, rank * rows, rows).reshape(1, rows)

    def body(rank_ref, window_ref, slope_ref, q_ref, own_ref, log_ref, grad_ref, att_ref, key_ref, value_ref, columns_ref,
             out_ref, key_out, value_out, key_sum, value_sum):
        head, block = pl.program_id(0), pl.program_id(1)
        slope = slope_ref[head] * LOG2E
        start = window_ref[2 * block]
        steps = window_ref[2 * block + 1]
        first = rank_ref[0] * rows + block * tall

        @pl.when(block == 0)
        def _():
            key_sum[...] = jnp.zeros(key_sum.shape, f32)
            value_sum[...] = jnp.zeros(value_sum.shape, f32)

        query = q_ref[...]
        grad = grad_ref[...]
        products = grad.astype(f32) * att_ref[...].astype(f32)
        delta = jnp.broadcast_to(jnp.sum(products, axis=-1, keepdims=True), (tall, 128)).T[0:1, :]
        log_row = log_ref[0]
        apart = (
            lax.broadcasted_iota(jnp.int32, (broad, tall), 1)
            - lax.broadcasted_iota(jnp.int32, (broad, tall), 0)
        ).astype(f32)

        def attend(count):
            query_sum = jnp.zeros((tall, HEAD_DIM), f32)
            for b in range(count):
                begin = pl.multiple_of(start + b * broad, 128)
                here = pl.ds(begin, broad)
                key = key_ref[here, :]
                score = dot_right(key, query) * (SCORE_SCALE * LOG2E)
                score = score - slope * jnp.abs(apart + (first - begin).astype(f32))
                score = jnp.where(own_ref[...] == columns_ref[here, :], score, MASKED)
                probs = jnp.exp2(score - log_row)
                prob_grad = dot_right(value_ref[here, :], grad)
                value_sum[here, :] += dot(probs.astype(bf16), grad)
                score_grad = (probs * (prob_grad - delta)).astype(bf16)
                key_sum[here, :] += dot(score_grad, query)
                query_sum = query_sum + dot_left(score_grad, key)
            out_ref[...] = (query_sum * SCORE_SCALE).astype(bf16)

        for count in range(1, most + 1):
            @pl.when(steps == count)
            def _(count=count):
                attend(count)

        @pl.when(block == pl.num_programs(1) - 1)
        def _():
            key_out[...] = (key_sum[...] * SCORE_SCALE).astype(bf16)
            value_out[...] = value_sum[...].astype(bf16)

    row_spec = pl.BlockSpec((tall, HEAD_DIM), lambda h, q: (q, h))
    key_spec = pl.BlockSpec((group, HEAD_DIM), lambda h, q: (0, h))
    return pl.pallas_call(
        body,
        grid=(HEADS, rows // tall),
        out_shape=(jax.ShapeDtypeStruct((rows, D), bf16),) + (jax.ShapeDtypeStruct((group, D), bf16),) * 2,
        in_specs=[
            SMEM, SMEM, SMEM,
            pl.BlockSpec((tall, HEAD_DIM), lambda h, q: (q, h)),
            pl.BlockSpec((1, tall), lambda h, q: (0, q)),
            pl.BlockSpec((1, 1, tall), lambda h, q: (h, 0, q)),
            row_spec, row_spec, key_spec,
            pl.BlockSpec((group, HEAD_DIM), lambda h, q: (0, HEADS + h)),
            const_spec((group, 1)),
        ],
        out_specs=(row_spec, key_spec, key_spec),
        scratch_shapes=[pltpu.VMEM((group, HEAD_DIM), f32)] * 2,
        compiler_params=params(),
        name="attention_backward",
    )(jnp.asarray(rank,jnp.int32).reshape(1), windows, slopes, queries, own, logs, grads, attended, keys, keys, segments.reshape(group, 1))


def conv_forward(stream, before, behind, gain, next_gain, weights, taps, masks):
    rows = stream.shape[0]
    tall = rows + 2 * HALO
    tile = row_tile(rows)
    wide = 256
    steps = D // wide

    def body(
        x_ref, before_ref, behind_ref, gain_ref, next_gain_ref, taps_ref, mask_ref, value_ref, gate_ref, out_w_ref,
        out_ref, linear_ref, gate_out_ref, next_ref, normed, glu,
    ):
        step = pl.program_id(0)

        @pl.when(step == 0)
        def _():
            gain_row = gain_ref[...]
            normed[0:HALO] = norm(before_ref[...], gain_row).astype(bf16)
            normed[rows + HALO :] = norm(behind_ref[...], gain_row).astype(bf16)
            for t in range(0, rows, tile):
                x = x_ref[t : t + tile]
                normed[HALO + t : HALO + t + tile] = norm(x, gain_row).astype(bf16)
                out_ref[t : t + tile] = x

        pieces = [(0, HALO)]
        pieces += [(HALO + t, tile) for t in range(0, rows, tile)]
        pieces += [(rows + HALO, HALO)]
        for t, size in pieces:
            here = slice(t, t + size)
            linear = dot(normed[here], value_ref[...])
            gate = dot(normed[here], gate_ref[...])
            linear_ref[here] = linear.astype(bf16)
            gate_out_ref[here] = gate.astype(bf16)
            glu[here] = linear * sigmoid(gate)
        for t in range(0, rows, tile):
            sums = []
            for half in range(0, wide, 128):
                total = jnp.zeros((tile, 128), f32)
                for k in range(KERNEL):
                    moved = glu[HALO + t + k - 2 : HALO + t + k - 2 + tile, half : half + 128]
                    if k != KERNEL // 2:
                        moved = moved * mask_ref[k, HALO + t : HALO + t + tile]
                    total = total + taps_ref[k : k + 1, half : half + 128] * moved
                sums.append(total)
            conved = jnp.concatenate(sums, axis=1)
            act = (conved * sigmoid(conved)).astype(bf16)
            out_ref[t : t + tile] += dot(act, out_w_ref[...])

        @pl.when(step == steps - 1)
        def _():
            for t in range(0, rows, tile):
                next_ref[t : t + tile] = norm(out_ref[t : t + tile], next_gain_ref[...]).astype(bf16)

    return pl.pallas_call(
        body,
        grid=(steps,),
        out_shape=(
            jax.ShapeDtypeStruct((rows, D), f32),
            jax.ShapeDtypeStruct((tall, D), bf16),
            jax.ShapeDtypeStruct((tall, D), bf16),
            jax.ShapeDtypeStruct((rows, D), bf16),
        ),
        in_specs=[
            const_spec((rows, D)),
            const_spec((HALO, D)),
            const_spec((HALO, D)),
            const_spec((1, D)),
            const_spec((1, D)),
            pl.BlockSpec((KERNEL, wide), lambda c: (0, c)),
            const_spec((KERNEL, tall, 128)),
            pl.BlockSpec((D, wide), lambda c: (at(CONV_VALUE), c)),
            pl.BlockSpec((D, wide), lambda c: (at(CONV_GATE), c)),
            pl.BlockSpec((wide, D), lambda c: (at(CONV_OUT) * 4 + c, 0)),
        ],
        out_specs=(
            const_spec((rows, D)),
            pl.BlockSpec((tall, wide), lambda c: (0, c)),
            pl.BlockSpec((tall, wide), lambda c: (0, c)),
            const_spec((rows, D)),
        ),
        scratch_shapes=[pltpu.VMEM((tall, D), bf16), pltpu.VMEM((tall, wide), f32)],
        compiler_params=params(),
        cost_estimate=cost(6 * rows * D * D, 6 * D * D + 12 * rows * D),
        name="conv_forward",
    )(stream, before, behind, gain, next_gain, taps, masks, weights, weights, weights)


def conv_backward(
    grad, before, behind, stream, gain, linear, gate, weights, taps, masks, sums, table, ranks
):
    rows = stream.shape[0]
    tall = rows + 2 * HALO
    tile = row_tile(rows)
    wide = 256
    steps = D // wide
    targets = len(sums)

    def body(
        table_ref, g_ref, before_ref, behind_ref, x_ref, gain_ref, linear_ref, gate_ref, taps_ref,
        mask_ref, value_ref, gate_w_ref, out_w_ref, *refs,
    ):
        out_ref, gain_out_ref, taps_out_ref = refs[targets : targets + 3]
        sums_ref = refs[targets + 3 : 2 * targets + 3]
        (
            low, normed_t, grad_sum, glu, conv_grad, act_t, value_grad, gate_grad, value_part,
            gate_part, out_part, value_sem, gate_sem, out_sem,
        ) = refs[2 * targets + 3 :]
        step = pl.program_id(0)
        slot = lax.rem(step, 2)

        @pl.when(step == 0)
        def _():
            low[0:HALO] = before_ref[...]
            low[rows + HALO :] = behind_ref[...]
            for t in range(0, rows, tile):
                here = slice(t, t + tile)
                low[HALO + t : HALO + t + tile] = g_ref[here].astype(bf16)
                normed_t[:, here] = norm(x_ref[here], gain_ref[...]).astype(bf16).T
                grad_sum[here] = jnp.zeros((tile, D), f32)

        pieces = [(0, HALO)]
        pieces += [(HALO + t, tile) for t in range(0, rows, tile)]
        pieces += [(rows + HALO, HALO)]
        for t, size in pieces:
            here = slice(t, t + size)
            glu[here] = linear_ref[here].astype(f32) * sigmoid(gate_ref[here].astype(f32))

        edge = 8
        pieces = [(HALO - edge, edge)]
        pieces += [(HALO + t, tile) for t in range(0, rows, tile)]
        pieces += [(rows + HALO, edge)]
        tap_sums = [[jnp.zeros((1, 128), f32) for k in range(KERNEL)] for half in range(2)]
        for t, size in pieces:
            totals, moved_rows = [], []
            for half in range(0, wide, 128):
                total = jnp.zeros((size, 128), f32)
                moved_rows.append([])
                for k in range(KERNEL):
                    moved = glu[t + k - 2 : t + k - 2 + size, half : half + 128]
                    if k != KERNEL // 2:
                        moved = moved * mask_ref[k, t : t + size]
                    moved_rows[-1].append(moved)
                    total = total + taps_ref[k : k + 1, half : half + 128] * moved
                totals.append(total)
            conved = jnp.concatenate(totals, axis=1)
            sigma = sigmoid(conved)
            act = conved * sigma
            if size == tile:
                act_t[:, t - HALO : t - HALO + size] = act.astype(bf16).T
                rows_grad = dot_right(low[t : t + size], out_w_ref[...])
            elif t < HALO:
                rows_grad = dot_right(low[0:HALO], out_w_ref[...])[edge:]
            else:
                rows_grad = dot_right(low[rows + HALO :], out_w_ref[...])[:edge]
            center = rows_grad * (sigma + act * (1.0 - sigma))
            conv_grad[t : t + size] = center
            if size == tile:
                for number in range(2):
                    lanes = center[:, number * 128 : (number + 1) * 128]
                    for k in range(KERNEL):
                        tap_sums[number][k] = tap_sums[number][k] + jnp.sum(
                            lanes * moved_rows[number][k], axis=0, keepdims=True
                        )

        for t in range(0, rows, tile):
            values, gates = [], []
            for number, half in enumerate(range(0, wide, 128)):
                lanes = slice(half, half + 128)
                start = HALO + t
                total = jnp.zeros((tile, 128), f32)
                for k in range(KERNEL):
                    moved = conv_grad[start + 2 - k : start + 2 - k + tile, lanes]
                    if k != KERNEL // 2:
                        moved = moved * mask_ref[KERNEL - 1 - k, start : start + tile]
                    total = total + taps_ref[k : k + 1, lanes] * moved
                sigma = sigmoid(gate_ref[start : start + tile, lanes].astype(f32))
                moved_value = total * sigma
                values.append(moved_value.astype(bf16))
                gates.append(
                    (
                        moved_value
                        * linear_ref[start : start + tile, lanes].astype(f32)
                        * (1.0 - sigma)
                    ).astype(bf16)
                )
            value_tile = jnp.concatenate(values, axis=1)
            gate_tile = jnp.concatenate(gates, axis=1)
            here = slice(t, t + tile)
            value_grad[here] = value_tile
            gate_grad[here] = gate_tile
            grad_sum[here] += dot_right(value_tile, value_ref[...]) + dot_right(
                gate_tile, gate_w_ref[...]
            )
        for k in range(KERNEL):
            taps_out_ref[k : k + 1] = jnp.concatenate([tap_sums[0][k], tap_sums[1][k]], axis=1)

        @pl.when(step >= 2)
        def _():
            wait_blocks(value_part.at[slot], value_sem.at[slot])
            wait_blocks(gate_part.at[slot], gate_sem.at[slot])
            wait_blocks(out_part.at[slot], out_sem.at[slot])

        for t in range(0, D, 256):
            value_part[slot, t : t + 256] = dot(normed_t[t : t + 256], value_grad[...]).astype(bf16)
            gate_part[slot, t : t + 256] = dot(normed_t[t : t + 256], gate_grad[...]).astype(bf16)
        out_part[slot] = dot(act_t[...], low[HALO : rows + HALO]).astype(bf16)
        start_blocks(
            table_ref, sums_ref, value_part.at[slot], value_sem.at[slot], CONV_VALUE, 0, step * 2,
            ranks,
        )
        start_blocks(
            table_ref, sums_ref, gate_part.at[slot], gate_sem.at[slot], CONV_GATE, 0, step * 2,
            ranks,
        )
        start_blocks(
            table_ref, sums_ref, out_part.at[slot], out_sem.at[slot], CONV_OUT, step * 2, 0, ranks
        )

        @pl.when(step == steps - 1)
        def _():
            gain_sum = jnp.zeros((1, D), f32)
            for t in range(0, rows, tile):
                here = slice(t, t + tile)
                back, part = norm_back(x_ref[here], gain_ref[...], grad_sum[here])
                gain_sum = gain_sum + part
                out_ref[here] = g_ref[here] + back
            gain_out_ref[...] = gain_sum
            for s in range(2):
                wait_blocks(value_part.at[s], value_sem.at[s])
                wait_blocks(gate_part.at[s], gate_sem.at[s])
                wait_blocks(out_part.at[s], out_sem.at[s])

    operands = [
        table, grad, before, behind, stream, gain, linear, gate, taps, masks, weights, weights,
        weights, *sums,
    ]
    return pl.pallas_call(
        body,
        grid=(steps,),
        out_shape=(
            jax.ShapeDtypeStruct((rows, D), f32),
            jax.ShapeDtypeStruct((1, D), f32),
            jax.ShapeDtypeStruct((KERNEL, D), f32),
            *[jax.ShapeDtypeStruct(target.shape, bf16) for target in sums],
        ),
        in_specs=[
            SMEM,
            const_spec((rows, D)),
            const_spec((HALO, D)),
            const_spec((HALO, D)),
            const_spec((rows, D)),
            const_spec((1, D)),
            pl.BlockSpec((tall, wide), lambda c: (0, c)),
            pl.BlockSpec((tall, wide), lambda c: (0, c)),
            pl.BlockSpec((KERNEL, wide), lambda c: (0, c)),
            const_spec((KERNEL, tall, 128)),
            pl.BlockSpec((D, wide), lambda c: (at(CONV_VALUE), c)),
            pl.BlockSpec((D, wide), lambda c: (at(CONV_GATE), c)),
            pl.BlockSpec((wide, D), lambda c: (at(CONV_OUT) * 4 + c, 0)),
        ]
        + [ANY] * targets,
        out_specs=(
            const_spec((rows, D)),
            const_spec((1, D)),
            pl.BlockSpec((KERNEL, wide), lambda c: (0, c)),
        )
        + (ANY,) * targets,
        scratch_shapes=[
            pltpu.VMEM((tall, D), bf16),
            pltpu.VMEM((D, rows), bf16),
            pltpu.VMEM((rows, D), f32),
            pltpu.VMEM((tall, wide), f32),
            pltpu.VMEM((tall, wide), f32),
            pltpu.VMEM((wide, rows), bf16),
            pltpu.VMEM((rows, wide), bf16),
            pltpu.VMEM((rows, wide), bf16),
            pltpu.VMEM((2, D, wide), bf16),
            pltpu.VMEM((2, D, wide), bf16),
            pltpu.VMEM((2, wide, D), bf16),
            pltpu.SemaphoreType.DMA((2,)),
            pltpu.SemaphoreType.DMA((2,)),
            pltpu.SemaphoreType.DMA((2,)),
        ],
        input_output_aliases={len(operands) - targets + n: 3 + n for n in range(targets)},
        compiler_params=params(has_side_effects=True),
        cost_estimate=cost(12 * rows * D * D, 12 * D * D + 16 * rows * D),
        name="conv_backward",
    )(*operands)


def shampoo(grads, arrivals, left_stats, right_stats, left_root, right_root, master, average):
    slots = master.shape[0]
    each = 8
    steps = (slots + each - 1) // each
    arrivals = jnp.pad(arrivals, (0, steps * each - slots))
    old_bias = 1.0 - DECAY_AVERAGE ** (STEP - 1)
    new_bias = 1.0 - DECAY_AVERAGE**STEP

    def body(index_ref, *refs):
        g_refs = refs[:each]
        ls_ref, rs_ref, lr_ref, rr_ref, m_ref, a_ref, go, lo, ro, mo, ao = refs[each:]
        for n in range(each):
            grad = g_refs[n][0]
            go[n] = grad.astype(f32)
            lo[n] = DECAY_STAT * ls_ref[n] + (1.0 - DECAY_STAT) * dot_right(grad, grad)
            ro[n] = DECAY_STAT * rs_ref[n] + (1.0 - DECAY_STAT) * dot_left(grad, grad)
            inner = dot(grad, rr_ref[n].astype(bf16))
            turned = dot(lr_ref[n].astype(bf16), inner.astype(bf16))
            mean_sq = jnp.mean(turned * turned, axis=(0, 1), keepdims=True)
            new = m_ref[n] - RATE_BLOCK * turned * lax.rsqrt(mean_sq + 1e-06)
            mo[n] = new
            ao[n] = (DECAY_AVERAGE * old_bias / new_bias) * a_ref[n] + (
                (1.0 - DECAY_AVERAGE) / new_bias
            ) * new

    spec = pl.BlockSpec((each, BLOCK, BLOCK), lambda s, index: (s, 0, 0))
    grad_specs = [
        pl.BlockSpec((1, BLOCK, BLOCK), lambda s, index, n=n: (index[s * each + n], 0, 0))
        for n in range(each)
    ]
    shape = jax.ShapeDtypeStruct((slots, BLOCK, BLOCK), f32)
    return pl.pallas_call(
        body,
        grid_spec=pltpu.PrefetchScalarGridSpec(
            num_scalar_prefetch=1,
            grid=(steps,),
            in_specs=grad_specs + [spec] * 6,
            out_specs=(spec,) * 5,
        ),
        out_shape=(shape,) * 5,
        compiler_params=params(),
        name="shampoo",
    )(arrivals, *[grads] * each, left_stats, right_stats, left_root, right_root, master, average)


def vector_step(values, grads):
    mean_sq = jnp.mean(grads * grads, axis=-1, keepdims=True)
    return values - RATE_VECTOR * grads * lax.rsqrt(mean_sq + 1e-06)


def round_places(number):
    place = 0
    for other, count in enumerate(ROUNDS):
        if other == number:
            break
        place = place + (32 if other == LARGE else 64) * count
    if number == LARGE:
        return place, 64 * sum(ROUNDS) - 32 * ROUNDS[LARGE]
    return place, place + 32 * ROUNDS[number]


def scatter_tables(owners_all, coords, slot_dev, blocks):
    own_rank, own_x, own_core = coords
    ranks = owners_all.shape[0]
    both = 2 * slot_dev
    chips = owners_all // both
    same = chips[:, :, None] == chips[:, None, :]
    later = jnp.arange(blocks)[None, :] > jnp.arange(blocks)[:, None]
    order = jnp.sum((same & later[None]).astype(jnp.int32), axis=-1)
    dx = (chips % 2) ^ own_x
    z_at = chips // 2
    dy = jnp.arange(ranks)[:, None] ^ own_rank
    position = jnp.zeros_like(owners_all)
    arrival = jnp.zeros_like(owners_all)
    starts, unused = offsets(ranks)
    good = jnp.array(True)
    done = 0
    for number, count in enumerate(ROUNDS):
        inside = order - 4 * done
        core = inside // (2 * count)
        kind = inside // count % 2
        slot = inside % count
        outer = jnp.where(kind == 0, dx, dy)
        inner = jnp.where(kind == 0, dy, dx)
        dc = core ^ own_core
        here = ((kind * 2 + outer) * 2 + inner) * 4 + z_at
        first, second = round_places(number)
        here = jnp.where(dc == 0, first, second) + here * count + slot
        valid = (inside >= 0) & (inside < 4 * count)
        position = jnp.where(valid, here, position)
        arrival = jnp.where(valid, dc * slot_dev + 2 * done + inside % (2 * count), arrival)
        done = done + count
        if number < len(EARLY):
            there = jnp.arange(blocks) >= starts[EARLY[number]]
            good = good & jnp.all((order >= 4 * done) | there[None])
    device = (lax.axis_index("z") * 2 + own_x) * 2 + own_core
    mine = lax.dynamic_index_in_dim(owners_all, own_rank, 0, keepdims=False)
    arrival = lax.dynamic_index_in_dim(arrival, own_rank, 0, keepdims=False)
    match = mine[None, :] == (device * slot_dev + jnp.arange(slot_dev))[:, None]
    index = jnp.sum(jnp.where(match, arrival[None, :], 0), axis=-1)
    return position.reshape(-1).astype(jnp.int32), index.astype(jnp.int32), good


def added(terms):
    return sum(term.astype(f32) for term in terms).astype(bf16)


def one_round(rounds, send, number):
    count = ROUNDS[number]
    offset = round_places(number)[0]
    (come,) = yield [(send, "core")]
    half, quarter = 16 * count, 8 * count

    def part(kind, first, length):
        start = offset + kind * half + first
        here = kind * half + first
        return [rounds.sums[start : start + length], come[here : here + length]]

    got = yield [
        (added(part(0, quarter, quarter)), "x"),
        (added(part(1, quarter, quarter)), "mp"),
    ]
    eighth = quarter // 2
    late = yield [
        (added(part(0, eighth, eighth) + [got[0][eighth:]]), "mp"),
        (added(part(1, eighth, eighth) + [got[1][eighth:]]), "x"),
    ]
    columns = [
        added(part(kind, 0, eighth) + [got[kind][:eighth], late[kind]])
        .reshape(4, count, BLOCK, BLOCK)
        for kind in range(2)
    ]
    column = jnp.concatenate(columns, axis=1)
    if number < len(ROUNDS) - 1:
        return column
    z_at = lax.axis_index("z")

    def for_z(step):
        return lax.dynamic_index_in_dim(column, jnp.clip(z_at + step, 0, 3), 0, keepdims=False)

    got = yield [(for_z(step), step) for step in (2, -2, 1, -1, 3, -3)]
    return added([for_z(0), *got])


def total_steps(values):
    for group in (("core", "x", "both"), ("mp", "near", "across"), ("far",)):
        got = yield [(values, move) for move in group]
        values = values + got[0]
        if len(got) > 1:
            values = values + (got[1] + got[2])
    return values


class Rounds:
    def __init__(self, sums, tail):
        self.running, self.waiting, self.results = {}, {}, {}
        self.sums, self.tail = sums, tail

    def add(self, name, steps):
        self.running[name] = steps
        self.waiting[name] = next(steps)

    def add_round(self, number):
        size = 32 * ROUNDS[number]
        offset = round_places(number)[1]
        send = self.tail if number == LARGE else self.sums[offset : offset + size]
        self.add(number, one_round(self, send, number))

    def beside(self, *held):
        names = list(self.waiting)
        values = [value for name in names for value, unused in self.waiting[name]]
        out = list(tied(*values, *held))
        for name in names:
            self.waiting[name] = [(out.pop(0), move) for unused, move in self.waiting[name]]
        return out

    def hold(self):
        moves = [[move for unused, move in pairs] for pairs in self.waiting.values()]
        values = [value for pairs in self.waiting.values() for value, unused in pairs]
        columns = list(self.results.items())
        out = list(tied(self.sums, *values, *[value for unused, value in columns]))
        self.sums = out.pop(0)
        for name, names in zip(self.waiting, moves):
            self.waiting[name] = [(out.pop(0), move) for move in names]
        for (name, unused), value in zip(columns, out):
            self.results[name] = value
        return self.sums, self.tail

    def step(self, names, *held, sums=None):
        names = [name for name in names if name in self.waiting]
        transfers = [pair for name in names for pair in self.waiting[name]]
        if sums is not None:
            got, held = together(transfers, *sums, *held)
            (self.sums, self.tail), held = held[:2], held[2:]
        else:
            got, held = together(transfers, *held)
        for name in names:
            count = len(self.waiting[name])
            mine, got = got[:count], got[count:]
            try:
                self.waiting[name] = self.running[name].send(mine)
            except StopIteration as end:
                self.results[name] = end.value
                del self.waiting[name]
        return held


def one_swap(value, move):
    (come,) = yield [(value, move)]
    return come


def joined(columns):
    return jnp.concatenate(columns, axis=1).reshape(-1, BLOCK, BLOCK)


def over_z(column):
    return lax.psum_scatter(column, "z", scatter_dimension=0, tiled=True)


def finish_rounds(rounds):
    rounds.add_round(3)
    rounds.step([1, 2, 3, "small"])
    rounds.add_round(4)
    rounds.step([2, 4, "small"])
    (column,) = rounds.beside(joined([rounds.results[number] for number in range(3)]))
    early = over_z(column)
    rounds.step([3, "small"])
    rounds.step([3])
    (column,) = rounds.beside(joined([rounds.results[3]]))
    late = over_z(column)
    for unused in range(3):
        rounds.step([4])
    mine = jnp.concatenate([early, late, rounds.results[4]], axis=0)
    return jnp.concatenate([mine, swap(mine, "core")], axis=0)


def all_rounds(sums, tail):
    rounds = Rounds(sums, tail)
    for number in range(3):
        rounds.add_round(number)
    rounds.step([0, 1, 2])
    rounds.step([0, 1])
    rounds.step([0])
    return finish_rounds(rounds)


def edges(first_rows, last_rows, ranks):
    before = lax.ppermute(last_rows, "mp", [(r, r + 1) for r in range(ranks - 1)])
    behind = lax.ppermute(first_rows, "mp", [(r + 1, r) for r in range(ranks - 1)])
    return before, behind


def local(fast):
    def run(
        stream, cotangent, segments, owners, master, average, left_stats, right_stats, left_root,
        right_root, gains, kernel,
    ):
        ranks = lax.axis_size("mp")
        rank = lax.axis_index("mp")
        coords = (rank, lax.axis_index("x"), lax.axis_index("core"))
        rows = stream.shape[0]
        slot_dev = master.shape[1]
        chips = lax.axis_size("z") * lax.axis_size("x") * 2
        slots = slot_dev * chips
        segment_ids = segments[0]
        group = segment_ids.shape[0]
        unused, blocks = offsets(ranks)

        if fast:
            pair = jnp.concatenate([owners, swap(owners, "mp")])
            owners_all = jnp.where(rank == 0, pair, pair[::-1])
        else:
            owners_all = lax.all_gather(owners, "mp", axis=0, tiled=True)
        places = jnp.asarray(weight_places(ranks))
        if fast:
            table, arrivals, good = scatter_tables(owners_all, coords, slot_dev, blocks)
        else:
            table = (owners_all + jnp.arange(ranks)[:, None] * slots).reshape(-1)
            arrivals = jnp.arange(slot_dev, dtype=jnp.int32)

        slopes = 2.0 ** (-8.0 * (jnp.arange(HEADS).astype(f32) + 1.0) / HEADS)
        padded = jnp.pad(segment_ids, (HALO, HALO), constant_values=-1)
        wide_ids = jnp.pad(padded, (2, 2), constant_values=-2)
        tall = rows + 2 * HALO
        here = lax.dynamic_slice_in_dim(padded, rank * rows, tall)
        masks = jnp.stack(
            [
                (lax.dynamic_slice_in_dim(wide_ids, rank * rows + k, tall) == here).astype(f32)
                for k in range(KERNEL)
            ]
        )
        masks = jnp.broadcast_to(masks[:, :, None], (KERNEL, tall, 128))
        windows = key_windows(segment_ids, rank, rows)

        def gain(n):
            return gains[n : n + 1]

        starts = [offsets(ranks)[0][first] for first, unused in GROUPS] + [blocks]
        low = master[0].astype(bf16)
        if fast:
            across = 1 - rank
            core_at = coords[2]
            own_places = places[rank]
            all_places = places.reshape(-1)
            column = lax.all_gather(low, ("z", "x", "core"), axis=0, tiled=True)
            normed_own = norm_rows(stream, gain(0))
            normed_other = swap(normed_own, "mp")

            def own_part(group):
                here = slice(starts[group], starts[group + 1])
                return unsort(
                    column, owners[0, here], own_places[here], GROUP_CHUNKS[group], True
                )

            def outgoing(listed, first, count):
                half = count // 2
                return lax.dynamic_slice_in_dim(listed, first + core_at * half, half)

            def put(weights, one, two, group, first):
                base = across * blocks + starts[group] + first
                half = one.shape[0]
                return place_weights(
                    weights, [one, two],
                    [base + core_at * half, base + (1 - core_at) * half], all_places,
                )

            w_attn, list_attn = own_part(1)
            send_attn = outgoing(list_attn, 0, 96)

            def first_half():
                w_one, list_one = own_part(0)
                (product,) = ffn_half(normed_other, w_one, UP1, DOWN1, rank, False)
                return w_one, list_one, product

            w_one, list_one, product = first_half()
            (come_attn,), (w_one, list_one, product) = together(
                [(send_attn, "mp")], w_one, list_one, product
            )
            own_product, pre_first = ffn_half(normed_own, w_one, UP1, DOWN1, rank, True)
            w_conv, list_conv = own_part(2)
            w_two, list_two = own_part(3)
            (product, beside), (own_product, w_conv, list_conv, w_two, list_two) = together(
                [(product, "mp"), (come_attn, "core")], own_product, w_conv, list_conv, w_two,
                list_two,
            )
            after_first, normed_attn = join(stream, own_product, product, gain(1))
            w_attn = put(w_attn, come_attn, beside, 1, 0)

            queries = project(normed_attn, w_attn, QUERY, 1)
            keys = project(normed_attn, w_attn, KEY, 2, rank, 2)
            (other,), (queries, keys) = together([(normed_attn, "mp")], queries, keys)
            part_two = outgoing(list_two, 0, 64)
            list_rest = jnp.concatenate(
                [outgoing(list_attn, 96, 32), outgoing(list_conv, 0, 96)]
            )
            keys = project(other, w_attn, KEY, 2, across, 2, keys)
            attended, logs = attention_forward(
                queries, keys, segment_ids, rank, windows, slopes
            )
            (come_rest, come_two), (attended, logs) = together(
                [(list_rest, "mp"), (part_two, "mp")], attended, logs
            )
            (beside,), unused = together([(come_rest, "core")])
            w_attn = put(w_attn, come_rest[:16], beside[:16], 1, 96)
            w_conv = put(w_conv, come_rest[16:], beside[16:], 2, 0)
            after_attn = project_out(attended, w_attn, OUT, after_first)
            before, behind = edges(after_attn[:HALO], after_attn[-HALO:], ranks)
            rest_two, before, behind = tied(outgoing(list_two, 64, 192), before, behind)
            after_conv, linear, gate, normed_two = conv_forward(
                after_attn, before, behind, gain(2), gain(3), w_conv, kernel, masks
            )
            own_product, pre_second = ffn_half(normed_two, w_two, UP2, DOWN2, rank, True)
            (more_two, beside), (own_product, pre_second, w_two) = together(
                [(rest_two, "mp"), (come_two, "core")], own_product, pre_second, w_two
            )
            (more_beside,), unused = together([(more_two, "core")])
            send_one, more_two = tied(outgoing(list_one, 0, 256), more_two)
            w_two = put(w_two, come_two, beside, 3, 0)
            w_two = put(w_two, more_two, more_beside, 3, 64)
            product, pre_second = ffn_half(
                normed_two, w_two, UP2, DOWN2, across, True, pre_second
            )
            after_second, output = join(after_conv, own_product, product, gain(4))
            sources = [(normed_attn, rank), (other, across)]
        else:
            everything = lax.all_gather(low, ("mp", "z", "x", "core"), axis=0, tiled=True)
            slot_of = owners_all + jnp.arange(ranks)[:, None] * slots
            arrays = []
            for number, chunks in enumerate(GROUP_CHUNKS):
                here = slice(starts[number], starts[number + 1])
                arrays += unsort(
                    everything, slot_of[:, here].reshape(-1).astype(jnp.int32),
                    places[:, here].reshape(-1), chunks, False,
                )
            w_one, w_attn, w_conv, w_two = arrays
            after_first, pre_first, normed_attn = ffn_forward(
                stream, gain(0), gain(1), w_one, UP1, DOWN1
            )
            other = lax.all_gather(normed_attn, "mp", axis=0, tiled=True)
            queries = project(normed_attn, w_attn, QUERY, 1)
            keys = project(other, w_attn, KEY, 2)
            sources = [(other, 0)]
            attended, logs = attention_forward(
                queries, keys, segment_ids, rank, windows, slopes
            )
            after_attn = project_out(attended, w_attn, OUT, after_first)
            before, behind = edges(after_attn[:HALO], after_attn[-HALO:], ranks)
            after_conv, linear, gate, normed_two = conv_forward(
                after_attn, before, behind, gain(2), gain(3), w_conv, kernel, masks
            )
            after_second, pre_second, output = ffn_forward(
                after_conv, gain(3), gain(4), w_two, UP2, DOWN2
            )

        if fast:
            last = 32 * ROUNDS[LARGE]
            sums = ((ranks * slots - last, BLOCK, BLOCK), (last, BLOCK, BLOCK))
        else:
            sums = ((ranks * slots, BLOCK, BLOCK),)
            if slots > blocks:
                sums = (jnp.zeros(sums[0], bf16),)
        grad_conv, gains_a, *sums = ffn_backward(
            after_second, gain(4), [cotangent], None, after_conv, gain(3), pre_second, w_two,
            UP2, DOWN2, sums, table, ranks,
        )
        if fast:
            (come_one,), (grad_conv, gains_a, *sums) = together(
                [(send_one, "mp")], grad_conv, gains_a, *sums
            )
            rounds = Rounds(*sums)
            rounds.add_round(0)
            sums = rounds.hold()
        before, behind = edges(
            grad_conv[:HALO].astype(bf16), grad_conv[-HALO:].astype(bf16), ranks
        )
        grad_attn, gains_b, tap_grads, *sums = conv_backward(
            grad_conv, before, behind, after_attn, gain(2), linear, gate, w_conv, kernel, masks,
            sums, table, ranks,
        )
        if fast:
            grad_attn, gains_b, tap_grads = rounds.step(
                [0], grad_attn, gains_b, tap_grads, sums=sums
            )
            rounds.add_round(1)
            sums = rounds.hold()
        mixed_grad, *sums = project_out_back(
            grad_attn, w_attn, OUT, attended, sums, table, ranks
        )
        query_grad, key_grad, value_grad = attention_backward(
            queries, keys, segment_ids, rank, windows, slopes, logs, mixed_grad, attended
        )
        if fast:
            rounds.add("core", one_swap(come_one, "core"))
            query_grad, key_grad, value_grad = rounds.step(
                [0, 1, "core"], query_grad, key_grad, value_grad, sums=sums
            )
            sums = rounds.hold()
            away = input_gradient(key_grad, value_grad, w_attn, 1 - rank, rows)
        else:
            away = input_gradient(key_grad, value_grad, w_attn, jnp.zeros((), jnp.int32), group)
            arrived = lax.psum_scatter(away, "mp", scatter_dimension=0, tiled=True)
        near, *sums = projections_back(
            normed_attn, query_grad, key_grad, value_grad, sources, fast, w_attn, sums, table, ranks
        )
        if fast:
            w_one = put(w_one, come_one, rounds.results.pop("core"), 0, 0)
            (arrived,), (near, w_one, *sums) = together([(away, "mp")], near, w_one, *sums)
            rounds.sums, rounds.tail = sums
            rounds.add_round(2)
            sums = rounds.hold()
        stream_grad, gains_c, *sums = ffn_backward(
            after_first, gain(1), [near, arrived], grad_attn, stream, gain(0), pre_first, w_one,
            UP1, DOWN1, sums, table, ranks, rank if fast else None,
        )
        if fast:
            stream_grad, gains_c = rounds.step([0, 1, 2], stream_grad, gains_c, sums=sums)
        small = jnp.concatenate(
            [gains_c[1:2], gains_c[0:1], gains_b, gains_a[1:2], gains_a[0:1], tap_grads]
        )
        everywhere = ("mp", "z", "x", "core")
        if fast:
            rounds.add("small", total_steps(small))
            sums = (rounds.sums, rounds.tail)
            own_grads = finish_rounds(rounds)
            small = rounds.results["small"]
            own_grads = lax.cond(
                good,
                lambda sums, tail, own: own,
                lambda sums, tail, own: all_rounds(sums, tail),
                *sums,
                own_grads,
            )
        else:
            own_grads = lax.psum_scatter(sums[0], everywhere, scatter_dimension=0, tiled=True)
            small = lax.psum(small, everywhere)
        gain_grads, kernel_grads = small[:5], small[5:]
        block_grads, left_new, right_new, master_new, average_new = shampoo(
            own_grads, arrivals, left_stats[0], right_stats[0], left_root[0], right_root[0], master[0],
            average[0],
        )
        return (
            output,
            stream_grad,
            block_grads[None],
            left_new[None],
            right_new[None],
            master_new[None],
            average_new[None],
            gain_grads,
            vector_step(gains, gain_grads),
            kernel_grads,
            vector_step(kernel, kernel_grads),
        )

    return run


def solution(mesh):
    ranks, pieces = mesh.shape["mp"], mesh.shape["dp"]
    fast = ranks == 2 and pieces == 16
    xs = 2 if fast else 1
    grid = Mesh(
        np.asarray(mesh.devices).reshape(ranks, pieces // (2 * xs), xs, 2), ("mp", "z", "x", "core")
    )
    dp = ("z", "x", "core")
    rows = P((*dp, "mp"), None)
    slots = P("mp", dp, None, None)
    return jax.shard_map(
        local(fast),
        mesh=grid,
        in_specs=(
            rows, rows, P(dp, None), P("mp", None), slots, slots, slots, slots, slots, slots, P(),
            P(),
        ),
        out_specs=(rows, rows, slots, slots, slots, slots, slots, P(), P(), P(), P()),
        check_vma=False,
    )
```

time: 2940 us -> 1110 us (0.38)
  Pallas kernels: 2050 us -> 544 us
  blocking collectives: 201 us -> 0 us
  waiting for transfers between devices: 461 us -> 324 us
  local copies, waits for them, and re-layouts: 109 us -> 64 us
  other arithmetic: 37.7 us -> 69.6 us
    pallas_call x15 -> x23, Pallas kernels: 1620 us -> 225 us  [the longest x4 64.8 us: ffn_half(): pl.pallas_call(body, grid_spec=pltpu.PrefetchScalarGridSpec(num_scalar_pr...]
    ppermute x74 -> x54, waiting for transfers between devices: 429 us -> 201 us  [swap(): return lax.ppermute(value, axis, pairs)]
    all_gather x9 -> x0, blocking collectives: 153 us -> none  [the longest x8 149 us: gather_weights(): column = lax.all_gather(own[first:first + count], 'z', axis=0, tiled=True)]
    all_gather x0 -> x1, waiting for transfers between devices: none -> 117 us  [run(): column = lax.all_gather(low, ('z', 'x', 'core'), axis=0, tiled=True)]
    pallas_call x1, Pallas kernels: 114 us -> 49.8 us  [attention_forward(): pl.pallas_call(body, grid=(HEADS, rows // tall), out_shape=(jax.ShapeDtyp...]
    pallas_call x1, Pallas kernels: 116 us -> 60.8 us  [attention_backward(): pl.pallas_call(body, grid=(HEADS, rows // tall), out_shape=(jax.ShapeDtyp...]
    psum x1 -> x0, blocking collectives: 47.9 us -> none  [total(): return lax.psum(values, ('mp', 'z', 'x', 'core'))]
    slice x23 -> x13, local copies, waits for them, and re-layouts: 61.7 us -> 26.9 us  [the longest x4 17.5 us: add_round(): send = self.tail if number == LARGE else self.sums[offset:offset + size]]
  transfers between devices with their start and end apart: 94 -> 61, of which waited for: 26 -> 27; matrix products, arithmetic and copies ran while one was open for 4% -> 7% of each run, Pallas kernels for 45% -> 46%
where the time goes in v2:
time: 1110 us; the launch traced here: 1100 us
  Pallas kernels  544 us (49%)
  waiting for transfers between devices  324 us (29%)
  starting transfers between devices  76.4 us (7%)
  other arithmetic  69.6 us (6%)
  local copies, waits for them, and re-layouts  64 us (6%)
  between operations  17.4 us (2%)
    ppermute x54, waiting for transfers between devices, swap(): return lax.ppermute(value, axis, pairs)  201 us
    pallas_call x2, Pallas kernels, ffn_backward(): pl.pallas_call(body, grid=(steps,), out_shape=(jax.ShapeDtypeStruct((rows...  128 us
    all_gather x1, waiting for transfers between devices, run(): column = lax.all_gather(low, ('z', 'x', 'core'), axis=0, tiled=True)  117 us
    ppermute x54, starting transfers between devices, swap(): return lax.ppermute(value, axis, pairs)  67.6 us
    pallas_call x4, Pallas kernels, ffn_half(): pl.pallas_call(body, grid_spec=pltpu.PrefetchScalarGridSpec(num_scalar_pr...  64.8 us
    pallas_call x1, Pallas kernels, attention_backward(): pl.pallas_call(body, grid=(HEADS, rows // tall), out_shape=(jax.ShapeDtyp...  60.8 us
    pallas_call x1, Pallas kernels, attention_forward(): pl.pallas_call(body, grid=(HEADS, rows // tall), out_shape=(jax.ShapeDtyp...  49.8 us
    convert_element_type x15, other arithmetic, added(): return sum((term.astype(f32) for term in terms)).astype(bf16)  47.9 us
  transfers between devices with their start and end apart: 61, of which 27 were waited for; matrix products, arithmetic and copies ran while one was open for 7% of the time, Pallas kernels for 46%

profile of v2, /device:TPU:0, one launch (start us, length us, event | category | flops | bytes accessed | tf_op | source)
XLA Modules:
  0.0 1096.9 jit_solution(16027072758167795974)
XLA Ops:
  7.2 3.2 bitcast_convert_fusion
  11.2 4.4 norm_rows.1.x_ref
  19.7 117.3 %all-gather.2.cloned.1.call-done.slots_ref = bf16[736,128,128]{2,1,0:T(8,128)(2,1)} async-done(((bf16[46,128,128]{2,1,0:T(8,128)(2,1)}), bf16[736,128,128]{2,1,0:T(8,128)(2,1)}) %all-gather.2.cloned.1.call-update) | async-done | bytes 24117264 | tf_op jit(solution)/shard_map/all_gather | solution.py:1684
  137.0 6.3 unsort.4
  148.8 11.6 %unsort.5 = (bf16[8192,1024]{1,0:T(8,128)(2,1)}, bf16[256,128,128]{2,1,0:T(8,128)(2,1)}) custom-call(s32[256]{0:T(256)} %bitcast.166, s32[256]{0:T(256)} %bitcast.164, bf16[736,128,128]{2,1,0:T(8,128)(2,1)} %all-gather.2.cloned.1.call-done.slots_ref), custom_call_target="tpu_custom_call" | custom-call | bytes 25165824 | tf_op jit(solution)/shard_map/unsort/pallas_call | solution.py:182
  161.7 15.4 %ffn_half.4 = bf16[1024,1024]{1,0:T(8,128)(2,1)} custom-call(s32[1]{0:T(128)} %bitcast.25.part_ref.rank_ref.refs_10_, bf16[1024,1024]{1,0:T(8,128)(2,1)} %copy-done.16, bf16[8192,1024]{1,0:T(8,128)(2,1)} %get-tuple-element.311.up_ref.down_ref.rest_2_, bf16[8192,1024]{1,0:T(8,128)(2,1)} %get-tuple-element.311.up_ref.down_ref.rest_2_), custom_call_target="tpu_custom_call" | custom-call | flops 8589934592 | bytes 8388608 | tf_op jit(solution)/shard_map/ffn_half/pallas_call | solution.py:445
  177.2 5.7 collective-permute-done.32.rest_0_
  185.5 5.5 unsort.6
  191.0 11.6 %unsort.7 = (bf16[8192,1024]{1,0:T(8,128)(2,1)}, bf16[256,128,128]{2,1,0:T(8,128)(2,1)}) custom-call(s32[256]{0:T(256)} %bitcast.165, s32[256]{0:T(256)} %bitcast.163, bf16[736,128,128]{2,1,0:T(8,128)(2,1)} %all-gather.2.cloned.1.call-done.slots_ref), custom_call_target="tpu_custom_call" | custom-call | bytes 25165824 | tf_op jit(solution)/shard_map/unsort/pallas_call | solution.py:182
  203.7 16.5 %ffn_half.5 = (bf16[1024,1024]{1,0:T(8,128)(2,1)}, bf16[1024,4096]{1,0:T(8,128)(2,1)}) custom-call(s32[1]{0:T(128)} %bitcast.25.part_ref.rank_ref.refs_10_, bf16[1024,1024]{1,0:T(8,128)(2,1)} %norm_rows.1.x_ref, bf16[8192,1024]{1,0:T(8,128)(2,1)} %get-tuple-element.311.up_ref.down_ref.rest_2_, bf16[8192,1024]{1,0:T(8,128)(2,1)} %get-tuple-element.311.up_ref.down_ref.rest_2_), custom_call_target="tpu_custom_call" | custom-call | flops 8589934592 | bytes 8388608 | tf_op jit(solution)/shard_map/ffn_half/pallas_call | solution.py:445
  220.1 9.9 collective-permute-done.34.other_ref
  231.4 6.1 join.2
  251.0 3.8 place_weights.6.w_ref.rest_2_
  254.8 5.9 project.3.q_ref
  260.7 8.4 project.4.rest_0_
  269.1 17.2 %collective-permute-done.38.x_ref.refs_1_ = bf16[1024,1024]{1,0:T(8,128)(2,1)S(1)} collective-permute-done((bf16[1024,1024]{1,0:T(8,128)(2,1)}, bf16[1024,1024]{1,0:T(8,128)(2,1)S(1)}, u32[]{:S(2)}, u32[]{:S(2)}) %collective-permute-start.38) | collective-permute-done | bytes 2097184 | tf_op jit(solution)/shard_map/ppermute | solution.py:252
  287.6 8.3 project.5.key_ref.value_ref
  295.9 49.8 %attention_forward.1 = (bf16[1024,1024]{1,0:T(8,128)(2,1)}, f32[8,1,1024]{2,1,0:T(1,128)}) custom-call(s32[1]{0:T(128)} %bitcast.25.part_ref.rank_ref.refs_10_, s32[4]{0:T(128)} %reshape.314.window_ref, f32[8]{0:T(128)} %multiply_power_fusion.slope_ref, bf16[1024,1024]{1,0:T(8,128)(2,1)} %project.3.q_ref, s32[1024,1]{1,0:T(8,128)} %copy.51.own_ref, ...), custom_call_target="tpu_custom_call" | custom-call | tf_op jit(solution)/shard_map/attention_forward/pallas_call | solution.py:987
  345.8 5.4 collective-permute-done.37.rest_0_
  358.8 7.3 project_out.1.x_ref
  367.0 3.4 collective-permute-start.40
  371.7 4.0 constant_dynamic-slice_fusion.14
  383.4 3.8 place_weights.8.value_ref.gate_ref.out_w_ref.gate_w_ref
  389.3 20.3 %conv_forward.1 = (f32[1024,1024]{1,0:T(8,128)}, bf16[1056,1024]{1,0:T(8,128)(2,1)}, bf16[1056,1024]{1,0:T(8,128)(2,1)}, bf16[1024,1024]{1,0:T(8,128)(2,1)}) custom-call(f32[1024,1024]{1,0:T(8,128)} %project_out.1.x_ref, f32[16,1024]{1,0:T(8,128)} %copy-done.38, f32[16,1024]{1,0:T(8,128)} %copy-done.39, f32[1,1024]{1,0:T(1,128)} %get-tuple-element.627.gain_ref, ...), custom_call_target="tpu_custom_call" | custom-call | flops 6442450944 | bytes 18874368 | tf_op jit(solution)/shard_map/conv_forward/pallas_call | solution.py:1142
  409.5 16.5 %ffn_half.6 = (bf16[1024,1024]{1,0:T(8,128)(2,1)}, bf16[1024,4096]{1,0:T(8,128)(2,1)}) custom-call(s32[1]{0:T(128)} %bitcast.25.part_ref.rank_ref.refs_10_, bf16[1024,1024]{1,0:T(8,128)(2,1)} %get-tuple-element.342.x_ref, bf16[8192,1024]{1,0:T(8,128)(2,1)} %get-tuple-element.351.up_ref.down_ref.rest_2_, ...), custom_call_target="tpu_custom_call" | custom-call | flops 8589934592 | bytes 8388608 | tf_op jit(solution)/shard_map/ffn_half/pallas_call | solution.py:445
  426.0 20.5 %collective-permute-done.42.rest_0_ = bf16[96,128,128]{2,1,0:T(8,128)(2,1)S(1)} collective-permute-done((bf16[96,128,128]{2,1,0:T(8,128)(2,1)}, bf16[96,128,128]{2,1,0:T(8,128)(2,1)S(1)}, u32[]{:S(2)}, u32[]{:S(2)}) %collective-permute-start.42) | collective-permute-done | bytes 3145760 | tf_op jit(solution)/shard_map/ppermute | solution.py:252
  453.8 4.8 constant_dynamic-slice_fusion.13
  464.1 5.8 place_weights.10.up_ref.down_ref.refs_5_.refs_6_
  469.9 16.4 %ffn_half.7 = (bf16[1024,1024]{1,0:T(8,128)(2,1)}, bf16[1024,4096]{1,0:T(8,128)(2,1)}) custom-call(s32[1]{0:T(128)} %bitcast.36.part_ref, bf16[1024,1024]{1,0:T(8,128)(2,1)} %get-tuple-element.342.x_ref, bf16[8192,1024]{1,0:T(8,128)(2,1)} %place_weights.10.up_ref.down_ref.refs_5_.refs_6_, ...), custom_call_target="tpu_custom_call", output_to_operand_aliasing={{1}: (4, {})} | custom-call | flops 8589934592 | bytes 8388608 | tf_op jit(solution)/shard_map/ffn_half/pallas_call | solution.py:445
  486.3 6.4 join.3
  492.7 60.0 %ffn_backward.2 = (f32[1024,1024]{1,0:T(8,128)}, f32[2,1024]{1,0:T(2,128)}, bf16[1184,128,128]{2,1,0:T(8,128)(2,1)}, bf16[288,128,128]{2,1,0:T(8,128)(2,1)}) custom-call(s32[1472]{0:T(1024)} %reshape.318.table_ref, f32[1024,1024]{1,0:T(8,128)} %get-tuple-element.356.refs_0_, f32[1,1024]{1,0:T(1,128)} %get-tuple-element.625.gain_ref.refs_1_, ...), custom_call_target="tpu_custom_call" | custom-call | flops 34359738368 | bytes 41943040 | tf_op jit(solution)/shard_map/ffn_backward/pallas_call | solution.py:616
  552.7 4.9 slice.635
  562.1 4.2 collective-permute-done.49.behind_ref
  566.9 43.2 %conv_backward.1 = (f32[1024,1024]{1,0:T(8,128)}, f32[1,1024]{1,0:T(1,128)}, f32[5,1024]{1,0:T(8,128)}, bf16[1184,128,128]{2,1,0:T(8,128)(2,1)}, bf16[288,128,128]{2,1,0:T(8,128)(2,1)}) custom-call(s32[1472]{0:T(1024)} %reshape.318.table_ref, f32[1024,1024]{1,0:T(8,128)} %get-tuple-element.364.g_ref, ...), custom_call_target="tpu_custom_call", output_to_operand_aliasing={{3}: (13, {}), {4}: (14, {})} | custom-call | flops 12884901888 | bytes 29360128 | tf_op jit(solution)/shard_map/conv_backward/pallas_call | solution.py:1325
  610.1 5.5 slice.642
  615.6 4.0 add_convert_fusion.38
  623.2 10.0 project_out_back.1
  633.2 60.8 %attention_backward.1 = (bf16[1024,1024]{1,0:T(8,128)(2,1)}, bf16[2048,1024]{1,0:T(8,128)(2,1)}, bf16[2048,1024]{1,0:T(8,128)(2,1)}) custom-call(s32[1]{0:T(128)} %bitcast.25.part_ref.rank_ref.refs_10_, s32[4]{0:T(128)} %reshape.314.window_ref, f32[8]{0:T(128)} %multiply_power_fusion.slope_ref, bf16[1024,1024]{1,0:T(8,128)(2,1)} %project.3.q_ref, ...), custom_call_target="tpu_custom_call" | custom-call | tf_op jit(solution)/shard_map/attention_backward/pallas_call | solution.py:1070
  694.1 9.8 input_gradient.1
  706.9 3.5 add_convert_fusion.50
  710.4 7.3 place_weights.11.refs_7_.refs_8_
  717.7 33.0 %projections_back.1 = (f32[1024,1024]{1,0:T(8,128)}, bf16[1184,128,128]{2,1,0:T(8,128)(2,1)}, bf16[288,128,128]{2,1,0:T(8,128)(2,1)}) custom-call(s32[2]{0:T(128)} %get-tuple-element.666.part_ref, s32[1472]{0:T(1024)} %reshape.318.table_ref, ...), custom_call_target="tpu_custom_call", output_to_operand_aliasing={{1}: (11, {}), {2}: (12, {})} | custom-call | flops 17179869184 | bytes 31457280 | tf_op jit(solution)/shard_map/projections_back/pallas_call | solution.py:898
  752.1 4.9 slice.653
  761.2 67.6 %ffn_backward.3 = (f32[1024,1024]{1,0:T(8,128)}, f32[2,1024]{1,0:T(2,128)}, bf16[1184,128,128]{2,1,0:T(8,128)(2,1)}, bf16[288,128,128]{2,1,0:T(8,128)(2,1)}) custom-call(s32[1472]{0:T(1024)} %reshape.318.table_ref, f32[1024,1024]{1,0:T(8,128)} %get-tuple-element.333.s_ref.refs_0_, ...), custom_call_target="tpu_custom_call", output_to_operand_aliasing={{2}: (12, {}), {3}: (13, {})} | custom-call | flops 34359738368 | bytes 41943040 | tf_op jit(solution)/shard_map/ffn_backward/pallas_call | solution.py:616
  829.6 4.3 add_convert_fusion.36
  840.3 10.7 collective-permute-done.65
  851.2 12.6 %collective-permute-done.66 = f32[10,1024]{1,0:T(8,128)S(1)} collective-permute-done((f32[10,1024]{1,0:T(8,128)S(1)}, f32[10,1024]{1,0:T(8,128)S(1)}, u32[]{:S(2)}, u32[]{:S(2)}) %collective-permute-start.66) | collective-permute-done | bytes 40992 | tf_op jit(solution)/shard_map/ppermute | solution.py:252
  868.4 5.9 collective-permute-done.60
  883.9 5.6 add_convert_fusion.30
  889.5 4.8 collective-permute-done.71
  899.4 4.4 add_convert_fusion.40
  903.9 4.7 add_convert_fusion.44
  918.7 44.6 %collective-permute-done.74 = bf16[72,128,128]{2,1,0:T(8,128)(2,1)S(1)} collective-permute-done((bf16[72,128,128]{2,1,0:T(8,128)(2,1)}, bf16[72,128,128]{2,1,0:T(8,128)(2,1)S(1)}, u32[]{:S(2)}, u32[]{:S(2)}) %collective-permute-start.74) | collective-permute-done | bytes 2359328 | tf_op jit(solution)/shard_map/ppermute | solution.py:252
  963.8 3.7 add_convert_fusion.34
  970.1 23.5 %collective-permute-done.77 = bf16[36,128,128]{2,1,0:T(8,128)(2,1)S(1)} collective-permute-done((bf16[36,128,128]{2,1,0:T(8,128)(2,1)S(1)}, bf16[36,128,128]{2,1,0:T(8,128)(2,1)S(1)}, u32[]{:S(2)}, u32[]{:S(2)}) %collective-permute-start.77) | collective-permute-done | bytes 1179680 | tf_op jit(solution)/shard_map/ppermute | solution.py:252
  994.3 4.3 add_convert_fusion.33
  1003.4 14.2 %collective-permute-done.79 = bf16[24,128,128]{2,1,0:T(8,128)(2,1)S(1)} collective-permute-done((bf16[24,128,128]{2,1,0:T(8,128)(2,1)S(1)}, bf16[24,128,128]{2,1,0:T(8,128)(2,1)S(1)}, u32[]{:S(2)}, u32[]{:S(2)}) %collective-permute-start.79) | collective-permute-done | bytes 786464 | tf_op jit(solution)/shard_map/ppermute | solution.py:252
  1022.4 4.9 collective-permute-done.81
  1030.7 4.4 collective-permute-start.83
  1036.5 3.5 collective-permute-start.85
  1041.3 7.5 collective-permute-start.87
  1050.3 7.3 collective-permute-done.84
  1057.7 4.9 collective-permute-done.88
  1073.4 16.6 %shampoo.1 = (f32[46,128,128]{2,1,0:T(8,128)}, f32[46,128,128]{2,1,0:T(8,128)}, f32[46,128,128]{2,1,0:T(8,128)}, f32[46,128,128]{2,1,0:T(8,128)}, f32[46,128,128]{2,1,0:T(8,128)}) custom-call(s32[48]{0:T(128)} %pad.14.index_ref, bf16[92,128,128]{2,1,0:T(8,128)(2,1)S(1)} %get-tuple-element.668.refs_0_.refs_1_.refs_2_.refs_3_.refs_4_.refs_5_.refs_6_.refs_7_, ...), custom_call_target="tpu_custom_call" | custom-call | tf_op jit(solution)/shard_map/shampoo/pallas_call | solution.py:1410
  (313 shorter events, 146.8 us)
Async XLA Ops:
  7.2 129.8 %all-gather.2.cloned.1.call-start = ((), (), s32[]{:S(2)}) async-start(), calls=%async_computation.6 | async-start | bytes 25624576 | tf_op jit(solution)/shard_map/all_gather | solution.py:1684
  10.5 1052.3 %reduce-scatter.9.cloned.1.call-start = ((), (), s32[]{:S(2)}) async-start(), calls=%async_computation.7 | async-start | bytes 3604480 | tf_op jit(solution)/shard_map/reduce_scatter | solution.py:1596
  15.6 144.8 %collective-permute-start.33 = (bf16[1024,1024]{1,0:T(8,128)(2,1)}, bf16[1024,1024]{1,0:T(8,128)(2,1)S(1)}, u32[]{:S(2)}, u32[]{:S(2)}) collective-permute-start(bf16[1024,1024]{1,0:T(8,128)(2,1)} %norm_rows.1.x_ref), channel_id=1, source_target_pairs={{0,16},{16,0},{1,17},{17,1},{2,18},{18,2},{3,19},{19,3},{4,20},{20... | collective-permute-start | bytes 6291464 | tf_op jit(solution)/shard_map/ppermute | solution.py:252
  146.0 36.9 %collective-permute-start.32 = (bf16[48,128,128]{2,1,0:T(8,128)(2,1)}, bf16[48,128,128]{2,1,0:T(8,128)(2,1)}, u32[]{:S(2)}, u32[]{:S(2)}) collective-permute-start(bf16[48,128,128]{2,1,0:T(8,128)(2,1)} %constant_dynamic-slice_fusion.18), channel_id=1, source_target_pairs={{0,16},{16,0},{1,17},{17,1},{2,18},{18,2},{3,19},{19,3},{4,20},{20... | collective-permute-start | bytes 4718600 | tf_op jit(solution)/shard_map/ppermute | solution.py:252
  182.9 47.2 %collective-permute-start.34 = (bf16[1024,1024]{1,0:T(8,128)(2,1)}, bf16[1024,1024]{1,0:T(8,128)(2,1)S(1)}, u32[]{:S(2)}, u32[]{:S(2)}) collective-permute-start(bf16[1024,1024]{1,0:T(8,128)(2,1)} %ffn_half.4), channel_id=1, source_target_pairs={{0,16},{16,0},{1,17},{17,1},{2,18},{18,2},{3,19},{19,3},{4,20},{20... | collective-permute-start | bytes 6291464 | tf_op jit(solution)/shard_map/ppermute | solution.py:252
  184.4 35.8 %collective-permute-start.35 = (bf16[48,128,128]{2,1,0:T(8,128)(2,1)}, bf16[48,128,128]{2,1,0:T(8,128)(2,1)}, u32[]{:S(2)}, u32[]{:S(2)}) collective-permute-start(bf16[48,128,128]{2,1,0:T(8,128)(2,1)} %collective-permute-done.32.rest_0_), channel_id=1, source_target_pairs={{0,1},{1,0},{2,3},{3,2},{4,5},{5,4},{6,7},{7,6},{8,9},{9,8},{10,11... | collective-permute-start | bytes 4718600 | tf_op jit(solution)/shard_map/ppermute | solution.py:252
  237.5 48.8 %collective-permute-start.38 = (bf16[1024,1024]{1,0:T(8,128)(2,1)}, bf16[1024,1024]{1,0:T(8,128)(2,1)S(1)}, u32[]{:S(2)}, u32[]{:S(2)}) collective-permute-start(bf16[1024,1024]{1,0:T(8,128)(2,1)} %get-tuple-element.323.x_ref.n_ref.refs_0_), channel_id=1, source_target_pairs={{0,16},{16,0},{1,17},{17,1},{2,18},{18,2},{3,19},{19,3},{4,20},{20... | collective-permute-start | bytes 6291464 | tf_op jit(solution)/shard_map/ppermute | solution.py:252
  244.3 106.9 %collective-permute-start.36 = (bf16[64,128,128]{2,1,0:T(8,128)(2,1)}, bf16[64,128,128]{2,1,0:T(8,128)(2,1)}, u32[]{:S(2)}, u32[]{:S(2)}) collective-permute-start(bf16[64,128,128]{2,1,0:T(8,128)(2,1)} %pad_maximum_fusion.5), channel_id=1, source_target_pairs={{0,16},{16,0},{1,17},{17,1},{2,18},{18,2},{3,19},{19,3},{4,20},{20... | collective-permute-start | bytes 6291464 | tf_op jit(solution)/shard_map/ppermute | solution.py:252
  247.2 104.1 %collective-permute-start.37 = (bf16[32,128,128]{2,1,0:T(8,128)(2,1)}, bf16[32,128,128]{2,1,0:T(8,128)(2,1)S(1)}, u32[]{:S(2)}, u32[]{:S(2)}) collective-permute-start(bf16[32,128,128]{2,1,0:T(8,128)(2,1)} %constant_dynamic-slice_fusion.16), channel_id=1, source_target_pairs={{0,16},{16,0},{1,17},{17,1},{2,18},{18,2},{3,19},{19,3},{4,20},{20... | collective-permute-start | bytes 3145736 | tf_op jit(solution)/shard_map/ppermute | solution.py:252
  351.2 4.4 collective-permute-start.39
  367.0 8.7 collective-permute-start.40
  370.4 6.2 collective-permute-start.41
  376.5 70.0 %collective-permute-start.42 = (bf16[96,128,128]{2,1,0:T(8,128)(2,1)}, bf16[96,128,128]{2,1,0:T(8,128)(2,1)S(1)}, u32[]{:S(2)}, u32[]{:S(2)}) collective-permute-start(bf16[96,128,128]{2,1,0:T(8,128)(2,1)} %constant_dynamic-slice_fusion.14), channel_id=1, source_target_pairs={{0,16},{16,0},{1,17},{17,1},{2,18},{18,2},{3,19},{19,3},{4,20},{20... | collective-permute-start | bytes 9437192 | tf_op jit(solution)/shard_map/ppermute | solution.py:252
  387.2 38.8 %collective-permute-start.43 = (bf16[32,128,128]{2,1,0:T(8,128)(2,1)S(1)}, bf16[32,128,128]{2,1,0:T(8,128)(2,1)S(1)}, u32[]{:S(2)}, u32[]{:S(2)}) collective-permute-start(bf16[32,128,128]{2,1,0:T(8,128)(2,1)S(1)} %copy-done.21), channel_id=1, source_target_pairs={{0,1},{1,0},{2,3},{3,2},{4,5},{5,4},{6,7},{7,6},{8,9},{9,8},{10,11... | collective-permute-start | bytes 3145736 | tf_op jit(solution)/shard_map/ppermute | solution.py:252
  426.0 20.5 %copy-start.22 = (bf16[32,128,128]{2,1,0:T(8,128)(2,1)}, bf16[32,128,128]{2,1,0:T(8,128)(2,1)S(1)}, u32[]{:S(2)}) copy-start(bf16[32,128,128]{2,1,0:T(8,128)(2,1)S(1)} %collective-permute-done.43.rest_1_) | copy-start | bytes 3145732
  446.5 17.6 %collective-permute-start.44 = (bf16[96,128,128]{2,1,0:T(8,128)(2,1)S(1)}, bf16[96,128,128]{2,1,0:T(8,128)(2,1)}, u32[]{:S(2)}, u32[]{:S(2)}) collective-permute-start(bf16[96,128,128]{2,1,0:T(8,128)(2,1)S(1)} %collective-permute-done.42.rest_0_), channel_id=1, source_target_pairs={{0,1},{1,0},{2,3},{3,2},{4,5},{5,4},{6,7},{7,6},{8,9},{9,8},{10,11... | collective-permute-start | bytes 9437192 | tf_op jit(solution)/shard_map/ppermute | solution.py:252
  446.5 4.1 collective-permute-start.46
  458.7 94.0 %collective-permute-start.45 = (bf16[128,128,128]{2,1,0:T(8,128)(2,1)}, bf16[128,128,128]{2,1,0:T(8,128)(2,1)}, u32[]{:S(2)}, u32[]{:S(2)}) collective-permute-start(bf16[128,128,128]{2,1,0:T(8,128)(2,1)} %constant_dynamic-slice_fusion.13), channel_id=1, source_target_pairs={{0,16},{16,0},{1,17},{17,1},{2,18},{18,2},{3,19},{19,3},{4,20},{20... | collective-permute-start | bytes 12582920 | tf_op jit(solution)/shard_map/ppermute | solution.py:252
  557.6 52.5 %collective-permute-start.47 = (bf16[128,128,128]{2,1,0:T(8,128)(2,1)}, bf16[128,128,128]{2,1,0:T(8,128)(2,1)S(1)}, u32[]{:S(2)}, u32[]{:S(2)}) collective-permute-start(bf16[128,128,128]{2,1,0:T(8,128)(2,1)} %slice.635), channel_id=1, source_target_pairs={{0,1},{1,0},{2,3},{3,2},{4,5},{5,4},{6,7},{7,6},{8,9},{9,8},{10,11... | collective-permute-start | bytes 12582920 | tf_op jit(solution)/shard_map/ppermute | solution.py:252
  557.9 4.2 collective-permute-start.48
  560.5 5.8 collective-permute-start.49
  619.6 74.5 %collective-permute-start.53 = (bf16[128,128,128]{2,1,0:T(8,128)(2,1)}, bf16[128,128,128]{2,1,0:T(8,128)(2,1)}, u32[]{:S(2)}, u32[]{:S(2)}) collective-permute-start(bf16[128,128,128]{2,1,0:T(8,128)(2,1)} %collective-permute-done.45.rest_0_), channel_id=1, source_target_pairs={{0,1},{1,0},{2,3},{3,2},{4,5},{5,4},{6,7},{7,6},{8,9},{9,8},{10,11... | collective-permute-start | bytes 12582920 | tf_op jit(solution)/shard_map/ppermute | solution.py:252
  619.6 74.5 %collective-permute-start.52 = (bf16[96,128,128]{2,1,0:T(8,128)(2,1)}, bf16[96,128,128]{2,1,0:T(8,128)(2,1)S(1)}, u32[]{:S(2)}, u32[]{:S(2)}) collective-permute-start(bf16[96,128,128]{2,1,0:T(8,128)(2,1)} %slice.642), channel_id=1, source_target_pairs={{0,1},{1,0},{2,3},{3,2},{4,5},{5,4},{6,7},{7,6},{8,9},{9,8},{10,11... | collective-permute-start | bytes 9437192 | tf_op jit(solution)/shard_map/ppermute | solution.py:252
  620.1 73.9 %collective-permute-start.50 = (bf16[32,128,128]{2,1,0:T(8,128)(2,1)}, bf16[32,128,128]{2,1,0:T(8,128)(2,1)}, u32[]{:S(2)}, u32[]{:S(2)}) collective-permute-start(bf16[32,128,128]{2,1,0:T(8,128)(2,1)} %get-tuple-element.380), channel_id=1, source_target_pairs={{0,2},{2,0},{1,3},{3,1},{4,6},{6,4},{5,7},{7,5},{8,10},{10,8},{9,1... | collective-permute-start | bytes 3145736 | tf_op jit(solution)/shard_map/ppermute | solution.py:252
  621.3 72.7 %collective-permute-start.51 = (bf16[32,128,128]{2,1,0:T(8,128)(2,1)}, bf16[32,128,128]{2,1,0:T(8,128)(2,1)}, u32[]{:S(2)}, u32[]{:S(2)}) collective-permute-start(bf16[32,128,128]{2,1,0:T(8,128)(2,1)} %get-tuple-element.381), channel_id=1, source_target_pairs={{0,16},{16,0},{1,17},{17,1},{2,18},{18,2},{3,19},{19,3},{4,20},{20... | collective-permute-start | bytes 3145736 | tf_op jit(solution)/shard_map/ppermute | solution.py:252
  703.8 47.0 %collective-permute-start.54 = (bf16[1024,1024]{1,0:T(8,128)(2,1)}, bf16[1024,1024]{1,0:T(8,128)(2,1)S(1)}, u32[]{:S(2)}, u32[]{:S(2)}) collective-permute-start(bf16[1024,1024]{1,0:T(8,128)(2,1)} %input_gradient.1), channel_id=1, source_target_pairs={{0,16},{16,0},{1,17},{17,1},{2,18},{18,2},{3,19},{19,3},{4,20},{20... | collective-permute-start | bytes 6291464 | tf_op jit(solution)/shard_map/ppermute | solution.py:252
  757.0 71.8 %collective-permute-start.59 = (bf16[128,128,128]{2,1,0:T(8,128)(2,1)}, bf16[128,128,128]{2,1,0:T(8,128)(2,1)S(1)}, u32[]{:S(2)}, u32[]{:S(2)}) collective-permute-start(bf16[128,128,128]{2,1,0:T(8,128)(2,1)} %slice.653), channel_id=1, source_target_pairs={{0,1},{1,0},{2,3},{3,2},{4,5},{5,4},{6,7},{7,6},{8,9},{9,8},{10,11... | collective-permute-start | bytes 12582920 | tf_op jit(solution)/shard_map/ppermute | solution.py:252
  757.0 71.8 %collective-permute-start.55 = (bf16[16,128,128]{2,1,0:T(8,128)(2,1)}, bf16[16,128,128]{2,1,0:T(8,128)(2,1)}, u32[]{:S(2)}, u32[]{:S(2)}) collective-permute-start(bf16[16,128,128]{2,1,0:T(8,128)(2,1)} %get-tuple-element.418), channel_id=1, source_target_pairs={{0,16},{16,0},{1,17},{17,1},{2,18},{18,2},{3,19},{19,3},{4,20},{20... | collective-permute-start | bytes 1572872 | tf_op jit(solution)/shard_map/ppermute | solution.py:252
  759.1 69.7 %collective-permute-start.56 = (bf16[16,128,128]{2,1,0:T(8,128)(2,1)}, bf16[16,128,128]{2,1,0:T(8,128)(2,1)}, u32[]{:S(2)}, u32[]{:S(2)}) collective-permute-start(bf16[16,128,128]{2,1,0:T(8,128)(2,1)} %get-tuple-element.419), channel_id=1, source_target_pairs={{0,2},{2,0},{1,3},{3,1},{4,6},{6,4},{5,7},{7,5},{8,10},{10,8},{9,1... | collective-permute-start | bytes 1572872 | tf_op jit(solution)/shard_map/ppermute | solution.py:252
  759.4 69.4 %collective-permute-start.57 = (bf16[24,128,128]{2,1,0:T(8,128)(2,1)S(1)}, bf16[24,128,128]{2,1,0:T(8,128)(2,1)}, u32[]{:S(2)}, u32[]{:S(2)}) collective-permute-start(bf16[24,128,128]{2,1,0:T(8,128)(2,1)S(1)} %copy-done.28), channel_id=1, source_target_pairs={{0,2},{2,0},{1,3},{3,1},{4,6},{6,4},{5,7},{7,5},{8,10},{10,8},{9,1... | collective-permute-start | bytes 2359304 | tf_op jit(solution)/shard_map/ppermute | solution.py:252
  761.1 67.7 %collective-permute-start.58 = (bf16[24,128,128]{2,1,0:T(8,128)(2,1)S(1)}, bf16[24,128,128]{2,1,0:T(8,128)(2,1)}, u32[]{:S(2)}, u32[]{:S(2)}) collective-permute-start(bf16[24,128,128]{2,1,0:T(8,128)(2,1)S(1)} %copy-done.27), channel_id=1, source_target_pairs={{0,16},{16,0},{1,17},{17,1},{2,18},{18,2},{3,19},{19,3},{4,20},{20... | collective-permute-start | bytes 2359304 | tf_op jit(solution)/shard_map/ppermute | solution.py:252
  836.2 39.7 %copy-start.6 = (bf16[128,128,128]{2,1,0:T(8,128)(2,1)S(1)}, bf16[128,128,128]{2,1,0:T(8,128)(2,1)}, u32[]{:S(2)}) copy-start(bf16[128,128,128]{2,1,0:T(8,128)(2,1)} %copy-done.5) | copy-start | bytes 12582916
  836.2 39.6 %collective-permute-start.64 = (bf16[288,128,128]{2,1,0:T(8,128)(2,1)}, bf16[288,128,128]{2,1,0:T(8,128)(2,1)S(1)}, u32[]{:S(2)}, u32[]{:S(2)}) collective-permute-start(bf16[288,128,128]{2,1,0:T(8,128)(2,1)} %get-tuple-element.447), channel_id=1, source_target_pairs={{0,1},{1,0},{2,3},{3,2},{4,5},{5,4},{6,7},{7,6},{8,9},{9,8},{10,11... | collective-permute-start | bytes 28311560 | tf_op jit(solution)/shard_map/ppermute | solution.py:252
  836.2 39.6 %collective-permute-start.62 = (bf16[32,128,128]{2,1,0:T(8,128)(2,1)}, bf16[32,128,128]{2,1,0:T(8,128)(2,1)S(1)}, u32[]{:S(2)}, u32[]{:S(2)}) collective-permute-start(bf16[32,128,128]{2,1,0:T(8,128)(2,1)} %get-tuple-element.445), channel_id=1, source_target_pairs={{0,2},{2,0},{1,3},{3,1},{4,6},{6,4},{5,7},{7,5},{8,10},{10,8},{9,1... | collective-permute-start | bytes 3145736 | tf_op jit(solution)/shard_map/ppermute | solution.py:252
  836.8 39.0 %collective-permute-start.63 = (bf16[32,128,128]{2,1,0:T(8,128)(2,1)S(1)}, bf16[32,128,128]{2,1,0:T(8,128)(2,1)S(1)}, u32[]{:S(2)}, u32[]{:S(2)}) collective-permute-start(bf16[32,128,128]{2,1,0:T(8,128)(2,1)S(1)} %get-tuple-element.446), channel_id=1, source_target_pairs={{0,16},{16,0},{1,17},{17,1},{2,18},{18,2},{3,19},{19,3},{4,20},{20... | collective-permute-start | bytes 3145736 | tf_op jit(solution)/shard_map/ppermute | solution.py:252
  838.6 12.4 %collective-permute-start.65 = (f32[10,1024]{1,0:T(8,128)S(1)}, f32[10,1024]{1,0:T(8,128)S(1)}, u32[]{:S(2)}, u32[]{:S(2)}) collective-permute-start(f32[10,1024]{1,0:T(8,128)S(1)} %concatenate.46), channel_id=1, source_target_pairs={{0,1},{1,0},{2,3},{3,2},{4,5},{5,4},{6,7},{7,6},{8,9},{9,8},{10,11... | collective-permute-start | bytes 122888 | tf_op jit(solution)/shard_map/ppermute | solution.py:252
  838.6 25.3 %collective-permute-start.66 = (f32[10,1024]{1,0:T(8,128)S(1)}, f32[10,1024]{1,0:T(8,128)S(1)}, u32[]{:S(2)}, u32[]{:S(2)}) collective-permute-start(f32[10,1024]{1,0:T(8,128)S(1)} %concatenate.46), channel_id=1, source_target_pairs={{0,2},{2,0},{1,3},{3,1},{4,6},{6,4},{5,7},{7,5},{8,10},{10,8},{9,1... | collective-permute-start | bytes 122888 | tf_op jit(solution)/shard_map/ppermute | solution.py:252
  851.0 14.9 %collective-permute-start.67 = (f32[10,1024]{1,0:T(8,128)S(1)}, f32[10,1024]{1,0:T(8,128)S(1)}, u32[]{:S(2)}, u32[]{:S(2)}) collective-permute-start(f32[10,1024]{1,0:T(8,128)S(1)} %concatenate.46), channel_id=1, source_target_pairs={{0,3},{1,2},{2,1},{3,0},{4,7},{5,6},{6,5},{7,4},{8,11},{9,10},{10,... | collective-permute-start | bytes 122888 | tf_op jit(solution)/shard_map/ppermute | solution.py:252
  863.9 10.5 collective-permute-start.60
  865.8 10.0 collective-permute-start.61
  878.3 21.1 %collective-permute-start.70 = (bf16[96,128,128]{2,1,0:T(8,128)(2,1)S(1)}, bf16[96,128,128]{2,1,0:T(8,128)(2,1)S(1)}, u32[]{:S(2)}, u32[]{:S(2)}) collective-permute-start(bf16[96,128,128]{2,1,0:T(8,128)(2,1)S(1)} %slice.674), channel_id=1, source_target_pairs={{0,1},{1,0},{2,3},{3,2},{4,5},{5,4},{6,7},{7,6},{8,9},{9,8},{10,11... | collective-permute-start | bytes 9437192 | tf_op jit(solution)/shard_map/ppermute | solution.py:252
  878.4 21.0 %collective-permute-start.68 = (bf16[16,128,128]{2,1,0:T(8,128)(2,1)S(1)}, bf16[16,128,128]{2,1,0:T(8,128)(2,1)S(1)}, u32[]{:S(2)}, u32[]{:S(2)}) collective-permute-start(bf16[16,128,128]{2,1,0:T(8,128)(2,1)S(1)} %get-tuple-element.456), channel_id=1, source_target_pairs={{0,16},{16,0},{1,17},{17,1},{2,18},{18,2},{3,19},{19,3},{4,20},{20... | collective-permute-start | bytes 1572872 | tf_op jit(solution)/shard_map/ppermute | solution.py:252
  880.3 19.1 %collective-permute-start.69 = (bf16[16,128,128]{2,1,0:T(8,128)(2,1)S(1)}, bf16[16,128,128]{2,1,0:T(8,128)(2,1)S(1)}, u32[]{:S(2)}, u32[]{:S(2)}) collective-permute-start(bf16[16,128,128]{2,1,0:T(8,128)(2,1)S(1)} %get-tuple-element.457), channel_id=1, source_target_pairs={{0,2},{2,0},{1,3},{3,1},{4,6},{6,4},{5,7},{7,5},{8,10},{10,8},{9,1... | collective-permute-start | bytes 1572872 | tf_op jit(solution)/shard_map/ppermute | solution.py:252
  880.6 13.6 %collective-permute-start.71 = (f32[10,1024]{1,0:T(8,128)S(1)}, f32[10,1024]{1,0:T(8,128)S(1)}, u32[]{:S(2)}, u32[]{:S(2)}) collective-permute-start(f32[10,1024]{1,0:T(8,128)S(1)} %add_add_fusion.1), channel_id=1, source_target_pairs={{0,16},{16,0},{1,17},{17,1},{2,18},{18,2},{3,19},{19,3},{4,20},{20... | collective-permute-start | bytes 122888 | tf_op jit(solution)/shard_map/ppermute | solution.py:252
  880.9 18.1 %collective-permute-start.72 = (f32[10,1024]{1,0:T(8,128)S(1)}, f32[10,1024]{1,0:T(8,128)S(1)}, u32[]{:S(2)}, u32[]{:S(2)}) collective-permute-start(f32[10,1024]{1,0:T(8,128)S(1)} %add_add_fusion.1), channel_id=1, source_target_pairs={{0,4},{4,0},{8,12},{12,8},{1,5},{5,1},{9,13},{13,9},{2,6},{6,2},{1... | collective-permute-start | bytes 122888 | tf_op jit(solution)/shard_map/ppermute | solution.py:252
  894.2 5.2 collective-permute-start.73
  910.6 152.2 %reduce-scatter.11.cloned.1.call-start = ((), (), s32[]{:S(2)}) async-start(), calls=%async_computation.8 | async-start | bytes 2949120 | tf_op jit(solution)/shard_map/reduce_scatter | solution.py:1596
  910.8 52.4 %collective-permute-start.74 = (bf16[72,128,128]{2,1,0:T(8,128)(2,1)}, bf16[72,128,128]{2,1,0:T(8,128)(2,1)S(1)}, u32[]{:S(2)}, u32[]{:S(2)}) collective-permute-start(bf16[72,128,128]{2,1,0:T(8,128)(2,1)} %get-tuple-element.479), channel_id=1, source_target_pairs={{0,2},{2,0},{1,3},{3,1},{4,6},{6,4},{5,7},{7,5},{8,10},{10,8},{9,1... | collective-permute-start | bytes 7077896 | tf_op jit(solution)/shard_map/ppermute | solution.py:252
  911.4 52.3 %collective-permute-start.75 = (bf16[72,128,128]{2,1,0:T(8,128)(2,1)}, bf16[72,128,128]{2,1,0:T(8,128)(2,1)S(1)}, u32[]{:S(2)}, u32[]{:S(2)}) collective-permute-start(bf16[72,128,128]{2,1,0:T(8,128)(2,1)} %get-tuple-element.480), channel_id=1, source_target_pairs={{0,16},{16,0},{1,17},{17,1},{2,18},{18,2},{3,19},{19,3},{4,20},{20... | collective-permute-start | bytes 7077896 | tf_op jit(solution)/shard_map/ppermute | solution.py:252
  912.9 5.7 collective-permute-start.76
  967.5 26.1 %collective-permute-start.77 = (bf16[36,128,128]{2,1,0:T(8,128)(2,1)S(1)}, bf16[36,128,128]{2,1,0:T(8,128)(2,1)S(1)}, u32[]{:S(2)}, u32[]{:S(2)}) collective-permute-start(bf16[36,128,128]{2,1,0:T(8,128)(2,1)S(1)} %get-tuple-element.484), channel_id=1, source_target_pairs={{0,16},{16,0},{1,17},{17,1},{2,18},{18,2},{3,19},{19,3},{4,20},{20... | collective-permute-start | bytes 3538952 | tf_op jit(solution)/shard_map/ppermute | solution.py:252
  968.8 25.5 %collective-permute-start.78 = (bf16[36,128,128]{2,1,0:T(8,128)(2,1)S(1)}, bf16[36,128,128]{2,1,0:T(8,128)(2,1)S(1)}, u32[]{:S(2)}, u32[]{:S(2)}) collective-permute-start(bf16[36,128,128]{2,1,0:T(8,128)(2,1)S(1)} %get-tuple-element.485), channel_id=1, source_target_pairs={{0,2},{2,0},{1,3},{3,1},{4,6},{6,4},{5,7},{7,5},{8,10},{10,8},{9,1... | collective-permute-start | bytes 3538952 | tf_op jit(solution)/shard_map/ppermute | solution.py:252
  1001.4 16.1 %collective-permute-start.79 = (bf16[24,128,128]{2,1,0:T(8,128)(2,1)S(1)}, bf16[24,128,128]{2,1,0:T(8,128)(2,1)S(1)}, u32[]{:S(2)}, u32[]{:S(2)}) collective-permute-start(bf16[24,128,128]{2,1,0:T(8,128)(2,1)S(1)} %copy-done.24), channel_id=1, source_target_pairs={{0,2},{2,0},{1,3},{3,1},{4,6},{6,4},{5,7},{7,5},{8,10},{10,8},{9,1... | collective-permute-start | bytes 2359304 | tf_op jit(solution)/shard_map/ppermute | solution.py:252
  1002.1 15.6 %collective-permute-start.80 = (bf16[24,128,128]{2,1,0:T(8,128)(2,1)S(1)}, bf16[24,128,128]{2,1,0:T(8,128)(2,1)S(1)}, u32[]{:S(2)}, u32[]{:S(2)}) collective-permute-start(bf16[24,128,128]{2,1,0:T(8,128)(2,1)S(1)} %copy-done.23), channel_id=1, source_target_pairs={{0,16},{16,0},{1,17},{17,1},{2,18},{18,2},{3,19},{19,3},{4,20},{20... | collective-permute-start | bytes 2359304 | tf_op jit(solution)/shard_map/ppermute | solution.py:252
  1019.5 7.8 collective-permute-start.81
  1021.0 7.8 collective-permute-start.82
  1030.7 18.1 %collective-permute-start.83 = (bf16[6,128,128]{2,1,0:T(8,128)(2,1)S(1)}, bf16[6,128,128]{2,1,0:T(8,128)(2,1)S(1)}, u32[]{:S(2)}, u32[]{:S(2)}) collective-permute-start(bf16[6,128,128]{2,1,0:T(8,128)(2,1)S(1)} %get-tuple-element.499), channel_id=1, source_target_pairs={{0,8},{4,12},{1,9},{5,13},{2,10},{6,14},{3,11},{7,15},{16,24},{20,... | collective-permute-start | bytes 589832 | tf_op jit(solution)/shard_map/ppermute | solution.py:252
  1035.2 22.4 %collective-permute-start.84 = (bf16[6,128,128]{2,1,0:T(8,128)(2,1)S(1)}, bf16[6,128,128]{2,1,0:T(8,128)(2,1)S(1)}, u32[]{:S(2)}, u32[]{:S(2)}) collective-permute-start(bf16[6,128,128]{2,1,0:T(8,128)(2,1)S(1)} %get-tuple-element.500), channel_id=1, source_target_pairs={{8,0},{12,4},{9,1},{13,5},{10,2},{14,6},{11,3},{15,7},{24,16},{28,... | collective-permute-start | bytes 589832 | tf_op jit(solution)/shard_map/ppermute | solution.py:252
  1036.5 21.1 %collective-permute-start.85 = (bf16[6,128,128]{2,1,0:T(8,128)(2,1)S(1)}, bf16[6,128,128]{2,1,0:T(8,128)(2,1)S(1)}, u32[]{:S(2)}, u32[]{:S(2)}) collective-permute-start(bf16[6,128,128]{2,1,0:T(8,128)(2,1)S(1)} %get-tuple-element.501), channel_id=1, source_target_pairs={{0,4},{4,8},{8,12},{1,5},{5,9},{9,13},{2,6},{6,10},{10,14},{3,7},{... | collective-permute-start | bytes 589832 | tf_op jit(solution)/shard_map/ppermute | solution.py:252
  1040.0 17.7 %collective-permute-start.86 = (bf16[6,128,128]{2,1,0:T(8,128)(2,1)S(1)}, bf16[6,128,128]{2,1,0:T(8,128)(2,1)S(1)}, u32[]{:S(2)}, u32[]{:S(2)}) collective-permute-start(bf16[6,128,128]{2,1,0:T(8,128)(2,1)S(1)} %get-tuple-element.502), channel_id=1, source_target_pairs={{4,0},{8,4},{12,8},{5,1},{9,5},{13,9},{6,2},{10,6},{14,10},{7,3},{... | collective-permute-start | bytes 589832 | tf_op jit(solution)/shard_map/ppermute | solution.py:252
  1041.3 16.4 %collective-permute-start.87 = (bf16[6,128,128]{2,1,0:T(8,128)(2,1)S(1)}, bf16[6,128,128]{2,1,0:T(8,128)(2,1)S(1)}, u32[]{:S(2)}, u32[]{:S(2)}) collective-permute-start(bf16[6,128,128]{2,1,0:T(8,128)(2,1)S(1)} %get-tuple-element.503), channel_id=1, source_target_pairs={{0,12},{1,13},{2,14},{3,15},{16,28},{17,29},{18,30},{19,31}} | collective-permute-start | bytes 589832 | tf_op jit(solution)/shard_map/ppermute | solution.py:252
  1048.9 13.7 %collective-permute-start.88 = (bf16[6,128,128]{2,1,0:T(8,128)(2,1)S(1)}, bf16[6,128,128]{2,1,0:T(8,128)(2,1)S(1)}, u32[]{:S(2)}, u32[]{:S(2)}) collective-permute-start(bf16[6,128,128]{2,1,0:T(8,128)(2,1)S(1)} %get-tuple-element.504), channel_id=1, source_target_pairs={{12,0},{13,1},{14,2},{15,3},{28,16},{29,17},{30,18},{31,19}} | collective-permute-start | bytes 589832 | tf_op jit(solution)/shard_map/ppermute | solution.py:252
  1050.3 18.0 %copy-start.37 = (f32[5,1024]{1,0:T(8,128)S(1)}, f32[5,1024]{1,0:T(8,128)}, u32[]{:S(2)}) copy-start(f32[5,1024]{1,0:T(8,128)} %param.25) | copy-start | bytes 61444
  1064.3 5.4 collective-permute-start.89
  (53 other events, 413.7 us)
Sparse Core Ops, SparseCore 0:
  10.6 126.3 all-gather.1
  910.7 57.2 reduce-scatter.8
  1000.4 56.8 reduce-scatter.10

commit v3 on v2

--- a/solution.py
+++ b/solution.py
@@ -112,6 +112,12 @@
                 place = ((chunk + column // WIDE) * 8 + row) * WIDE + column % WIDE
                 places[block_number(matrix, row, column, ranks)] = place
     return places.reshape(ranks, total)
+
+
+def chunks_first(blocks):
+    up = blocks[:128].reshape(8, 16)
+    down = blocks[128:]
+    return [up[:, :8].reshape(-1), down[:64], up[:, 8:].reshape(-1), down[64:]]
 
 
 def copy_in_place(out, source, place, sem):
@@ -400,10 +406,9 @@
     )(values, gain)
 
 
-def ffn_half(normed, weights, upper, lower, part, keep, pre=None):
+def ffn_part(normed, weights, upper, lower, first, steps, keep, pre=None):
     rows = normed.shape[0]
     tile = row_tile(rows)
-    steps = FF // D // 2
 
     def body(part_ref, x_ref, up_ref, down_ref, *rest):
         out_ref = rest[-3] if keep else rest[-2]
@@ -418,6 +423,10 @@
             act = (value * sigmoid(value)).astype(bf16)
             new = dot(act, down_ref[...])
 
+            if steps == 1:
+                out_ref[here] = new.astype(bf16)
+                continue
+
             @pl.when(step == 0)
             def _(new=new, here=here):
                 total[here] = new
@@ -426,18 +435,18 @@
             def _(new=new, here=here):
                 out_ref[here] = (total[here] + new).astype(bf16)
 
-    operands = [part.reshape(1), normed, weights, weights]
+    operands = [first.reshape(1), normed, weights, weights]
     specs = [
         pl.BlockSpec((rows, D), lambda f, p: (0, 0), pipeline_mode=pl.Buffered(1)),
-        pl.BlockSpec((D, D), lambda f, p: (at(upper) + p[0] * steps + f, 0)),
-        pl.BlockSpec((D, D), lambda f, p: (at(lower) + p[0] * steps + f, 0)),
+        pl.BlockSpec((D, D), lambda f, p: (at(upper) + p[0] + f, 0)),
+        pl.BlockSpec((D, D), lambda f, p: (at(lower) + p[0] + f, 0)),
     ]
     shapes = [jax.ShapeDtypeStruct((rows, D), bf16)]
     out_specs = [pl.BlockSpec((rows, D), lambda f, p: (0, 0), pipeline_mode=pl.Buffered(1))]
     aliases = {}
     if keep:
         shapes.append(jax.ShapeDtypeStruct((rows, FF), bf16))
-        out_specs.append(pl.BlockSpec((rows, D), lambda f, p: (0, p[0] * steps + f)))
+        out_specs.append(pl.BlockSpec((rows, D), lambda f, p: (0, p[0] + f)))
         if pre is not None:
             aliases = {len(operands): 1}
             operands.append(pre)
@@ -454,17 +463,21 @@
         out_shape=tuple(shapes),
         input_output_aliases=aliases,
         compiler_params=params(),
-        cost_estimate=cost(2 * rows * D * FF, 2 * D * FF),
-        name="ffn_half",
+        cost_estimate=cost(4 * rows * D * D * steps, 4 * D * D * steps),
+        name="ffn_part",
     )(*operands)
 
 
-def join(base, one, other, next_gain):
+def join(base, products, next_gain):
     rows = base.shape[0]
     tile = row_tile(rows)
-
-    def body(base_ref, one_ref, other_ref, gain_ref, out_ref, next_ref):
-        both = one_ref[...].astype(f32) + other_ref[...].astype(f32)
+    count = len(products)
+
+    def body(base_ref, *refs):
+        gain_ref, out_ref, next_ref = refs[count:]
+        both = refs[0][...].astype(f32)
+        for ref in refs[1:count]:
+            both = both + ref[...].astype(f32)
         y = base_ref[...].astype(f32) + 0.5 * both
         out_ref[...] = y
         next_ref[...] = norm(y, gain_ref[...]).astype(bf16)
@@ -477,21 +490,22 @@
             jax.ShapeDtypeStruct((rows, D), f32),
             jax.ShapeDtypeStruct((rows, D), bf16),
         ),
-        in_specs=[spec, spec, spec, const_spec((1, D))],
+        in_specs=[spec] * (count + 1) + [const_spec((1, D))],
         out_specs=(spec, spec),
         compiler_params=params(),
         name="join",
-    )(base, one, other, next_gain)
+    )(base, *products, next_gain)
 
 
 def ffn_backward(
     after, after_gain, after_grads, base, stream, gain, pre, weights, upper, lower, sums, table,
-    ranks, kept=None,
+    ranks, kept=None, first=0, last=None, carry=None,
 ):
     rows = stream.shape[0]
     tile = row_tile(rows)
     wide = 512
-    steps = FF // wide
+    steps = (FF // wide if last is None else last) - first
+    whole = FF // wide
     parts = len(after_grads)
     targets = len(sums)
     with_base = base is not None
@@ -499,21 +513,25 @@
 
     def body(table_ref, *refs):
         refs = list(refs)
-        after_ref, after_gain_ref = refs[0], refs[1]
-        grad_refs = refs[2 : 2 + parts]
-        at_ref = 2 + parts
+        at_ref = 0
+        if parts > 0:
+            after_ref, after_gain_ref = refs[0], refs[1]
+            grad_refs = refs[2 : 2 + parts]
+            at_ref = 2 + parts
         base_ref = None
         if with_base:
             base_ref = refs[at_ref]
             at_ref += 1
         x_ref, gain_ref, up_ref, down_ref, pre_ref = refs[at_ref : at_ref + 5]
         kept_ref = refs[at_ref + 5]
-        out_ref, gains_ref = refs[-13 - targets : -11 - targets]
-        sums_ref = refs[-11 - targets : -11]
+        outs = refs[at_ref + 5 + again + (carry is not None) + aliased :]
+        out_ref, gains_ref = outs[:2]
+        sums_ref = outs[2 : 2 + targets]
+        carry_ref = refs[at_ref + 5 + again]
+        grad_sum = outs[2 + targets]
         (
-            half, normed, pre_here, normed_t, grad_sum, pre_grad, act_t, up_part, down_part, up_sem,
-            down_sem,
-        ) = refs[-11:]
+            half, normed, pre_here, normed_t, pre_grad, act_t, up_part, down_part, up_sem, down_sem,
+        ) = outs[3 + targets :]
         step = pl.program_id(0)
 
         @pl.when(step == 0)
@@ -521,29 +539,32 @@
             gain_sum = jnp.zeros((1, D), f32)
             for t in range(0, rows, tile):
                 here = slice(t, t + tile)
-                grad = grad_refs[0][here].astype(f32)
-                for other in grad_refs[1:]:
-                    grad = grad + other[here].astype(f32)
-                back, part = norm_back(after_ref[here], after_gain_ref[...], grad)
-                gain_sum = gain_sum + part
-                if with_base:
-                    back = back + base_ref[here]
+                if parts == 0:
+                    back = base_ref[here]
+                else:
+                    grad = grad_refs[0][here].astype(f32)
+                    for other in grad_refs[1:]:
+                        grad = grad + other[here].astype(f32)
+                    back, part = norm_back(after_ref[here], after_gain_ref[...], grad)
+                    gain_sum = gain_sum + part
+                    if with_base:
+                        back = back + base_ref[here]
                 out_ref[here] = back
                 half[here] = (0.5 * back).astype(bf16)
                 low = norm(x_ref[here].astype(f32), gain_ref[...]).astype(bf16)
                 if again:
                     normed[here] = low
                 normed_t[:, here] = low.T
-                grad_sum[here] = jnp.zeros((tile, D), f32)
+                grad_sum[here] = jnp.zeros((tile, D), f32) if carry is None else carry_ref[here]
             gains_ref[0:1] = gain_sum
 
         if again:
 
-            @pl.when(step // (steps // 2) == kept_ref[0])
+            @pl.when((first + step) // (whole // 2) == kept_ref[0])
             def _():
                 pre_here[...] = pre_ref[...]
 
-            @pl.when(step // (steps // 2) != kept_ref[0])
+            @pl.when((first + step) // (whole // 2) != kept_ref[0])
             def _():
                 for t in range(0, rows, tile):
                     here = slice(t, t + tile)
@@ -571,14 +592,18 @@
         for t in range(0, wide, 256):
             down_part[t : t + 256] = dot(act_t[t : t + 256], half[...]).astype(bf16)
         start_blocks(
-            table_ref, sums_ref, up_part, up_sem, upper, 0, step * 4, ranks
+            table_ref, sums_ref, up_part, up_sem, upper, 0, (first + step) * 4, ranks
         )
         start_blocks(
-            table_ref, sums_ref, down_part, down_sem, lower, step * 4, 0, ranks
+            table_ref, sums_ref, down_part, down_sem, lower, (first + step) * 4, 0, ranks
         )
 
         @pl.when(step == steps - 1)
         def _():
+            wait_blocks(up_part, up_sem)
+            wait_blocks(down_part, down_sem)
+            if last is not None:
+                return
             gain_sum = jnp.zeros((1, D), f32)
             for t in range(0, rows, tile):
                 here = slice(t, t + tile)
@@ -586,11 +611,12 @@
                 gain_sum = gain_sum + part
                 out_ref[here] += back
             gains_ref[1:2] = gain_sum
-            wait_blocks(up_part, up_sem)
-            wait_blocks(down_part, down_sem)
-
-    operands = [table, after, after_gain, *after_grads]
-    specs = [SMEM, const_spec((rows, D)), const_spec((1, D))] + [const_spec((rows, D))] * parts
+
+    operands = [table]
+    specs = [SMEM]
+    if parts > 0:
+        operands += [after, after_gain, *after_grads]
+        specs += [const_spec((rows, D)), const_spec((1, D))] + [const_spec((rows, D))] * parts
     if with_base:
         operands.append(base)
         specs.append(const_spec((rows, D)))
@@ -598,15 +624,19 @@
     specs += [
         const_spec((rows, D)),
         const_spec((1, D)),
-        pl.BlockSpec((D, wide), lambda f: (at(upper) + f // 2, f % 2)),
-        pl.BlockSpec((wide, D), lambda f: (at(lower) * 2 + f, 0)),
+        pl.BlockSpec((D, wide), lambda f: (at(upper) + (first + f) // 2, (first + f) % 2)),
+        pl.BlockSpec((wide, D), lambda f: (at(lower) * 2 + first + f, 0)),
     ]
     operands.append(pre)
-    specs.append(pl.BlockSpec((rows, wide), lambda f: (0, f)))
+    specs.append(pl.BlockSpec((rows, wide), lambda f: (0, first + f)))
     if again:
         operands.append(kept.reshape(1))
         specs.append(SMEM)
+    if carry is not None:
+        operands.append(carry)
+        specs.append(const_spec((rows, D)))
     aliases = {}
+    aliased = 0 if isinstance(sums[0], tuple) else targets
     if not isinstance(sums[0], tuple):
         for n, target in enumerate(sums):
             aliases[len(operands)] = 2 + n
@@ -620,15 +650,18 @@
             jax.ShapeDtypeStruct((rows, D), f32),
             jax.ShapeDtypeStruct((2, D), f32),
             *[jax.ShapeDtypeStruct(shape, bf16) for shape in sums],
-        ),
+        )
+        + ((jax.ShapeDtypeStruct((rows, D), f32),) if last is not None else ()),
         in_specs=specs,
-        out_specs=(const_spec((rows, D)), const_spec((2, D))) + (ANY,) * targets,
-        scratch_shapes=[
+        out_specs=(const_spec((rows, D)), const_spec((2, D)))
+        + (ANY,) * targets
+        + ((const_spec((rows, D)),) if last is not None else ()),
+        scratch_shapes=([pltpu.VMEM((rows, D), f32)] if last is None else [])
+        + [
             pltpu.VMEM((rows, D), bf16),
             pltpu.VMEM((rows, D) if again else (16, 128), bf16),
             pltpu.VMEM((rows, wide) if again else (16, 128), bf16),
             pltpu.VMEM((D, rows), bf16),
-            pltpu.VMEM((rows, D), f32),
             pltpu.VMEM((rows, wide), bf16),
             pltpu.VMEM((wide, rows), bf16),
             pltpu.VMEM((D, wide), bf16),
@@ -638,7 +671,7 @@
         ],
         input_output_aliases=aliases,
         compiler_params=params(has_side_effects=True),
-        cost_estimate=cost(8 * rows * D * FF, 8 * D * FF + 2 * rows * FF),
+        cost_estimate=cost(8 * rows * D * wide * steps, 8 * D * wide * steps),
         name="ffn_backward",
     )(*operands)
 
@@ -1555,7 +1588,7 @@
     def hold(self):
         moves = [[move for unused, move in pairs] for pairs in self.waiting.values()]
         values = [value for pairs in self.waiting.values() for value, unused in pairs]
-        columns = list(self.results.items())
+        columns = [(name, value) for name, value in self.results.items() if isinstance(name, int)]
         out = list(tied(self.sums, *values, *[value for unused, value in columns]))
         self.sums = out.pop(0)
         for name, names in zip(self.waiting, moves):
@@ -1583,9 +1616,12 @@
         return held
 
 
-def one_swap(value, move):
-    (come,) = yield [(value, move)]
-    return come
+def both_swaps(value, moves):
+    arrived = []
+    for move in moves:
+        (value,) = yield [(value, move)]
+        arrived.append(value)
+    return arrived
 
 
 def joined(columns):
@@ -1598,17 +1634,17 @@
 
 def finish_rounds(rounds):
     rounds.add_round(3)
-    rounds.step([1, 2, 3, "small"])
+    rounds.step([2, 3])
     rounds.add_round(4)
-    rounds.step([2, 4, "small"])
     (column,) = rounds.beside(joined([rounds.results[number] for number in range(3)]))
     early = over_z(column)
+    rounds.step([3, 4, "small"])
     rounds.step([3, "small"])
-    rounds.step([3])
     (column,) = rounds.beside(joined([rounds.results[3]]))
     late = over_z(column)
-    for unused in range(3):
-        rounds.step([4])
+    rounds.step([4, "small"])
+    rounds.step([4])
+    rounds.step([4])
     mine = jnp.concatenate([early, late, rounds.results[4]], axis=0)
     return jnp.concatenate([mine, swap(mine, "core")], axis=0)
 
@@ -1618,8 +1654,8 @@
     for number in range(3):
         rounds.add_round(number)
     rounds.step([0, 1, 2])
+    rounds.step([0, 1, 2])
     rounds.step([0, 1])
-    rounds.step([0])
     return finish_rounds(rounds)
 
 
@@ -1680,16 +1716,32 @@
             across = 1 - rank
             core_at = coords[2]
             own_places = places[rank]
-            all_places = places.reshape(-1)
+            all_places = np.concatenate(
+                [
+                    part
+                    for own in weight_places(ranks)
+                    for part in [
+                        *chunks_first(own[: starts[1]]),
+                        own[starts[1] : starts[3]],
+                        *chunks_first(own[starts[3] :]),
+                    ]
+                ]
+            )
+            all_places = jnp.asarray(all_places)
             column = lax.all_gather(low, ("z", "x", "core"), axis=0, tiled=True)
             normed_own = norm_rows(stream, gain(0))
             normed_other = swap(normed_own, "mp")
+            column, normed_other, table, arrivals, good, windows, masks = tied(
+                column, normed_other, table, arrivals, good, windows, masks
+            )
 
             def own_part(group):
                 here = slice(starts[group], starts[group + 1])
-                return unsort(
-                    column, owners[0, here], own_places[here], GROUP_CHUNKS[group], True
-                )
+                slot, place = owners[0, here], own_places[here]
+                if group in (0, 3):
+                    slot = jnp.concatenate(chunks_first(slot))
+                    place = jnp.concatenate(chunks_first(place))
+                return unsort(column, slot, place, GROUP_CHUNKS[group], True)
 
             def outgoing(listed, first, count):
                 half = count // 2
@@ -1708,58 +1760,69 @@
 
             def first_half():
                 w_one, list_one = own_part(0)
-                (product,) = ffn_half(normed_other, w_one, UP1, DOWN1, rank, False)
+                (product,) = ffn_part(normed_other, w_one, UP1, DOWN1, 2 * rank, 2, False)
                 return w_one, list_one, product
 
             w_one, list_one, product = first_half()
             (come_attn,), (w_one, list_one, product) = together(
                 [(send_attn, "mp")], w_one, list_one, product
             )
-            own_product, pre_first = ffn_half(normed_own, w_one, UP1, DOWN1, rank, True)
+            own_product, pre_first = ffn_part(normed_own, w_one, UP1, DOWN1, 2 * rank, 2, True)
             w_conv, list_conv = own_part(2)
             w_two, list_two = own_part(3)
             (product, beside), (own_product, w_conv, list_conv, w_two, list_two) = together(
                 [(product, "mp"), (come_attn, "core")], own_product, w_conv, list_conv, w_two,
                 list_two,
             )
-            after_first, normed_attn = join(stream, own_product, product, gain(1))
+            after_first, normed_attn = join(stream, [own_product, product], gain(1))
             w_attn = put(w_attn, come_attn, beside, 1, 0)
 
             queries = project(normed_attn, w_attn, QUERY, 1)
             keys = project(normed_attn, w_attn, KEY, 2, rank, 2)
-            (other,), (queries, keys) = together([(normed_attn, "mp")], queries, keys)
-            part_two = outgoing(list_two, 0, 64)
-            list_rest = jnp.concatenate(
-                [outgoing(list_attn, 96, 32), outgoing(list_conv, 0, 96)]
+            sends = [
+                outgoing(list_attn, 96, 32),
+                outgoing(list_conv, 0, 96),
+                outgoing(list_two, 0, 64),
+                outgoing(list_two, 64, 48),
+                outgoing(list_two, 112, 144),
+                outgoing(list_one, 0, 128),
+                outgoing(list_one, 128, 128),
+            ]
+            (other,), (queries, keys, *sends) = together(
+                [(normed_attn, "mp")], queries, keys, *sends
             )
             keys = project(other, w_attn, KEY, 2, across, 2, keys)
             attended, logs = attention_forward(
                 queries, keys, segment_ids, rank, windows, slopes
             )
-            (come_rest, come_two), (attended, logs) = together(
-                [(list_rest, "mp"), (part_two, "mp")], attended, logs
-            )
-            (beside,), unused = together([(come_rest, "core")])
-            w_attn = put(w_attn, come_rest[:16], beside[:16], 1, 96)
-            w_conv = put(w_conv, come_rest[16:], beside[16:], 2, 0)
+            come, (attended, logs) = together([(send, "mp") for send in sends[:3]], attended, logs)
+            beside, unused = together([(value, "core") for value in come])
+            more_two, send_two, *send_one = sends[3:]
+            more_two, *beside = tied(more_two, *beside)
+            w_attn = put(w_attn, come[0], beside[0], 1, 96)
+            w_conv = put(w_conv, come[1], beside[1], 2, 0)
+            w_two = put(w_two, come[2], beside[2], 3, 0)
             after_attn = project_out(attended, w_attn, OUT, after_first)
+            (more_two,), (after_attn, w_conv, w_two) = together(
+                [(more_two, "mp")], after_attn, w_conv, w_two
+            )
             before, behind = edges(after_attn[:HALO], after_attn[-HALO:], ranks)
-            rest_two, before, behind = tied(outgoing(list_two, 64, 192), before, behind)
+            send_two, before, behind = tied(send_two, before, behind)
             after_conv, linear, gate, normed_two = conv_forward(
                 after_attn, before, behind, gain(2), gain(3), w_conv, kernel, masks
             )
-            own_product, pre_second = ffn_half(normed_two, w_two, UP2, DOWN2, rank, True)
-            (more_two, beside), (own_product, pre_second, w_two) = together(
-                [(rest_two, "mp"), (come_two, "core")], own_product, pre_second, w_two
-            )
-            (more_beside,), unused = together([(more_two, "core")])
-            send_one, more_two = tied(outgoing(list_one, 0, 256), more_two)
-            w_two = put(w_two, come_two, beside, 3, 0)
-            w_two = put(w_two, more_two, more_beside, 3, 64)
-            product, pre_second = ffn_half(
-                normed_two, w_two, UP2, DOWN2, across, True, pre_second
-            )
-            after_second, output = join(after_conv, own_product, product, gain(4))
+            own_product, pre_second = ffn_part(normed_two, w_two, UP2, DOWN2, 2 * rank, 2, True)
+            (two, beside), (own_product, pre_second, w_two) = together(
+                [(send_two, "mp"), (more_two, "core")], own_product, pre_second, w_two
+            )
+            w_two = put(w_two, more_two, beside, 3, 64)
+            two, *send_one = tied(two, *send_one)
+            (beside,), (w_two,) = together([(two, "core")], w_two)
+            w_two = put(w_two, two, beside, 3, 112)
+            product, pre_second = ffn_part(
+                normed_two, w_two, UP2, DOWN2, 2 * across, 2, True, pre_second
+            )
+            after_second, output = join(after_conv, [own_product, product], gain(4))
             sources = [(normed_attn, rank), (other, across)]
         else:
             everything = lax.all_gather(low, ("mp", "z", "x", "core"), axis=0, tiled=True)
@@ -1804,7 +1867,7 @@
         )
         if fast:
             (come_one,), (grad_conv, gains_a, *sums) = together(
-                [(send_one, "mp")], grad_conv, gains_a, *sums
+                [(send_one[0], "mp")], grad_conv, gains_a, *sums
             )
             rounds = Rounds(*sums)
             rounds.add_round(0)
@@ -1812,13 +1875,17 @@
         before, behind = edges(
             grad_conv[:HALO].astype(bf16), grad_conv[-HALO:].astype(bf16), ranks
         )
+        if fast:
+            send_last, before, behind = tied(send_one[1], before, behind)
         grad_attn, gains_b, tap_grads, *sums = conv_backward(
             grad_conv, before, behind, after_attn, gain(2), linear, gate, w_conv, kernel, masks,
             sums, table, ranks,
         )
         if fast:
+            rounds.add("first", both_swaps(come_one, ["core"]))
+            rounds.add("second", both_swaps(send_last, ["mp", "core"]))
             grad_attn, gains_b, tap_grads = rounds.step(
-                [0], grad_attn, gains_b, tap_grads, sums=sums
+                [0, "first", "second"], grad_attn, gains_b, tap_grads, sums=sums
             )
             rounds.add_round(1)
             sums = rounds.hold()
@@ -1829,12 +1896,11 @@
             queries, keys, segment_ids, rank, windows, slopes, logs, mixed_grad, attended
         )
         if fast:
-            rounds.add("core", one_swap(come_one, "core"))
-            query_grad, key_grad, value_grad = rounds.step(
-                [0, 1, "core"], query_grad, key_grad, value_grad, sums=sums
+            away = input_gradient(key_grad, value_grad, w_attn, 1 - rank, rows)
+            query_grad, key_grad, value_grad, away = rounds.step(
+                [0, 1, "second"], query_grad, key_grad, value_grad, away, sums=sums
             )
             sums = rounds.hold()
-            away = input_gradient(key_grad, value_grad, w_attn, 1 - rank, rows)
         else:
             away = input_gradient(key_grad, value_grad, w_attn, jnp.zeros((), jnp.int32), group)
             arrived = lax.psum_scatter(away, "mp", scatter_dimension=0, tiled=True)
@@ -1842,17 +1908,34 @@
             normed_attn, query_grad, key_grad, value_grad, sources, fast, w_attn, sums, table, ranks
         )
         if fast:
-            w_one = put(w_one, come_one, rounds.results.pop("core"), 0, 0)
-            (arrived,), (near, w_one, *sums) = together([(away, "mp")], near, w_one, *sums)
-            rounds.sums, rounds.tail = sums
+            (beside,), (second, more) = rounds.results.pop("first"), rounds.results.pop("second")
+            beside, more, away = tied(beside, more, away)
+            w_one = put(put(w_one, come_one, beside, 0, 0), second, more, 0, 128)
+            rounds.add("away", both_swaps(away, ["mp"]))
+            near, w_one = rounds.step(["away"], near, w_one, sums=sums)
+            (arrived,) = rounds.results.pop("away")
             rounds.add_round(2)
             sums = rounds.hold()
-        stream_grad, gains_c, *sums = ffn_backward(
-            after_first, gain(1), [near, arrived], grad_attn, stream, gain(0), pre_first, w_one,
-            UP1, DOWN1, sums, table, ranks, rank if fast else None,
-        )
+        first_args = (gain(0), pre_first, w_one, UP1, DOWN1)
         if fast:
-            stream_grad, gains_c = rounds.step([0, 1, 2], stream_grad, gains_c, sums=sums)
+            middle = FF // 512 // 2
+            so_far, gains_c, *sums, carry = ffn_backward(
+                after_first, gain(1), [near, arrived], grad_attn, stream, *first_args, sums, table,
+                ranks, rank, 0, middle,
+            )
+            so_far, gains_c, carry = rounds.step([0, 1, 2], so_far, gains_c, carry, sums=sums)
+            sums = rounds.hold()
+            stream_grad, gains_d, *sums = ffn_backward(
+                None, None, [], so_far, stream, *first_args, sums, table, ranks, rank, middle,
+                carry=carry,
+            )
+            stream_grad, gains_d = rounds.step([1, 2], stream_grad, gains_d, sums=sums)
+            gains_c = jnp.concatenate([gains_c[0:1], gains_d[1:2]])
+        else:
+            stream_grad, gains_c, *sums = ffn_backward(
+                after_first, gain(1), [near, arrived], grad_attn, stream, *first_args, sums, table,
+                ranks,
+            )
         small = jnp.concatenate(
             [gains_c[1:2], gains_c[0:1], gains_b, gains_a[1:2], gains_a[0:1], tap_grads]
         )

time: 1110 us -> 1090 us (0.982)
  waiting for transfers between devices: 324 us -> 293 us
  Pallas kernels: 544 us -> 560 us
    all_gather x1, waiting for transfers between devices: 117 us -> 71 us  [run(): column = lax.all_gather(low, ('z', 'x', 'core'), axis=0, tiled=True)]
    ppermute x54 -> x60, waiting for transfers between devices: 201 us -> 217 us  [swap(): return lax.ppermute(value, axis, pairs)]
    pallas_call x2 -> x3, Pallas kernels: 128 us -> 141 us  [ffn_backward(): pl.pallas_call(body, grid=(steps,), out_shape=(jax.ShapeDtypeStruct((rows...]
    pallas_call x6 -> x8, Pallas kernels: 26.1 us -> 29.2 us  [place_weights(): pl.pallas_call(body, grid=(count // each,), out_shape=jax.ShapeDtypeStruc...]
    ppermute x54 -> x60, starting transfers between devices: 67.6 us -> 68.2 us  [swap(): return lax.ppermute(value, axis, pairs)]
    convert_element_type x15 -> x16, other arithmetic: 47.9 us -> 48 us  [added(): return sum((term.astype(f32) for term in terms)).astype(bf16)]
  transfers between devices with their start and end apart: 61 -> 67, of which waited for: 27 -> 28; matrix products, arithmetic and copies ran while one was open for 7% -> 7% of each run, Pallas kernels for 46% -> 49%
where the time goes in v3:
time: 1090 us; the launch traced here: 1080 us
  Pallas kernels  560 us (51%)
  waiting for transfers between devices  293 us (27%)
  starting transfers between devices  77.4 us (7%)
  other arithmetic  72.1 us (7%)
  local copies, waits for them, and re-layouts  57.5 us (5%)
  between operations  17.5 us (2%)
    ppermute x60, waiting for transfers between devices, swap(): return lax.ppermute(value, axis, pairs)  217 us
    pallas_call x3, Pallas kernels, ffn_backward(): pl.pallas_call(body, grid=(steps,), out_shape=(jax.ShapeDtypeStruct((rows...  141 us
    all_gather x1, waiting for transfers between devices, run(): column = lax.all_gather(low, ('z', 'x', 'core'), axis=0, tiled=True)  71 us
    ppermute x60, starting transfers between devices, swap(): return lax.ppermute(value, axis, pairs)  68.2 us
    pallas_call x4, Pallas kernels, ffn_part(): pl.pallas_call(body, grid_spec=pltpu.PrefetchScalarGridSpec(num_scalar_pr...  65 us
    pallas_call x1, Pallas kernels, attention_backward(): pl.pallas_call(body, grid=(HEADS, rows // tall), out_shape=(jax.ShapeDtyp...  60.7 us
    pallas_call x1, Pallas kernels, attention_forward(): pl.pallas_call(body, grid=(HEADS, rows // tall), out_shape=(jax.ShapeDtyp...  50.1 us
    convert_element_type x16, other arithmetic, added(): return sum((term.astype(f32) for term in terms)).astype(bf16)  48 us
  transfers between devices with their start and end apart: 67, of which 28 were waited for; matrix products, arithmetic and copies ran while one was open for 7% of the time, Pallas kernels for 49%

profile of v3, /device:TPU:0, one launch (start us, length us, event | category | flops | bytes accessed | tf_op | source)
XLA Modules:
  0.0 1078.9 jit_solution(10778303484164048941)
XLA Ops:
  7.2 3.2 bitcast_convert_fusion
  14.2 4.4 norm_rows.1.x_ref
  29.1 36.9 %collective-permute-done.32.x_ref = bf16[1024,1024]{1,0:T(8,128)(2,1)S(1)} collective-permute-done((bf16[1024,1024]{1,0:T(8,128)(2,1)}, bf16[1024,1024]{1,0:T(8,128)(2,1)S(1)}, u32[]{:S(2)}, u32[]{:S(2)}) %collective-permute-start.32) | collective-permute-done | bytes 2097184 | tf_op jit(solution)/shard_map/ppermute | solution.py:258
  66.0 71.0 %all-gather.2.cloned.1.call-done.slots_ref = bf16[736,128,128]{2,1,0:T(8,128)(2,1)} async-done(((bf16[46,128,128]{2,1,0:T(8,128)(2,1)}), bf16[736,128,128]{2,1,0:T(8,128)(2,1)}) %all-gather.2.cloned.1.call-update) | async-done | bytes 24117264 | tf_op jit(solution)/shard_map/all_gather | solution.py:1731
  138.9 6.4 unsort.4
  149.7 11.7 %unsort.5 = (bf16[8192,1024]{1,0:T(8,128)(2,1)}, bf16[256,128,128]{2,1,0:T(8,128)(2,1)}) custom-call(s32[256]{0:T(256)} %get-tuple-element.807.source_ref, s32[256]{0:T(256)} %get-tuple-element.808.place_ref, bf16[736,128,128]{2,1,0:T(8,128)(2,1)} %all-gather.2.cloned.1.call-done.slots_ref), custom_call_target="tpu_custom_call" | custom-call | bytes 25165824 | tf_op jit(solution)/shard_map/unsort/pallas_call | solution.py:188
  161.4 15.4 %ffn_part.4 = bf16[1024,1024]{1,0:T(8,128)(2,1)} custom-call(s32[1]{0:T(128)} %bitcast.30.part_ref, bf16[1024,1024]{1,0:T(8,128)(2,1)} %copy-done.12, bf16[8192,1024]{1,0:T(8,128)(2,1)} %get-tuple-element.375.up_ref.down_ref.rest_2_, bf16[8192,1024]{1,0:T(8,128)(2,1)} %get-tuple-element.375.up_ref.down_ref.rest_2_), custom_call_target="tpu_custom_call" | custom-call | flops 8589934592 | bytes 8388608 | tf_op jit(solution)/shard_map/ffn_part/pallas_call | solution.py:454
  176.8 6.7 collective-permute-done.34.rest_0_
  188.4 11.7 %unsort.7 = (bf16[8192,1024]{1,0:T(8,128)(2,1)}, bf16[256,128,128]{2,1,0:T(8,128)(2,1)}) custom-call(s32[256]{0:T(256)} %get-tuple-element.809.source_ref, s32[256]{0:T(256)} %get-tuple-element.810.place_ref, bf16[736,128,128]{2,1,0:T(8,128)(2,1)} %all-gather.2.cloned.1.call-done.slots_ref), custom_call_target="tpu_custom_call" | custom-call | bytes 25165824 | tf_op jit(solution)/shard_map/unsort/pallas_call | solution.py:188
  200.1 5.5 unsort.6
  205.6 16.7 %ffn_part.5 = (bf16[1024,1024]{1,0:T(8,128)(2,1)}, bf16[1024,4096]{1,0:T(8,128)(2,1)}) custom-call(s32[1]{0:T(128)} %bitcast.30.part_ref, bf16[1024,1024]{1,0:T(8,128)(2,1)} %norm_rows.1.x_ref, bf16[8192,1024]{1,0:T(8,128)(2,1)} %get-tuple-element.375.up_ref.down_ref.rest_2_, bf16[8192,1024]{1,0:T(8,128)(2,1)} %get-tuple-element.375.up_ref.down_ref.rest_2_), custom_call_target="tpu_custom_call" | custom-call | flops 8589934592 | bytes 8388608 | tf_op jit(solution)/shard_map/ffn_part/pallas_call | solution.py:454
  222.2 9.6 collective-permute-done.35.refs_1_
  233.2 6.1 join.2
  243.1 4.7 constant_dynamic-slice_fusion.12
  247.9 3.8 place_weights.8.w_ref.rest_2_
  257.5 3.4 constant_dynamic-slice_fusion.14
  260.9 5.9 project.3.q_ref
  266.7 8.3 project.4.rest_0_
  275.0 10.6 collective-permute-done.37.x_ref.refs_1_
  290.5 8.3 project.5.key_ref.value_ref
  298.8 50.1 %attention_forward.1 = (bf16[1024,1024]{1,0:T(8,128)(2,1)}, f32[8,1,1024]{2,1,0:T(1,128)}) custom-call(s32[1]{0:T(128)} %bitcast.39.part_ref.rank_ref.refs_10_.refs_6_, s32[4]{0:T(128)} %reshape.372.window_ref, f32[8]{0:T(128)} %multiply_power_fusion.slope_ref, bf16[1024,1024]{1,0:T(8,128)(2,1)} %project.3.q_ref, s32[1024,1]{1,0:T(8,128)} %copy.56.own_ref, ...), custom_call_target="tpu_custom_call" | custom-call | tf_op jit(solution)/shard_map/attention_forward/pallas_call | solution.py:1020
  348.9 4.6 collective-permute-done.38.rest_0_
  354.2 5.3 collective-permute-done.41.rest_1_
  368.4 3.7 place_weights.10.value_ref.gate_ref.out_w_ref.gate_w_ref
  372.1 7.4 project_out.1.x_ref
  381.2 3.3 collective-permute-start.45
  386.4 4.3 collective-permute-done.46.behind_ref
  391.3 20.3 %conv_forward.1 = (f32[1024,1024]{1,0:T(8,128)}, bf16[1056,1024]{1,0:T(8,128)(2,1)}, bf16[1056,1024]{1,0:T(8,128)(2,1)}, bf16[1024,1024]{1,0:T(8,128)(2,1)}) custom-call(f32[1024,1024]{1,0:T(8,128)} %project_out.1.x_ref, f32[16,1024]{1,0:T(8,128)} %copy-done.46, f32[16,1024]{1,0:T(8,128)} %copy-done.47, f32[1,1024]{1,0:T(1,128)} %get-tuple-element.756.gain_ref, ...), custom_call_target="tpu_custom_call" | custom-call | flops 6442450944 | bytes 18874368 | tf_op jit(solution)/shard_map/conv_forward/pallas_call | solution.py:1175
  411.6 16.4 %ffn_part.6 = (bf16[1024,1024]{1,0:T(8,128)(2,1)}, bf16[1024,4096]{1,0:T(8,128)(2,1)}) custom-call(s32[1]{0:T(128)} %bitcast.30.part_ref, bf16[1024,1024]{1,0:T(8,128)(2,1)} %get-tuple-element.430.x_ref, bf16[8192,1024]{1,0:T(8,128)(2,1)} %place_weights.11.up_ref.down_ref.rest_2_, bf16[8192,1024]{1,0:T(8,128)(2,1)} %place_weights.11.up_ref.down_ref.rest_2_), custom_call_target="tpu_custom_call" | custom-call | flops 8589934592 | bytes 8388608 | tf_op jit(solution)/shard_map/ffn_part/pallas_call | solution.py:454
  428.0 13.7 %collective-permute-done.47.rest_0_ = bf16[72,128,128]{2,1,0:T(8,128)(2,1)S(1)} collective-permute-done((bf16[72,128,128]{2,1,0:T(8,128)(2,1)S(1)}, bf16[72,128,128]{2,1,0:T(8,128)(2,1)S(1)}, u32[]{:S(2)}, u32[]{:S(2)}) %collective-permute-start.47) | collective-permute-done | bytes 2359328 | tf_op jit(solution)/shard_map/ppermute | solution.py:258
  446.4 4.9 place_weights.13.up_ref.down_ref.refs_5_.refs_6_
  451.2 16.5 %ffn_part.7 = (bf16[1024,1024]{1,0:T(8,128)(2,1)}, bf16[1024,4096]{1,0:T(8,128)(2,1)}) custom-call(s32[1]{0:T(128)} %bitcast.48.part_ref, bf16[1024,1024]{1,0:T(8,128)(2,1)} %get-tuple-element.430.x_ref, bf16[8192,1024]{1,0:T(8,128)(2,1)} %place_weights.13.up_ref.down_ref.refs_5_.refs_6_, ...), custom_call_target="tpu_custom_call", output_to_operand_aliasing={{1}: (4, {})} | custom-call | flops 8589934592 | bytes 8388608 | tf_op jit(solution)/shard_map/ffn_part/pallas_call | solution.py:454
  467.7 6.4 join.3
  474.1 60.8 %ffn_backward.3 = (f32[1024,1024]{1,0:T(8,128)}, f32[2,1024]{1,0:T(2,128)}, bf16[1184,128,128]{2,1,0:T(8,128)(2,1)}, bf16[288,128,128]{2,1,0:T(8,128)(2,1)}) custom-call(s32[1472]{0:T(1024)} %reshape.370.table_ref, f32[1024,1024]{1,0:T(8,128)} %get-tuple-element.448.refs_0_, f32[1,1024]{1,0:T(1,128)} %get-tuple-element.754.refs_2_.refs_1_, ...), custom_call_target="tpu_custom_call" | custom-call | flops 34359738368 | bytes 33554432 | tf_op jit(solution)/shard_map/ffn_backward/pallas_call | solution.py:646
  534.9 3.3 convert.12
  542.7 4.7 slice.741
  550.7 43.2 %conv_backward.1 = (f32[1024,1024]{1,0:T(8,128)}, f32[1,1024]{1,0:T(1,128)}, f32[5,1024]{1,0:T(8,128)}, bf16[1184,128,128]{2,1,0:T(8,128)(2,1)}, bf16[288,128,128]{2,1,0:T(8,128)(2,1)}) custom-call(s32[1472]{0:T(1024)} %reshape.370.table_ref, f32[1024,1024]{1,0:T(8,128)} %get-tuple-element.458.g_ref, ...), custom_call_target="tpu_custom_call", output_to_operand_aliasing={{3}: (13, {}), {4}: (14, {})} | custom-call | flops 12884901888 | bytes 29360128 | tf_op jit(solution)/shard_map/conv_backward/pallas_call | solution.py:1358
  596.9 5.5 slice.748
  602.4 4.0 add_convert_fusion.38
  613.0 10.0 project_out_back.1
  623.0 60.7 %attention_backward.1 = (bf16[1024,1024]{1,0:T(8,128)(2,1)}, bf16[2048,1024]{1,0:T(8,128)(2,1)}, bf16[2048,1024]{1,0:T(8,128)(2,1)}) custom-call(s32[1]{0:T(128)} %bitcast.39.part_ref.rank_ref.refs_10_.refs_6_, s32[4]{0:T(128)} %reshape.372.window_ref, f32[8]{0:T(128)} %multiply_power_fusion.slope_ref, bf16[1024,1024]{1,0:T(8,128)(2,1)} %project.3.q_ref, ...), custom_call_target="tpu_custom_call" | custom-call | tf_op jit(solution)/shard_map/attention_backward/pallas_call | solution.py:1103
  683.7 8.7 input_gradient.1
  700.3 4.5 place_weights.14.rest_2_
  704.8 4.5 place_weights.15.refs_7_.refs_8_.refs_3_.refs_4_
  709.3 32.8 %projections_back.1 = (f32[1024,1024]{1,0:T(8,128)}, bf16[1184,128,128]{2,1,0:T(8,128)(2,1)}, bf16[288,128,128]{2,1,0:T(8,128)(2,1)}) custom-call(s32[2]{0:T(128)} %pad_add_fusion.12.part_ref, s32[1472]{0:T(1024)} %reshape.370.table_ref, bf16[1024,1024]{1,0:T(8,128)(2,1)} %get-tuple-element.383.x_ref.n_ref.refs_0_, ...), custom_call_target="tpu_custom_call", output_to_operand_aliasing={{1}: (11, {}), {2}: (12, {})} | custom-call | flops 17179869184 | bytes 31457280 | tf_op jit(solution)/shard_map/projections_back/pallas_call | solution.py:931
  742.1 4.7 slice.759
  750.8 39.4 %ffn_backward.4 = (f32[1024,1024]{1,0:T(8,128)}, f32[2,1024]{1,0:T(2,128)}, bf16[1184,128,128]{2,1,0:T(8,128)(2,1)}, bf16[288,128,128]{2,1,0:T(8,128)(2,1)}, f32[1024,1024]{1,0:T(8,128)}) custom-call(s32[1472]{0:T(1024)} %reshape.370.table_ref, f32[1024,1024]{1,0:T(8,128)} %get-tuple-element.414.s_ref.refs_0_, ...), custom_call_target="tpu_custom_call", output_to_operand_aliasing={{2}: (12, {}), {3}: (13, {})} | custom-call | flops 17179869184 | bytes 16777216 | tf_op jit(solution)/shard_map/ffn_backward/pallas_call | solution.py:646
  790.3 4.2 add_convert_fusion.36
  799.9 5.8 collective-permute-start.69
  807.6 41.2 %ffn_backward.5 = (f32[1024,1024]{1,0:T(8,128)}, f32[2,1024]{1,0:T(2,128)}, bf16[1184,128,128]{2,1,0:T(8,128)(2,1)}, bf16[288,128,128]{2,1,0:T(8,128)(2,1)}) custom-call(s32[1472]{0:T(1024)} %reshape.370.table_ref, f32[1024,1024]{1,0:T(8,128)} %get-tuple-element.553.refs_0_, ...), custom_call_target="tpu_custom_call", output_to_operand_aliasing={{2}: (9, {}), {3}: (10, {})} | custom-call | flops 17179869184 | bytes 16777216 | tf_op jit(solution)/shard_map/ffn_backward/pallas_call | solution.py:646
  848.9 4.1 add_convert_fusion.46
  853.2 4.0 slice.790
  860.0 11.7 %collective-permute-done.70 = bf16[16,128,128]{2,1,0:T(8,128)(2,1)S(1)} collective-permute-done((bf16[16,128,128]{2,1,0:T(8,128)(2,1)}, bf16[16,128,128]{2,1,0:T(8,128)(2,1)S(1)}, u32[]{:S(2)}, u32[]{:S(2)}) %collective-permute-start.70) | collective-permute-done | bytes 524320 | tf_op jit(solution)/shard_map/ppermute | solution.py:258
  871.9 6.4 add_convert_fusion.30
  887.3 50.4 %collective-permute-done.77 = f32[10,1024]{1,0:T(8,128)S(1)} collective-permute-done((f32[10,1024]{1,0:T(8,128)S(1)}, f32[10,1024]{1,0:T(8,128)S(1)}, u32[]{:S(2)}, u32[]{:S(2)}) %collective-permute-start.77) | collective-permute-done | bytes 40992 | tf_op jit(solution)/shard_map/ppermute | solution.py:258
  937.7 3.8 add_convert_fusion.34
  949.3 23.6 %collective-permute-done.81 = f32[10,1024]{1,0:T(8,128)S(1)} collective-permute-done((f32[10,1024]{1,0:T(8,128)S(1)}, f32[10,1024]{1,0:T(8,128)S(1)}, u32[]{:S(2)}, u32[]{:S(2)}) %collective-permute-start.81) | collective-permute-done | bytes 40992 | tf_op jit(solution)/shard_map/ppermute | solution.py:258
  972.8 4.3 add_convert_fusion.33
  987.0 11.1 %collective-permute-done.84 = bf16[24,128,128]{2,1,0:T(8,128)(2,1)S(1)} collective-permute-done((bf16[24,128,128]{2,1,0:T(8,128)(2,1)S(1)}, bf16[24,128,128]{2,1,0:T(8,128)(2,1)S(1)}, u32[]{:S(2)}, u32[]{:S(2)}) %collective-permute-start.84) | collective-permute-done | bytes 786464 | tf_op jit(solution)/shard_map/ppermute | solution.py:258
  1003.2 7.6 collective-permute-done.87
  1013.9 4.7 collective-permute-start.89
  1023.3 7.5 collective-permute-start.93
  1036.6 9.6 collective-permute-done.94
  1055.2 16.7 %shampoo.1 = (f32[46,128,128]{2,1,0:T(8,128)}, f32[46,128,128]{2,1,0:T(8,128)}, f32[46,128,128]{2,1,0:T(8,128)}, f32[46,128,128]{2,1,0:T(8,128)}, f32[46,128,128]{2,1,0:T(8,128)}) custom-call(s32[48]{0:T(128)} %pad.14.index_ref, bf16[92,128,128]{2,1,0:T(8,128)(2,1)S(1)} %get-tuple-element.813.refs_0_.refs_1_.refs_2_.refs_3_.refs_4_.refs_5_.refs_6_.refs_7_, ...), custom_call_target="tpu_custom_call" | custom-call | tf_op jit(solution)/shard_map/shampoo/pallas_call | solution.py:1443
  (320 shorter events, 151.1 us)
Async XLA Ops:
  7.2 129.8 %all-gather.2.cloned.1.call-start = ((), (), s32[]{:S(2)}) async-start(), calls=%async_computation.6 | async-start | bytes 25624576 | tf_op jit(solution)/shard_map/all_gather | solution.py:1731
  10.5 1035.9 %reduce-scatter.9.cloned.1.call-start = ((), (), s32[]{:S(2)}) async-start(), calls=%async_computation.7 | async-start | bytes 3604480 | tf_op jit(solution)/shard_map/reduce_scatter | solution.py:1632
  10.6 12.4 %collective-permute-start.33 = (s32[1,736]{1,0:T(1,128)S(1)}, s32[1,736]{1,0:T(1,128)S(1)}, u32[]{:S(2)}, u32[]{:S(2)}) collective-permute-start(s32[1,736]{1,0:T(1,128)S(1)} %copy-done.52), channel_id=1, source_target_pairs={{0,16},{16,0},{1,17},{17,1},{2,18},{18,2},{3,19},{19,3},{4,20},{20... | collective-permute-start | bytes 8840 | tf_op jit(solution)/shard_map/ppermute | solution.py:258
  18.7 47.3 %collective-permute-start.32 = (bf16[1024,1024]{1,0:T(8,128)(2,1)}, bf16[1024,1024]{1,0:T(8,128)(2,1)S(1)}, u32[]{:S(2)}, u32[]{:S(2)}) collective-permute-start(bf16[1024,1024]{1,0:T(8,128)(2,1)} %norm_rows.1.x_ref), channel_id=1, source_target_pairs={{0,16},{16,0},{1,17},{17,1},{2,18},{18,2},{3,19},{19,3},{4,20},{20... | collective-permute-start | bytes 6291464 | tf_op jit(solution)/shard_map/ppermute | solution.py:258
  146.9 36.6 %collective-permute-start.34 = (bf16[48,128,128]{2,1,0:T(8,128)(2,1)S(1)}, bf16[48,128,128]{2,1,0:T(8,128)(2,1)S(1)}, u32[]{:S(2)}, u32[]{:S(2)}) collective-permute-start(bf16[48,128,128]{2,1,0:T(8,128)(2,1)S(1)} %constant_dynamic-slice_fusion.19), channel_id=1, source_target_pairs={{0,16},{16,0},{1,17},{17,1},{2,18},{18,2},{3,19},{19,3},{4,20},{20... | collective-permute-start | bytes 4718600 | tf_op jit(solution)/shard_map/ppermute | solution.py:258
  184.6 47.2 %collective-permute-start.35 = (bf16[1024,1024]{1,0:T(8,128)(2,1)}, bf16[1024,1024]{1,0:T(8,128)(2,1)S(1)}, u32[]{:S(2)}, u32[]{:S(2)}) collective-permute-start(bf16[1024,1024]{1,0:T(8,128)(2,1)} %ffn_part.4), channel_id=1, source_target_pairs={{0,16},{16,0},{1,17},{17,1},{2,18},{18,2},{3,19},{19,3},{4,20},{20... | collective-permute-start | bytes 6291464 | tf_op jit(solution)/shard_map/ppermute | solution.py:258
  186.1 36.2 %collective-permute-start.36 = (bf16[48,128,128]{2,1,0:T(8,128)(2,1)}, bf16[48,128,128]{2,1,0:T(8,128)(2,1)}, u32[]{:S(2)}, u32[]{:S(2)}) collective-permute-start(bf16[48,128,128]{2,1,0:T(8,128)(2,1)} %copy-done.16), channel_id=1, source_target_pairs={{0,1},{1,0},{2,3},{3,2},{4,5},{5,4},{6,7},{7,6},{8,9},{9,8},{10,11... | collective-permute-start | bytes 4718600 | tf_op jit(solution)/shard_map/ppermute | solution.py:258
  239.3 46.3 %collective-permute-start.37 = (bf16[1024,1024]{1,0:T(8,128)(2,1)}, bf16[1024,1024]{1,0:T(8,128)(2,1)S(1)}, u32[]{:S(2)}, u32[]{:S(2)}) collective-permute-start(bf16[1024,1024]{1,0:T(8,128)(2,1)} %get-tuple-element.383.x_ref.n_ref.refs_0_), channel_id=1, source_target_pairs={{0,16},{16,0},{1,17},{17,1},{2,18},{18,2},{3,19},{19,3},{4,20},{20... | collective-permute-start | bytes 6291464 | tf_op jit(solution)/shard_map/ppermute | solution.py:258
  285.6 67.9 %collective-permute-start.39 = (bf16[48,128,128]{2,1,0:T(8,128)(2,1)}, bf16[48,128,128]{2,1,0:T(8,128)(2,1)}, u32[]{:S(2)}, u32[]{:S(2)}) collective-permute-start(bf16[48,128,128]{2,1,0:T(8,128)(2,1)} %constant_dynamic-slice_fusion.17), channel_id=1, source_target_pairs={{0,16},{16,0},{1,17},{17,1},{2,18},{18,2},{3,19},{19,3},{4,20},{20... | collective-permute-start | bytes 4718600 | tf_op jit(solution)/shard_map/ppermute | solution.py:258
  286.9 66.6 %collective-permute-start.40 = (bf16[32,128,128]{2,1,0:T(8,128)(2,1)}, bf16[32,128,128]{2,1,0:T(8,128)(2,1)S(1)}, u32[]{:S(2)}, u32[]{:S(2)}) collective-permute-start(bf16[32,128,128]{2,1,0:T(8,128)(2,1)} %constant_dynamic-slice_fusion.16), channel_id=1, source_target_pairs={{0,16},{16,0},{1,17},{17,1},{2,18},{18,2},{3,19},{19,3},{4,20},{20... | collective-permute-start | bytes 3145736 | tf_op jit(solution)/shard_map/ppermute | solution.py:258
  287.6 65.9 %collective-permute-start.38 = (bf16[16,128,128]{2,1,0:T(8,128)(2,1)}, bf16[16,128,128]{2,1,0:T(8,128)(2,1)}, u32[]{:S(2)}, u32[]{:S(2)}) collective-permute-start(bf16[16,128,128]{2,1,0:T(8,128)(2,1)} %constant_dynamic-slice_fusion.18), channel_id=1, source_target_pairs={{0,16},{16,0},{1,17},{17,1},{2,18},{18,2},{3,19},{19,3},{4,20},{20... | collective-permute-start | bytes 1572872 | tf_op jit(solution)/shard_map/ppermute | solution.py:258
  353.5 5.9 collective-permute-start.42
  353.6 5.9 collective-permute-start.43
  354.1 5.4 collective-permute-start.41
  360.4 19.9 %collective-permute-start.44 = (bf16[24,128,128]{2,1,0:T(8,128)(2,1)}, bf16[24,128,128]{2,1,0:T(8,128)(2,1)}, u32[]{:S(2)}, u32[]{:S(2)}) collective-permute-start(bf16[24,128,128]{2,1,0:T(8,128)(2,1)} %constant_dynamic-slice_fusion.15), channel_id=1, source_target_pairs={{0,16},{16,0},{1,17},{17,1},{2,18},{18,2},{3,19},{19,3},{4,20},{20... | collective-permute-start | bytes 2359304 | tf_op jit(solution)/shard_map/ppermute | solution.py:258
  381.2 5.2 collective-permute-start.45
  384.5 6.2 collective-permute-start.46
  390.7 51.0 %collective-permute-start.47 = (bf16[72,128,128]{2,1,0:T(8,128)(2,1)S(1)}, bf16[72,128,128]{2,1,0:T(8,128)(2,1)S(1)}, u32[]{:S(2)}, u32[]{:S(2)}) collective-permute-start(bf16[72,128,128]{2,1,0:T(8,128)(2,1)S(1)} %copy-done.11), channel_id=1, source_target_pairs={{0,16},{16,0},{1,17},{17,1},{2,18},{18,2},{3,19},{19,3},{4,20},{20... | collective-permute-start | bytes 7077896 | tf_op jit(solution)/shard_map/ppermute | solution.py:258
  390.7 37.3 %collective-permute-start.48 = (bf16[24,128,128]{2,1,0:T(8,128)(2,1)}, bf16[24,128,128]{2,1,0:T(8,128)(2,1)S(1)}, u32[]{:S(2)}, u32[]{:S(2)}) collective-permute-start(bf16[24,128,128]{2,1,0:T(8,128)(2,1)} %collective-permute-done.44.rest_0_), channel_id=1, source_target_pairs={{0,1},{1,0},{2,3},{3,2},{4,5},{5,4},{6,7},{7,6},{8,9},{9,8},{10,11... | collective-permute-start | bytes 2359304 | tf_op jit(solution)/shard_map/ppermute | solution.py:258
  443.0 91.9 %collective-permute-start.50 = (bf16[64,128,128]{2,1,0:T(8,128)(2,1)}, bf16[64,128,128]{2,1,0:T(8,128)(2,1)S(1)}, u32[]{:S(2)}, u32[]{:S(2)}) collective-permute-start(bf16[64,128,128]{2,1,0:T(8,128)(2,1)} %get-tuple-element.446), channel_id=1, source_target_pairs={{0,16},{16,0},{1,17},{17,1},{2,18},{18,2},{3,19},{19,3},{4,20},{20... | collective-permute-start | bytes 6291464 | tf_op jit(solution)/shard_map/ppermute | solution.py:258
  538.2 9.2 collective-permute-start.51
  541.4 6.0 collective-permute-start.52
  547.5 49.4 %collective-permute-start.53 = (bf16[128,128,128]{2,1,0:T(8,128)(2,1)}, bf16[128,128,128]{2,1,0:T(8,128)(2,1)S(1)}, u32[]{:S(2)}, u32[]{:S(2)}) collective-permute-start(bf16[128,128,128]{2,1,0:T(8,128)(2,1)} %slice.741), channel_id=1, source_target_pairs={{0,1},{1,0},{2,3},{3,2},{4,5},{5,4},{6,7},{7,6},{8,9},{9,8},{10,11... | collective-permute-start | bytes 12582920 | tf_op jit(solution)/shard_map/ppermute | solution.py:258
  547.6 46.3 %collective-permute-start.54 = (bf16[64,128,128]{2,1,0:T(8,128)(2,1)}, bf16[64,128,128]{2,1,0:T(8,128)(2,1)}, u32[]{:S(2)}, u32[]{:S(2)}) collective-permute-start(bf16[64,128,128]{2,1,0:T(8,128)(2,1)} %copy-done.13), channel_id=1, source_target_pairs={{0,1},{1,0},{2,3},{3,2},{4,5},{5,4},{6,7},{7,6},{8,9},{9,8},{10,11... | collective-permute-start | bytes 6291464 | tf_op jit(solution)/shard_map/ppermute | solution.py:258
  548.1 48.8 %collective-permute-start.55 = (bf16[64,128,128]{2,1,0:T(8,128)(2,1)}, bf16[64,128,128]{2,1,0:T(8,128)(2,1)}, u32[]{:S(2)}, u32[]{:S(2)}) collective-permute-start(bf16[64,128,128]{2,1,0:T(8,128)(2,1)} %get-tuple-element.462), channel_id=1, source_target_pairs={{0,16},{16,0},{1,17},{17,1},{2,18},{18,2},{3,19},{19,3},{4,20},{20... | collective-permute-start | bytes 6291464 | tf_op jit(solution)/shard_map/ppermute | solution.py:258
  606.4 86.1 %collective-permute-start.58 = (bf16[96,128,128]{2,1,0:T(8,128)(2,1)}, bf16[96,128,128]{2,1,0:T(8,128)(2,1)S(1)}, u32[]{:S(2)}, u32[]{:S(2)}) collective-permute-start(bf16[96,128,128]{2,1,0:T(8,128)(2,1)} %slice.748), channel_id=1, source_target_pairs={{0,1},{1,0},{2,3},{3,2},{4,5},{5,4},{6,7},{7,6},{8,9},{9,8},{10,11... | collective-permute-start | bytes 9437192 | tf_op jit(solution)/shard_map/ppermute | solution.py:258
  606.4 86.0 %collective-permute-start.59 = (bf16[64,128,128]{2,1,0:T(8,128)(2,1)}, bf16[64,128,128]{2,1,0:T(8,128)(2,1)}, u32[]{:S(2)}, u32[]{:S(2)}) collective-permute-start(bf16[64,128,128]{2,1,0:T(8,128)(2,1)} %collective-permute-done.55.rest_0_), channel_id=1, source_target_pairs={{0,1},{1,0},{2,3},{3,2},{4,5},{5,4},{6,7},{7,6},{8,9},{9,8},{10,11... | collective-permute-start | bytes 6291464 | tf_op jit(solution)/shard_map/ppermute | solution.py:258
  606.9 85.5 %collective-permute-start.56 = (bf16[32,128,128]{2,1,0:T(8,128)(2,1)}, bf16[32,128,128]{2,1,0:T(8,128)(2,1)}, u32[]{:S(2)}, u32[]{:S(2)}) collective-permute-start(bf16[32,128,128]{2,1,0:T(8,128)(2,1)} %get-tuple-element.482), channel_id=1, source_target_pairs={{0,2},{2,0},{1,3},{3,1},{4,6},{6,4},{5,7},{7,5},{8,10},{10,8},{9,1... | collective-permute-start | bytes 3145736 | tf_op jit(solution)/shard_map/ppermute | solution.py:258
  608.1 84.3 %collective-permute-start.57 = (bf16[32,128,128]{2,1,0:T(8,128)(2,1)}, bf16[32,128,128]{2,1,0:T(8,128)(2,1)}, u32[]{:S(2)}, u32[]{:S(2)}) collective-permute-start(bf16[32,128,128]{2,1,0:T(8,128)(2,1)} %get-tuple-element.483), channel_id=1, source_target_pairs={{0,16},{16,0},{1,17},{17,1},{2,18},{18,2},{3,19},{19,3},{4,20},{20... | collective-permute-start | bytes 3145736 | tf_op jit(solution)/shard_map/ppermute | solution.py:258
  694.1 48.0 %collective-permute-start.60 = (bf16[1024,1024]{1,0:T(8,128)(2,1)}, bf16[1024,1024]{1,0:T(8,128)(2,1)}, u32[]{:S(2)}, u32[]{:S(2)}) collective-permute-start(bf16[1024,1024]{1,0:T(8,128)(2,1)} %input_gradient.1), channel_id=1, source_target_pairs={{0,16},{16,0},{1,17},{17,1},{2,18},{18,2},{3,19},{19,3},{4,20},{20... | collective-permute-start | bytes 6291464 | tf_op jit(solution)/shard_map/ppermute | solution.py:258
  746.8 43.5 %collective-permute-start.65 = (bf16[128,128,128]{2,1,0:T(8,128)(2,1)}, bf16[128,128,128]{2,1,0:T(8,128)(2,1)}, u32[]{:S(2)}, u32[]{:S(2)}) collective-permute-start(bf16[128,128,128]{2,1,0:T(8,128)(2,1)} %slice.759), channel_id=1, source_target_pairs={{0,1},{1,0},{2,3},{3,2},{4,5},{5,4},{6,7},{7,6},{8,9},{9,8},{10,11... | collective-permute-start | bytes 12582920 | tf_op jit(solution)/shard_map/ppermute | solution.py:258
  746.8 43.5 %collective-permute-start.63 = (bf16[24,128,128]{2,1,0:T(8,128)(2,1)S(1)}, bf16[24,128,128]{2,1,0:T(8,128)(2,1)}, u32[]{:S(2)}, u32[]{:S(2)}) collective-permute-start(bf16[24,128,128]{2,1,0:T(8,128)(2,1)S(1)} %get-tuple-element.525), channel_id=1, source_target_pairs={{0,2},{2,0},{1,3},{3,1},{4,6},{6,4},{5,7},{7,5},{8,10},{10,8},{9,1... | collective-permute-start | bytes 2359304 | tf_op jit(solution)/shard_map/ppermute | solution.py:258
  747.4 42.9 %collective-permute-start.64 = (bf16[24,128,128]{2,1,0:T(8,128)(2,1)S(1)}, bf16[24,128,128]{2,1,0:T(8,128)(2,1)}, u32[]{:S(2)}, u32[]{:S(2)}) collective-permute-start(bf16[24,128,128]{2,1,0:T(8,128)(2,1)S(1)} %get-tuple-element.526), channel_id=1, source_target_pairs={{0,16},{16,0},{1,17},{17,1},{2,18},{18,2},{3,19},{19,3},{4,20},{20... | collective-permute-start | bytes 2359304 | tf_op jit(solution)/shard_map/ppermute | solution.py:258
  748.3 41.9 %collective-permute-start.61 = (bf16[16,128,128]{2,1,0:T(8,128)(2,1)}, bf16[16,128,128]{2,1,0:T(8,128)(2,1)}, u32[]{:S(2)}, u32[]{:S(2)}) collective-permute-start(bf16[16,128,128]{2,1,0:T(8,128)(2,1)} %get-tuple-element.523), channel_id=1, source_target_pairs={{0,16},{16,0},{1,17},{17,1},{2,18},{18,2},{3,19},{19,3},{4,20},{20... | collective-permute-start | bytes 1572872 | tf_op jit(solution)/shard_map/ppermute | solution.py:258
  749.4 40.9 %collective-permute-start.62 = (bf16[16,128,128]{2,1,0:T(8,128)(2,1)}, bf16[16,128,128]{2,1,0:T(8,128)(2,1)}, u32[]{:S(2)}, u32[]{:S(2)}) collective-permute-start(bf16[16,128,128]{2,1,0:T(8,128)(2,1)} %get-tuple-element.524), channel_id=1, source_target_pairs={{0,2},{2,0},{1,3},{3,1},{4,6},{6,4},{5,7},{7,5},{8,10},{10,8},{9,1... | collective-permute-start | bytes 1572872 | tf_op jit(solution)/shard_map/ppermute | solution.py:258
  799.2 49.6 %collective-permute-start.68 = (bf16[32,128,128]{2,1,0:T(8,128)(2,1)}, bf16[32,128,128]{2,1,0:T(8,128)(2,1)S(1)}, u32[]{:S(2)}, u32[]{:S(2)}) collective-permute-start(bf16[32,128,128]{2,1,0:T(8,128)(2,1)} %get-tuple-element.551), channel_id=1, source_target_pairs={{0,2},{2,0},{1,3},{3,1},{4,6},{6,4},{5,7},{7,5},{8,10},{10,8},{9,1... | collective-permute-start | bytes 3145736 | tf_op jit(solution)/shard_map/ppermute | solution.py:258
  799.9 49.0 %collective-permute-start.69 = (bf16[32,128,128]{2,1,0:T(8,128)(2,1)S(1)}, bf16[32,128,128]{2,1,0:T(8,128)(2,1)S(1)}, u32[]{:S(2)}, u32[]{:S(2)}) collective-permute-start(bf16[32,128,128]{2,1,0:T(8,128)(2,1)S(1)} %get-tuple-element.552), channel_id=1, source_target_pairs={{0,16},{16,0},{1,17},{17,1},{2,18},{18,2},{3,19},{19,3},{4,20},{20... | collective-permute-start | bytes 3145736 | tf_op jit(solution)/shard_map/ppermute | solution.py:258
  805.6 43.2 %collective-permute-start.66 = (bf16[12,128,128]{2,1,0:T(8,128)(2,1)S(1)}, bf16[12,128,128]{2,1,0:T(8,128)(2,1)S(1)}, u32[]{:S(2)}, u32[]{:S(2)}) collective-permute-start(bf16[12,128,128]{2,1,0:T(8,128)(2,1)S(1)} %get-tuple-element.549), channel_id=1, source_target_pairs={{0,16},{16,0},{1,17},{17,1},{2,18},{18,2},{3,19},{19,3},{4,20},{20... | collective-permute-start | bytes 1179656 | tf_op jit(solution)/shard_map/ppermute | solution.py:258
  805.7 43.1 %collective-permute-start.67 = (bf16[12,128,128]{2,1,0:T(8,128)(2,1)S(1)}, bf16[12,128,128]{2,1,0:T(8,128)(2,1)S(1)}, u32[]{:S(2)}, u32[]{:S(2)}) collective-permute-start(bf16[12,128,128]{2,1,0:T(8,128)(2,1)S(1)} %get-tuple-element.550), channel_id=1, source_target_pairs={{0,2},{2,0},{1,3},{3,1},{4,6},{6,4},{5,7},{7,5},{8,10},{10,8},{9,1... | collective-permute-start | bytes 1179656 | tf_op jit(solution)/shard_map/ppermute | solution.py:258
  853.0 18.9 %collective-permute-start.72 = (bf16[288,128,128]{2,1,0:T(8,128)(2,1)}, bf16[288,128,128]{2,1,0:T(8,128)(2,1)}, u32[]{:S(2)}, u32[]{:S(2)}) collective-permute-start(bf16[288,128,128]{2,1,0:T(8,128)(2,1)} %get-tuple-element.575), channel_id=1, source_target_pairs={{0,1},{1,0},{2,3},{3,2},{4,5},{5,4},{6,7},{7,6},{8,9},{9,8},{10,11... | collective-permute-start | bytes 28311560 | tf_op jit(solution)/shard_map/ppermute | solution.py:258
  857.2 14.5 %collective-permute-start.70 = (bf16[16,128,128]{2,1,0:T(8,128)(2,1)}, bf16[16,128,128]{2,1,0:T(8,128)(2,1)S(1)}, u32[]{:S(2)}, u32[]{:S(2)}) collective-permute-start(bf16[16,128,128]{2,1,0:T(8,128)(2,1)} %get-tuple-element.573), channel_id=1, source_target_pairs={{0,16},{16,0},{1,17},{17,1},{2,18},{18,2},{3,19},{19,3},{4,20},{20... | collective-permute-start | bytes 1572872 | tf_op jit(solution)/shard_map/ppermute | solution.py:258
  857.2 14.7 %collective-permute-start.71 = (bf16[16,128,128]{2,1,0:T(8,128)(2,1)}, bf16[16,128,128]{2,1,0:T(8,128)(2,1)}, u32[]{:S(2)}, u32[]{:S(2)}) collective-permute-start(bf16[16,128,128]{2,1,0:T(8,128)(2,1)} %get-tuple-element.574), channel_id=1, source_target_pairs={{0,2},{2,0},{1,3},{3,1},{4,6},{6,4},{5,7},{7,5},{8,10},{10,8},{9,1... | collective-permute-start | bytes 1572872 | tf_op jit(solution)/shard_map/ppermute | solution.py:258
  880.8 56.9 %collective-permute-start.75 = (bf16[96,128,128]{2,1,0:T(8,128)(2,1)}, bf16[96,128,128]{2,1,0:T(8,128)(2,1)}, u32[]{:S(2)}, u32[]{:S(2)}) collective-permute-start(bf16[96,128,128]{2,1,0:T(8,128)(2,1)} %slice.790), channel_id=1, source_target_pairs={{0,1},{1,0},{2,3},{3,2},{4,5},{5,4},{6,7},{7,6},{8,9},{9,8},{10,11... | collective-permute-start | bytes 9437192 | tf_op jit(solution)/shard_map/ppermute | solution.py:258
  882.4 164.1 %reduce-scatter.11.cloned.1.call-start = ((), (), s32[]{:S(2)}) async-start(), calls=%async_computation.8 | async-start | bytes 2949120 | tf_op jit(solution)/shard_map/reduce_scatter | solution.py:1632
  882.4 55.3 %collective-permute-start.73 = (bf16[72,128,128]{2,1,0:T(8,128)(2,1)}, bf16[72,128,128]{2,1,0:T(8,128)(2,1)S(1)}, u32[]{:S(2)}, u32[]{:S(2)}) collective-permute-start(bf16[72,128,128]{2,1,0:T(8,128)(2,1)} %get-tuple-element.589), channel_id=1, source_target_pairs={{0,2},{2,0},{1,3},{3,1},{4,6},{6,4},{5,7},{7,5},{8,10},{10,8},{9,1... | collective-permute-start | bytes 7077896 | tf_op jit(solution)/shard_map/ppermute | solution.py:258
  882.8 54.9 %collective-permute-start.74 = (bf16[72,128,128]{2,1,0:T(8,128)(2,1)}, bf16[72,128,128]{2,1,0:T(8,128)(2,1)S(1)}, u32[]{:S(2)}, u32[]{:S(2)}) collective-permute-start(bf16[72,128,128]{2,1,0:T(8,128)(2,1)} %get-tuple-element.590), channel_id=1, source_target_pairs={{0,16},{16,0},{1,17},{17,1},{2,18},{18,2},{3,19},{19,3},{4,20},{20... | collective-permute-start | bytes 7077896 | tf_op jit(solution)/shard_map/ppermute | solution.py:258
  884.5 53.2 %collective-permute-start.77 = (f32[10,1024]{1,0:T(8,128)S(1)}, f32[10,1024]{1,0:T(8,128)S(1)}, u32[]{:S(2)}, u32[]{:S(2)}) collective-permute-start(f32[10,1024]{1,0:T(8,128)S(1)} %concatenate.62), channel_id=1, source_target_pairs={{0,2},{2,0},{1,3},{3,1},{4,6},{6,4},{5,7},{7,5},{8,10},{10,8},{9,1... | collective-permute-start | bytes 122888 | tf_op jit(solution)/shard_map/ppermute | solution.py:258
  886.6 51.1 %collective-permute-start.78 = (f32[10,1024]{1,0:T(8,128)S(1)}, f32[10,1024]{1,0:T(8,128)S(1)}, u32[]{:S(2)}, u32[]{:S(2)}) collective-permute-start(f32[10,1024]{1,0:T(8,128)S(1)} %concatenate.62), channel_id=1, source_target_pairs={{0,3},{1,2},{2,1},{3,0},{4,7},{5,6},{6,5},{7,4},{8,11},{9,10},{10,... | collective-permute-start | bytes 122888 | tf_op jit(solution)/shard_map/ppermute | solution.py:258
  941.5 31.3 %collective-permute-start.79 = (bf16[36,128,128]{2,1,0:T(8,128)(2,1)S(1)}, bf16[36,128,128]{2,1,0:T(8,128)(2,1)S(1)}, u32[]{:S(2)}, u32[]{:S(2)}) collective-permute-start(bf16[36,128,128]{2,1,0:T(8,128)(2,1)S(1)} %get-tuple-element.600), channel_id=1, source_target_pairs={{0,16},{16,0},{1,17},{17,1},{2,18},{18,2},{3,19},{19,3},{4,20},{20... | collective-permute-start | bytes 3538952 | tf_op jit(solution)/shard_map/ppermute | solution.py:258
  943.0 29.8 %collective-permute-start.80 = (bf16[36,128,128]{2,1,0:T(8,128)(2,1)S(1)}, bf16[36,128,128]{2,1,0:T(8,128)(2,1)S(1)}, u32[]{:S(2)}, u32[]{:S(2)}) collective-permute-start(bf16[36,128,128]{2,1,0:T(8,128)(2,1)S(1)} %get-tuple-element.601), channel_id=1, source_target_pairs={{0,2},{2,0},{1,3},{3,1},{4,6},{6,4},{5,7},{7,5},{8,10},{10,8},{9,1... | collective-permute-start | bytes 3538952 | tf_op jit(solution)/shard_map/ppermute | solution.py:258
  943.4 29.4 %collective-permute-start.81 = (f32[10,1024]{1,0:T(8,128)S(1)}, f32[10,1024]{1,0:T(8,128)S(1)}, u32[]{:S(2)}, u32[]{:S(2)}) collective-permute-start(f32[10,1024]{1,0:T(8,128)S(1)} %add_add_fusion.1), channel_id=1, source_target_pairs={{0,16},{16,0},{1,17},{17,1},{2,18},{18,2},{3,19},{19,3},{4,20},{20... | collective-permute-start | bytes 122888 | tf_op jit(solution)/shard_map/ppermute | solution.py:258
  943.9 28.9 %collective-permute-start.82 = (f32[10,1024]{1,0:T(8,128)S(1)}, f32[10,1024]{1,0:T(8,128)S(1)}, u32[]{:S(2)}, u32[]{:S(2)}) collective-permute-start(f32[10,1024]{1,0:T(8,128)S(1)} %add_add_fusion.1), channel_id=1, source_target_pairs={{0,4},{4,0},{8,12},{12,8},{1,5},{5,1},{9,13},{13,9},{2,6},{6,2},{1... | collective-permute-start | bytes 122888 | tf_op jit(solution)/shard_map/ppermute | solution.py:258
  945.4 27.4 %collective-permute-start.83 = (f32[10,1024]{1,0:T(8,128)S(1)}, f32[10,1024]{1,0:T(8,128)S(1)}, u32[]{:S(2)}, u32[]{:S(2)}) collective-permute-start(f32[10,1024]{1,0:T(8,128)S(1)} %add_add_fusion.1), channel_id=1, source_target_pairs={{0,20},{4,16},{8,28},{12,24},{16,4},{20,0},{24,12},{28,8},{1,21},{... | collective-permute-start | bytes 122888 | tf_op jit(solution)/shard_map/ppermute | solution.py:258
  978.8 19.3 %collective-permute-start.84 = (bf16[24,128,128]{2,1,0:T(8,128)(2,1)S(1)}, bf16[24,128,128]{2,1,0:T(8,128)(2,1)S(1)}, u32[]{:S(2)}, u32[]{:S(2)}) collective-permute-start(bf16[24,128,128]{2,1,0:T(8,128)(2,1)S(1)} %get-tuple-element.615), channel_id=1, source_target_pairs={{0,2},{2,0},{1,3},{3,1},{4,6},{6,4},{5,7},{7,5},{8,10},{10,8},{9,1... | collective-permute-start | bytes 2359304 | tf_op jit(solution)/shard_map/ppermute | solution.py:258
  979.5 19.3 %collective-permute-start.85 = (bf16[24,128,128]{2,1,0:T(8,128)(2,1)S(1)}, bf16[24,128,128]{2,1,0:T(8,128)(2,1)S(1)}, u32[]{:S(2)}, u32[]{:S(2)}) collective-permute-start(bf16[24,128,128]{2,1,0:T(8,128)(2,1)S(1)} %get-tuple-element.616), channel_id=1, source_target_pairs={{0,16},{16,0},{1,17},{17,1},{2,18},{18,2},{3,19},{19,3},{4,20},{20... | collective-permute-start | bytes 2359304 | tf_op jit(solution)/shard_map/ppermute | solution.py:258
  981.1 5.9 collective-permute-start.86
  1000.6 10.2 collective-permute-start.87
  1002.2 9.8 collective-permute-start.88
  1013.9 16.9 %collective-permute-start.89 = (bf16[6,128,128]{2,1,0:T(8,128)(2,1)S(1)}, bf16[6,128,128]{2,1,0:T(8,128)(2,1)S(1)}, u32[]{:S(2)}, u32[]{:S(2)}) collective-permute-start(bf16[6,128,128]{2,1,0:T(8,128)(2,1)S(1)} %get-tuple-element.624), channel_id=1, source_target_pairs={{0,8},{4,12},{1,9},{5,13},{2,10},{6,14},{3,11},{7,15},{16,24},{20,... | collective-permute-start | bytes 589832 | tf_op jit(solution)/shard_map/ppermute | solution.py:258
  1018.6 16.0 %collective-permute-start.90 = (bf16[6,128,128]{2,1,0:T(8,128)(2,1)S(1)}, bf16[6,128,128]{2,1,0:T(8,128)(2,1)S(1)}, u32[]{:S(2)}, u32[]{:S(2)}) collective-permute-start(bf16[6,128,128]{2,1,0:T(8,128)(2,1)S(1)} %get-tuple-element.625), channel_id=1, source_target_pairs={{8,0},{12,4},{9,1},{13,5},{10,2},{14,6},{11,3},{15,7},{24,16},{28,... | collective-permute-start | bytes 589832 | tf_op jit(solution)/shard_map/ppermute | solution.py:258
  1019.9 14.7 %collective-permute-start.91 = (bf16[6,128,128]{2,1,0:T(8,128)(2,1)S(1)}, bf16[6,128,128]{2,1,0:T(8,128)(2,1)S(1)}, u32[]{:S(2)}, u32[]{:S(2)}) collective-permute-start(bf16[6,128,128]{2,1,0:T(8,128)(2,1)S(1)} %get-tuple-element.626), channel_id=1, source_target_pairs={{0,4},{4,8},{8,12},{1,5},{5,9},{9,13},{2,6},{6,10},{10,14},{3,7},{... | collective-permute-start | bytes 589832 | tf_op jit(solution)/shard_map/ppermute | solution.py:258
  1022.0 13.3 %collective-permute-start.92 = (bf16[6,128,128]{2,1,0:T(8,128)(2,1)S(1)}, bf16[6,128,128]{2,1,0:T(8,128)(2,1)S(1)}, u32[]{:S(2)}, u32[]{:S(2)}) collective-permute-start(bf16[6,128,128]{2,1,0:T(8,128)(2,1)S(1)} %get-tuple-element.627), channel_id=1, source_target_pairs={{4,0},{8,4},{12,8},{5,1},{9,5},{13,9},{6,2},{10,6},{14,10},{7,3},{... | collective-permute-start | bytes 589832 | tf_op jit(solution)/shard_map/ppermute | solution.py:258
  1023.3 13.3 %collective-permute-start.93 = (bf16[6,128,128]{2,1,0:T(8,128)(2,1)S(1)}, bf16[6,128,128]{2,1,0:T(8,128)(2,1)S(1)}, u32[]{:S(2)}, u32[]{:S(2)}) collective-permute-start(bf16[6,128,128]{2,1,0:T(8,128)(2,1)S(1)} %get-tuple-element.628), channel_id=1, source_target_pairs={{0,12},{1,13},{2,14},{3,15},{16,28},{17,29},{18,30},{19,31}} | collective-permute-start | bytes 589832 | tf_op jit(solution)/shard_map/ppermute | solution.py:258
  1030.9 15.3 %collective-permute-start.94 = (bf16[6,128,128]{2,1,0:T(8,128)(2,1)S(1)}, bf16[6,128,128]{2,1,0:T(8,128)(2,1)S(1)}, u32[]{:S(2)}, u32[]{:S(2)}) collective-permute-start(bf16[6,128,128]{2,1,0:T(8,128)(2,1)S(1)} %get-tuple-element.629), channel_id=1, source_target_pairs={{12,0},{13,1},{14,2},{15,3},{28,16},{29,17},{30,18},{31,19}} | collective-permute-start | bytes 589832 | tf_op jit(solution)/shard_map/ppermute | solution.py:258
  (46 other events, 627.9 us)
Sparse Core Ops, SparseCore 0:
  10.6 126.3 all-gather.1
  882.5 56.7 reduce-scatter.8
  978.9 52.1 reduce-scatter.10

commit v4 on v3

--- a/solution.py
+++ b/solution.py
@@ -114,12 +114,6 @@
     return places.reshape(ranks, total)
 
 
-def chunks_first(blocks):
-    up = blocks[:128].reshape(8, 16)
-    down = blocks[128:]
-    return [up[:, :8].reshape(-1), down[:64], up[:, 8:].reshape(-1), down[64:]]
-
-
 def copy_in_place(out, source, place, sem):
     row = pl.multiple_of((place // WIDE) * BLOCK, BLOCK)
     column = pl.multiple_of((place % WIDE) * BLOCK, BLOCK)
@@ -128,15 +122,13 @@
     ).start()
 
 
-def unsort(slots, sources, places, chunks, listed):
+def unsort(slots, sources, places, chunks, into=None):
     count = sources.shape[0]
     each = max(n for n in range(1, 65) if count % n == 0)
     steps = count // each
 
     def body(source_ref, place_ref, slots_ref, *rest):
-        out = rest[0]
-        list_ref = rest[1] if listed else None
-        held, read_sem, write_sem, list_sem = rest[-4:]
+        out, held, read_sem, write_sem = rest[-4:]
         step = pl.program_id(0)
         slot = lax.rem(step, 2)
 
@@ -151,8 +143,6 @@
 
         def written(number, into):
             pltpu.make_async_copy(held.at[into], held.at[into], write_sem.at[into]).wait()
-            if listed:
-                pltpu.make_async_copy(held.at[into], held.at[into], list_sem.at[into]).wait()
 
         @pl.when(step == 0)
         def _():
@@ -173,69 +163,29 @@
             return unused
 
         lax.fori_loop(0, each, one, 0)
-        if listed:
-            pltpu.make_async_copy(
-                held.at[slot], list_ref.at[pl.ds(step * each, each)], list_sem.at[slot]
-            ).start()
 
         @pl.when(step == steps - 1)
         def _():
             written(step, slot)
 
-    shapes = [jax.ShapeDtypeStruct((chunks * D, D), bf16)]
-    if listed:
-        shapes.append(jax.ShapeDtypeStruct((count, BLOCK, BLOCK), bf16))
+    operands = [sources, places, slots]
+    if into is not None:
+        operands.append(into)
     return pl.pallas_call(
         body,
         grid=(steps,),
-        out_shape=tuple(shapes),
-        in_specs=[SMEM, SMEM, ANY],
-        out_specs=(ANY,) * len(shapes),
+        out_shape=jax.ShapeDtypeStruct((chunks * D, D), bf16),
+        in_specs=[SMEM, SMEM] + [ANY] * (len(operands) - 2),
+        out_specs=ANY,
         scratch_shapes=[
             pltpu.VMEM((2, each, BLOCK, BLOCK), bf16),
             pltpu.SemaphoreType.DMA((2,)),
             pltpu.SemaphoreType.DMA((2,)),
-            pltpu.SemaphoreType.DMA((2,)),
         ],
+        input_output_aliases={} if into is None else {3: 0},
         compiler_params=params(has_side_effects=True),
-        cost_estimate=cost(0, 3 * count * BLOCK * BLOCK * 2),
+        cost_estimate=cost(0, 2 * count * BLOCK * BLOCK * 2),
         name="unsort",
-    )(sources, places, slots)
-
-
-def place_weights(weights, arrays, bases, places):
-    count = arrays[0].shape[0]
-    number = len(arrays)
-    each = max(n for n in range(1, 128 // number + 1) if count % n == 0)
-
-    def body(table, base_ref, *rest):
-        sources = rest[:number]
-        out, sem = rest[-2], rest[-1]
-        start = pl.program_id(0) * each
-
-        def one(t, unused):
-            for a, source in enumerate(sources):
-                copy_in_place(out, source.at[t], table[base_ref[a] + start + t], sem.at[a])
-            return unused
-
-        lax.fori_loop(0, each, one, 0)
-        for a, source in enumerate(sources):
-            pltpu.make_async_copy(source, source, sem.at[a]).wait()
-
-    operands = [places, jnp.stack(bases).astype(jnp.int32), *arrays, weights]
-    return pl.pallas_call(
-        body,
-        grid=(count // each,),
-        out_shape=jax.ShapeDtypeStruct(weights.shape, bf16),
-        in_specs=[SMEM, SMEM]
-        + [pl.BlockSpec((each, BLOCK, BLOCK), lambda n: (n, 0, 0))] * number
-        + [ANY],
-        out_specs=ANY,
-        scratch_shapes=[pltpu.SemaphoreType.DMA((number,))],
-        input_output_aliases={len(operands) - 1: 0},
-        compiler_params=params(has_side_effects=True),
-        cost_estimate=cost(0, 2 * number * count * BLOCK * BLOCK * 2),
-        name="place_weights",
     )(*operands)
 
 
@@ -430,6 +380,10 @@
             @pl.when(step == 0)
             def _(new=new, here=here):
                 total[here] = new
+
+            @pl.when((step > 0) & (step < steps - 1))
+            def _(new=new, here=here):
+                total[here] += new
 
             @pl.when(step == steps - 1)
             def _(new=new, here=here):
@@ -1714,115 +1668,52 @@
         low = master[0].astype(bf16)
         if fast:
             across = 1 - rank
-            core_at = coords[2]
-            own_places = places[rank]
-            all_places = np.concatenate(
-                [
-                    part
-                    for own in weight_places(ranks)
-                    for part in [
-                        *chunks_first(own[: starts[1]]),
-                        own[starts[1] : starts[3]],
-                        *chunks_first(own[starts[3] :]),
-                    ]
-                ]
-            )
-            all_places = jnp.asarray(all_places)
-            column = lax.all_gather(low, ("z", "x", "core"), axis=0, tiled=True)
+            dp = ("z", "x", "core")
             normed_own = norm_rows(stream, gain(0))
-            normed_other = swap(normed_own, "mp")
+            low_other, normed_other = swap(low, "mp"), swap(normed_own, "mp")
+            column = lax.all_gather(low, dp, axis=0, tiled=True)
             column, normed_other, table, arrivals, good, windows, masks = tied(
                 column, normed_other, table, arrivals, good, windows, masks
             )
-
-            def own_part(group):
-                here = slice(starts[group], starts[group + 1])
-                slot, place = owners[0, here], own_places[here]
-                if group in (0, 3):
-                    slot = jnp.concatenate(chunks_first(slot))
-                    place = jnp.concatenate(chunks_first(place))
-                return unsort(column, slot, place, GROUP_CHUNKS[group], True)
-
-            def outgoing(listed, first, count):
-                half = count // 2
-                return lax.dynamic_slice_in_dim(listed, first + core_at * half, half)
-
-            def put(weights, one, two, group, first):
-                base = across * blocks + starts[group] + first
-                half = one.shape[0]
-                return place_weights(
-                    weights, [one, two],
-                    [base + core_at * half, base + (1 - core_at) * half], all_places,
+            low_other, column = tied(low_other, column)
+            column_other = lax.all_gather(low_other, dp, axis=0, tiled=True)
+
+            def of_index(slots, index, number, into=None):
+                here = slice(starts[number], starts[number + 1])
+                return unsort(
+                    slots, owners_all[index, here], places[index, here], GROUP_CHUNKS[number], into
                 )
 
-            w_attn, list_attn = own_part(1)
-            send_attn = outgoing(list_attn, 0, 96)
-
-            def first_half():
-                w_one, list_one = own_part(0)
-                (product,) = ffn_part(normed_other, w_one, UP1, DOWN1, 2 * rank, 2, False)
-                return w_one, list_one, product
-
-            w_one, list_one, product = first_half()
-            (come_attn,), (w_one, list_one, product) = together(
-                [(send_attn, "mp")], w_one, list_one, product
-            )
+            w_one = of_index(column, rank, 0)
+            (product,) = ffn_part(normed_other, w_one, UP1, DOWN1, 2 * rank, 2, False)
             own_product, pre_first = ffn_part(normed_own, w_one, UP1, DOWN1, 2 * rank, 2, True)
-            w_conv, list_conv = own_part(2)
-            w_two, list_two = own_part(3)
-            (product, beside), (own_product, w_conv, list_conv, w_two, list_two) = together(
-                [(product, "mp"), (come_attn, "core")], own_product, w_conv, list_conv, w_two,
-                list_two,
+            w_attn, w_conv, w_two = [of_index(column, rank, number) for number in (1, 2, 3)]
+            (product,), (own_product, w_attn, w_conv, w_two) = together(
+                [(product, "mp")], own_product, w_attn, w_conv, w_two
             )
             after_first, normed_attn = join(stream, [own_product, product], gain(1))
-            w_attn = put(w_attn, come_attn, beside, 1, 0)
-
+            (other,), unused = together([(normed_attn, "mp")])
+            column_other, other = tied(column_other, other)
+
+            w_attn = of_index(column_other, across, 1, w_attn)
             queries = project(normed_attn, w_attn, QUERY, 1)
             keys = project(normed_attn, w_attn, KEY, 2, rank, 2)
-            sends = [
-                outgoing(list_attn, 96, 32),
-                outgoing(list_conv, 0, 96),
-                outgoing(list_two, 0, 64),
-                outgoing(list_two, 64, 48),
-                outgoing(list_two, 112, 144),
-                outgoing(list_one, 0, 128),
-                outgoing(list_one, 128, 128),
-            ]
-            (other,), (queries, keys, *sends) = together(
-                [(normed_attn, "mp")], queries, keys, *sends
-            )
             keys = project(other, w_attn, KEY, 2, across, 2, keys)
             attended, logs = attention_forward(
                 queries, keys, segment_ids, rank, windows, slopes
             )
-            come, (attended, logs) = together([(send, "mp") for send in sends[:3]], attended, logs)
-            beside, unused = together([(value, "core") for value in come])
-            more_two, send_two, *send_one = sends[3:]
-            more_two, *beside = tied(more_two, *beside)
-            w_attn = put(w_attn, come[0], beside[0], 1, 96)
-            w_conv = put(w_conv, come[1], beside[1], 2, 0)
-            w_two = put(w_two, come[2], beside[2], 3, 0)
             after_attn = project_out(attended, w_attn, OUT, after_first)
-            (more_two,), (after_attn, w_conv, w_two) = together(
-                [(more_two, "mp")], after_attn, w_conv, w_two
-            )
+            w_conv = of_index(column_other, across, 2, w_conv)
+            w_two = of_index(column_other, across, 3, w_two)
+            w_one = of_index(column_other, across, 0, tied(w_one, own_product)[0])
             before, behind = edges(after_attn[:HALO], after_attn[-HALO:], ranks)
-            send_two, before, behind = tied(send_two, before, behind)
             after_conv, linear, gate, normed_two = conv_forward(
                 after_attn, before, behind, gain(2), gain(3), w_conv, kernel, masks
             )
-            own_product, pre_second = ffn_part(normed_two, w_two, UP2, DOWN2, 2 * rank, 2, True)
-            (two, beside), (own_product, pre_second, w_two) = together(
-                [(send_two, "mp"), (more_two, "core")], own_product, pre_second, w_two
+            product, pre_second = ffn_part(
+                normed_two, w_two, UP2, DOWN2, jnp.zeros((), jnp.int32), 4, True
             )
-            w_two = put(w_two, more_two, beside, 3, 64)
-            two, *send_one = tied(two, *send_one)
-            (beside,), (w_two,) = together([(two, "core")], w_two)
-            w_two = put(w_two, two, beside, 3, 112)
-            product, pre_second = ffn_part(
-                normed_two, w_two, UP2, DOWN2, 2 * across, 2, True, pre_second
-            )
-            after_second, output = join(after_conv, [own_product, product], gain(4))
+            after_second, output = join(after_conv, [product], gain(4))
             sources = [(normed_attn, rank), (other, across)]
         else:
             everything = lax.all_gather(low, ("mp", "z", "x", "core"), axis=0, tiled=True)
@@ -1830,10 +1721,11 @@
             arrays = []
             for number, chunks in enumerate(GROUP_CHUNKS):
                 here = slice(starts[number], starts[number + 1])
-                arrays += unsort(
+                array = unsort(
                     everything, slot_of[:, here].reshape(-1).astype(jnp.int32),
-                    places[:, here].reshape(-1), chunks, False,
+                    places[:, here].reshape(-1), chunks,
                 )
+                arrays.append(array)
             w_one, w_attn, w_conv, w_two = arrays
             after_first, pre_first, normed_attn = ffn_forward(
                 stream, gain(0), gain(1), w_one, UP1, DOWN1
@@ -1866,26 +1758,19 @@
             UP2, DOWN2, sums, table, ranks,
         )
         if fast:
-            (come_one,), (grad_conv, gains_a, *sums) = together(
-                [(send_one[0], "mp")], grad_conv, gains_a, *sums
-            )
             rounds = Rounds(*sums)
             rounds.add_round(0)
             sums = rounds.hold()
         before, behind = edges(
             grad_conv[:HALO].astype(bf16), grad_conv[-HALO:].astype(bf16), ranks
         )
-        if fast:
-            send_last, before, behind = tied(send_one[1], before, behind)
         grad_attn, gains_b, tap_grads, *sums = conv_backward(
             grad_conv, before, behind, after_attn, gain(2), linear, gate, w_conv, kernel, masks,
             sums, table, ranks,
         )
         if fast:
-            rounds.add("first", both_swaps(come_one, ["core"]))
-            rounds.add("second", both_swaps(send_last, ["mp", "core"]))
             grad_attn, gains_b, tap_grads = rounds.step(
-                [0, "first", "second"], grad_attn, gains_b, tap_grads, sums=sums
+                [0], grad_attn, gains_b, tap_grads, sums=sums
             )
             rounds.add_round(1)
             sums = rounds.hold()
@@ -1898,7 +1783,7 @@
         if fast:
             away = input_gradient(key_grad, value_grad, w_attn, 1 - rank, rows)
             query_grad, key_grad, value_grad, away = rounds.step(
-                [0, 1, "second"], query_grad, key_grad, value_grad, away, sums=sums
+                [0, 1], query_grad, key_grad, value_grad, away, sums=sums
             )
             sums = rounds.hold()
         else:
@@ -1908,11 +1793,8 @@
             normed_attn, query_grad, key_grad, value_grad, sources, fast, w_attn, sums, table, ranks
         )
         if fast:
-            (beside,), (second, more) = rounds.results.pop("first"), rounds.results.pop("second")
-            beside, more, away = tied(beside, more, away)
-            w_one = put(put(w_one, come_one, beside, 0, 0), second, more, 0, 128)
             rounds.add("away", both_swaps(away, ["mp"]))
-            near, w_one = rounds.step(["away"], near, w_one, sums=sums)
+            (near,) = rounds.step(["away"], near, sums=sums)
             (arrived,) = rounds.results.pop("away")
             rounds.add_round(2)
             sums = rounds.hold()

time: 1090 us -> 1040 us (0.954)
  Pallas kernels: 560 us -> 516 us
  starting transfers between devices: 77.4 us -> 108 us
  local copies, waits for them, and re-layouts: 57.5 us -> 36.8 us
    all_gather x1 -> x2, waiting for transfers between devices: 71 us -> 45.2 us  [the longest x1 45.2 us: run(): column = lax.all_gather(low, dp, axis=0, tiled=True)]
    ppermute x60 -> x45, starting transfers between devices: 68.2 us -> 92.7 us  [swap(): return lax.ppermute(value, axis, pairs)]
    ppermute x60 -> x45, waiting for transfers between devices: 217 us -> 240 us  [swap(): return lax.ppermute(value, axis, pairs)]
    dynamic_slice x7 -> x1, local copies, waits for them, and re-layouts: 17.3 us -> 0.67 us  [of_index(): places[index, here]]
    pallas_call x1, Pallas kernels: 60.7 us -> 45.5 us  [attention_backward(): pl.pallas_call(body, grid=(HEADS, rows // tall), out_shape=(jax.ShapeDtyp...]
    pallas_call x1, Pallas kernels: 50.1 us -> 35.8 us  [attention_forward(): pl.pallas_call(body, grid=(HEADS, rows // tall), out_shape=(jax.ShapeDtyp...]
    pallas_call x12 -> x8, Pallas kernels: 64.5 us -> 55.7 us  [unsort(): pl.pallas_call(body, grid=(steps,), out_shape=jax.ShapeDtypeStruct((chunk...]
    pallas_call x4 -> x3, Pallas kernels: 65 us -> 60 us  [ffn_part(): pl.pallas_call(body, grid_spec=pltpu.PrefetchScalarGridSpec(num_scalar_pr...]
  transfers between devices with their start and end apart: 67 -> 53, of which waited for: 28 -> 20; matrix products, arithmetic and copies ran while one was open for 7% -> 4% of each run, Pallas kernels for 49% -> 30%
where the time goes in v4:
time: 1040 us; the launch traced here: 1030 us
  Pallas kernels  516 us (50%)
  waiting for transfers between devices  287 us (28%)
  starting transfers between devices  108 us (10%)
  other arithmetic  63.3 us (6%)
  local copies, waits for them, and re-layouts  36.8 us (4%)
  between operations  17.4 us (2%)
    ppermute x45, waiting for transfers between devices, swap(): return lax.ppermute(value, axis, pairs)  240 us
    pallas_call x3, Pallas kernels, ffn_backward(): pl.pallas_call(body, grid=(steps,), out_shape=(jax.ShapeDtypeStruct((rows...  141 us
    ppermute x45, starting transfers between devices, swap(): return lax.ppermute(value, axis, pairs)  92.7 us
    pallas_call x3, Pallas kernels, ffn_part(): pl.pallas_call(body, grid_spec=pltpu.PrefetchScalarGridSpec(num_scalar_pr...  60 us
    pallas_call x8, Pallas kernels, unsort(): pl.pallas_call(body, grid=(steps,), out_shape=jax.ShapeDtypeStruct((chunk...  55.7 us
    convert_element_type x16, other arithmetic, added(): return sum((term.astype(f32) for term in terms)).astype(bf16)  47.9 us
    pallas_call x1, Pallas kernels, attention_backward(): pl.pallas_call(body, grid=(HEADS, rows // tall), out_shape=(jax.ShapeDtyp...  45.5 us
    all_gather x1, waiting for transfers between devices, run(): column = lax.all_gather(low, dp, axis=0, tiled=True)  45.2 us
  transfers between devices with their start and end apart: 53, of which 20 were waited for; matrix products, arithmetic and copies ran while one was open for 4% of the time, Pallas kernels for 30%

profile of v4, /device:TPU:0, one launch (start us, length us, event | category | flops | bytes accessed | tf_op | source)
XLA Modules:
  0.0 1031.0 jit_solution(15806446103504325302)
XLA Ops:
  7.2 3.2 bitcast_convert_fusion
  10.6 3.0 collective-permute-start.34
  14.3 4.4 norm_rows.1.x_ref
  23.7 24.1 %collective-permute-done.33 = s32[1,736]{1,0:T(1,128)S(1)} collective-permute-done((s32[1,736]{1,0:T(1,128)S(1)}, s32[1,736]{1,0:T(1,128)S(1)}, u32[]{:S(2)}, u32[]{:S(2)}) %collective-permute-start.33) | collective-permute-done | bytes 2976 | tf_op jit(solution)/shard_map/ppermute | solution.py:208
  53.9 37.9 %collective-permute-done.32.x_ref = bf16[1024,1024]{1,0:T(8,128)(2,1)S(1)} collective-permute-done((bf16[1024,1024]{1,0:T(8,128)(2,1)}, bf16[1024,1024]{1,0:T(8,128)(2,1)S(1)}, u32[]{:S(2)}, u32[]{:S(2)}) %collective-permute-start.32) | collective-permute-done | bytes 2097184 | tf_op jit(solution)/shard_map/ppermute | solution.py:208
  91.8 45.2 %all-gather.3.cloned.1.call-done.slots_ref = bf16[736,128,128]{2,1,0:T(8,128)(2,1)} async-done(((bf16[46,128,128]{2,1,0:T(8,128)(2,1)}), bf16[736,128,128]{2,1,0:T(8,128)(2,1)}) %all-gather.3.cloned.1.call-update) | async-done | bytes 24117264 | tf_op jit(solution)/shard_map/all_gather | solution.py:1674
  139.9 9.4 unsort.8.up_ref.down_ref.rest_0_
  149.3 15.5 %ffn_part.3 = bf16[1024,1024]{1,0:T(8,128)(2,1)} custom-call(s32[1]{0:T(128)} %bitcast.25.part_ref, bf16[1024,1024]{1,0:T(8,128)(2,1)} %copy-done.11, bf16[8192,1024]{1,0:T(8,128)(2,1)} %unsort.8.up_ref.down_ref.rest_0_, bf16[8192,1024]{1,0:T(8,128)(2,1)} %unsort.8.up_ref.down_ref.rest_0_), custom_call_target="tpu_custom_call" | custom-call | flops 8589934592 | bytes 8388608 | tf_op jit(solution)/shard_map/ffn_part/pallas_call | solution.py:408
  167.3 4.6 unsort.10.rest_0_
  172.0 5.1 unsort.9.rest_0_
  177.1 8.8 unsort.11.rest_0_
  185.9 16.4 %ffn_part.4 = (bf16[1024,1024]{1,0:T(8,128)(2,1)}, bf16[1024,4096]{1,0:T(8,128)(2,1)}) custom-call(s32[1]{0:T(128)} %bitcast.25.part_ref, bf16[1024,1024]{1,0:T(8,128)(2,1)} %norm_rows.1.x_ref, bf16[8192,1024]{1,0:T(8,128)(2,1)} %unsort.8.up_ref.down_ref.rest_0_, bf16[8192,1024]{1,0:T(8,128)(2,1)} %unsort.8.up_ref.down_ref.rest_0_), custom_call_target="tpu_custom_call" | custom-call | flops 8589934592 | bytes 8388608 | tf_op jit(solution)/shard_map/ffn_part/pallas_call | solution.py:408
  202.3 10.4 %collective-permute-done.35.refs_1_ = bf16[1024,1024]{1,0:T(8,128)(2,1)S(1)} collective-permute-done((bf16[1024,1024]{1,0:T(8,128)(2,1)}, bf16[1024,1024]{1,0:T(8,128)(2,1)S(1)}, u32[]{:S(2)}, u32[]{:S(2)}) %collective-permute-start.35) | collective-permute-done | bytes 2097184 | tf_op jit(solution)/shard_map/ppermute | solution.py:208
  214.1 6.2 join.2
  223.3 44.2 %collective-permute-done.36.x_ref.refs_1_ = bf16[1024,1024]{1,0:T(8,128)(2,1)S(1)} collective-permute-done((bf16[1024,1024]{1,0:T(8,128)(2,1)}, bf16[1024,1024]{1,0:T(8,128)(2,1)S(1)}, u32[]{:S(2)}, u32[]{:S(2)}) %collective-permute-start.36) | collective-permute-done | bytes 2097184 | tf_op jit(solution)/shard_map/ppermute | solution.py:208
  267.5 5.4 unsort.12.w_ref.wk_ref.wv_ref.refs_6_
  273.0 5.9 project.3.q_ref
  278.8 8.3 project.4.rest_0_
  287.1 8.3 project.5.key_ref.value_ref
  295.4 35.8 %attention_forward.1 = (bf16[1024,1024]{1,0:T(8,128)(2,1)}, f32[8,1,1024]{2,1,0:T(1,128)}) custom-call(s32[1]{0:T(128)} %bitcast.20.part_ref.rank_ref.refs_10_.refs_6_, s32[4]{0:T(128)} %reshape.309.window_ref, f32[8]{0:T(128)} %multiply_power_fusion.slope_ref, bf16[1024,1024]{1,0:T(8,128)(2,1)} %project.3.q_ref, s32[1024,1]{1,0:T(8,128)} %copy.50.own_ref, ...), custom_call_target="tpu_custom_call" | custom-call | tf_op jit(solution)/shard_map/attention_forward/pallas_call | solution.py:974
  331.2 7.3 project_out.1.x_ref
  340.7 8.2 collective-permute-start.37
  348.9 9.0 unsort.14.up_ref.down_ref.refs_5_.refs_6_
  357.8 4.6 unsort.13.value_ref.gate_ref.out_w_ref.gate_w_ref
  363.1 20.3 %conv_forward.1 = (f32[1024,1024]{1,0:T(8,128)}, bf16[1056,1024]{1,0:T(8,128)(2,1)}, bf16[1056,1024]{1,0:T(8,128)(2,1)}, bf16[1024,1024]{1,0:T(8,128)(2,1)}) custom-call(f32[1024,1024]{1,0:T(8,128)} %project_out.1.x_ref, f32[16,1024]{1,0:T(8,128)} %copy-done.34, f32[16,1024]{1,0:T(8,128)} %copy-done.33, f32[1,1024]{1,0:T(1,128)} %get-tuple-element.590.gain_ref, ...), custom_call_target="tpu_custom_call" | custom-call | flops 6442450944 | bytes 18874368 | tf_op jit(solution)/shard_map/conv_forward/pallas_call | solution.py:1129
  383.3 28.1 %ffn_part.5 = (bf16[1024,1024]{1,0:T(8,128)(2,1)}, bf16[1024,4096]{1,0:T(8,128)(2,1)}) custom-call(s32[1]{0:T(128)} %constant.391.clone.1.part_ref, bf16[1024,1024]{1,0:T(8,128)(2,1)} %get-tuple-element.303.x_ref, bf16[8192,1024]{1,0:T(8,128)(2,1)} %unsort.14.up_ref.down_ref.refs_5_.refs_6_, bf16[8192,1024]{1,0:T(8,128)(2,1)} %unsort.14.up_ref.down_ref.refs_5_.refs_6_), custom_call_target="tpu_custom_call" | custom-call | flops 17179869184 | bytes 16777216 | tf_op jit(solution)/shard_map/ffn_part/pallas_call | solution.py:408
  411.4 5.8 join.3
  417.2 60.8 %ffn_backward.3 = (f32[1024,1024]{1,0:T(8,128)}, f32[2,1024]{1,0:T(2,128)}, bf16[1184,128,128]{2,1,0:T(8,128)(2,1)}, bf16[288,128,128]{2,1,0:T(8,128)(2,1)}) custom-call(s32[1472]{0:T(1024)} %reshape.307.table_ref, f32[1024,1024]{1,0:T(8,128)} %get-tuple-element.308.refs_0_, f32[1,1024]{1,0:T(1,128)} %get-tuple-element.588.refs_1_, ...), custom_call_target="tpu_custom_call" | custom-call | flops 34359738368 | bytes 33554432 | tf_op jit(solution)/shard_map/ffn_backward/pallas_call | solution.py:600
  478.1 4.9 slice.571
  482.9 8.2 collective-permute-start.39
  492.8 4.5 collective-permute-start.40
  499.5 43.0 %conv_backward.1 = (f32[1024,1024]{1,0:T(8,128)}, f32[1,1024]{1,0:T(1,128)}, f32[5,1024]{1,0:T(8,128)}, bf16[1184,128,128]{2,1,0:T(8,128)(2,1)}, bf16[288,128,128]{2,1,0:T(8,128)(2,1)}) custom-call(s32[1472]{0:T(1024)} %reshape.307.table_ref, f32[1024,1024]{1,0:T(8,128)} %get-tuple-element.312.g_ref, ...), custom_call_target="tpu_custom_call", output_to_operand_aliasing={{3}: (13, {}), {4}: (14, {})} | custom-call | flops 12884901888 | bytes 29360128 | tf_op jit(solution)/shard_map/conv_backward/pallas_call | solution.py:1312
  542.6 5.5 slice.578
  548.1 4.0 add_convert_fusion.38
  552.1 3.4 collective-permute-start.42
  559.8 10.0 project_out_back.1
  569.7 45.5 %attention_backward.1 = (bf16[1024,1024]{1,0:T(8,128)(2,1)}, bf16[2048,1024]{1,0:T(8,128)(2,1)}, bf16[2048,1024]{1,0:T(8,128)(2,1)}) custom-call(s32[1]{0:T(128)} %bitcast.20.part_ref.rank_ref.refs_10_.refs_6_, s32[4]{0:T(128)} %reshape.309.window_ref, f32[8]{0:T(128)} %multiply_power_fusion.slope_ref, bf16[1024,1024]{1,0:T(8,128)(2,1)} %project.3.q_ref, ...), custom_call_target="tpu_custom_call" | custom-call | tf_op jit(solution)/shard_map/attention_backward/pallas_call | solution.py:1057
  615.3 8.7 input_gradient.1
  625.8 6.1 collective-permute-start.45
  634.5 3.1 add_convert_fusion.50
  637.6 32.9 %projections_back.1 = (f32[1024,1024]{1,0:T(8,128)}, bf16[1184,128,128]{2,1,0:T(8,128)(2,1)}, bf16[288,128,128]{2,1,0:T(8,128)(2,1)}) custom-call(s32[2]{0:T(128)} %pad_add_fusion.2.part_ref, s32[1472]{0:T(1024)} %reshape.307.table_ref, bf16[1024,1024]{1,0:T(8,128)(2,1)} %get-tuple-element.293.x_ref.n_ref.refs_0_, ...), custom_call_target="tpu_custom_call", output_to_operand_aliasing={{1}: (11, {}), {2}: (12, {})} | custom-call | flops 17179869184 | bytes 31457280 | tf_op jit(solution)/shard_map/projections_back/pallas_call | solution.py:885
  670.6 4.8 slice.589
  675.4 9.7 collective-permute-start.50
  685.1 8.8 unsort.15.refs_7_.refs_8_.refs_3_.refs_4_
  695.2 8.0 collective-permute-start.47
  704.9 39.5 %ffn_backward.4 = (f32[1024,1024]{1,0:T(8,128)}, f32[2,1024]{1,0:T(2,128)}, bf16[1184,128,128]{2,1,0:T(8,128)(2,1)}, bf16[288,128,128]{2,1,0:T(8,128)(2,1)}, f32[1024,1024]{1,0:T(8,128)}) custom-call(s32[1472]{0:T(1024)} %reshape.307.table_ref, f32[1024,1024]{1,0:T(8,128)} %get-tuple-element.299.s_ref.refs_0_, ...), custom_call_target="tpu_custom_call", output_to_operand_aliasing={{2}: (12, {}), {3}: (13, {})} | custom-call | flops 17179869184 | bytes 16777216 | tf_op jit(solution)/shard_map/ffn_backward/pallas_call | solution.py:600
  744.5 4.2 add_convert_fusion.36
  753.4 5.1 collective-permute-start.51
  760.7 41.1 %ffn_backward.5 = (f32[1024,1024]{1,0:T(8,128)}, f32[2,1024]{1,0:T(2,128)}, bf16[1184,128,128]{2,1,0:T(8,128)(2,1)}, bf16[288,128,128]{2,1,0:T(8,128)(2,1)}) custom-call(s32[1472]{0:T(1024)} %reshape.307.table_ref, f32[1024,1024]{1,0:T(8,128)} %get-tuple-element.393.refs_0_, ...), custom_call_target="tpu_custom_call", output_to_operand_aliasing={{2}: (9, {}), {3}: (10, {})} | custom-call | flops 17179869184 | bytes 16777216 | tf_op jit(solution)/shard_map/ffn_backward/pallas_call | solution.py:600
  801.9 4.1 add_convert_fusion.46
  806.2 4.0 slice.620
  815.0 9.8 collective-permute-done.55
  825.3 6.4 add_convert_fusion.30
  841.5 49.8 %collective-permute-done.62 = f32[10,1024]{1,0:T(8,128)S(1)} collective-permute-done((f32[10,1024]{1,0:T(8,128)S(1)}, f32[10,1024]{1,0:T(8,128)S(1)}, u32[]{:S(2)}, u32[]{:S(2)}) %collective-permute-start.62) | collective-permute-done | bytes 40992 | tf_op jit(solution)/shard_map/ppermute | solution.py:208
  891.3 3.8 add_convert_fusion.34
  904.0 22.3 %collective-permute-done.66 = f32[10,1024]{1,0:T(8,128)S(1)} collective-permute-done((f32[10,1024]{1,0:T(8,128)S(1)}, f32[10,1024]{1,0:T(8,128)S(1)}, u32[]{:S(2)}, u32[]{:S(2)}) %collective-permute-start.66) | collective-permute-done | bytes 40992 | tf_op jit(solution)/shard_map/ppermute | solution.py:208
  926.3 4.3 add_convert_fusion.33
  935.3 5.3 collective-permute-done.71
  940.5 10.9 %collective-permute-done.69 = bf16[24,128,128]{2,1,0:T(8,128)(2,1)S(1)} collective-permute-done((bf16[24,128,128]{2,1,0:T(8,128)(2,1)S(1)}, bf16[24,128,128]{2,1,0:T(8,128)(2,1)S(1)}, u32[]{:S(2)}, u32[]{:S(2)}) %collective-permute-start.69) | collective-permute-done | bytes 786464 | tf_op jit(solution)/shard_map/ppermute | solution.py:208
  956.5 7.6 collective-permute-done.72
  969.8 5.6 collective-permute-start.76
  976.8 7.5 collective-permute-start.78
  989.1 9.3 collective-permute-done.79
  1007.4 16.6 %shampoo.1 = (f32[46,128,128]{2,1,0:T(8,128)}, f32[46,128,128]{2,1,0:T(8,128)}, f32[46,128,128]{2,1,0:T(8,128)}, f32[46,128,128]{2,1,0:T(8,128)}, f32[46,128,128]{2,1,0:T(8,128)}) custom-call(s32[48]{0:T(128)} %pad.14.index_ref, bf16[92,128,128]{2,1,0:T(8,128)(2,1)S(1)} %get-tuple-element.647.refs_0_.refs_1_.refs_2_.refs_3_.refs_4_.refs_5_.refs_6_.refs_7_, ...), custom_call_target="tpu_custom_call" | custom-call | tf_op jit(solution)/shard_map/shampoo/pallas_call | solution.py:1397
  (235 shorter events, 98.9 us)
Async XLA Ops:
  7.2 129.8 %all-gather.3.cloned.1.call-start = ((), (), s32[]{:S(2)}) async-start(), calls=%async_computation.6 | async-start | bytes 25624576 | tf_op jit(solution)/shard_map/all_gather | solution.py:1674
  10.5 10.7 %copy-start.27 = (s32[1,2048]{1,0:T(1,128)S(1)}, s32[1,2048]{1,0:T(1,128)}, u32[]{:S(2)}) copy-start(s32[1,2048]{1,0:T(1,128)} %columns_ref.1) | copy-start | bytes 24580
  10.5 257.0 %all-gather.5.cloned.1.call-start = ((), (), s32[]{:S(2)}) async-start(), calls=%async_computation.7 | async-start | bytes 25624576 | tf_op jit(solution)/shard_map/all_gather | solution.py:1679
  10.6 128.4 %collective-permute-start.34 = (bf16[46,128,128]{2,1,0:T(8,128)(2,1)}, bf16[46,128,128]{2,1,0:T(8,128)(2,1)}, u32[]{:S(2)}, u32[]{:S(2)}) collective-permute-start(bf16[46,128,128]{2,1,0:T(8,128)(2,1)} %bitcast_convert_fusion), channel_id=1, source_target_pairs={{0,16},{16,0},{1,17},{17,1},{2,18},{18,2},{3,19},{19,3},{4,20},{20... | collective-permute-start | bytes 4521992 | tf_op jit(solution)/shard_map/ppermute | solution.py:208
  13.6 34.1 %collective-permute-start.33 = (s32[1,736]{1,0:T(1,128)S(1)}, s32[1,736]{1,0:T(1,128)S(1)}, u32[]{:S(2)}, u32[]{:S(2)}) collective-permute-start(s32[1,736]{1,0:T(1,128)S(1)} %copy-done.39), channel_id=1, source_target_pairs={{0,16},{16,0},{1,17},{17,1},{2,18},{18,2},{3,19},{19,3},{4,20},{20... | collective-permute-start | bytes 8840 | tf_op jit(solution)/shard_map/ppermute | solution.py:208
  18.7 73.1 %collective-permute-start.32 = (bf16[1024,1024]{1,0:T(8,128)(2,1)}, bf16[1024,1024]{1,0:T(8,128)(2,1)S(1)}, u32[]{:S(2)}, u32[]{:S(2)}) collective-permute-start(bf16[1024,1024]{1,0:T(8,128)(2,1)} %norm_rows.1.x_ref), channel_id=1, source_target_pairs={{0,16},{16,0},{1,17},{17,1},{2,18},{18,2},{3,19},{19,3},{4,20},{20... | collective-permute-start | bytes 6291464 | tf_op jit(solution)/shard_map/ppermute | solution.py:208
  21.8 199.9 %copy-start.35 = (s32[1,1024]{1,0:T(1,128)}, s32[1,1024]{1,0:T(1,128)S(1)}, u32[]{:S(2)}) copy-start(s32[1,1024]{1,0:T(1,128)S(1)} %get-tuple-element.494.own_ref) | copy-start | bytes 12292
  49.3 90.0 %copy-start.41 = (s32[2,736]{1,0:T(2,128)S(1)}, s32[2,736]{1,0:T(2,128)}, u32[]{:S(2)}) copy-start(s32[2,736]{1,0:T(2,128)} %constant.397.clone) | copy-start | bytes 17668
  91.8 57.5 %copy-start.11 = (bf16[1024,1024]{1,0:T(8,128)(2,1)}, bf16[1024,1024]{1,0:T(8,128)(2,1)S(1)}, u32[]{:S(2)}) copy-start(bf16[1024,1024]{1,0:T(8,128)(2,1)S(1)} %collective-permute-done.32.x_ref) | copy-start | bytes 6291460
  139.0 859.7 %reduce-scatter.9.cloned.1.call-start = ((), (), s32[]{:S(2)}) async-start(), calls=%async_computation.8 | async-start | bytes 3604480 | tf_op jit(solution)/shard_map/reduce_scatter | solution.py:1586
  164.8 48.0 %collective-permute-start.35 = (bf16[1024,1024]{1,0:T(8,128)(2,1)}, bf16[1024,1024]{1,0:T(8,128)(2,1)S(1)}, u32[]{:S(2)}, u32[]{:S(2)}) collective-permute-start(bf16[1024,1024]{1,0:T(8,128)(2,1)} %ffn_part.3), channel_id=1, source_target_pairs={{0,16},{16,0},{1,17},{17,1},{2,18},{18,2},{3,19},{19,3},{4,20},{20... | collective-permute-start | bytes 6291464 | tf_op jit(solution)/shard_map/ppermute | solution.py:208
  220.3 47.3 %collective-permute-start.36 = (bf16[1024,1024]{1,0:T(8,128)(2,1)}, bf16[1024,1024]{1,0:T(8,128)(2,1)S(1)}, u32[]{:S(2)}, u32[]{:S(2)}) collective-permute-start(bf16[1024,1024]{1,0:T(8,128)(2,1)} %get-tuple-element.293.x_ref.n_ref.refs_0_), channel_id=1, source_target_pairs={{0,16},{16,0},{1,17},{17,1},{2,18},{18,2},{3,19},{19,3},{4,20},{20... | collective-permute-start | bytes 6291464 | tf_op jit(solution)/shard_map/ppermute | solution.py:208
  339.4 23.0 %collective-permute-start.38 = (f32[16,1024]{1,0:T(8,128)S(1)}, f32[16,1024]{1,0:T(8,128)S(1)}, u32[]{:S(2)}, u32[]{:S(2)}) collective-permute-start(f32[16,1024]{1,0:T(8,128)S(1)} %get-tuple-element.576), channel_id=1, source_target_pairs={{16,0},{17,1},{18,2},{19,3},{20,4},{21,5},{22,6},{23,7},{24,8},{25... | collective-permute-start | bytes 196616 | tf_op jit(solution)/shard_map/ppermute | solution.py:1618
  340.7 21.8 %collective-permute-start.37 = (f32[16,1024]{1,0:T(8,128)S(1)}, f32[16,1024]{1,0:T(8,128)S(1)}, u32[]{:S(2)}, u32[]{:S(2)}) collective-permute-start(f32[16,1024]{1,0:T(8,128)S(1)} %get-tuple-element.577), channel_id=1, source_target_pairs={{0,16},{1,17},{2,18},{3,19},{4,20},{5,21},{6,22},{7,23},{8,24},{9,... | collective-permute-start | bytes 196616 | tf_op jit(solution)/shard_map/ppermute | solution.py:1617
  478.0 13.1 %copy-start = (f32[1024,1024]{1,0:T(8,128)S(1)}, f32[1024,1024]{1,0:T(8,128)}, u32[]{:S(2)}) copy-start(f32[1024,1024]{1,0:T(8,128)} %get-tuple-element.312.g_ref) | copy-start | bytes 12582916
  482.9 59.7 %collective-permute-start.39 = (bf16[128,128,128]{2,1,0:T(8,128)(2,1)}, bf16[128,128,128]{2,1,0:T(8,128)(2,1)S(1)}, u32[]{:S(2)}, u32[]{:S(2)}) collective-permute-start(bf16[128,128,128]{2,1,0:T(8,128)(2,1)} %slice.571), channel_id=1, source_target_pairs={{0,1},{1,0},{2,3},{3,2},{4,5},{5,4},{6,7},{7,6},{8,9},{9,8},{10,11... | collective-permute-start | bytes 12582920 | tf_op jit(solution)/shard_map/ppermute | solution.py:208
  491.5 5.9 collective-permute-start.41
  492.8 6.1 collective-permute-start.40
  548.1 9.7 copy-start.28
  552.1 71.8 %collective-permute-start.44 = (bf16[96,128,128]{2,1,0:T(8,128)(2,1)}, bf16[96,128,128]{2,1,0:T(8,128)(2,1)S(1)}, u32[]{:S(2)}, u32[]{:S(2)}) collective-permute-start(bf16[96,128,128]{2,1,0:T(8,128)(2,1)} %slice.578), channel_id=1, source_target_pairs={{0,1},{1,0},{2,3},{3,2},{4,5},{5,4},{6,7},{7,6},{8,9},{9,8},{10,11... | collective-permute-start | bytes 9437192 | tf_op jit(solution)/shard_map/ppermute | solution.py:208
  552.1 71.8 %collective-permute-start.42 = (bf16[32,128,128]{2,1,0:T(8,128)(2,1)}, bf16[32,128,128]{2,1,0:T(8,128)(2,1)}, u32[]{:S(2)}, u32[]{:S(2)}) collective-permute-start(bf16[32,128,128]{2,1,0:T(8,128)(2,1)} %get-tuple-element.327), channel_id=1, source_target_pairs={{0,2},{2,0},{1,3},{3,1},{4,6},{6,4},{5,7},{7,5},{8,10},{10,8},{9,1... | collective-permute-start | bytes 3145736 | tf_op jit(solution)/shard_map/ppermute | solution.py:208
  555.5 68.5 %collective-permute-start.43 = (bf16[32,128,128]{2,1,0:T(8,128)(2,1)}, bf16[32,128,128]{2,1,0:T(8,128)(2,1)}, u32[]{:S(2)}, u32[]{:S(2)}) collective-permute-start(bf16[32,128,128]{2,1,0:T(8,128)(2,1)} %get-tuple-element.328), channel_id=1, source_target_pairs={{0,16},{16,0},{1,17},{17,1},{2,18},{18,2},{3,19},{19,3},{4,20},{20... | collective-permute-start | bytes 3145736 | tf_op jit(solution)/shard_map/ppermute | solution.py:208
  625.8 44.8 %collective-permute-start.45 = (bf16[1024,1024]{1,0:T(8,128)(2,1)}, bf16[1024,1024]{1,0:T(8,128)(2,1)}, u32[]{:S(2)}, u32[]{:S(2)}) collective-permute-start(bf16[1024,1024]{1,0:T(8,128)(2,1)} %input_gradient.1), channel_id=1, source_target_pairs={{0,16},{16,0},{1,17},{17,1},{2,18},{18,2},{3,19},{19,3},{4,20},{20... | collective-permute-start | bytes 6291464 | tf_op jit(solution)/shard_map/ppermute | solution.py:208
  675.4 69.1 %collective-permute-start.50 = (bf16[128,128,128]{2,1,0:T(8,128)(2,1)}, bf16[128,128,128]{2,1,0:T(8,128)(2,1)}, u32[]{:S(2)}, u32[]{:S(2)}) collective-permute-start(bf16[128,128,128]{2,1,0:T(8,128)(2,1)} %slice.589), channel_id=1, source_target_pairs={{0,1},{1,0},{2,3},{3,2},{4,5},{5,4},{6,7},{7,6},{8,9},{9,8},{10,11... | collective-permute-start | bytes 12582920 | tf_op jit(solution)/shard_map/ppermute | solution.py:208
  693.9 50.6 %collective-permute-start.46 = (bf16[16,128,128]{2,1,0:T(8,128)(2,1)}, bf16[16,128,128]{2,1,0:T(8,128)(2,1)}, u32[]{:S(2)}, u32[]{:S(2)}) collective-permute-start(bf16[16,128,128]{2,1,0:T(8,128)(2,1)} %get-tuple-element.363), channel_id=1, source_target_pairs={{0,16},{16,0},{1,17},{17,1},{2,18},{18,2},{3,19},{19,3},{4,20},{20... | collective-permute-start | bytes 1572872 | tf_op jit(solution)/shard_map/ppermute | solution.py:208
  695.2 49.3 %collective-permute-start.47 = (bf16[16,128,128]{2,1,0:T(8,128)(2,1)}, bf16[16,128,128]{2,1,0:T(8,128)(2,1)}, u32[]{:S(2)}, u32[]{:S(2)}) collective-permute-start(bf16[16,128,128]{2,1,0:T(8,128)(2,1)} %get-tuple-element.364), channel_id=1, source_target_pairs={{0,2},{2,0},{1,3},{3,1},{4,6},{6,4},{5,7},{7,5},{8,10},{10,8},{9,1... | collective-permute-start | bytes 1572872 | tf_op jit(solution)/shard_map/ppermute | solution.py:208
  703.2 41.3 %collective-permute-start.48 = (bf16[24,128,128]{2,1,0:T(8,128)(2,1)S(1)}, bf16[24,128,128]{2,1,0:T(8,128)(2,1)}, u32[]{:S(2)}, u32[]{:S(2)}) collective-permute-start(bf16[24,128,128]{2,1,0:T(8,128)(2,1)S(1)} %get-tuple-element.365), channel_id=1, source_target_pairs={{0,2},{2,0},{1,3},{3,1},{4,6},{6,4},{5,7},{7,5},{8,10},{10,8},{9,1... | collective-permute-start | bytes 2359304 | tf_op jit(solution)/shard_map/ppermute | solution.py:208
  703.2 41.3 %collective-permute-start.49 = (bf16[24,128,128]{2,1,0:T(8,128)(2,1)S(1)}, bf16[24,128,128]{2,1,0:T(8,128)(2,1)}, u32[]{:S(2)}, u32[]{:S(2)}) collective-permute-start(bf16[24,128,128]{2,1,0:T(8,128)(2,1)S(1)} %get-tuple-element.366), channel_id=1, source_target_pairs={{0,16},{16,0},{1,17},{17,1},{2,18},{18,2},{3,19},{19,3},{4,20},{20... | collective-permute-start | bytes 2359304 | tf_op jit(solution)/shard_map/ppermute | solution.py:208
  753.4 48.5 %collective-permute-start.51 = (bf16[12,128,128]{2,1,0:T(8,128)(2,1)S(1)}, bf16[12,128,128]{2,1,0:T(8,128)(2,1)S(1)}, u32[]{:S(2)}, u32[]{:S(2)}) collective-permute-start(bf16[12,128,128]{2,1,0:T(8,128)(2,1)S(1)} %get-tuple-element.389), channel_id=1, source_target_pairs={{0,16},{16,0},{1,17},{17,1},{2,18},{18,2},{3,19},{19,3},{4,20},{20... | collective-permute-start | bytes 1179656 | tf_op jit(solution)/shard_map/ppermute | solution.py:208
  758.5 43.3 %collective-permute-start.52 = (bf16[12,128,128]{2,1,0:T(8,128)(2,1)S(1)}, bf16[12,128,128]{2,1,0:T(8,128)(2,1)S(1)}, u32[]{:S(2)}, u32[]{:S(2)}) collective-permute-start(bf16[12,128,128]{2,1,0:T(8,128)(2,1)S(1)} %get-tuple-element.390), channel_id=1, source_target_pairs={{0,2},{2,0},{1,3},{3,1},{4,6},{6,4},{5,7},{7,5},{8,10},{10,8},{9,1... | collective-permute-start | bytes 1179656 | tf_op jit(solution)/shard_map/ppermute | solution.py:208
  760.5 41.4 %collective-permute-start.53 = (bf16[32,128,128]{2,1,0:T(8,128)(2,1)}, bf16[32,128,128]{2,1,0:T(8,128)(2,1)S(1)}, u32[]{:S(2)}, u32[]{:S(2)}) collective-permute-start(bf16[32,128,128]{2,1,0:T(8,128)(2,1)} %get-tuple-element.391), channel_id=1, source_target_pairs={{0,2},{2,0},{1,3},{3,1},{4,6},{6,4},{5,7},{7,5},{8,10},{10,8},{9,1... | collective-permute-start | bytes 3145736 | tf_op jit(solution)/shard_map/ppermute | solution.py:208
  760.6 41.4 %collective-permute-start.54 = (bf16[32,128,128]{2,1,0:T(8,128)(2,1)S(1)}, bf16[32,128,128]{2,1,0:T(8,128)(2,1)S(1)}, u32[]{:S(2)}, u32[]{:S(2)}) collective-permute-start(bf16[32,128,128]{2,1,0:T(8,128)(2,1)S(1)} %get-tuple-element.392), channel_id=1, source_target_pairs={{0,16},{16,0},{1,17},{17,1},{2,18},{18,2},{3,19},{19,3},{4,20},{20... | collective-permute-start | bytes 3145736 | tf_op jit(solution)/shard_map/ppermute | solution.py:208
  806.0 19.2 %collective-permute-start.57 = (bf16[288,128,128]{2,1,0:T(8,128)(2,1)}, bf16[288,128,128]{2,1,0:T(8,128)(2,1)}, u32[]{:S(2)}, u32[]{:S(2)}) collective-permute-start(bf16[288,128,128]{2,1,0:T(8,128)(2,1)} %get-tuple-element.415), channel_id=1, source_target_pairs={{0,1},{1,0},{2,3},{3,2},{4,5},{5,4},{6,7},{7,6},{8,9},{9,8},{10,11... | collective-permute-start | bytes 28311560 | tf_op jit(solution)/shard_map/ppermute | solution.py:208
  810.2 14.6 %collective-permute-start.55 = (bf16[16,128,128]{2,1,0:T(8,128)(2,1)}, bf16[16,128,128]{2,1,0:T(8,128)(2,1)S(1)}, u32[]{:S(2)}, u32[]{:S(2)}) collective-permute-start(bf16[16,128,128]{2,1,0:T(8,128)(2,1)} %get-tuple-element.413), channel_id=1, source_target_pairs={{0,16},{16,0},{1,17},{17,1},{2,18},{18,2},{3,19},{19,3},{4,20},{20... | collective-permute-start | bytes 1572872 | tf_op jit(solution)/shard_map/ppermute | solution.py:208
  810.3 15.0 %collective-permute-start.56 = (bf16[16,128,128]{2,1,0:T(8,128)(2,1)}, bf16[16,128,128]{2,1,0:T(8,128)(2,1)}, u32[]{:S(2)}, u32[]{:S(2)}) collective-permute-start(bf16[16,128,128]{2,1,0:T(8,128)(2,1)} %get-tuple-element.414), channel_id=1, source_target_pairs={{0,2},{2,0},{1,3},{3,1},{4,6},{6,4},{5,7},{7,5},{8,10},{10,8},{9,1... | collective-permute-start | bytes 1572872 | tf_op jit(solution)/shard_map/ppermute | solution.py:208
  814.9 16.7 %copy-start.14 = (bf16[32,128,128]{2,1,0:T(8,128)(2,1)S(1)}, bf16[32,128,128]{2,1,0:T(8,128)(2,1)}, u32[]{:S(2)}) copy-start(bf16[32,128,128]{2,1,0:T(8,128)(2,1)} %copy-done.13) | copy-start | bytes 3145732
  815.0 16.7 %copy-start.16 = (bf16[32,128,128]{2,1,0:T(8,128)(2,1)S(1)}, bf16[32,128,128]{2,1,0:T(8,128)(2,1)}, u32[]{:S(2)}) copy-start(bf16[32,128,128]{2,1,0:T(8,128)(2,1)} %copy-done.15) | copy-start | bytes 3145732
  834.2 57.1 %collective-permute-start.60 = (bf16[96,128,128]{2,1,0:T(8,128)(2,1)}, bf16[96,128,128]{2,1,0:T(8,128)(2,1)}, u32[]{:S(2)}, u32[]{:S(2)}) collective-permute-start(bf16[96,128,128]{2,1,0:T(8,128)(2,1)} %slice.620), channel_id=1, source_target_pairs={{0,1},{1,0},{2,3},{3,2},{4,5},{5,4},{6,7},{7,6},{8,9},{9,8},{10,11... | collective-permute-start | bytes 9437192 | tf_op jit(solution)/shard_map/ppermute | solution.py:208
  835.8 162.9 %reduce-scatter.11.cloned.1.call-start = ((), (), s32[]{:S(2)}) async-start(), calls=%async_computation.9 | async-start | bytes 2949120 | tf_op jit(solution)/shard_map/reduce_scatter | solution.py:1586
  835.8 55.4 %collective-permute-start.58 = (bf16[72,128,128]{2,1,0:T(8,128)(2,1)}, bf16[72,128,128]{2,1,0:T(8,128)(2,1)S(1)}, u32[]{:S(2)}, u32[]{:S(2)}) collective-permute-start(bf16[72,128,128]{2,1,0:T(8,128)(2,1)} %get-tuple-element.429), channel_id=1, source_target_pairs={{0,2},{2,0},{1,3},{3,1},{4,6},{6,4},{5,7},{7,5},{8,10},{10,8},{9,1... | collective-permute-start | bytes 7077896 | tf_op jit(solution)/shard_map/ppermute | solution.py:208
  837.6 53.6 %collective-permute-start.59 = (bf16[72,128,128]{2,1,0:T(8,128)(2,1)}, bf16[72,128,128]{2,1,0:T(8,128)(2,1)S(1)}, u32[]{:S(2)}, u32[]{:S(2)}) collective-permute-start(bf16[72,128,128]{2,1,0:T(8,128)(2,1)} %get-tuple-element.430), channel_id=1, source_target_pairs={{0,16},{16,0},{1,17},{17,1},{2,18},{18,2},{3,19},{19,3},{4,20},{20... | collective-permute-start | bytes 7077896 | tf_op jit(solution)/shard_map/ppermute | solution.py:208
  839.3 1.3 collective-permute-start.61
  839.3 52.0 %collective-permute-start.62 = (f32[10,1024]{1,0:T(8,128)S(1)}, f32[10,1024]{1,0:T(8,128)S(1)}, u32[]{:S(2)}, u32[]{:S(2)}) collective-permute-start(f32[10,1024]{1,0:T(8,128)S(1)} %concatenate.46), channel_id=1, source_target_pairs={{0,2},{2,0},{1,3},{3,1},{4,6},{6,4},{5,7},{7,5},{8,10},{10,8},{9,1... | collective-permute-start | bytes 122888 | tf_op jit(solution)/shard_map/ppermute | solution.py:208
  840.5 50.7 %collective-permute-start.63 = (f32[10,1024]{1,0:T(8,128)S(1)}, f32[10,1024]{1,0:T(8,128)S(1)}, u32[]{:S(2)}, u32[]{:S(2)}) collective-permute-start(f32[10,1024]{1,0:T(8,128)S(1)} %concatenate.46), channel_id=1, source_target_pairs={{0,3},{1,2},{2,1},{3,0},{4,7},{5,6},{6,5},{7,4},{8,11},{9,10},{10,... | collective-permute-start | bytes 122888 | tf_op jit(solution)/shard_map/ppermute | solution.py:208
  895.1 31.2 %collective-permute-start.64 = (bf16[36,128,128]{2,1,0:T(8,128)(2,1)S(1)}, bf16[36,128,128]{2,1,0:T(8,128)(2,1)S(1)}, u32[]{:S(2)}, u32[]{:S(2)}) collective-permute-start(bf16[36,128,128]{2,1,0:T(8,128)(2,1)S(1)} %get-tuple-element.440), channel_id=1, source_target_pairs={{0,16},{16,0},{1,17},{17,1},{2,18},{18,2},{3,19},{19,3},{4,20},{20... | collective-permute-start | bytes 3538952 | tf_op jit(solution)/shard_map/ppermute | solution.py:208
  896.6 29.7 %collective-permute-start.65 = (bf16[36,128,128]{2,1,0:T(8,128)(2,1)S(1)}, bf16[36,128,128]{2,1,0:T(8,128)(2,1)S(1)}, u32[]{:S(2)}, u32[]{:S(2)}) collective-permute-start(bf16[36,128,128]{2,1,0:T(8,128)(2,1)S(1)} %get-tuple-element.441), channel_id=1, source_target_pairs={{0,2},{2,0},{1,3},{3,1},{4,6},{6,4},{5,7},{7,5},{8,10},{10,8},{9,1... | collective-permute-start | bytes 3538952 | tf_op jit(solution)/shard_map/ppermute | solution.py:208
  898.1 28.2 %collective-permute-start.66 = (f32[10,1024]{1,0:T(8,128)S(1)}, f32[10,1024]{1,0:T(8,128)S(1)}, u32[]{:S(2)}, u32[]{:S(2)}) collective-permute-start(f32[10,1024]{1,0:T(8,128)S(1)} %add_add_fusion.1), channel_id=1, source_target_pairs={{0,16},{16,0},{1,17},{17,1},{2,18},{18,2},{3,19},{19,3},{4,20},{20... | collective-permute-start | bytes 122888 | tf_op jit(solution)/shard_map/ppermute | solution.py:208
  898.7 27.6 %collective-permute-start.67 = (f32[10,1024]{1,0:T(8,128)S(1)}, f32[10,1024]{1,0:T(8,128)S(1)}, u32[]{:S(2)}, u32[]{:S(2)}) collective-permute-start(f32[10,1024]{1,0:T(8,128)S(1)} %add_add_fusion.1), channel_id=1, source_target_pairs={{0,4},{4,0},{8,12},{12,8},{1,5},{5,1},{9,13},{13,9},{2,6},{6,2},{1... | collective-permute-start | bytes 122888 | tf_op jit(solution)/shard_map/ppermute | solution.py:208
  898.7 27.6 %collective-permute-start.68 = (f32[10,1024]{1,0:T(8,128)S(1)}, f32[10,1024]{1,0:T(8,128)S(1)}, u32[]{:S(2)}, u32[]{:S(2)}) collective-permute-start(f32[10,1024]{1,0:T(8,128)S(1)} %add_add_fusion.1), channel_id=1, source_target_pairs={{0,20},{4,16},{8,28},{12,24},{16,4},{20,0},{24,12},{28,8},{1,21},{... | collective-permute-start | bytes 122888 | tf_op jit(solution)/shard_map/ppermute | solution.py:208
  932.3 19.2 %collective-permute-start.69 = (bf16[24,128,128]{2,1,0:T(8,128)(2,1)S(1)}, bf16[24,128,128]{2,1,0:T(8,128)(2,1)S(1)}, u32[]{:S(2)}, u32[]{:S(2)}) collective-permute-start(bf16[24,128,128]{2,1,0:T(8,128)(2,1)S(1)} %get-tuple-element.455), channel_id=1, source_target_pairs={{0,2},{2,0},{1,3},{3,1},{4,6},{6,4},{5,7},{7,5},{8,10},{10,8},{9,1... | collective-permute-start | bytes 2359304 | tf_op jit(solution)/shard_map/ppermute | solution.py:208
  933.9 18.8 %collective-permute-start.70 = (bf16[24,128,128]{2,1,0:T(8,128)(2,1)S(1)}, bf16[24,128,128]{2,1,0:T(8,128)(2,1)S(1)}, u32[]{:S(2)}, u32[]{:S(2)}) collective-permute-start(bf16[24,128,128]{2,1,0:T(8,128)(2,1)S(1)} %get-tuple-element.456), channel_id=1, source_target_pairs={{0,16},{16,0},{1,17},{17,1},{2,18},{18,2},{3,19},{19,3},{4,20},{20... | collective-permute-start | bytes 2359304 | tf_op jit(solution)/shard_map/ppermute | solution.py:208
  935.3 5.3 collective-permute-start.71
  954.5 9.6 collective-permute-start.72
  955.9 9.3 collective-permute-start.73
  967.2 17.1 %collective-permute-start.74 = (bf16[6,128,128]{2,1,0:T(8,128)(2,1)S(1)}, bf16[6,128,128]{2,1,0:T(8,128)(2,1)S(1)}, u32[]{:S(2)}, u32[]{:S(2)}) collective-permute-start(bf16[6,128,128]{2,1,0:T(8,128)(2,1)S(1)} %get-tuple-element.464), channel_id=1, source_target_pairs={{0,8},{4,12},{1,9},{5,13},{2,10},{6,14},{3,11},{7,15},{16,24},{20,... | collective-permute-start | bytes 589832 | tf_op jit(solution)/shard_map/ppermute | solution.py:208
  968.5 19.6 %collective-permute-start.75 = (bf16[6,128,128]{2,1,0:T(8,128)(2,1)S(1)}, bf16[6,128,128]{2,1,0:T(8,128)(2,1)S(1)}, u32[]{:S(2)}, u32[]{:S(2)}) collective-permute-start(bf16[6,128,128]{2,1,0:T(8,128)(2,1)S(1)} %get-tuple-element.465), channel_id=1, source_target_pairs={{8,0},{12,4},{9,1},{13,5},{10,2},{14,6},{11,3},{15,7},{24,16},{28,... | collective-permute-start | bytes 589832 | tf_op jit(solution)/shard_map/ppermute | solution.py:208
  969.8 18.3 %collective-permute-start.76 = (bf16[6,128,128]{2,1,0:T(8,128)(2,1)S(1)}, bf16[6,128,128]{2,1,0:T(8,128)(2,1)S(1)}, u32[]{:S(2)}, u32[]{:S(2)}) collective-permute-start(bf16[6,128,128]{2,1,0:T(8,128)(2,1)S(1)} %get-tuple-element.466), channel_id=1, source_target_pairs={{0,4},{4,8},{8,12},{1,5},{5,9},{9,13},{2,6},{6,10},{10,14},{3,7},{... | collective-permute-start | bytes 589832 | tf_op jit(solution)/shard_map/ppermute | solution.py:208
  975.5 12.7 %collective-permute-start.77 = (bf16[6,128,128]{2,1,0:T(8,128)(2,1)S(1)}, bf16[6,128,128]{2,1,0:T(8,128)(2,1)S(1)}, u32[]{:S(2)}, u32[]{:S(2)}) collective-permute-start(bf16[6,128,128]{2,1,0:T(8,128)(2,1)S(1)} %get-tuple-element.467), channel_id=1, source_target_pairs={{4,0},{8,4},{12,8},{5,1},{9,5},{13,9},{6,2},{10,6},{14,10},{7,3},{... | collective-permute-start | bytes 589832 | tf_op jit(solution)/shard_map/ppermute | solution.py:208
  976.8 12.4 %collective-permute-start.78 = (bf16[6,128,128]{2,1,0:T(8,128)(2,1)S(1)}, bf16[6,128,128]{2,1,0:T(8,128)(2,1)S(1)}, u32[]{:S(2)}, u32[]{:S(2)}) collective-permute-start(bf16[6,128,128]{2,1,0:T(8,128)(2,1)S(1)} %get-tuple-element.468), channel_id=1, source_target_pairs={{0,12},{1,13},{2,14},{3,15},{16,28},{17,29},{18,30},{19,31}} | collective-permute-start | bytes 589832 | tf_op jit(solution)/shard_map/ppermute | solution.py:208
  984.3 14.1 %collective-permute-start.79 = (bf16[6,128,128]{2,1,0:T(8,128)(2,1)S(1)}, bf16[6,128,128]{2,1,0:T(8,128)(2,1)S(1)}, u32[]{:S(2)}, u32[]{:S(2)}) collective-permute-start(bf16[6,128,128]{2,1,0:T(8,128)(2,1)S(1)} %get-tuple-element.469), channel_id=1, source_target_pairs={{12,0},{13,1},{14,2},{15,3},{28,16},{29,17},{30,18},{31,19}} | collective-permute-start | bytes 589832 | tf_op jit(solution)/shard_map/ppermute | solution.py:208
  985.6 14.6 %copy-start.45 = (s32[46]{0:T(128)S(1)}, s32[46]{0:T(128)}, u32[]{:S(2)}) copy-start(s32[46]{0:T(128)} %select_reduce_fusion) | copy-start | bytes 556
  985.6 15.3 %copy-start.32 = (f32[5,1024]{1,0:T(8,128)S(1)}, f32[5,1024]{1,0:T(8,128)}, u32[]{:S(2)}) copy-start(f32[5,1024]{1,0:T(8,128)} %param.25) | copy-start | bytes 61444
  985.6 16.0 %copy-start.26 = (f32[5,1024]{1,0:T(8,128)S(1)}, f32[5,1024]{1,0:T(8,128)}, u32[]{:S(2)}) copy-start(f32[5,1024]{1,0:T(8,128)} %taps_ref.3) | copy-start | bytes 61444
  1000.1 3.5 collective-permute-start.80
  (23 other events, 85.3 us)
Sparse Core Ops, SparseCore 0:
  10.6 126.3 all-gather.2
  139.1 123.6 all-gather.4
  835.9 56.6 reduce-scatter.8
  932.4 54.1 reduce-scatter.10

commit v5 on v4

--- a/solution.py
+++ b/solution.py
@@ -668,7 +668,7 @@
 
 def project_out(values, weights, matrix, stream):
     rows = values.shape[0]
-    tile = row_tile(rows)
+    tile = 512 if rows % 512 == 0 else row_tile(rows)
 
     def body(x_ref, w_ref, s_ref, out_ref):
         out_ref[...] = s_ref[...] + dot(x_ref[...], w_ref[...])

time: 1040 us -> 1040 us (level)
  transfers between devices with their start and end apart: 53 -> 53, of which waited for: 20 -> 21; matrix products, arithmetic and copies ran while one was open for 4% -> 4% of each run, Pallas kernels for 30% -> 31%
where the time goes in v5:
time: 1040 us; the launch traced here: 1030 us
  Pallas kernels  526 us (51%)
  waiting for transfers between devices  278 us (27%)
  starting transfers between devices  107 us (10%)
  other arithmetic  63.5 us (6%)
  local copies, waits for them, and re-layouts  37.2 us (4%)
  between operations  17.4 us (2%)
    ppermute x45, waiting for transfers between devices, swap(): return lax.ppermute(value, axis, pairs)  231 us
    pallas_call x3, Pallas kernels, ffn_backward(): pl.pallas_call(body, grid=(steps,), out_shape=(jax.ShapeDtypeStruct((rows...  142 us
    ppermute x45, starting transfers between devices, swap(): return lax.ppermute(value, axis, pairs)  94.7 us
    pallas_call x3, Pallas kernels, ffn_part(): pl.pallas_call(body, grid_spec=pltpu.PrefetchScalarGridSpec(num_scalar_pr...  60 us
    pallas_call x8, Pallas kernels, unsort(): pl.pallas_call(body, grid=(steps,), out_shape=jax.ShapeDtypeStruct((chunk...  55.7 us
    pallas_call x1, Pallas kernels, attention_backward(): pl.pallas_call(body, grid=(HEADS, rows // tall), out_shape=(jax.ShapeDtyp...  51.6 us
    convert_element_type x16, other arithmetic, added(): return sum((term.astype(f32) for term in terms)).astype(bf16)  48.1 us
    all_gather x1, waiting for transfers between devices, run(): column = lax.all_gather(low, dp, axis=0, tiled=True)  45.2 us
  transfers between devices with their start and end apart: 53, of which 21 were waited for; matrix products, arithmetic and copies ran while one was open for 4% of the time, Pallas kernels for 31%

profile of v5, /device:TPU:0, one launch (start us, length us, event | category | flops | bytes accessed | tf_op | source)
XLA Modules:
  0.0 1030.5 jit_solution(5643166603636742586)
XLA Ops:
  7.2 3.2 bitcast_convert_fusion
  10.6 3.0 collective-permute-start.34
  14.3 4.4 norm_rows.1.x_ref
  23.7 24.1 %collective-permute-done.33 = s32[1,736]{1,0:T(1,128)S(1)} collective-permute-done((s32[1,736]{1,0:T(1,128)S(1)}, s32[1,736]{1,0:T(1,128)S(1)}, u32[]{:S(2)}, u32[]{:S(2)}) %collective-permute-start.33) | collective-permute-done | bytes 2976 | tf_op jit(solution)/shard_map/ppermute | solution.py:208
  53.9 37.9 %collective-permute-done.32.x_ref = bf16[1024,1024]{1,0:T(8,128)(2,1)S(1)} collective-permute-done((bf16[1024,1024]{1,0:T(8,128)(2,1)}, bf16[1024,1024]{1,0:T(8,128)(2,1)S(1)}, u32[]{:S(2)}, u32[]{:S(2)}) %collective-permute-start.32) | collective-permute-done | bytes 2097184 | tf_op jit(solution)/shard_map/ppermute | solution.py:208
  91.8 45.2 %all-gather.3.cloned.1.call-done.slots_ref = bf16[736,128,128]{2,1,0:T(8,128)(2,1)} async-done(((bf16[46,128,128]{2,1,0:T(8,128)(2,1)}), bf16[736,128,128]{2,1,0:T(8,128)(2,1)}) %all-gather.3.cloned.1.call-update) | async-done | bytes 24117264 | tf_op jit(solution)/shard_map/all_gather | solution.py:1674
  139.9 9.4 unsort.8.up_ref.down_ref.rest_0_
  149.3 15.5 %ffn_part.3 = bf16[1024,1024]{1,0:T(8,128)(2,1)} custom-call(s32[1]{0:T(128)} %bitcast.25.part_ref, bf16[1024,1024]{1,0:T(8,128)(2,1)} %copy-done.11, bf16[8192,1024]{1,0:T(8,128)(2,1)} %unsort.8.up_ref.down_ref.rest_0_, bf16[8192,1024]{1,0:T(8,128)(2,1)} %unsort.8.up_ref.down_ref.rest_0_), custom_call_target="tpu_custom_call" | custom-call | flops 8589934592 | bytes 8388608 | tf_op jit(solution)/shard_map/ffn_part/pallas_call | solution.py:408
  167.3 4.6 unsort.10.rest_0_
  172.0 5.1 unsort.9.rest_0_
  177.1 8.8 unsort.11.rest_0_
  185.9 16.4 %ffn_part.4 = (bf16[1024,1024]{1,0:T(8,128)(2,1)}, bf16[1024,4096]{1,0:T(8,128)(2,1)}) custom-call(s32[1]{0:T(128)} %bitcast.25.part_ref, bf16[1024,1024]{1,0:T(8,128)(2,1)} %norm_rows.1.x_ref, bf16[8192,1024]{1,0:T(8,128)(2,1)} %unsort.8.up_ref.down_ref.rest_0_, bf16[8192,1024]{1,0:T(8,128)(2,1)} %unsort.8.up_ref.down_ref.rest_0_), custom_call_target="tpu_custom_call" | custom-call | flops 8589934592 | bytes 8388608 | tf_op jit(solution)/shard_map/ffn_part/pallas_call | solution.py:408
  202.3 10.4 %collective-permute-done.35.refs_1_ = bf16[1024,1024]{1,0:T(8,128)(2,1)S(1)} collective-permute-done((bf16[1024,1024]{1,0:T(8,128)(2,1)}, bf16[1024,1024]{1,0:T(8,128)(2,1)S(1)}, u32[]{:S(2)}, u32[]{:S(2)}) %collective-permute-start.35) | collective-permute-done | bytes 2097184 | tf_op jit(solution)/shard_map/ppermute | solution.py:208
  214.1 6.2 join.2
  223.3 44.2 %collective-permute-done.36.x_ref.refs_1_ = bf16[1024,1024]{1,0:T(8,128)(2,1)S(1)} collective-permute-done((bf16[1024,1024]{1,0:T(8,128)(2,1)}, bf16[1024,1024]{1,0:T(8,128)(2,1)S(1)}, u32[]{:S(2)}, u32[]{:S(2)}) %collective-permute-start.36) | collective-permute-done | bytes 2097184 | tf_op jit(solution)/shard_map/ppermute | solution.py:208
  267.5 5.4 unsort.12.w_ref.wk_ref.wv_ref.refs_6_
  273.0 5.9 project.3.q_ref
  278.8 8.3 project.4.rest_0_
  287.1 8.3 project.5.key_ref.value_ref
  295.4 40.4 %attention_forward.1 = (bf16[1024,1024]{1,0:T(8,128)(2,1)}, f32[8,1,1024]{2,1,0:T(1,128)}) custom-call(s32[1]{0:T(128)} %bitcast.20.part_ref.rank_ref.refs_10_.refs_6_, s32[4]{0:T(128)} %reshape.309.window_ref, f32[8]{0:T(128)} %multiply_power_fusion.slope_ref, bf16[1024,1024]{1,0:T(8,128)(2,1)} %project.3.q_ref, s32[1024,1]{1,0:T(8,128)} %copy.50.own_ref, ...), custom_call_target="tpu_custom_call" | custom-call | tf_op jit(solution)/shard_map/attention_forward/pallas_call | solution.py:974
  335.8 6.4 project_out.1.x_ref
  344.4 4.5 collective-permute-start.37
  349.0 9.0 unsort.14.up_ref.down_ref.refs_5_.refs_6_
  358.0 4.6 unsort.13.value_ref.gate_ref.out_w_ref.gate_w_ref
  363.2 20.3 %conv_forward.1 = (f32[1024,1024]{1,0:T(8,128)}, bf16[1056,1024]{1,0:T(8,128)(2,1)}, bf16[1056,1024]{1,0:T(8,128)(2,1)}, bf16[1024,1024]{1,0:T(8,128)(2,1)}) custom-call(f32[1024,1024]{1,0:T(8,128)} %project_out.1.x_ref, f32[16,1024]{1,0:T(8,128)} %copy-done.34, f32[16,1024]{1,0:T(8,128)} %copy-done.33, f32[1,1024]{1,0:T(1,128)} %get-tuple-element.590.gain_ref, ...), custom_call_target="tpu_custom_call" | custom-call | flops 6442450944 | bytes 18874368 | tf_op jit(solution)/shard_map/conv_forward/pallas_call | solution.py:1129
  383.4 28.1 %ffn_part.5 = (bf16[1024,1024]{1,0:T(8,128)(2,1)}, bf16[1024,4096]{1,0:T(8,128)(2,1)}) custom-call(s32[1]{0:T(128)} %constant.391.clone.1.part_ref, bf16[1024,1024]{1,0:T(8,128)(2,1)} %get-tuple-element.303.x_ref, bf16[8192,1024]{1,0:T(8,128)(2,1)} %unsort.14.up_ref.down_ref.refs_5_.refs_6_, bf16[8192,1024]{1,0:T(8,128)(2,1)} %unsort.14.up_ref.down_ref.refs_5_.refs_6_), custom_call_target="tpu_custom_call" | custom-call | flops 17179869184 | bytes 16777216 | tf_op jit(solution)/shard_map/ffn_part/pallas_call | solution.py:408
  411.6 5.8 join.3
  417.4 60.8 %ffn_backward.3 = (f32[1024,1024]{1,0:T(8,128)}, f32[2,1024]{1,0:T(2,128)}, bf16[1184,128,128]{2,1,0:T(8,128)(2,1)}, bf16[288,128,128]{2,1,0:T(8,128)(2,1)}) custom-call(s32[1472]{0:T(1024)} %reshape.307.table_ref, f32[1024,1024]{1,0:T(8,128)} %get-tuple-element.308.refs_0_, f32[1,1024]{1,0:T(1,128)} %get-tuple-element.588.refs_1_, ...), custom_call_target="tpu_custom_call" | custom-call | flops 34359738368 | bytes 33554432 | tf_op jit(solution)/shard_map/ffn_backward/pallas_call | solution.py:600
  478.2 4.9 slice.571
  483.1 7.3 collective-permute-start.39
  492.0 4.5 collective-permute-start.40
  498.7 43.0 %conv_backward.1 = (f32[1024,1024]{1,0:T(8,128)}, f32[1,1024]{1,0:T(1,128)}, f32[5,1024]{1,0:T(8,128)}, bf16[1184,128,128]{2,1,0:T(8,128)(2,1)}, bf16[288,128,128]{2,1,0:T(8,128)(2,1)}) custom-call(s32[1472]{0:T(1024)} %reshape.307.table_ref, f32[1024,1024]{1,0:T(8,128)} %get-tuple-element.312.g_ref, ...), custom_call_target="tpu_custom_call", output_to_operand_aliasing={{3}: (13, {}), {4}: (14, {})} | custom-call | flops 12884901888 | bytes 29360128 | tf_op jit(solution)/shard_map/conv_backward/pallas_call | solution.py:1312
  541.8 5.5 slice.578
  547.3 4.0 add_convert_fusion.38
  557.9 10.0 project_out_back.1
  567.9 51.6 %attention_backward.1 = (bf16[1024,1024]{1,0:T(8,128)(2,1)}, bf16[2048,1024]{1,0:T(8,128)(2,1)}, bf16[2048,1024]{1,0:T(8,128)(2,1)}) custom-call(s32[1]{0:T(128)} %bitcast.20.part_ref.rank_ref.refs_10_.refs_6_, s32[4]{0:T(128)} %reshape.309.window_ref, f32[8]{0:T(128)} %multiply_power_fusion.slope_ref, bf16[1024,1024]{1,0:T(8,128)(2,1)} %project.3.q_ref, ...), custom_call_target="tpu_custom_call" | custom-call | tf_op jit(solution)/shard_map/attention_backward/pallas_call | solution.py:1057
  619.5 8.7 input_gradient.1
  630.0 2.8 add_convert_fusion.42
  633.1 3.1 add_convert_fusion.50
  636.3 32.9 %projections_back.1 = (f32[1024,1024]{1,0:T(8,128)}, bf16[1184,128,128]{2,1,0:T(8,128)(2,1)}, bf16[288,128,128]{2,1,0:T(8,128)(2,1)}) custom-call(s32[2]{0:T(128)} %pad_add_fusion.2.part_ref, s32[1472]{0:T(1024)} %reshape.307.table_ref, bf16[1024,1024]{1,0:T(8,128)(2,1)} %get-tuple-element.293.x_ref.n_ref.refs_0_, ...), custom_call_target="tpu_custom_call", output_to_operand_aliasing={{1}: (11, {}), {2}: (12, {})} | custom-call | flops 17179869184 | bytes 31457280 | tf_op jit(solution)/shard_map/projections_back/pallas_call | solution.py:885
  670.5 4.8 slice.589
  675.3 8.1 collective-permute-start.50
  683.4 8.8 unsort.15.refs_7_.refs_8_.refs_3_.refs_4_
  696.4 39.5 %ffn_backward.4 = (f32[1024,1024]{1,0:T(8,128)}, f32[2,1024]{1,0:T(2,128)}, bf16[1184,128,128]{2,1,0:T(8,128)(2,1)}, bf16[288,128,128]{2,1,0:T(8,128)(2,1)}, f32[1024,1024]{1,0:T(8,128)}) custom-call(s32[1472]{0:T(1024)} %reshape.307.table_ref, f32[1024,1024]{1,0:T(8,128)} %get-tuple-element.299.s_ref.refs_0_, ...), custom_call_target="tpu_custom_call", output_to_operand_aliasing={{2}: (12, {}), {3}: (13, {})} | custom-call | flops 17179869184 | bytes 16777216 | tf_op jit(solution)/shard_map/ffn_backward/pallas_call | solution.py:600
  735.9 4.2 add_convert_fusion.36
  744.8 5.8 collective-permute-start.51
  752.8 41.2 %ffn_backward.5 = (f32[1024,1024]{1,0:T(8,128)}, f32[2,1024]{1,0:T(2,128)}, bf16[1184,128,128]{2,1,0:T(8,128)(2,1)}, bf16[288,128,128]{2,1,0:T(8,128)(2,1)}) custom-call(s32[1472]{0:T(1024)} %reshape.307.table_ref, f32[1024,1024]{1,0:T(8,128)} %get-tuple-element.393.refs_0_, ...), custom_call_target="tpu_custom_call", output_to_operand_aliasing={{2}: (9, {}), {3}: (10, {})} | custom-call | flops 17179869184 | bytes 16777216 | tf_op jit(solution)/shard_map/ffn_backward/pallas_call | solution.py:600
  794.1 4.1 add_convert_fusion.46
  798.4 4.0 slice.620
  805.2 11.8 %collective-permute-done.55 = bf16[16,128,128]{2,1,0:T(8,128)(2,1)S(1)} collective-permute-done((bf16[16,128,128]{2,1,0:T(8,128)(2,1)}, bf16[16,128,128]{2,1,0:T(8,128)(2,1)S(1)}, u32[]{:S(2)}, u32[]{:S(2)}) %collective-permute-start.55) | collective-permute-done | bytes 524320 | tf_op jit(solution)/shard_map/ppermute | solution.py:208
  817.2 6.4 add_convert_fusion.30
  832.5 50.5 %collective-permute-done.62 = f32[10,1024]{1,0:T(8,128)S(1)} collective-permute-done((f32[10,1024]{1,0:T(8,128)S(1)}, f32[10,1024]{1,0:T(8,128)S(1)}, u32[]{:S(2)}, u32[]{:S(2)}) %collective-permute-start.62) | collective-permute-done | bytes 40992 | tf_op jit(solution)/shard_map/ppermute | solution.py:208
  883.0 3.8 add_convert_fusion.34
  889.3 9.3 collective-permute-start.67
  901.9 16.5 %collective-permute-done.66 = f32[10,1024]{1,0:T(8,128)S(1)} collective-permute-done((f32[10,1024]{1,0:T(8,128)S(1)}, f32[10,1024]{1,0:T(8,128)S(1)}, u32[]{:S(2)}, u32[]{:S(2)}) %collective-permute-start.66) | collective-permute-done | bytes 40992 | tf_op jit(solution)/shard_map/ppermute | solution.py:208
  918.4 4.3 add_convert_fusion.33
  926.4 6.8 collective-permute-start.71
  935.5 8.4 collective-permute-done.69
  948.8 7.3 collective-permute-done.72
  959.3 8.5 collective-permute-start.74
  969.1 5.7 collective-permute-start.76
  976.1 7.5 collective-permute-start.78
  988.4 9.4 collective-permute-done.79
  1006.8 16.6 %shampoo.1 = (f32[46,128,128]{2,1,0:T(8,128)}, f32[46,128,128]{2,1,0:T(8,128)}, f32[46,128,128]{2,1,0:T(8,128)}, f32[46,128,128]{2,1,0:T(8,128)}, f32[46,128,128]{2,1,0:T(8,128)}) custom-call(s32[48]{0:T(128)} %pad.14.index_ref, bf16[92,128,128]{2,1,0:T(8,128)(2,1)S(1)} %get-tuple-element.647.refs_0_.refs_1_.refs_2_.refs_3_.refs_4_.refs_5_.refs_6_.refs_7_, ...), custom_call_target="tpu_custom_call" | custom-call | tf_op jit(solution)/shard_map/shampoo/pallas_call | solution.py:1397
  (235 shorter events, 95.2 us)
Async XLA Ops:
  7.2 129.8 %all-gather.3.cloned.1.call-start = ((), (), s32[]{:S(2)}) async-start(), calls=%async_computation.6 | async-start | bytes 25624576 | tf_op jit(solution)/shard_map/all_gather | solution.py:1674
  10.5 10.7 %copy-start.27 = (s32[1,2048]{1,0:T(1,128)S(1)}, s32[1,2048]{1,0:T(1,128)}, u32[]{:S(2)}) copy-start(s32[1,2048]{1,0:T(1,128)} %columns_ref.1) | copy-start | bytes 24580
  10.5 257.0 %all-gather.5.cloned.1.call-start = ((), (), s32[]{:S(2)}) async-start(), calls=%async_computation.7 | async-start | bytes 25624576 | tf_op jit(solution)/shard_map/all_gather | solution.py:1679
  10.6 128.4 %collective-permute-start.34 = (bf16[46,128,128]{2,1,0:T(8,128)(2,1)}, bf16[46,128,128]{2,1,0:T(8,128)(2,1)}, u32[]{:S(2)}, u32[]{:S(2)}) collective-permute-start(bf16[46,128,128]{2,1,0:T(8,128)(2,1)} %bitcast_convert_fusion), channel_id=1, source_target_pairs={{0,16},{16,0},{1,17},{17,1},{2,18},{18,2},{3,19},{19,3},{4,20},{20... | collective-permute-start | bytes 4521992 | tf_op jit(solution)/shard_map/ppermute | solution.py:208
  13.6 34.1 %collective-permute-start.33 = (s32[1,736]{1,0:T(1,128)S(1)}, s32[1,736]{1,0:T(1,128)S(1)}, u32[]{:S(2)}, u32[]{:S(2)}) collective-permute-start(s32[1,736]{1,0:T(1,128)S(1)} %copy-done.39), channel_id=1, source_target_pairs={{0,16},{16,0},{1,17},{17,1},{2,18},{18,2},{3,19},{19,3},{4,20},{20... | collective-permute-start | bytes 8840 | tf_op jit(solution)/shard_map/ppermute | solution.py:208
  18.7 73.1 %collective-permute-start.32 = (bf16[1024,1024]{1,0:T(8,128)(2,1)}, bf16[1024,1024]{1,0:T(8,128)(2,1)S(1)}, u32[]{:S(2)}, u32[]{:S(2)}) collective-permute-start(bf16[1024,1024]{1,0:T(8,128)(2,1)} %norm_rows.1.x_ref), channel_id=1, source_target_pairs={{0,16},{16,0},{1,17},{17,1},{2,18},{18,2},{3,19},{19,3},{4,20},{20... | collective-permute-start | bytes 6291464 | tf_op jit(solution)/shard_map/ppermute | solution.py:208
  21.8 199.9 %copy-start.35 = (s32[1,1024]{1,0:T(1,128)}, s32[1,1024]{1,0:T(1,128)S(1)}, u32[]{:S(2)}) copy-start(s32[1,1024]{1,0:T(1,128)S(1)} %get-tuple-element.494.own_ref) | copy-start | bytes 12292
  49.3 90.0 %copy-start.41 = (s32[2,736]{1,0:T(2,128)S(1)}, s32[2,736]{1,0:T(2,128)}, u32[]{:S(2)}) copy-start(s32[2,736]{1,0:T(2,128)} %constant.397.clone) | copy-start | bytes 17668
  91.8 57.5 %copy-start.11 = (bf16[1024,1024]{1,0:T(8,128)(2,1)}, bf16[1024,1024]{1,0:T(8,128)(2,1)S(1)}, u32[]{:S(2)}) copy-start(bf16[1024,1024]{1,0:T(8,128)(2,1)S(1)} %collective-permute-done.32.x_ref) | copy-start | bytes 6291460
  139.0 859.1 %reduce-scatter.9.cloned.1.call-start = ((), (), s32[]{:S(2)}) async-start(), calls=%async_computation.8 | async-start | bytes 3604480 | tf_op jit(solution)/shard_map/reduce_scatter | solution.py:1586
  164.8 48.0 %collective-permute-start.35 = (bf16[1024,1024]{1,0:T(8,128)(2,1)}, bf16[1024,1024]{1,0:T(8,128)(2,1)S(1)}, u32[]{:S(2)}, u32[]{:S(2)}) collective-permute-start(bf16[1024,1024]{1,0:T(8,128)(2,1)} %ffn_part.3), channel_id=1, source_target_pairs={{0,16},{16,0},{1,17},{17,1},{2,18},{18,2},{3,19},{19,3},{4,20},{20... | collective-permute-start | bytes 6291464 | tf_op jit(solution)/shard_map/ppermute | solution.py:208
  220.3 47.3 %collective-permute-start.36 = (bf16[1024,1024]{1,0:T(8,128)(2,1)}, bf16[1024,1024]{1,0:T(8,128)(2,1)S(1)}, u32[]{:S(2)}, u32[]{:S(2)}) collective-permute-start(bf16[1024,1024]{1,0:T(8,128)(2,1)} %get-tuple-element.293.x_ref.n_ref.refs_0_), channel_id=1, source_target_pairs={{0,16},{16,0},{1,17},{17,1},{2,18},{18,2},{3,19},{19,3},{4,20},{20... | collective-permute-start | bytes 6291464 | tf_op jit(solution)/shard_map/ppermute | solution.py:208
  343.1 19.4 %collective-permute-start.38 = (f32[16,1024]{1,0:T(8,128)S(1)}, f32[16,1024]{1,0:T(8,128)S(1)}, u32[]{:S(2)}, u32[]{:S(2)}) collective-permute-start(f32[16,1024]{1,0:T(8,128)S(1)} %get-tuple-element.576), channel_id=1, source_target_pairs={{16,0},{17,1},{18,2},{19,3},{20,4},{21,5},{22,6},{23,7},{24,8},{25... | collective-permute-start | bytes 196616 | tf_op jit(solution)/shard_map/ppermute | solution.py:1618
  344.4 18.1 %collective-permute-start.37 = (f32[16,1024]{1,0:T(8,128)S(1)}, f32[16,1024]{1,0:T(8,128)S(1)}, u32[]{:S(2)}, u32[]{:S(2)}) collective-permute-start(f32[16,1024]{1,0:T(8,128)S(1)} %get-tuple-element.577), channel_id=1, source_target_pairs={{0,16},{1,17},{2,18},{3,19},{4,20},{5,21},{6,22},{7,23},{8,24},{9,... | collective-permute-start | bytes 196616 | tf_op jit(solution)/shard_map/ppermute | solution.py:1617
  478.2 12.1 %copy-start = (f32[1024,1024]{1,0:T(8,128)S(1)}, f32[1024,1024]{1,0:T(8,128)}, u32[]{:S(2)}) copy-start(f32[1024,1024]{1,0:T(8,128)} %get-tuple-element.312.g_ref) | copy-start | bytes 12582916
  483.1 58.7 %collective-permute-start.39 = (bf16[128,128,128]{2,1,0:T(8,128)(2,1)}, bf16[128,128,128]{2,1,0:T(8,128)(2,1)S(1)}, u32[]{:S(2)}, u32[]{:S(2)}) collective-permute-start(bf16[128,128,128]{2,1,0:T(8,128)(2,1)} %slice.571), channel_id=1, source_target_pairs={{0,1},{1,0},{2,3},{3,2},{4,5},{5,4},{6,7},{7,6},{8,9},{9,8},{10,11... | collective-permute-start | bytes 12582920 | tf_op jit(solution)/shard_map/ppermute | solution.py:208
  490.7 5.9 collective-permute-start.41
  492.0 6.1 collective-permute-start.40
  547.3 8.7 copy-start.28
  551.3 76.8 %collective-permute-start.44 = (bf16[96,128,128]{2,1,0:T(8,128)(2,1)}, bf16[96,128,128]{2,1,0:T(8,128)(2,1)S(1)}, u32[]{:S(2)}, u32[]{:S(2)}) collective-permute-start(bf16[96,128,128]{2,1,0:T(8,128)(2,1)} %slice.578), channel_id=1, source_target_pairs={{0,1},{1,0},{2,3},{3,2},{4,5},{5,4},{6,7},{7,6},{8,9},{9,8},{10,11... | collective-permute-start | bytes 9437192 | tf_op jit(solution)/shard_map/ppermute | solution.py:208
  551.3 76.8 %collective-permute-start.42 = (bf16[32,128,128]{2,1,0:T(8,128)(2,1)}, bf16[32,128,128]{2,1,0:T(8,128)(2,1)}, u32[]{:S(2)}, u32[]{:S(2)}) collective-permute-start(bf16[32,128,128]{2,1,0:T(8,128)(2,1)} %get-tuple-element.327), channel_id=1, source_target_pairs={{0,2},{2,0},{1,3},{3,1},{4,6},{6,4},{5,7},{7,5},{8,10},{10,8},{9,1... | collective-permute-start | bytes 3145736 | tf_op jit(solution)/shard_map/ppermute | solution.py:208
  553.7 74.5 %collective-permute-start.43 = (bf16[32,128,128]{2,1,0:T(8,128)(2,1)}, bf16[32,128,128]{2,1,0:T(8,128)(2,1)}, u32[]{:S(2)}, u32[]{:S(2)}) collective-permute-start(bf16[32,128,128]{2,1,0:T(8,128)(2,1)} %get-tuple-element.328), channel_id=1, source_target_pairs={{0,16},{16,0},{1,17},{17,1},{2,18},{18,2},{3,19},{19,3},{4,20},{20... | collective-permute-start | bytes 3145736 | tf_op jit(solution)/shard_map/ppermute | solution.py:208
  630.0 40.5 %collective-permute-start.45 = (bf16[1024,1024]{1,0:T(8,128)(2,1)}, bf16[1024,1024]{1,0:T(8,128)(2,1)}, u32[]{:S(2)}, u32[]{:S(2)}) collective-permute-start(bf16[1024,1024]{1,0:T(8,128)(2,1)} %input_gradient.1), channel_id=1, source_target_pairs={{0,16},{16,0},{1,17},{17,1},{2,18},{18,2},{3,19},{19,3},{4,20},{20... | collective-permute-start | bytes 6291464 | tf_op jit(solution)/shard_map/ppermute | solution.py:208
  675.3 60.6 %collective-permute-start.50 = (bf16[128,128,128]{2,1,0:T(8,128)(2,1)}, bf16[128,128,128]{2,1,0:T(8,128)(2,1)}, u32[]{:S(2)}, u32[]{:S(2)}) collective-permute-start(bf16[128,128,128]{2,1,0:T(8,128)(2,1)} %slice.589), channel_id=1, source_target_pairs={{0,1},{1,0},{2,3},{3,2},{4,5},{5,4},{6,7},{7,6},{8,9},{9,8},{10,11... | collective-permute-start | bytes 12582920 | tf_op jit(solution)/shard_map/ppermute | solution.py:208
  692.3 43.6 %collective-permute-start.46 = (bf16[16,128,128]{2,1,0:T(8,128)(2,1)}, bf16[16,128,128]{2,1,0:T(8,128)(2,1)}, u32[]{:S(2)}, u32[]{:S(2)}) collective-permute-start(bf16[16,128,128]{2,1,0:T(8,128)(2,1)} %get-tuple-element.363), channel_id=1, source_target_pairs={{0,16},{16,0},{1,17},{17,1},{2,18},{18,2},{3,19},{19,3},{4,20},{20... | collective-permute-start | bytes 1572872 | tf_op jit(solution)/shard_map/ppermute | solution.py:208
  693.3 42.6 %collective-permute-start.47 = (bf16[16,128,128]{2,1,0:T(8,128)(2,1)}, bf16[16,128,128]{2,1,0:T(8,128)(2,1)}, u32[]{:S(2)}, u32[]{:S(2)}) collective-permute-start(bf16[16,128,128]{2,1,0:T(8,128)(2,1)} %get-tuple-element.364), channel_id=1, source_target_pairs={{0,2},{2,0},{1,3},{3,1},{4,6},{6,4},{5,7},{7,5},{8,10},{10,8},{9,1... | collective-permute-start | bytes 1572872 | tf_op jit(solution)/shard_map/ppermute | solution.py:208
  693.3 42.6 %collective-permute-start.48 = (bf16[24,128,128]{2,1,0:T(8,128)(2,1)S(1)}, bf16[24,128,128]{2,1,0:T(8,128)(2,1)}, u32[]{:S(2)}, u32[]{:S(2)}) collective-permute-start(bf16[24,128,128]{2,1,0:T(8,128)(2,1)S(1)} %get-tuple-element.365), channel_id=1, source_target_pairs={{0,2},{2,0},{1,3},{3,1},{4,6},{6,4},{5,7},{7,5},{8,10},{10,8},{9,1... | collective-permute-start | bytes 2359304 | tf_op jit(solution)/shard_map/ppermute | solution.py:208
  695.3 40.6 %collective-permute-start.49 = (bf16[24,128,128]{2,1,0:T(8,128)(2,1)S(1)}, bf16[24,128,128]{2,1,0:T(8,128)(2,1)}, u32[]{:S(2)}, u32[]{:S(2)}) collective-permute-start(bf16[24,128,128]{2,1,0:T(8,128)(2,1)S(1)} %get-tuple-element.366), channel_id=1, source_target_pairs={{0,16},{16,0},{1,17},{17,1},{2,18},{18,2},{3,19},{19,3},{4,20},{20... | collective-permute-start | bytes 2359304 | tf_op jit(solution)/shard_map/ppermute | solution.py:208
  744.8 49.2 %collective-permute-start.51 = (bf16[12,128,128]{2,1,0:T(8,128)(2,1)S(1)}, bf16[12,128,128]{2,1,0:T(8,128)(2,1)S(1)}, u32[]{:S(2)}, u32[]{:S(2)}) collective-permute-start(bf16[12,128,128]{2,1,0:T(8,128)(2,1)S(1)} %get-tuple-element.389), channel_id=1, source_target_pairs={{0,16},{16,0},{1,17},{17,1},{2,18},{18,2},{3,19},{19,3},{4,20},{20... | collective-permute-start | bytes 1179656 | tf_op jit(solution)/shard_map/ppermute | solution.py:208
  750.7 43.4 %collective-permute-start.52 = (bf16[12,128,128]{2,1,0:T(8,128)(2,1)S(1)}, bf16[12,128,128]{2,1,0:T(8,128)(2,1)S(1)}, u32[]{:S(2)}, u32[]{:S(2)}) collective-permute-start(bf16[12,128,128]{2,1,0:T(8,128)(2,1)S(1)} %get-tuple-element.390), channel_id=1, source_target_pairs={{0,2},{2,0},{1,3},{3,1},{4,6},{6,4},{5,7},{7,5},{8,10},{10,8},{9,1... | collective-permute-start | bytes 1179656 | tf_op jit(solution)/shard_map/ppermute | solution.py:208
  750.7 43.3 %collective-permute-start.53 = (bf16[32,128,128]{2,1,0:T(8,128)(2,1)}, bf16[32,128,128]{2,1,0:T(8,128)(2,1)S(1)}, u32[]{:S(2)}, u32[]{:S(2)}) collective-permute-start(bf16[32,128,128]{2,1,0:T(8,128)(2,1)} %get-tuple-element.391), channel_id=1, source_target_pairs={{0,2},{2,0},{1,3},{3,1},{4,6},{6,4},{5,7},{7,5},{8,10},{10,8},{9,1... | collective-permute-start | bytes 3145736 | tf_op jit(solution)/shard_map/ppermute | solution.py:208
  752.7 41.4 %collective-permute-start.54 = (bf16[32,128,128]{2,1,0:T(8,128)(2,1)S(1)}, bf16[32,128,128]{2,1,0:T(8,128)(2,1)S(1)}, u32[]{:S(2)}, u32[]{:S(2)}) collective-permute-start(bf16[32,128,128]{2,1,0:T(8,128)(2,1)S(1)} %get-tuple-element.392), channel_id=1, source_target_pairs={{0,16},{16,0},{1,17},{17,1},{2,18},{18,2},{3,19},{19,3},{4,20},{20... | collective-permute-start | bytes 3145736 | tf_op jit(solution)/shard_map/ppermute | solution.py:208
  798.2 19.0 %collective-permute-start.57 = (bf16[288,128,128]{2,1,0:T(8,128)(2,1)}, bf16[288,128,128]{2,1,0:T(8,128)(2,1)}, u32[]{:S(2)}, u32[]{:S(2)}) collective-permute-start(bf16[288,128,128]{2,1,0:T(8,128)(2,1)} %get-tuple-element.415), channel_id=1, source_target_pairs={{0,1},{1,0},{2,3},{3,2},{4,5},{5,4},{6,7},{7,6},{8,9},{9,8},{10,11... | collective-permute-start | bytes 28311560 | tf_op jit(solution)/shard_map/ppermute | solution.py:208
  802.4 14.6 %collective-permute-start.55 = (bf16[16,128,128]{2,1,0:T(8,128)(2,1)}, bf16[16,128,128]{2,1,0:T(8,128)(2,1)S(1)}, u32[]{:S(2)}, u32[]{:S(2)}) collective-permute-start(bf16[16,128,128]{2,1,0:T(8,128)(2,1)} %get-tuple-element.413), channel_id=1, source_target_pairs={{0,16},{16,0},{1,17},{17,1},{2,18},{18,2},{3,19},{19,3},{4,20},{20... | collective-permute-start | bytes 1572872 | tf_op jit(solution)/shard_map/ppermute | solution.py:208
  802.5 14.7 %collective-permute-start.56 = (bf16[16,128,128]{2,1,0:T(8,128)(2,1)}, bf16[16,128,128]{2,1,0:T(8,128)(2,1)}, u32[]{:S(2)}, u32[]{:S(2)}) collective-permute-start(bf16[16,128,128]{2,1,0:T(8,128)(2,1)} %get-tuple-element.414), channel_id=1, source_target_pairs={{0,2},{2,0},{1,3},{3,1},{4,6},{6,4},{5,7},{7,5},{8,10},{10,8},{9,1... | collective-permute-start | bytes 1572872 | tf_op jit(solution)/shard_map/ppermute | solution.py:208
  805.2 18.4 %copy-start.14 = (bf16[32,128,128]{2,1,0:T(8,128)(2,1)S(1)}, bf16[32,128,128]{2,1,0:T(8,128)(2,1)}, u32[]{:S(2)}) copy-start(bf16[32,128,128]{2,1,0:T(8,128)(2,1)} %copy-done.13) | copy-start | bytes 3145732
  805.2 18.4 %copy-start.16 = (bf16[32,128,128]{2,1,0:T(8,128)(2,1)S(1)}, bf16[32,128,128]{2,1,0:T(8,128)(2,1)}, u32[]{:S(2)}) copy-start(bf16[32,128,128]{2,1,0:T(8,128)(2,1)} %copy-done.15) | copy-start | bytes 3145732
  826.1 56.9 %collective-permute-start.60 = (bf16[96,128,128]{2,1,0:T(8,128)(2,1)}, bf16[96,128,128]{2,1,0:T(8,128)(2,1)}, u32[]{:S(2)}, u32[]{:S(2)}) collective-permute-start(bf16[96,128,128]{2,1,0:T(8,128)(2,1)} %slice.620), channel_id=1, source_target_pairs={{0,1},{1,0},{2,3},{3,2},{4,5},{5,4},{6,7},{7,6},{8,9},{9,8},{10,11... | collective-permute-start | bytes 9437192 | tf_op jit(solution)/shard_map/ppermute | solution.py:208
  827.7 170.4 %reduce-scatter.11.cloned.1.call-start = ((), (), s32[]{:S(2)}) async-start(), calls=%async_computation.9 | async-start | bytes 2949120 | tf_op jit(solution)/shard_map/reduce_scatter | solution.py:1586
  827.7 55.3 %collective-permute-start.58 = (bf16[72,128,128]{2,1,0:T(8,128)(2,1)}, bf16[72,128,128]{2,1,0:T(8,128)(2,1)S(1)}, u32[]{:S(2)}, u32[]{:S(2)}) collective-permute-start(bf16[72,128,128]{2,1,0:T(8,128)(2,1)} %get-tuple-element.429), channel_id=1, source_target_pairs={{0,2},{2,0},{1,3},{3,1},{4,6},{6,4},{5,7},{7,5},{8,10},{10,8},{9,1... | collective-permute-start | bytes 7077896 | tf_op jit(solution)/shard_map/ppermute | solution.py:208
  828.1 54.9 %collective-permute-start.59 = (bf16[72,128,128]{2,1,0:T(8,128)(2,1)}, bf16[72,128,128]{2,1,0:T(8,128)(2,1)S(1)}, u32[]{:S(2)}, u32[]{:S(2)}) collective-permute-start(bf16[72,128,128]{2,1,0:T(8,128)(2,1)} %get-tuple-element.430), channel_id=1, source_target_pairs={{0,16},{16,0},{1,17},{17,1},{2,18},{18,2},{3,19},{19,3},{4,20},{20... | collective-permute-start | bytes 7077896 | tf_op jit(solution)/shard_map/ppermute | solution.py:208
  829.7 2.2 collective-permute-start.61
  829.7 53.2 %collective-permute-start.62 = (f32[10,1024]{1,0:T(8,128)S(1)}, f32[10,1024]{1,0:T(8,128)S(1)}, u32[]{:S(2)}, u32[]{:S(2)}) collective-permute-start(f32[10,1024]{1,0:T(8,128)S(1)} %concatenate.46), channel_id=1, source_target_pairs={{0,2},{2,0},{1,3},{3,1},{4,6},{6,4},{5,7},{7,5},{8,10},{10,8},{9,1... | collective-permute-start | bytes 122888 | tf_op jit(solution)/shard_map/ppermute | solution.py:208
  831.9 51.1 %collective-permute-start.63 = (f32[10,1024]{1,0:T(8,128)S(1)}, f32[10,1024]{1,0:T(8,128)S(1)}, u32[]{:S(2)}, u32[]{:S(2)}) collective-permute-start(f32[10,1024]{1,0:T(8,128)S(1)} %concatenate.46), channel_id=1, source_target_pairs={{0,3},{1,2},{2,1},{3,0},{4,7},{5,6},{6,5},{7,4},{8,11},{9,10},{10,... | collective-permute-start | bytes 122888 | tf_op jit(solution)/shard_map/ppermute | solution.py:208
  886.8 31.6 %collective-permute-start.64 = (bf16[36,128,128]{2,1,0:T(8,128)(2,1)S(1)}, bf16[36,128,128]{2,1,0:T(8,128)(2,1)S(1)}, u32[]{:S(2)}, u32[]{:S(2)}) collective-permute-start(bf16[36,128,128]{2,1,0:T(8,128)(2,1)S(1)} %get-tuple-element.440), channel_id=1, source_target_pairs={{0,16},{16,0},{1,17},{17,1},{2,18},{18,2},{3,19},{19,3},{4,20},{20... | collective-permute-start | bytes 3538952 | tf_op jit(solution)/shard_map/ppermute | solution.py:208
  888.2 30.2 %collective-permute-start.65 = (bf16[36,128,128]{2,1,0:T(8,128)(2,1)S(1)}, bf16[36,128,128]{2,1,0:T(8,128)(2,1)S(1)}, u32[]{:S(2)}, u32[]{:S(2)}) collective-permute-start(bf16[36,128,128]{2,1,0:T(8,128)(2,1)S(1)} %get-tuple-element.441), channel_id=1, source_target_pairs={{0,2},{2,0},{1,3},{3,1},{4,6},{6,4},{5,7},{7,5},{8,10},{10,8},{9,1... | collective-permute-start | bytes 3538952 | tf_op jit(solution)/shard_map/ppermute | solution.py:208
  888.7 29.7 %collective-permute-start.66 = (f32[10,1024]{1,0:T(8,128)S(1)}, f32[10,1024]{1,0:T(8,128)S(1)}, u32[]{:S(2)}, u32[]{:S(2)}) collective-permute-start(f32[10,1024]{1,0:T(8,128)S(1)} %add_add_fusion.1), channel_id=1, source_target_pairs={{0,16},{16,0},{1,17},{17,1},{2,18},{18,2},{3,19},{19,3},{4,20},{20... | collective-permute-start | bytes 122888 | tf_op jit(solution)/shard_map/ppermute | solution.py:208
  889.3 29.1 %collective-permute-start.67 = (f32[10,1024]{1,0:T(8,128)S(1)}, f32[10,1024]{1,0:T(8,128)S(1)}, u32[]{:S(2)}, u32[]{:S(2)}) collective-permute-start(f32[10,1024]{1,0:T(8,128)S(1)} %add_add_fusion.1), channel_id=1, source_target_pairs={{0,4},{4,0},{8,12},{12,8},{1,5},{5,1},{9,13},{13,9},{2,6},{6,2},{1... | collective-permute-start | bytes 122888 | tf_op jit(solution)/shard_map/ppermute | solution.py:208
  898.6 19.8 %collective-permute-start.68 = (f32[10,1024]{1,0:T(8,128)S(1)}, f32[10,1024]{1,0:T(8,128)S(1)}, u32[]{:S(2)}, u32[]{:S(2)}) collective-permute-start(f32[10,1024]{1,0:T(8,128)S(1)} %add_add_fusion.1), channel_id=1, source_target_pairs={{0,20},{4,16},{8,28},{12,24},{16,4},{20,0},{24,12},{28,8},{1,21},{... | collective-permute-start | bytes 122888 | tf_op jit(solution)/shard_map/ppermute | solution.py:208
  924.4 19.5 %collective-permute-start.69 = (bf16[24,128,128]{2,1,0:T(8,128)(2,1)S(1)}, bf16[24,128,128]{2,1,0:T(8,128)(2,1)S(1)}, u32[]{:S(2)}, u32[]{:S(2)}) collective-permute-start(bf16[24,128,128]{2,1,0:T(8,128)(2,1)S(1)} %get-tuple-element.455), channel_id=1, source_target_pairs={{0,2},{2,0},{1,3},{3,1},{4,6},{6,4},{5,7},{7,5},{8,10},{10,8},{9,1... | collective-permute-start | bytes 2359304 | tf_op jit(solution)/shard_map/ppermute | solution.py:208
  925.0 19.2 %collective-permute-start.70 = (bf16[24,128,128]{2,1,0:T(8,128)(2,1)S(1)}, bf16[24,128,128]{2,1,0:T(8,128)(2,1)S(1)}, u32[]{:S(2)}, u32[]{:S(2)}) collective-permute-start(bf16[24,128,128]{2,1,0:T(8,128)(2,1)S(1)} %get-tuple-element.456), channel_id=1, source_target_pairs={{0,16},{16,0},{1,17},{17,1},{2,18},{18,2},{3,19},{19,3},{4,20},{20... | collective-permute-start | bytes 2359304 | tf_op jit(solution)/shard_map/ppermute | solution.py:208
  926.4 9.0 collective-permute-start.71
  946.0 10.1 collective-permute-start.72
  947.5 9.8 collective-permute-start.73
  959.3 24.4 %collective-permute-start.74 = (bf16[6,128,128]{2,1,0:T(8,128)(2,1)S(1)}, bf16[6,128,128]{2,1,0:T(8,128)(2,1)S(1)}, u32[]{:S(2)}, u32[]{:S(2)}) collective-permute-start(bf16[6,128,128]{2,1,0:T(8,128)(2,1)S(1)} %get-tuple-element.464), channel_id=1, source_target_pairs={{0,8},{4,12},{1,9},{5,13},{2,10},{6,14},{3,11},{7,15},{16,24},{20,... | collective-permute-start | bytes 589832 | tf_op jit(solution)/shard_map/ppermute | solution.py:208
  967.8 19.7 %collective-permute-start.75 = (bf16[6,128,128]{2,1,0:T(8,128)(2,1)S(1)}, bf16[6,128,128]{2,1,0:T(8,128)(2,1)S(1)}, u32[]{:S(2)}, u32[]{:S(2)}) collective-permute-start(bf16[6,128,128]{2,1,0:T(8,128)(2,1)S(1)} %get-tuple-element.465), channel_id=1, source_target_pairs={{8,0},{12,4},{9,1},{13,5},{10,2},{14,6},{11,3},{15,7},{24,16},{28,... | collective-permute-start | bytes 589832 | tf_op jit(solution)/shard_map/ppermute | solution.py:208
  969.1 18.4 %collective-permute-start.76 = (bf16[6,128,128]{2,1,0:T(8,128)(2,1)S(1)}, bf16[6,128,128]{2,1,0:T(8,128)(2,1)S(1)}, u32[]{:S(2)}, u32[]{:S(2)}) collective-permute-start(bf16[6,128,128]{2,1,0:T(8,128)(2,1)S(1)} %get-tuple-element.466), channel_id=1, source_target_pairs={{0,4},{4,8},{8,12},{1,5},{5,9},{9,13},{2,6},{6,10},{10,14},{3,7},{... | collective-permute-start | bytes 589832 | tf_op jit(solution)/shard_map/ppermute | solution.py:208
  974.8 12.7 %collective-permute-start.77 = (bf16[6,128,128]{2,1,0:T(8,128)(2,1)S(1)}, bf16[6,128,128]{2,1,0:T(8,128)(2,1)S(1)}, u32[]{:S(2)}, u32[]{:S(2)}) collective-permute-start(bf16[6,128,128]{2,1,0:T(8,128)(2,1)S(1)} %get-tuple-element.467), channel_id=1, source_target_pairs={{4,0},{8,4},{12,8},{5,1},{9,5},{13,9},{6,2},{10,6},{14,10},{7,3},{... | collective-permute-start | bytes 589832 | tf_op jit(solution)/shard_map/ppermute | solution.py:208
  976.1 12.4 %collective-permute-start.78 = (bf16[6,128,128]{2,1,0:T(8,128)(2,1)S(1)}, bf16[6,128,128]{2,1,0:T(8,128)(2,1)S(1)}, u32[]{:S(2)}, u32[]{:S(2)}) collective-permute-start(bf16[6,128,128]{2,1,0:T(8,128)(2,1)S(1)} %get-tuple-element.468), channel_id=1, source_target_pairs={{0,12},{1,13},{2,14},{3,15},{16,28},{17,29},{18,30},{19,31}} | collective-permute-start | bytes 589832 | tf_op jit(solution)/shard_map/ppermute | solution.py:208
  983.6 14.2 %collective-permute-start.79 = (bf16[6,128,128]{2,1,0:T(8,128)(2,1)S(1)}, bf16[6,128,128]{2,1,0:T(8,128)(2,1)S(1)}, u32[]{:S(2)}, u32[]{:S(2)}) collective-permute-start(bf16[6,128,128]{2,1,0:T(8,128)(2,1)S(1)} %get-tuple-element.469), channel_id=1, source_target_pairs={{12,0},{13,1},{14,2},{15,3},{28,16},{29,17},{30,18},{31,19}} | collective-permute-start | bytes 589832 | tf_op jit(solution)/shard_map/ppermute | solution.py:208
  984.9 14.7 %copy-start.45 = (s32[46]{0:T(128)S(1)}, s32[46]{0:T(128)}, u32[]{:S(2)}) copy-start(s32[46]{0:T(128)} %select_reduce_fusion) | copy-start | bytes 556
  984.9 15.4 %copy-start.32 = (f32[5,1024]{1,0:T(8,128)S(1)}, f32[5,1024]{1,0:T(8,128)}, u32[]{:S(2)}) copy-start(f32[5,1024]{1,0:T(8,128)} %param.25) | copy-start | bytes 61444
  984.9 16.1 %copy-start.26 = (f32[5,1024]{1,0:T(8,128)S(1)}, f32[5,1024]{1,0:T(8,128)}, u32[]{:S(2)}) copy-start(f32[5,1024]{1,0:T(8,128)} %taps_ref.3) | copy-start | bytes 61444
  999.5 3.5 collective-permute-start.80
  (23 other events, 75.9 us)
Sparse Core Ops, SparseCore 0:
  10.6 126.3 all-gather.2
  139.1 123.6 all-gather.4
  827.8 64.0 reduce-scatter.8
  924.5 61.3 reduce-scatter.10
